TPU v7x, 32 devices: a whole 2x2x4 slice. The times are simulated.
32 devices in a mesh: dp: 4 (over z), row: 2 (over core), col: 4 (over y, x).
Axes of the slice: x: 2, y: 2, z: 4, core: 2. Of those that a mesh axis runs over, the one named last changes fastest.
Arguments:
- x_input: bfloat16 [4, 32, 64, 640], P('dp', 'row', 'col'), may hold values from -6 to 6
- pre_act: bfloat16 [4, 32, 64, 640], P('dp', 'row', 'col'), may hold values from -6 to 6
- out_grad: bfloat16 [4, 32, 64, 640], P('dp', 'row', 'col'), may hold values from -0.15625 to 0.15625
- conv_weight: bfloat16 [3, 3, 640, 640], replicated, may hold values from -0.078125 to 0.078125
- q_prev: float32 [5760, 2, 64], replicated, may hold values from -6 to 6
Outputs:
- p_basis: float32 [640, 2, 64], P('dp')
- q_next: float32 [5760, 2, 64], P('dp')
All inputs are finite; a program needn't handle non-finite values.
Results may differ from a plain program's by a relative error of at most 0.0036.
Values may be sent and summed in bfloat16 or wider, within the bound.
No kernel may reach another device: no remote copies, remote signals or barrier semaphores. Data moves between devices by JAX's collectives and lax.ppermute only.
A program may use at most 128 MiB of HBM per device.

v0:
```python
import jax
import jax.numpy as jnp
from jax import lax
from jax.sharding import PartitionSpec as P


def padded_2(value, sides, width):
    for axis, dim in sides:
        size, length = (lax.axis_size(axis), value.shape[dim])
        up = [(i, (i + 1) % size) for i in range(size - 1)]
        down = [(j, i) for i, j in up]
        last = lax.slice_in_dim(value, length - width, length, axis=dim)
        leading = lax.slice_in_dim(value, 0, width, axis=dim)
        before = lax.ppermute(last, axis, up)
        after = lax.ppermute(leading, axis, down)
        value = jnp.concatenate([before, value, after], axis=dim)
    return value


def silu_slope(pre_float):
    sigma = jax.nn.sigmoid(pre_float)
    return sigma * (1.0 + pre_float * (1.0 - sigma))


def contract_first(left, right, exact):
    if exact:
        return lax.dot_general(
            left,
            right,
            (((0,), (0,)), ((), ())),
            precision=lax.Precision.HIGHEST,
            preferred_element_type=jnp.float32,
        )
    return lax.dot_general(
        left, right, (((0,), (0,)), ((), ())), preferred_element_type=jnp.float32
    )


def tap_window(padded, shift_row, shift_col, height, breadth):
    return padded[
        1 + shift_row : 1 + shift_row + height, 1 + shift_col : 1 + shift_col + breadth, :
    ].reshape(height * breadth, padded.shape[2])


def column_terms(moments, q_prev):
    return jnp.stack(
        [contract_first(moments[layer], q_prev[:, layer, :], True) for layer in range(2)], axis=1
    )


def row_terms(moments, ortho_basis):
    return jnp.stack(
        [
            jnp.dot(
                moments[layer],
                ortho_basis[:, layer, :],
                precision=lax.Precision.HIGHEST,
                preferred_element_type=jnp.float32,
            )
            for layer in range(2)
        ],
        axis=1,
    )


def gram_of(power_raw):
    return jnp.einsum(
        "mqn,mqg->qng",
        power_raw,
        power_raw,
        precision=lax.Precision.HIGHEST,
        preferred_element_type=jnp.float32,
    )


def orthonormal(power_raw, gram_matrix):
    bases = []
    for layer in range(2):
        lower = jnp.linalg.cholesky(gram_matrix[layer])
        bases.append(
            lax.linalg.triangular_solve(
                lower, power_raw[:, layer, :], left_side=False, lower=True, transpose_a=True
            )
        )
    return jnp.stack(bases, axis=1)


def on_device(x_input, pre_act, out_grad, conv_weight, q_prev):
    height, breadth, channels = (x_input.shape[1], x_input.shape[2], x_input.shape[3])
    pixels = height * breadth
    input_tile = x_input.reshape(height, breadth, channels)
    grad_tile = out_grad.reshape(height, breadth, channels)
    pre_float = pre_act.reshape(pixels, channels).astype(jnp.float32)
    hidden_flat = jax.nn.silu(pre_float).astype(jnp.bfloat16)
    grad_pad = padded_2(grad_tile, (("row", 0), ("col", 1)), 1)
    back_grad = jnp.zeros((pixels, channels), jnp.float32)
    second_taps = []
    for shift_row in (-1, 0, 1):
        for shift_col in (-1, 0, 1):
            window = tap_window(grad_pad, -shift_row, -shift_col, height, breadth)
            back_grad = back_grad + lax.dot_general(
                window,
                conv_weight[shift_row + 1, shift_col + 1],
                (((1,), (1,)), ((), ())),
                preferred_element_type=jnp.float32,
            )
            second_taps.append(contract_first(hidden_flat, window, False))
    pre_grad = (back_grad * silu_slope(pre_float)).astype(jnp.bfloat16)
    first_taps = []
    deriv_pad = padded_2(pre_grad.reshape(height, breadth, channels), (("row", 0), ("col", 1)), 1)
    input_flat = input_tile.reshape(pixels, channels)
    for shift_row in (-1, 0, 1):
        for shift_col in (-1, 0, 1):
            first_taps.append(
                contract_first(
                    input_flat,
                    tap_window(deriv_pad, -shift_row, -shift_col, height, breadth),
                    False,
                )
            )
    moments = jnp.stack(
        [
            jnp.stack(first_taps).reshape(9 * channels, channels),
            jnp.stack(second_taps).reshape(9 * channels, channels),
        ]
    )
    kernel_rows = moments.shape[1]
    owner = lax.axis_index("dp")
    basis_count = channels // lax.axis_size("dp")
    factor_count = kernel_rows // lax.axis_size("dp")
    power_raw = lax.psum(column_terms(moments, q_prev), ("dp", "row", "col"))
    ortho_basis = orthonormal(power_raw, gram_of(power_raw))
    factor_full = lax.psum(row_terms(moments, ortho_basis), ("dp", "row", "col"))
    basis_out = lax.dynamic_slice_in_dim(ortho_basis, owner * basis_count, basis_count, 0)
    factor_out = lax.dynamic_slice_in_dim(factor_full, owner * factor_count, factor_count, 0)
    return (basis_out, factor_out)


def solution(mesh):
    placed = (
        P("dp", "row", "col", None),
        P("dp", "row", "col", None),
        P("dp", "row", "col", None),
        P(),
        P(),
    )
    return jax.shard_map(
        on_device,
        mesh=mesh,
        in_specs=placed,
        out_specs=(P("dp", None, None), P("dp", None, None)),
        check_vma=False,
    )
```

profile of v0, /device:TPU:0, one launch (start us, length us, event | category | flops | bytes accessed | tf_op | source)
XLA Modules:
  0.0 412.3 jit_solution(13808722130785662484)
XLA Ops:
  7.2 0.8 slice_bitcast_fusion.9
  8.0 1.3 collective-permute-start.1
  9.3 3.0 collective-permute-start
  12.3 1.2 fusion.43
  13.5 1.2 fusion.38
  14.7 1.1 pad_maximum_fusion.11
  15.8 4.8 %collective-permute-start.3 = (bf16[18,1,640]{2,1,0:T(2,128)(2,1)S(1)}, bf16[18,1,640]{2,1,0:T(2,128)(2,1)S(1)}, u32[]{:S(2)}, u32[]{:S(2)}) collective-permute-start(bf16[18,1,640]{2,1,0:T(2,128)(2,1)S(1)} %get-tuple-element.22), channel_id=1, source_target_pairs={{0,1},{1,2},{2,3},{4,5},{5,6},{6,7},{8,9},{9,10},{10,11},{12,13},{... | collective-permute-start | bytes 69128 | tf_op jit(solution)/shard_map/ppermute | solution.py:14
  20.7 1.3 collective-permute-start.2
  22.0 1.1 pad_maximum_fusion.5
  23.1 1.6 fusion.23
  24.8 1.9 collective-permute-done.2
  26.6 1.3 maximum_maximum_fusion
  28.6 0.5 bitcast_dynamic-update-slice_fusion.16
  29.0 0.5 bitcast_dynamic-update-slice_fusion.15
  29.5 0.5 bitcast_dynamic-update-slice_fusion.14
  30.0 0.5 bitcast_dynamic-update-slice_fusion.13
  30.6 1.1 slice-done.4
  31.7 1.1 slice-done.5
  33.8 0.5 bitcast_dynamic-update-slice_fusion.11
  34.2 0.5 bitcast_dynamic-update-slice_fusion.10
  34.7 0.5 bitcast_dynamic-update-slice_fusion.9
  35.7 0.5 convolution_add_fusion.5
  38.0 0.5 fusion.8
  38.5 1.4 collective-permute-start.5
  40.0 3.5 collective-permute-start.4
  43.5 8.8 %fusion.12 = f32[640,1,64]{0,2,1:T(8,128)S(1)} fusion(f32[5760,640]{1,0:T(8,128)S(1)} %bitcast.253, f32[5760,2,64]{0,2,1:T(8,128)S(1)} %copy-done.5), kind=kOutput, calls=%fused_computation.38 | convolution fusion | flops 2831155200 | bytes 16384000 | tf_op jit(solution)/shard_map/dot_general | solution.py:27
  52.4 4.3 %collective-permute-start.7 = (bf16[18,1,640]{2,1,0:T(2,128)(2,1)S(1)}, bf16[18,1,640]{2,1,0:T(2,128)(2,1)S(1)}, u32[]{:S(2)}, u32[]{:S(2)}) collective-permute-start(bf16[18,1,640]{2,1,0:T(2,128)(2,1)S(1)} %get-tuple-element.18), channel_id=1, source_target_pairs={{0,1},{1,2},{2,3},{4,5},{5,6},{6,7},{8,9},{9,10},{10,11},{12,13},{... | collective-permute-start | bytes 69128 | tf_op jit(solution)/shard_map/ppermute | solution.py:14
  56.7 1.5 collective-permute-start.6
  58.4 4.2 %collective-permute-done.6 = bf16[18,1,640]{2,1,0:T(2,128)(2,1)S(1)} collective-permute-done((bf16[18,1,640]{2,1,0:T(2,128)(2,1)S(1)}, bf16[18,1,640]{2,1,0:T(2,128)(2,1)S(1)}, u32[]{:S(2)}, u32[]{:S(2)}) %collective-permute-start.6) | collective-permute-done | bytes 23072 | tf_op jit(solution)/shard_map/ppermute | solution.py:15
  67.4 9.0 %fusion.9 = f32[640,1,64]{0,2,1:T(8,128)S(1)} fusion(f32[5760,640]{1,0:T(8,128)S(1)} %bitcast.249, f32[5760,2,64]{0,2,1:T(8,128)S(1)} %copy-done.5), kind=kOutput, calls=%fused_computation.37 | convolution fusion | flops 2831155200 | bytes 16384000 | tf_op jit(solution)/shard_map/dot_general | solution.py:27
  76.4 0.7 pad_maximum_fusion.7
  77.3 126.3 %all-reduce.3.cloned.1.call-done = f32[640,2,64]{0,2,1:T(8,128)} async-done(((f32[640,2,64]{0,2,1:T(8,128)}), f32[640,2,64]{0,2,1:T(8,128)}) %all-reduce.3.cloned.1.call-update) | async-done | bytes 327696 | tf_op jit(solution)/shard_map/psum | solution.py:131
  203.5 1.5 fusion.62
  205.3 5.8 %cholesky.44 = f32[64,64]{1,0:T(8,128)S(1)} custom-call(f32[64,64]{1,0:T(8,128)S(1)} %get-tuple-element.33), custom_call_target="Cholesky" | custom-call | tf_op jit(solution)/shard_map/jit(cholesky)/cholesky | solution.py:79
  211.1 0.6 compare_reduce_fusion.1
  211.8 0.7 fusion.50
  212.4 4.9 %custom-call.6 = f32[1,64,64]{1,2,0:T(8,128)S(1)} custom-call(f32[1,64,64]{2,1,0:T(8,128)S(1)} %fusion.50), custom_call_target="InvertDiagBlocksLowerTriangular" | custom-call | tf_op jit(solution)/shard_map/triangular_solve/custom-call.0 | solution.py:81
  217.3 5.9 %cholesky.55 = f32[64,64]{1,0:T(8,128)S(1)} custom-call(f32[64,64]{1,0:T(8,128)S(1)} %get-tuple-element.32), custom_call_target="Cholesky" | custom-call | tf_op jit(solution)/shard_map/jit(cholesky)/cholesky | solution.py:79
  223.2 0.6 compare_reduce_fusion
  223.9 0.7 fusion.51
  224.5 4.9 %custom-call.7 = f32[1,64,64]{1,2,0:T(8,128)S(1)} custom-call(f32[1,64,64]{2,1,0:T(8,128)S(1)} %fusion.51), custom_call_target="InvertDiagBlocksLowerTriangular" | custom-call | tf_op jit(solution)/shard_map/triangular_solve/custom-call.0 | solution.py:81
  229.5 1.4 fusion.45
  230.9 17.4 %convolution_bitcast_fusion = f32[5760,1,64]{0,2,1:T(8,128)S(1)} fusion(f32[5760,640]{1,0:T(8,128)} %bitcast.254, f32[64,640]{1,0:T(8,128)S(1)} %fusion.45), kind=kOutput, calls=%fused_computation | convolution fusion | flops 2831155200 | bytes 16384000 | tf_op jit(solution)/shard_map/dot_general | solution.py:54
  248.7 14.2 %convolution_bitcast_fusion.1 = f32[5760,1,64]{0,2,1:T(8,128)S(1)} fusion(f32[5760,640]{1,0:T(8,128)S(1)} %bitcast.252, f32[64,640]{1,0:T(8,128)S(1)} %fusion.46), kind=kOutput, calls=%fused_computation.1 | convolution fusion | flops 2831155200 | bytes 16384000 | tf_op jit(solution)/shard_map/dot_general | solution.py:54
  262.9 1.8 pad_maximum_fusion
  264.8 0.8 fusion.49
  265.5 137.2 %all-reduce.5.cloned.1.call-done = f32[5760,2,64]{0,2,1:T(8,128)} async-done(((f32[5760,2,64]{0,2,1:T(8,128)}), f32[5760,2,64]{0,2,1:T(8,128)}) %all-reduce.5.cloned.1.call-update) | async-done | bytes 2949136 | tf_op jit(solution)/shard_map/psum | solution.py:133
  402.7 2.3 constant_dynamic-slice_fusion
  (67 shorter events, 9.6 us)
Async XLA Ops:
  7.2 56.0 %copy-start = (bf16[1,16,16,640]{3,2,1,0:T(8,128)(2,1)S(1)}, bf16[1,16,16,640]{3,2,1,0:T(8,128)(2,1)}, u32[]{:S(2)}) copy-start(bf16[1,16,16,640]{3,2,1,0:T(8,128)(2,1)} %param.8) | copy-start | bytes 983044
  7.2 196.3 %all-reduce.3.cloned.1.call-start = ((), (), s32[]{:S(2)}) async-start(), calls=%async_computation | async-start | bytes 655360 | tf_op jit(solution)/shard_map/psum | solution.py:131
  8.0 6.7 %collective-permute-start.1 = (bf16[1,16,640]{2,1,0:T(8,128)(2,1)S(1)}, bf16[1,16,640]{2,1,0:T(8,128)(2,1)S(1)}, u32[]{:S(2)}, u32[]{:S(2)}) collective-permute-start(bf16[1,16,640]{2,1,0:T(8,128)(2,1)S(1)} %get-tuple-element.31), channel_id=1, source_target_pairs={{4,0},{5,1},{6,2},{7,3},{12,8},{13,9},{14,10},{15,11},{20,16},{21,... | collective-permute-start | bytes 61448 | tf_op jit(solution)/shard_map/ppermute | solution.py:15
  9.3 5.4 %collective-permute-start = (bf16[1,16,640]{2,1,0:T(8,128)(2,1)S(1)}, bf16[1,16,640]{2,1,0:T(8,128)(2,1)S(1)}, u32[]{:S(2)}, u32[]{:S(2)}) collective-permute-start(bf16[1,16,640]{2,1,0:T(8,128)(2,1)S(1)} %get-tuple-element.30), channel_id=1, source_target_pairs={{0,4},{1,5},{2,6},{3,7},{8,12},{9,13},{10,14},{11,15},{16,20},{17,... | collective-permute-start | bytes 61448 | tf_op jit(solution)/shard_map/ppermute | solution.py:14
  15.8 8.9 %collective-permute-start.3 = (bf16[18,1,640]{2,1,0:T(2,128)(2,1)S(1)}, bf16[18,1,640]{2,1,0:T(2,128)(2,1)S(1)}, u32[]{:S(2)}, u32[]{:S(2)}) collective-permute-start(bf16[18,1,640]{2,1,0:T(2,128)(2,1)S(1)} %get-tuple-element.22), channel_id=1, source_target_pairs={{0,1},{1,2},{2,3},{4,5},{5,6},{6,7},{8,9},{9,10},{10,11},{12,13},{... | collective-permute-start | bytes 69128 | tf_op jit(solution)/shard_map/ppermute | solution.py:14
  20.7 6.0 %collective-permute-start.2 = (bf16[18,1,640]{2,1,0:T(2,128)(2,1)S(1)}, bf16[18,1,640]{2,1,0:T(2,128)(2,1)S(1)}, u32[]{:S(2)}, u32[]{:S(2)}) collective-permute-start(bf16[18,1,640]{2,1,0:T(2,128)(2,1)S(1)} %get-tuple-element.23), channel_id=1, source_target_pairs={{1,0},{2,1},{3,2},{5,4},{6,5},{7,6},{9,8},{10,9},{11,10},{13,12},{... | collective-permute-start | bytes 69128 | tf_op jit(solution)/shard_map/ppermute | solution.py:15
  24.7 5.3 %copy-start.3 = (bf16[1,16,16,640]{3,2,1,0:T(8,128)(2,1)S(1)}, bf16[1,16,16,640]{3,2,1,0:T(8,128)(2,1)}, u32[]{:S(2)}) copy-start(bf16[1,16,16,640]{3,2,1,0:T(8,128)(2,1)} %param.10) | copy-start | bytes 983044
  24.7 5.3 %copy-start.6 = (bf16[1,16,16,640]{3,2,1,0:T(8,128)(2,1)S(1)}, bf16[1,16,16,640]{3,2,1,0:T(8,128)(2,1)}, u32[]{:S(2)}) copy-start(bf16[1,16,16,640]{3,2,1,0:T(8,128)(2,1)} %param.9) | copy-start | bytes 983044
  29.5 2.2 slice-start.4
  30.0 2.8 slice-start.5
  35.2 8.3 %copy-start.2 = (f32[9,640,640]{2,1,0:T(8,128)}, f32[9,640,640]{2,1,0:T(8,128)S(1)}, u32[]{:S(2)}) copy-start(f32[9,640,640]{2,1,0:T(8,128)S(1)} %bitcast_dynamic-update-slice_fusion.9) | copy-start | bytes 44236804
  35.6 7.8 %copy-start.5 = (f32[5760,2,64]{0,2,1:T(8,128)S(1)}, f32[5760,2,64]{0,2,1:T(8,128)}, u32[]{:S(2)}) copy-start(f32[5760,2,64]{0,2,1:T(8,128)} %param.12) | copy-start | bytes 8847364
  38.5 13.8 %collective-permute-start.5 = (bf16[1,16,640]{2,1,0:T(8,128)(2,1)S(1)}, bf16[1,16,640]{2,1,0:T(8,128)(2,1)S(1)}, u32[]{:S(2)}, u32[]{:S(2)}) collective-permute-start(bf16[1,16,640]{2,1,0:T(8,128)(2,1)S(1)} %get-tuple-element.27), channel_id=1, source_target_pairs={{4,0},{5,1},{6,2},{7,3},{12,8},{13,9},{14,10},{15,11},{20,16},{21,... | collective-permute-start | bytes 61448 | tf_op jit(solution)/shard_map/ppermute | solution.py:15
  40.0 12.4 %collective-permute-start.4 = (bf16[1,16,640]{2,1,0:T(8,128)(2,1)S(1)}, bf16[1,16,640]{2,1,0:T(8,128)(2,1)S(1)}, u32[]{:S(2)}, u32[]{:S(2)}) collective-permute-start(bf16[1,16,640]{2,1,0:T(8,128)(2,1)S(1)} %get-tuple-element.26), channel_id=1, source_target_pairs={{0,4},{1,5},{2,6},{3,7},{8,12},{9,13},{10,14},{11,15},{16,20},{17,... | collective-permute-start | bytes 61448 | tf_op jit(solution)/shard_map/ppermute | solution.py:14
  52.4 6.0 %collective-permute-start.7 = (bf16[18,1,640]{2,1,0:T(2,128)(2,1)S(1)}, bf16[18,1,640]{2,1,0:T(2,128)(2,1)S(1)}, u32[]{:S(2)}, u32[]{:S(2)}) collective-permute-start(bf16[18,1,640]{2,1,0:T(2,128)(2,1)S(1)} %get-tuple-element.18), channel_id=1, source_target_pairs={{0,1},{1,2},{2,3},{4,5},{5,6},{6,7},{8,9},{9,10},{10,11},{12,13},{... | collective-permute-start | bytes 69128 | tf_op jit(solution)/shard_map/ppermute | solution.py:14
  56.7 6.0 %collective-permute-start.6 = (bf16[18,1,640]{2,1,0:T(2,128)(2,1)S(1)}, bf16[18,1,640]{2,1,0:T(2,128)(2,1)S(1)}, u32[]{:S(2)}, u32[]{:S(2)}) collective-permute-start(bf16[18,1,640]{2,1,0:T(2,128)(2,1)S(1)} %get-tuple-element.19), channel_id=1, source_target_pairs={{1,0},{2,1},{3,2},{5,4},{6,5},{7,6},{9,8},{10,9},{11,10},{13,12},{... | collective-permute-start | bytes 69128 | tf_op jit(solution)/shard_map/ppermute | solution.py:15
  67.4 9.1 %copy-start.1 = (f32[9,640,640]{2,1,0:T(8,128)}, f32[9,640,640]{2,1,0:T(8,128)S(1)}, u32[]{:S(2)}) copy-start(f32[9,640,640]{2,1,0:T(8,128)S(1)} %bitcast_dynamic-update-slice_fusion) | copy-start | bytes 44236804
  77.2 325.5 %all-reduce.5.cloned.1.call-start = ((), (), s32[]{:S(2)}) async-start(), calls=%async_computation.1 | async-start | bytes 5898240 | tf_op jit(solution)/shard_map/psum | solution.py:133
  229.4 19.2 %slice-start = ((s8[14745600]{0:T(1024)(128)(4,1)}), s8[4194304]{0:T(1024)(128)(4,1)S(1)}, s32[]{:S(2)}) async-start(s8[14745600]{0:T(1024)(128)(4,1)} %bitcast.250), calls=%async_computation.2 | async-start | bytes 8388608
  230.9 17.4 %copy-start.4 = (f32[640,2,64]{0,2,1:T(8,128)S(1)}, f32[640,2,64]{0,2,1:T(8,128)}, u32[]{:S(2)}) copy-start(f32[640,2,64]{0,2,1:T(8,128)} %all-reduce.3.cloned.1.call-done) | copy-start | bytes 983044
  230.9 17.8 %slice-start.1 = ((s8[14745600]{0:T(1024)(128)(4,1)}), s8[4194304]{0:T(1024)(128)(4,1)S(1)}, s32[]{:S(2)}) async-start(s8[14745600]{0:T(1024)(128)(4,1)} %bitcast.250), calls=%async_computation.3 | async-start | bytes 8388608
  230.9 17.8 %slice-start.2 = ((s8[14745600]{0:T(1024)(128)(4,1)}), s8[4194304]{0:T(1024)(128)(4,1)S(1)}, s32[]{:S(2)}) async-start(s8[14745600]{0:T(1024)(128)(4,1)} %bitcast.250), calls=%async_computation.4 | async-start | bytes 8388608
  230.9 17.8 %slice-start.3 = ((s8[14745600]{0:T(1024)(128)(4,1)}), s8[2162688]{0:T(1024)(128)(4,1)S(1)}, s32[]{:S(2)}) async-start(s8[14745600]{0:T(1024)(128)(4,1)} %bitcast.250), calls=%async_computation.5 | async-start | bytes 4325376
Sparse Core Ops, SparseCore 0:
  77.3 126.1 all-reduce.2
  264.9 137.7 all-reduce.4
where the time goes:
time: 419 us; the launch traced here: 412 us
  waiting for transfers between devices  270 us (64%)
  matrix products  66.5 us (16%)
  other arithmetic  33.8 us (8%)
  starting transfers between devices  21.2 us (5%)
  between operations  15.1 us (4%)
  local copies, waits for them, and re-layouts  5.97 us (1%)
    psum x1, waiting for transfers between devices, on_device(): lax.psum(row_terms(moments, ortho_basis), ('dp', 'row', 'col'))  137 us
    psum x1, waiting for transfers between devices, on_device(): power_raw = lax.psum(column_terms(moments, q_prev), ('dp', 'row', 'col'))  126 us
    dot_general x2, matrix products, row_terms(): jnp.dot(moments[layer], ortho_basis[:, layer, :], precision=lax.Precision...  31.6 us
    dot_general x2, matrix products, contract_first(): lax.dot_general(left, right, (((0,), (0,)), ((), ())), precision=lax.Prec...  17.9 us
    ppermute x4, starting transfers between devices, padded_2(): before = lax.ppermute(last, axis, up)  15.7 us
    another operation x6, other arithmetic, orthonormal(): lower = jnp.linalg.cholesky(gram_matrix[layer])  13.1 us
    another operation x4, other arithmetic, orthonormal(): lax.linalg.triangular_solve(lower, power_raw[:, layer, :], left_side=Fals...  11.1 us
    dot_general x18, matrix products, contract_first(): lax.dot_general(left, right, (((0,), (0,)), ((), ())), preferred_element_...  8.41 us
  transfers between devices with their start and end apart: 10, of which 5 were waited for; matrix products, arithmetic and copies ran while one was open for 4% of the time, Pallas kernels for 0%

commit v1 on v0

v1 whole, which is shorter than its diff:
```python
import jax
import jax.numpy as jnp
from jax import lax
from jax.sharding import PartitionSpec as P

PLANE = ("row", "col")
ALL = ("dp", "row", "col")
TAPS = [(a, b) for a in (-1, 0, 1) for b in (-1, 0, 1)]
BF = jnp.bfloat16
F32 = jnp.float32


def dot(left, right, dims):
    return lax.dot_general(left, right, (dims, ((), ())), preferred_element_type=F32)


def halves(value):
    high = lax.reduce_precision(value, 8, 7)
    return high.astype(BF), (value - high).astype(BF)


def exchange(chunks, axes):
    return lax.all_to_all(chunks, axes, 0, 0, tiled=True)


def rim_exchange(tile):
    height, width, channels = tile.shape
    rows, cols = lax.axis_size("row"), lax.axis_size("col")
    row, col = lax.axis_index("row"), lax.axis_index("col")
    edge = jnp.where(row == 0, tile[-1], tile[0])
    first, last = tile[:, 0], tile[:, -1]
    none = jnp.zeros_like(edge)
    chunks = []
    for r in range(rows):
        for c in range(cols):
            step = c - col
            along = jnp.where(step == 1, last, jnp.where(step == -1, first, none))
            cross = jnp.where(
                step == 0,
                edge,
                jnp.where(step == 1, edge[-1:], jnp.where(step == -1, edge[:1], none)),
            )
            chunks.append(jnp.where(row == r, along, cross))
    got = exchange(jnp.stack(chunks), PLANE).reshape(rows, cols, height, channels)
    other = rows - 1 - row
    west, east = jnp.maximum(col - 1, 0), jnp.minimum(col + 1, cols - 1)
    has_west, has_east = col > 0, col < cols - 1
    zero = jnp.zeros_like(edge)
    left = jnp.where(has_west, got[row, west], zero)
    right = jnp.where(has_east, got[row, east], zero)
    beside = got[other, col]
    corner_w = jnp.where(has_west, got[other, west][:1], zero[:1])
    corner_e = jnp.where(has_east, got[other, east][:1], zero[:1])
    line = jnp.concatenate([corner_w, beside, corner_e], axis=0)
    top = jnp.where(row == 0, jnp.zeros_like(line), line)[None]
    bottom = jnp.where(row == 0, line, jnp.zeros_like(line))[None]
    middle = jnp.concatenate([left[:, None], tile, right[:, None]], axis=1)
    return jnp.concatenate([top, middle, bottom], axis=0)


def on_device(x_input, pre_act, out_grad, conv_weight, q_prev):
    height, width, channels = x_input.shape[1:]
    pixels = height * width
    rank = q_prev.shape[2]
    images, rows, cols = (lax.axis_size(a) for a in ALL)
    z, row, col = (lax.axis_index(a) for a in ALL)
    plane = rows * cols
    share = channels // cols
    x_tile, act_tile, g_tile = (
        v.reshape(height, width, channels) for v in (x_input, pre_act, out_grad)
    )
    act = act_tile.astype(F32)
    sigma = jax.nn.sigmoid(act)
    hidden = (act * sigma).astype(BF)

    padded = rim_exchange(jnp.concatenate([x_tile, g_tile], axis=-1))
    x_pad, g_pad = padded[..., :channels], padded[..., channels:]

    both = jnp.stack(
        [x_tile.reshape(pixels, channels).T, hidden.reshape(pixels, channels).T]
    ).reshape(plane, share, pixels)
    slices = exchange(both, PLANE)

    back = jnp.zeros((pixels, channels), F32)
    for a, b in TAPS:
        window = g_pad[1 - a : 1 - a + height, 1 - b : 1 - b + width].reshape(pixels, channels)
        back = back + dot(window, conv_weight[a + 1, b + 1], ((1,), (1,)))
    slope = sigma * (1.0 + act * (1.0 - sigma))
    pre_grad = (back * slope.reshape(pixels, channels)).astype(BF)

    q_t = q_prev.transpose(1, 2, 0)
    q_hl = jnp.concatenate(halves(q_t), axis=1).reshape(2, 2 * rank, 9, channels)
    y_one = jnp.einsum(
        "yxi,mti->yxtm", x_pad, q_hl[0], preferred_element_type=F32
    )
    y_two = jnp.einsum("yxi,mti->yxtm", hidden, q_hl[1], preferred_element_type=F32)
    y_two = jnp.pad(y_two, ((2, 2), (2, 2), (0, 0), (0, 0)))
    z_one = jnp.zeros((height, width, 2 * rank), F32)
    z_two = jnp.zeros((height + 2, width + 2, 2 * rank), F32)
    for t, (a, b) in enumerate(TAPS):
        z_one = z_one + y_one[1 + a : 1 + a + height, 1 + b : 1 + b + width, t]
        z_two = z_two + y_two[1 + a : 3 + a + height, 1 + b : 3 + b + width, t]
    z_one = (z_one[..., :rank] + z_one[..., rank:]).reshape(pixels, rank)
    z_two = (z_two[..., :rank] + z_two[..., rank:]).reshape(-1, rank)
    p_parts = []
    for left, right in ((z_one, pre_grad), (z_two, g_pad.reshape(-1, channels))):
        high, low = halves(left)
        p_parts.append(dot(high, right, ((0,), (0,))) + dot(low, right, ((0,), (0,))))
    p_t = jnp.concatenate(p_parts, axis=0)

    devices = images * plane
    if (2 * rank) % devices == 0:
        rows_each = 2 * rank // devices
        mine = exchange(p_t.reshape(devices, rows_each, channels), ALL).sum(0)
        p_t = exchange(jnp.broadcast_to(mine, (devices, rows_each, channels)), ALL)
        p_t = p_t.reshape(2 * rank, channels)
    else:
        p_t = lax.psum(p_t, ALL)

    p_hl = jnp.stack(halves(p_t))
    w_parts = []
    for layer, right in ((0, pre_grad), (1, g_tile.reshape(pixels, channels))):
        part = p_hl[:, layer * rank : (layer + 1) * rank]
        w_parts.append(dot(right, part[0], ((1,), (1,))) + dot(right, part[1], ((1,), (1,))))
    w_own = jnp.concatenate(halves(jnp.stack(w_parts)), axis=-1)
    w_all = exchange(
        jnp.broadcast_to(w_own[:, None], (2, cols, pixels, 2 * rank)).reshape(
            plane, pixels, 2 * rank
        ),
        PLANE,
    )

    p_layers = p_t.reshape(2, rank, channels)
    gram = jnp.einsum("lrm,lsm->lrs", p_layers, p_layers, precision=lax.Precision.HIGHEST)
    lower = jnp.linalg.cholesky(gram)
    eye = jnp.broadcast_to(jnp.eye(rank, dtype=F32), (2, rank, rank))
    inverse = lax.linalg.triangular_solve(lower, eye, left_side=True, lower=True)
    basis = jnp.einsum("lsr,lrm->lsm", inverse, p_layers, precision=lax.Precision.HIGHEST)
    count = channels // images
    basis_out = lax.dynamic_slice_in_dim(basis, z * count, count, 2).transpose(2, 0, 1)

    def image_of(tiles):
        return (
            tiles.reshape(rows, cols, height, width, -1)
            .transpose(0, 2, 1, 3, 4)
            .reshape(rows * height, cols * width, -1)
        )

    w_image = jnp.pad(image_of(w_all), ((1, 1), (1, 1), (0, 0)))
    x_image = image_of(slices.transpose(0, 2, 1)).reshape(-1, share)
    u_parts = []
    for a, b in TAPS:
        window = w_image[1 - a : 1 - a + rows * height, 1 - b : 1 - b + cols * width]
        u_parts.append(dot(window.reshape(-1, 2 * rank), x_image, ((0,), (0,))))
    u = jnp.stack(u_parts)
    u = u[:, :rank] + u[:, rank:]
    own_inverse = inverse[row]
    if images == 4 and cols == 4 and rows == 2:
        u = jnp.pad(u, ((0, 1), (0, 0), (0, 0)))
        parts = [
            lax.dynamic_slice_in_dim(u, (9 * k - col + 3) // 4, 3, 0) for k in range(images)
        ]
        got = exchange(jnp.stack(parts), ("dp",)).sum(0)
        mine = jnp.einsum(
            "sr,tri->tsi", own_inverse, got, precision=lax.Precision.HIGHEST
        ).astype(BF)
        every = exchange(jnp.broadcast_to(mine, (plane,) + mine.shape), PLANE)
        every = every.reshape(rows, cols, 3, rank, share)
        blocks = [
            lax.dynamic_index_in_dim(every, (z + j) % cols, 1, False)[:, j // 4] for j in range(9)
        ]
        q_out = jnp.concatenate(blocks, axis=-1).astype(F32).transpose(2, 0, 1)
    else:
        u = lax.psum(u, "dp")
        mine = jnp.einsum("sr,tri->tsi", own_inverse, u, precision=lax.Precision.HIGHEST)
        every = lax.all_gather(mine, PLANE).reshape(rows, cols, 9, rank, share)
        every = every.transpose(2, 1, 4, 0, 3).reshape(9 * channels, rows, rank)
        count = 9 * channels // images
        q_out = lax.dynamic_slice_in_dim(every, z * count, count, 0)
    return basis_out, q_out


def solution(mesh):
    tiles = P("dp", "row", "col", None)
    return jax.shard_map(
        on_device,
        mesh=mesh,
        in_specs=(tiles, tiles, tiles, P(), P()),
        out_specs=(P("dp", None, None), P("dp", None, None)),
        check_vma=False,
    )
```

time: 419 us -> 153 us (0.37); the launches traced: 412 us -> 152 us
  waiting for transfers between devices: 270 us -> 39 us
  matrix products: 66.5 us -> 14.7 us
  blocking collectives: 0 us -> 18.7 us
  between operations: 15.1 us -> 1.61 us
  local copies, waits for them, and re-layouts: 5.97 us -> 13.9 us
  other arithmetic: 33.8 us -> 41.5 us
    psum x2 -> x0, waiting for transfers between devices: 263 us -> none  [the longest x1 137 us: on_device(): lax.psum(row_terms(moments, ortho_basis), ('dp', 'row', 'col'))]
    dot_general x32 -> x31, matrix products: 64.7 us -> 14.4 us  [the longest x26 11.5 us: dot(): lax.dot_general(left, right, (dims, ((), ())), preferred_element_type=F32)]
    all_to_all x0 -> x6, waiting for transfers between devices: none -> 39 us  [exchange(): return lax.all_to_all(chunks, axes, 0, 0, tiled=True)]
    all_to_all x0 -> x6, starting transfers between devices: none -> 22.5 us  [exchange(): return lax.all_to_all(chunks, axes, 0, 0, tiled=True)]
    ppermute x8 -> x0, starting transfers between devices: 21.1 us -> none  [the longest x4 15.7 us: padded_2(): before = lax.ppermute(last, axis, up)]
    all_to_all x0 -> x1, blocking collectives: none -> 18.7 us  [exchange(): return lax.all_to_all(chunks, axes, 0, 0, tiled=True)]
    ppermute x8 -> x0, waiting for transfers between devices: 6.29 us -> none  [the longest x4 6.12 us: padded_2(): after = lax.ppermute(leading, axis, down)]
    unnamed x2 -> x9, other arithmetic: 0.01 us -> 4.56 us
  transfers between devices with their start and end apart: 10 -> 6, of which waited for: 5 -> 4; matrix products, arithmetic and copies ran while one was open for 4% -> 25% of each run, Pallas kernels for 0% -> 0%
where the time goes in v1:
time: 153 us; the launch traced here: 152 us
  other arithmetic  41.5 us (27%)
  waiting for transfers between devices  39 us (25%)
  starting transfers between devices  22.5 us (15%)
  blocking collectives  18.7 us (12%)
  matrix products  14.7 us (10%)
  local copies, waits for them, and re-layouts  13.9 us (9%)
  between operations  1.61 us (1%)
    all_to_all x6, waiting for transfers between devices, exchange(): return lax.all_to_all(chunks, axes, 0, 0, tiled=True)  39 us
    all_to_all x6, starting transfers between devices, exchange(): return lax.all_to_all(chunks, axes, 0, 0, tiled=True)  22.5 us
    all_to_all x1, blocking collectives, exchange(): return lax.all_to_all(chunks, axes, 0, 0, tiled=True)  18.7 us
    another operation x4, other arithmetic, on_device(): lower = jnp.linalg.cholesky(gram)  11.9 us
    dot_general x26, matrix products, dot(): lax.dot_general(left, right, (dims, ((), ())), preferred_element_type=F32)  11.5 us
    another operation x3, other arithmetic, on_device(): lax.linalg.triangular_solve(lower, eye, left_side=True, lower=True)  9.92 us
    unnamed x13, local copies, waits for them, and re-layouts  5.01 us
    unnamed x9, other arithmetic  4.56 us
  transfers between devices with their start and end apart: 6, of which 4 were waited for; matrix products, arithmetic and copies ran while one was open for 25% of the time, Pallas kernels for 0%

profile of v1, /device:TPU:0, one launch (start us, length us, event | category | flops | bytes accessed | tf_op | source)
XLA Modules:
  0.0 151.9 jit_solution(1167543563072881092)
XLA Ops:
  0.7 1.4 pad_maximum_fusion.24
  2.1 0.8 fusion.73
  3.0 0.6 fusion.80
  3.6 0.6 fusion.78
  4.3 0.6 fusion.76
  4.9 0.6 fusion.74
  5.6 0.6 fusion.81
  6.2 0.6 fusion.79
  6.9 0.6 fusion.77
  7.5 0.6 fusion.75
  8.1 5.2 %all-to-all-start = ((bf16[8,16,1280]{2,1,0:T(8,128)(2,1)}), bf16[8,16,1280]{2,1,0:T(8,128)(2,1)}, u32[]{:S(2)}, u32[]{:S(2)}) async-start(bf16[8,16,1280]{2,1,0:T(8,128)(2,1)} %fusion.75), calls=%async_computation | async-start | bytes 655360 | tf_op jit(solution)/shard_map/all_to_all | solution.py:23
  13.3 3.9 %copy.108 = f32[5760,2,64]{2,0,1:T(8,128)} copy(f32[5760,2,64]{0,2,1:T(8,128)S(1)} %copy-done.2) | data formatting | bytes 5898240 | tf_op args[4]
  17.2 3.6 %reduce-precision_convert_fusion = (bf16[2,64,5760]{1,2,0:T(8,128)(2,1)S(1)}, bf16[2,64,5760]{1,2,0:T(8,128)(2,1)S(1)}) fusion(f32[5760,2,64]{2,0,1:T(8,128)} %copy.108), kind=kLoop, calls=%fused_computation.1 | loop fusion | flops 2949120 | bytes 5898240 | tf_op jit(solution)/shard_map/convert_element_type | solution.py:19
  20.8 1.6 %fusion.1 = (bf16[1,128,5760]{1,2,0:T(8,128)(2,1)S(1)}, bf16[1,128,5760]{1,2,0:T(8,128)(2,1)S(1)}) fusion(bf16[2,64,5760]{1,2,0:T(8,128)(2,1)S(1)} %get-tuple-element.11, bf16[2,64,5760]{1,2,0:T(8,128)(2,1)S(1)} %get-tuple-element.12), kind=kLoop, calls=%fused_computation.15 | loop fusion | flops 5898240 | bytes 5898240 | tf_op jit(solution)/shard_map/concatenate | solution.py:92
  22.4 0.7 convolution_bitcast_fusion.1
  23.3 1.3 fusion.46
  24.6 0.8 fusion.86
  25.3 0.8 select_bitcast_fusion.2
  28.4 1.0 convolution_bitcast_fusion
  29.7 1.1 slice-done.1
  35.6 18.7 %all_to_all.35 = f32[32,4,640]{2,1,0:T(4,128)S(1)} all-to-all(f32[32,4,640]{2,1,0:T(4,128)S(1)} %reshape.513), channel_id=1, replica_groups=mesh['dp'=4,'row'=2,'col'=4] {'dp','row','col'}, dimensions={0} | all-to-all | bytes 655360 | tf_op jit(solution)/shard_map/all_to_all | solution.py:23
  54.3 0.8 broadcast_in_dim.86
  55.1 2.6 %all-to-all-start.2 = ((f32[32,4,640]{2,1,0:T(4,128)}), f32[32,4,640]{2,1,0:T(4,128)S(1)}, u32[]{:S(2)}, u32[]{:S(2)}) async-start(f32[32,4,640]{2,1,0:T(4,128)} %broadcast_in_dim.86), calls=%async_computation.2 | async-start | bytes 655360 | tf_op jit(solution)/shard_map/all_to_all | solution.py:23
  57.8 1.1 copy.121
  58.9 11.1 %all-to-all-done.2 = f32[32,4,640]{2,1,0:T(4,128)S(1)} async-done(((f32[32,4,640]{2,1,0:T(4,128)}), f32[32,4,640]{2,1,0:T(4,128)S(1)}, u32[]{:S(2)}, u32[]{:S(2)}) %all-to-all-start.2) | async-done | bytes 327712 | tf_op jit(solution)/shard_map/all_to_all | solution.py:23
  70.0 3.5 %all-to-all-start.4 = ((bf16[8,160,256]{2,1,0:T(8,128)(2,1)}), bf16[8,160,256]{2,1,0:T(8,128)(2,1)S(1)}, u32[]{:S(2)}, u32[]{:S(2)}) async-start(bf16[8,160,256]{2,1,0:T(8,128)(2,1)} %bitcast.67), calls=%async_computation.4 | async-start | bytes 1310720 | tf_op jit(solution)/shard_map/all_to_all | solution.py:23
  74.8 9.3 %all-to-all-done.4 = bf16[8,160,256]{2,1,0:T(8,128)(2,1)S(1)} async-done(((bf16[8,160,256]{2,1,0:T(8,128)(2,1)}), bf16[8,160,256]{2,1,0:T(8,128)(2,1)S(1)}, u32[]{:S(2)}, u32[]{:S(2)}) %all-to-all-start.4) | async-done | bytes 655392 | tf_op jit(solution)/shard_map/all_to_all | solution.py:23
  84.1 0.9 broadcast_in_dim.88
  85.0 4.2 %all-to-all-start.3 = ((bf16[8,256,128]{2,1,0:T(8,128)(2,1)}), bf16[8,256,128]{2,1,0:T(8,128)(2,1)}, u32[]{:S(2)}, u32[]{:S(2)}) async-start(bf16[8,256,128]{2,1,0:T(8,128)(2,1)} %bitcast.57), calls=%async_computation.3 | async-start | bytes 1048576 | tf_op jit(solution)/shard_map/all_to_all | solution.py:23
  89.2 0.5 copy.122
  90.5 7.9 %all-to-all-done.3 = bf16[8,256,128]{2,1,0:T(8,128)(2,1)} async-done(((bf16[8,256,128]{2,1,0:T(8,128)(2,1)}), bf16[8,256,128]{2,1,0:T(8,128)(2,1)}, u32[]{:S(2)}, u32[]{:S(2)}) %all-to-all-start.3) | async-done | bytes 524320 | tf_op jit(solution)/shard_map/all_to_all | solution.py:23
  98.4 1.1 copy.120
  99.5 0.9 pad_slice_fusion.11
  100.5 0.5 fusion.14
  101.0 0.5 fusion.13
  102.0 0.5 fusion.11
  102.5 1.5 %fusion.10 = f32[9,128,160]{1,2,0:T(8,128)S(1)} fusion(f32[9,128,160]{1,2,0:T(8,128)S(1)} %fusion.11, bf16[2,4,16,16,128]{4,3,2,1,0:T(8,128)(2,1)} %bitcast.58, bf16[2,4,16,16,160]{4,3,2,1,0:T(8,128)(2,1)S(1)} %bitcast.365), kind=kOutput, calls=%fused_computation.43 | convolution fusion | flops 83886080 | bytes 1654784 | tf_op jit(solution)/shard_map/dot_general | solution.py:14
  104.0 0.5 fusion.9
  105.5 0.5 fusion.6
  106.9 0.9 pad_maximum_fusion.2
  107.9 3.5 %all-to-all-start.5 = ((f32[4,3,64,160]{3,2,1,0:T(8,128)}), f32[4,3,64,160]{3,2,1,0:T(8,128)S(1)}, u32[]{:S(2)}, u32[]{:S(2)}) async-start(f32[4,3,64,160]{3,2,1,0:T(8,128)} %pad_maximum_fusion.2), calls=%async_computation.5 | async-start | bytes 1572864 | tf_op jit(solution)/shard_map/all_to_all | solution.py:23
  111.4 11.7 %custom-call.7 = f32[2,64,64]{2,1,0:T(8,128)S(1)} custom-call(f32[2,64,64]{2,1,0:T(8,128)S(1)} %fusion.72), custom_call_target="Cholesky" | custom-call | tf_op jit(solution)/shard_map/jit(cholesky)/cholesky | solution.py:135
  123.4 9.8 %custom-call.8 = f32[2,1,64,64]{2,3,1,0:T(8,128)S(1)} custom-call(f32[2,1,64,64]{3,2,1,0:T(8,128)S(1)} %select_bitcast_fusion), custom_call_target="InvertDiagBlocksLowerTriangular" | custom-call | tf_op jit(solution)/shard_map/triangular_solve | solution.py:137
  133.9 1.0 broadcast_in_dim.89
  134.9 3.5 %all-to-all-start.6 = ((bf16[8,3,64,160]{3,2,1,0:T(8,128)(2,1)}), bf16[8,3,64,160]{3,2,1,0:T(8,128)(2,1)S(1)}, u32[]{:S(2)}, u32[]{:S(2)}) async-start(bf16[8,3,64,160]{3,2,1,0:T(8,128)(2,1)} %broadcast_in_dim.89), calls=%async_computation.6 | async-start | bytes 1572864 | tf_op jit(solution)/shard_map/all_to_all | solution.py:23
  139.0 0.8 dynamic-slice_bitcast_fusion.9
  139.8 10.7 %all-to-all-done.6 = bf16[8,3,64,160]{3,2,1,0:T(8,128)(2,1)S(1)} async-done(((bf16[8,3,64,160]{3,2,1,0:T(8,128)(2,1)}), bf16[8,3,64,160]{3,2,1,0:T(8,128)(2,1)S(1)}, u32[]{:S(2)}, u32[]{:S(2)}) %all-to-all-start.6) | async-done | bytes 491552 | tf_op jit(solution)/shard_map/all_to_all | solution.py:23
  150.9 1.0 convert_bitcast_fusion
  (82 shorter events, 13.6 us)
Async XLA Ops:
  0.6 12.7 %copy-start.2 = (f32[5760,2,64]{0,2,1:T(8,128)S(1)}, f32[5760,2,64]{0,2,1:T(8,128)}, u32[]{:S(2)}) copy-start(f32[5760,2,64]{0,2,1:T(8,128)} %param.9) | copy-start | bytes 8847364
  8.1 16.4 %all-to-all-start = ((bf16[8,16,1280]{2,1,0:T(8,128)(2,1)}), bf16[8,16,1280]{2,1,0:T(8,128)(2,1)}, u32[]{:S(2)}, u32[]{:S(2)}) async-start(bf16[8,16,1280]{2,1,0:T(8,128)(2,1)} %fusion.75), calls=%async_computation | async-start | bytes 655360 | tf_op jit(solution)/shard_map/all_to_all | solution.py:23
  20.8 1.6 %copy-start.3 = (bf16[1,16,16,640]{3,2,1,0:T(8,128)(2,1)S(1)}, bf16[1,16,16,640]{3,2,1,0:T(8,128)(2,1)}, u32[]{:S(2)}) copy-start(bf16[1,16,16,640]{3,2,1,0:T(8,128)(2,1)} %param.6) | copy-start | bytes 983044
  23.1 3.3 %copy-start = (bf16[1,16,16,640]{3,2,1,0:T(8,128)(2,1)S(1)}, bf16[1,16,16,640]{3,2,1,0:T(8,128)(2,1)}, u32[]{:S(2)}) copy-start(bf16[1,16,16,640]{3,2,1,0:T(8,128)(2,1)} %param.7) | copy-start | bytes 983044
  23.1 3.3 %copy-start.1 = (bf16[1,16,16,640]{3,2,1,0:T(8,128)(2,1)S(1)}, bf16[1,16,16,640]{3,2,1,0:T(8,128)(2,1)}, u32[]{:S(2)}) copy-start(bf16[1,16,16,640]{3,2,1,0:T(8,128)(2,1)} %param.5) | copy-start | bytes 983044
  27.3 2.4 %slice-start = ((s8[7372800]{0:T(1024)(128)(4,1)}), s8[3178496]{0:T(1024)(128)(4,1)S(1)}, s32[]{:S(2)}) async-start(s8[7372800]{0:T(1024)(128)(4,1)} %bitcast.362), calls=%async_computation.7 | async-start | bytes 6356992
  28.4 2.4 %slice-start.1 = ((s8[7372800]{0:T(1024)(128)(4,1)}), s8[4194304]{0:T(1024)(128)(4,1)S(1)}, s32[]{:S(2)}) async-start(s8[7372800]{0:T(1024)(128)(4,1)} %bitcast.362), calls=%async_computation.8 | async-start | bytes 8388608
  55.1 14.9 %all-to-all-start.2 = ((f32[32,4,640]{2,1,0:T(4,128)}), f32[32,4,640]{2,1,0:T(4,128)S(1)}, u32[]{:S(2)}, u32[]{:S(2)}) async-start(f32[32,4,640]{2,1,0:T(4,128)} %broadcast_in_dim.86), calls=%async_computation.2 | async-start | bytes 655360 | tf_op jit(solution)/shard_map/all_to_all | solution.py:23
  70.0 14.1 %all-to-all-start.4 = ((bf16[8,160,256]{2,1,0:T(8,128)(2,1)}), bf16[8,160,256]{2,1,0:T(8,128)(2,1)S(1)}, u32[]{:S(2)}, u32[]{:S(2)}) async-start(bf16[8,160,256]{2,1,0:T(8,128)(2,1)} %bitcast.67), calls=%async_computation.4 | async-start | bytes 1310720 | tf_op jit(solution)/shard_map/all_to_all | solution.py:23
  85.0 13.4 %all-to-all-start.3 = ((bf16[8,256,128]{2,1,0:T(8,128)(2,1)}), bf16[8,256,128]{2,1,0:T(8,128)(2,1)}, u32[]{:S(2)}, u32[]{:S(2)}) async-start(bf16[8,256,128]{2,1,0:T(8,128)(2,1)} %bitcast.57), calls=%async_computation.3 | async-start | bytes 1048576 | tf_op jit(solution)/shard_map/all_to_all | solution.py:23
  107.9 25.6 %all-to-all-start.5 = ((f32[4,3,64,160]{3,2,1,0:T(8,128)}), f32[4,3,64,160]{3,2,1,0:T(8,128)S(1)}, u32[]{:S(2)}, u32[]{:S(2)}) async-start(f32[4,3,64,160]{3,2,1,0:T(8,128)} %pad_maximum_fusion.2), calls=%async_computation.5 | async-start | bytes 1572864 | tf_op jit(solution)/shard_map/all_to_all | solution.py:23
  134.9 15.6 %all-to-all-start.6 = ((bf16[8,3,64,160]{3,2,1,0:T(8,128)(2,1)}), bf16[8,3,64,160]{3,2,1,0:T(8,128)(2,1)S(1)}, u32[]{:S(2)}, u32[]{:S(2)}) async-start(bf16[8,3,64,160]{3,2,1,0:T(8,128)(2,1)} %broadcast_in_dim.89), calls=%async_computation.6 | async-start | bytes 1572864 | tf_op jit(solution)/shard_map/all_to_all | solution.py:23

commit v2 on v0

v2 whole, which is shorter than its diff:
```python
import jax
import jax.numpy as jnp
from jax import lax
from jax.experimental import pallas as pl
from jax.experimental.pallas import tpu as pltpu
from jax.sharding import PartitionSpec as P

PLANE = ("row", "col")
ALL = ("dp", "row", "col")
BF = jnp.bfloat16
F32 = jnp.float32
NN = ((1,), (0,))
NT = ((1,), (1,))
TN = ((0,), (0,))
VMEM_LIMIT = 40 * 1024 * 1024


def dot(left, right, dims, precision=None):
    return lax.dot_general(
        left, right, (dims, ((), ())), precision=precision, preferred_element_type=F32
    )


def call(body, out, flops, moved, **extra):
    return pl.pallas_call(
        body,
        out_shape=out,
        cost_estimate=pl.CostEstimate(flops=flops, bytes_accessed=moved, transcendentals=0),
        compiler_params=pltpu.CompilerParams(vmem_limit_bytes=VMEM_LIMIT),
        **extra,
    )


def exchange(chunks, axes):
    return lax.all_to_all(chunks, axes, 0, 0, tiled=True)


def stacked_halves(value):
    high = value.astype(BF)
    return jnp.concatenate([high, (value - high.astype(F32)).astype(BF)], axis=0)


def paired_halves(value):
    total = value + pltpu.roll(value, 64, 1)
    high = total.astype(BF).astype(F32)
    lane = lax.broadcasted_iota(jnp.int32, value.shape, 1)
    return jnp.where(lane < 64, high, total - high)


def rim_body(place, x_ref, g_ref, out_ref):
    row, col = place[1], place[2]
    rows, cols = 2, out_ref.shape[0] // 2
    for i, ref in enumerate((x_ref, g_ref)):
        tile = ref[...].astype(F32)
        first, last = tile[:, 0, :], tile[:, -1, :]
        edge = jnp.where(row == 0, tile[-1], tile[0])
        span = slice(16 * i, 16 * i + 16)
        for r in range(rows):
            for c in range(cols):
                along = jnp.where(c > col, last, first)
                out_ref[r * cols + c, span] = jnp.where(row == r, along, edge).astype(BF)


def rim_pick(row, col, cols):
    shape = (3, 18, 16)
    s, y, x = (lax.broadcasted_iota(jnp.int32, shape, i) for i in range(3))
    y, x = y - 1, x + s - 1
    up = jnp.where(y < 0, -1, jnp.where(y > 15, 1, 0))
    side = jnp.where(x < 0, -1, jnp.where(x > 15, 1, 0))
    there_r, there_c = row + up, col + side
    inside = (there_r >= 0) & (there_r < 2) & (there_c >= 0) & (there_c < cols)
    cell = jnp.where(up != 0, x - 16 * side, y)
    got = 256 + (there_r * cols + there_c) * 16 + cell
    index = jnp.where((up == 0) & (side == 0), 16 * y + x, got)
    index = jnp.where(inside, index, -1).reshape(3, 288, 1)
    width = 256 + 32 * cols
    return (index == lax.broadcasted_iota(jnp.int32, (3, 288, width), 2)).astype(BF)


def prepare_body(x_ref, act_ref, q_ref, slices_ref, q_one_ref, y_ref, hidden_ref):
    share = slices_ref.shape[1]

    @pl.when(pl.program_id(0) == 0)
    def _():
        act = act_ref[...].astype(F32)
        hidden_ref[...] = (act / (1.0 + jnp.exp(-act))).astype(BF)
        for layer, ref in enumerate((x_ref, hidden_ref)):
            turned = ref[...].astype(F32).T
            for k in range(4):
                pieces = [turned[160 * j + 40 * k : 160 * j + 40 * k + 40] for j in range(4)]
                slices_ref[4 * layer + k] = jnp.concatenate(pieces, axis=0).astype(BF)

    q = q_ref[...]
    q_one_ref[...] = stacked_halves(q[:64])
    y = dot(stacked_halves(q[64:]), hidden_ref[...], NT)
    y_ref[0] = stacked_halves(y[:64] + y[64:])


def power_body(
    x_ref, g_ref, got_ref, pick_ref, act_ref, q_ref, y_ref, w_ref,
    grad_ref, p_ref, x_win, g_win, back, z_sum, p_sum,
):
    t = pl.program_id(0)

    @pl.when(t == 0)
    def _():
        for i, (ref, win) in enumerate(((x_ref, x_win), (g_ref, g_win))):
            cells = got_ref[:, 16 * i : 16 * i + 16, :].reshape(-1, 640)
            cells = jnp.concatenate([ref[...], cells], axis=0)
            for s in range(3):
                win[s] = dot(pick_ref[s], cells, NN).astype(BF)
        back[...] = jnp.zeros_like(back)
        z_sum[...] = jnp.zeros_like(z_sum)
        p_sum[...] = jnp.zeros_like(p_sum)

    a, b = t // 3, t % 3
    grads = g_win[2 - b, pl.ds(pl.multiple_of(16 * (2 - a), 16), 256), :]
    inputs = x_win[b, pl.ds(pl.multiple_of(16 * a, 16), 256), :]
    back[...] += dot(grads, w_ref[0, 0], NT)
    z_sum[...] += dot(inputs, q_ref[...], NT)
    p_sum[...] += dot(y_ref[0], grads, NN)

    @pl.when(t == 8)
    def _():
        act = act_ref[...].astype(F32)
        sigma = 1.0 / (1.0 + jnp.exp(-act))
        grad = (back[...] * (sigma * (1.0 + act * (1.0 - sigma)))).astype(BF)
        grad_ref[...] = grad
        one = dot(paired_halves(z_sum[...]).astype(BF), grad, TN)
        two = p_sum[...]
        each = p_ref.shape[1]
        for layer, value in enumerate((one, two)):
            value = value[:64] + value[64:]
            for i in range(64 // each):
                p_ref[layer * (64 // each) + i] = value[i * each : (i + 1) * each]


def sum_body(got_ref, out_ref):
    total = jnp.sum(got_ref[...], axis=0)
    for i in range(out_ref.shape[0]):
        out_ref[i] = total


def project_body(got_ref, grad_ref, g_ref, w_ref, p_ref):
    each = got_ref.shape[1]
    for i in range(16):
        rows = [got_ref[i * (8 // each) + j] for j in range(8 // each)]
        p_ref[8 * i : 8 * i + 8, :] = jnp.concatenate(rows, axis=0)
    for layer, ref in enumerate((grad_ref, g_ref)):
        factor = stacked_halves(p_ref[64 * layer : 64 * layer + 64, :])
        out = paired_halves(dot(ref[...], factor, NT)).astype(BF)
        for k in range(4):
            w_ref[4 * layer + k] = out


def factor_body(p_ref, inverse_ref, basis_ref):
    high = lax.Precision.HIGHEST
    line = lax.broadcasted_iota(jnp.int32, (64, 128), 0)
    lane = lax.broadcasted_iota(jnp.int32, (64, 128), 1)
    unit = jnp.where(lane == line + 64, 1.0, 0.0)
    tables = []
    for layer in range(2):
        p = p_ref[64 * layer : 64 * layer + 64, :]
        gram = dot(p, p, NT, high)
        tables.append(jnp.concatenate([gram, unit[:, 64:]], axis=1))
    for k in range(64):
        for layer in range(2):
            table = tables[layer]
            pivot_row = table[k : k + 1, :]
            scaled = pivot_row / pivot_row[:, k : k + 1]
            column = jnp.where(line[:, :1] > k, table[:, k : k + 1], 0.0)
            tables[layer] = table - column * scaled
    for layer in range(2):
        table = tables[layer]
        pivots = jnp.sum(jnp.where(line == lane, table, 0.0), axis=1, keepdims=True)
        inverse = table[:, 64:] / jnp.sqrt(pivots)
        inverse_ref[layer] = inverse
        basis_ref[layer] = dot(inverse, p_ref[64 * layer : 64 * layer + 64, :], NN, high)


def taps_body(w_ref, x_ref, out_ref, image, sums):
    zero = jnp.zeros((1, 4, 16, 384), BF)
    image[0:1] = zero
    image[33:34] = zero
    at = lax.broadcasted_iota(jnp.int32, (1024, 128), 0) % 64
    for r in range(2):
        tiles = [w_ref[4 * r + c].astype(F32).reshape(16, 16, 128) for c in range(4)]
        flat = jnp.stack(tiles, axis=1).reshape(1024, 128)
        left = jnp.where(at == 63, 0.0, pltpu.roll(flat, 1023, 0))
        right = jnp.where(at == 0, 0.0, pltpu.roll(flat, 1, 0))
        for i, value in enumerate((left, flat, right)):
            image[1 + 16 * r : 17 + 16 * r, :, :, 128 * i : 128 * i + 128] = value.astype(BF).reshape(
                16, 4, 16, 128
            )
    for a in range(3):
        total = jnp.zeros((160, 384), F32)
        for r in range(2):
            for c in range(4):
                window = image[16 * r + 2 - a : 16 * r + 18 - a, c].reshape(256, 384)
                total = total + dot(x_ref[4 * r + c], window, NN)
        for b in range(3):
            t = 3 * a + b
            sums[160 * t : 160 * t + 160, :] = paired_halves(total[:, 128 * b : 128 * b + 128])
    sums[1440:1472, :] = jnp.zeros((32, 128), F32)
    for i in range(4):
        out_ref[i] = sums[360 * i : 360 * i + 384, :].astype(BF)


def rotate_body(place, got_ref, inverse_ref, out_ref):
    total = got_ref[0].astype(F32)
    for i in range(1, got_ref.shape[0]):
        total = total + got_ref[i].astype(F32)
    total = total + pltpu.roll(total, 64, 1)
    out = dot(inverse_ref[place[1]], total[:, :64], NT, lax.Precision.HIGHEST).astype(BF)
    for i in range(out_ref.shape[0]):
        out_ref[i] = out


def place_body(got_ref, out_ref):
    for layer in range(2):
        for k in range(4):
            value = got_ref[4 * layer + k].astype(F32)
            for j in range(9):
                start = 160 * j + 40 * k
                out_ref[layer, :, start : start + 40] = value[:, 40 * j : 40 * j + 40]


def on_device(x_input, pre_act, out_grad, conv_weight, q_prev):
    shape = jax.ShapeDtypeStruct
    whole = pl.BlockSpec(memory_space=pltpu.VMEM)
    small = pl.BlockSpec(memory_space=pltpu.SMEM)
    images, rows, cols = (lax.axis_size(a) for a in ALL)
    z, row, col = (lax.axis_index(a) for a in ALL)
    place = jnp.stack([z, row, col]).astype(jnp.int32)
    plane, devices = rows * cols, images * rows * cols
    x_tile, g_tile = x_input.reshape(16, 16, 640), out_grad.reshape(16, 16, 640)
    x, act, g = (v.reshape(256, 640) for v in (x_input, pre_act, out_grad))
    q_t = q_prev.transpose(1, 2, 0).reshape(128, 5760)

    rims = call(
        rim_body,
        shape((plane, 32, 640), BF),
        0,
        1 << 20,
        in_specs=[small, whole, whole],
    )(place, x_tile, g_tile)
    got = exchange(rims, PLANE)

    full = lambda *dims: pl.BlockSpec(dims, lambda t: (0,) * len(dims))
    slices, q_one, y_two = call(
        prepare_body,
        (shape((8, 160, 256), BF), shape((128, 5760), BF), shape((9, 128, 256), BF)),
        2 * 1152 * 640 * 256,
        8 << 20,
        grid=(9,),
        in_specs=[full(256, 640), full(256, 640), pl.BlockSpec((128, 640), lambda t: (0, t))],
        out_specs=(
            full(8, 160, 256),
            pl.BlockSpec((128, 640), lambda t: (0, t)),
            pl.BlockSpec((1, 128, 256), lambda t: (t, 0, 0)),
        ),
        scratch_shapes=[pltpu.VMEM((256, 640), BF)],
    )(x, act, q_t)
    slices = exchange(slices, PLANE)

    each = 2 * 64 // devices if 128 % devices == 0 and devices >= 16 else 8
    parts = 128 // each
    pre_grad, p_part = call(
        power_body,
        (shape((256, 640), BF), shape((parts, each, 640), F32)),
        2 * 256 * 5760 * 1100,
        12 << 20,
        grid=(9,),
        in_specs=[
            full(256, 640),
            full(256, 640),
            full(plane, 32, 640),
            full(3, 288, 256 + 32 * cols),
            full(256, 640),
            pl.BlockSpec((128, 640), lambda t: (0, t)),
            pl.BlockSpec((1, 128, 256), lambda t: (t, 0, 0)),
            pl.BlockSpec((1, 1, 640, 640), lambda t: (t // 3, t % 3, 0, 0)),
        ],
        out_specs=(full(256, 640), full(parts, each, 640)),
        scratch_shapes=[
            pltpu.VMEM((3, 288, 640), BF),
            pltpu.VMEM((3, 288, 640), BF),
            pltpu.VMEM((256, 640), F32),
            pltpu.VMEM((256, 128), F32),
            pltpu.VMEM((128, 640), F32),
        ],
    )(x, g, got, rim_pick(row, col, cols), act, q_one, y_two, conv_weight)

    if parts == devices:
        p_got = exchange(p_part, ALL)
        p_got = call(sum_body, shape((parts, each, 640), F32), 0, 1 << 20)(p_got)
        p_all = exchange(p_got, ALL)
    else:
        p_all = lax.psum(p_part, ALL)

    w_own, p_t = call(
        project_body,
        (shape((8, 256, 128), BF), shape((128, 640), F32)),
        2 * 512 * 640 * 128,
        2 << 20,
    )(p_all, pre_grad, g)
    w_all = exchange(w_own, PLANE)
    inverse, basis = call(
        factor_body,
        (shape((2, 64, 64), F32), shape((2, 64, 640), F32)),
        1 << 30,
        1 << 20,
    )(p_t)
    count = 640 // images
    basis_out = lax.dynamic_slice_in_dim(basis, z * count, count, 2).transpose(2, 0, 1)

    sums = call(
        taps_body,
        shape((4, 384, 128), BF),
        2 * 160 * 2048 * 1152,
        2 << 20,
        scratch_shapes=[pltpu.VMEM((34, 4, 16, 384), BF), pltpu.VMEM((1472, 128), F32)],
    )(w_all, slices)

    if images == 4:
        sums = exchange(sums, ("dp",))
        mine = call(
            rotate_body,
            shape((plane, 64, 384), BF),
            1 << 24,
            1 << 20,
            in_specs=[small, whole, whole],
        )(place, sums, inverse)
        every = exchange(mine, PLANE)
        q_out = call(place_body, shape((2, 64, 1440), F32), 0, 1 << 20)(every)
        q_out = q_out.transpose(2, 0, 1)
    else:
        sums = sums[:, :360, :64].astype(F32) + sums[:, :360, 64:].astype(F32)
        sums = lax.psum(sums, "dp")
        mine = jnp.einsum("sr,cir->csi", inverse[row], sums, precision=lax.Precision.HIGHEST)
        every = lax.all_gather(mine, PLANE).reshape(rows, cols, 4, 64, 9, 40)
        every = every.transpose(2, 4, 1, 5, 0, 3).reshape(5760, 2, 64)
        count = 5760 // images
        q_out = lax.dynamic_slice_in_dim(every, z * count, count, 0)
    return basis_out, q_out


def solution(mesh):
    tiles = P("dp", "row", "col", None)
    return jax.shard_map(
        on_device,
        mesh=mesh,
        in_specs=(tiles, tiles, tiles, P(), P()),
        out_specs=(P("dp", None, None), P("dp", None, None)),
        check_vma=False,
    )
```

time: 419 us -> 121 us (0.29); the launches traced: 412 us -> 121 us
  waiting for transfers between devices: 270 us -> 23 us
  matrix products: 66.5 us -> 0 us
  blocking collectives: 0 us -> 44.4 us
  other arithmetic: 33.8 us -> 0.3 us
  Pallas kernels: 0 us -> 25.6 us
  between operations: 15.1 us -> 0.79 us
  starting transfers between devices: 21.2 us -> 15.6 us
  local copies, waits for them, and re-layouts: 5.97 us -> 10.9 us
    psum x2 -> x0, waiting for transfers between devices: 263 us -> none  [the longest x1 137 us: on_device(): lax.psum(row_terms(moments, ortho_basis), ('dp', 'row', 'col'))]
    dot_general x32 -> x0, matrix products: 64.7 us -> none  [the longest x2 31.6 us: row_terms(): jnp.dot(moments[layer], ortho_basis[:, layer, :], precision=lax.Precision...]
    all_to_all x0 -> x3, blocking collectives: none -> 44.4 us  [exchange(): return lax.all_to_all(chunks, axes, 0, 0, tiled=True)]
    another operation x13 -> x1, other arithmetic: 27.5 us -> 0.08 us  [on_device(): place = jnp.stack([z, row, col]).astype(jnp.int32)]
    pallas_call x0 -> x9, Pallas kernels: none -> 25.6 us  [the longest x1 7.95 us: on_device(): call(power_body, (shape((256, 640), BF), shape((parts, each, 640), F32)),...]
    all_to_all x0 -> x4, waiting for transfers between devices: none -> 23 us  [exchange(): return lax.all_to_all(chunks, axes, 0, 0, tiled=True)]
    ppermute x8 -> x0, starting transfers between devices: 21.1 us -> none  [the longest x4 15.7 us: padded_2(): before = lax.ppermute(last, axis, up)]
    all_to_all x0 -> x4, starting transfers between devices: none -> 15.6 us  [exchange(): return lax.all_to_all(chunks, axes, 0, 0, tiled=True)]
  transfers between devices with their start and end apart: 10 -> 4, of which waited for: 5 -> 3; matrix products, arithmetic and copies ran while one was open for 4% -> 1% of each run, Pallas kernels for 0% -> 9%
where the time goes in v2:
time: 121 us
  blocking collectives  44.4 us (37%)
  Pallas kernels  25.6 us (21%)
  waiting for transfers between devices  23 us (19%)
  starting transfers between devices  15.6 us (13%)
  local copies, waits for them, and re-layouts  10.9 us (9%)
    all_to_all x3, blocking collectives, exchange(): return lax.all_to_all(chunks, axes, 0, 0, tiled=True)  44.4 us
    all_to_all x4, waiting for transfers between devices, exchange(): return lax.all_to_all(chunks, axes, 0, 0, tiled=True)  23 us
    all_to_all x4, starting transfers between devices, exchange(): return lax.all_to_all(chunks, axes, 0, 0, tiled=True)  15.6 us
    unnamed x18, local copies, waits for them, and re-layouts  9.39 us
    pallas_call x1, Pallas kernels, on_device(): call(power_body, (shape((256, 640), BF), shape((parts, each, 640), F32)),...  7.95 us
    pallas_call x1, Pallas kernels, on_device(): call(factor_body, (shape((2, 64, 64), F32), shape((2, 64, 640), F32)), 1...  6.43 us
    pallas_call x1, Pallas kernels, on_device(): call(prepare_body, (shape((8, 160, 256), BF), shape((128, 5760), BF), sha...  3.89 us
  transfers between devices with their start and end apart: 4, of which 3 were waited for; matrix products, arithmetic and copies ran while one was open for 1% of the time, Pallas kernels for 9%

profile of v2, /device:TPU:0, one launch (start us, length us, event | category | flops | bytes accessed | tf_op | source)
XLA Modules:
  0.0 120.7 jit_solution(15367376005192817991)
XLA Ops:
  0.6 0.1 pad_add_fusion.place
  0.7 0.0 copy-start.1
  0.7 1.0 copy-done.1
  1.7 0.0 copy-start.3
  1.7 1.0 copy-done.3
  2.7 0.0 copy-start.2
  2.7 0.0 copy-start.5
  2.7 1.6 %shard_map.68 = bf16[8,32,640]{2,1,0:T(8,128)(2,1)} custom-call(s32[3]{0:T(128)S(1)} %pad_add_fusion.place, bf16[16,16,640]{2,1,0:T(8,128)(2,1)S(1)} %bitcast.15, bf16[16,16,640]{2,1,0:T(8,128)(2,1)S(1)} %bitcast.18), custom_call_target="tpu_custom_call" | custom-call | bytes 1048576 | tf_op jit(solution)/shard_map/pallas_call | solution.py:240
  4.3 5.2 %all-to-all-start = ((bf16[8,32,640]{2,1,0:T(8,128)(2,1)}), bf16[8,32,640]{2,1,0:T(8,128)(2,1)S(1)}, u32[]{:S(2)}, u32[]{:S(2)}) async-start(bf16[8,32,640]{2,1,0:T(8,128)(2,1)} %shard_map.68), calls=%async_computation | async-start | bytes 655360 | tf_op jit(solution)/shard_map/all_to_all | solution.py:35
  9.5 0.1 iota.100
  9.6 0.1 iota.101
  9.6 0.1 iota.103
  9.7 0.1 select_n.80
  9.8 0.1 iota.112
  9.9 0.1 iota.113
  9.9 0.1 iota.109
  10.0 0.1 iota.110
  10.1 0.1 iota.106
  10.2 0.0 copy-done.2
  10.2 0.0 copy-done.5
  10.3 0.0 copy-start
  10.3 1.8 %copy-done = f32[5760,2,64]{0,2,1:T(8,128)S(1)} copy-done((f32[5760,2,64]{0,2,1:T(8,128)S(1)}, f32[5760,2,64]{0,2,1:T(8,128)}, u32[]{:S(2)}) %copy-start) | copy-done | bytes 2949144
  12.1 0.0 copy-start.4
  12.1 3.9 %shard_map.69 = (bf16[8,160,256]{2,1,0:T(8,128)(2,1)}, bf16[128,5760]{1,0:T(8,128)(2,1)S(1)}, bf16[9,128,256]{2,1,0:T(8,128)(2,1)S(1)}) custom-call(bf16[256,640]{1,0:T(8,128)(2,1)S(1)} %bitcast.16, bf16[256,640]{1,0:T(8,128)(2,1)S(1)} %bitcast.21, f32[128,5760]{1,0:T(8,128)S(1)} %bitcast.14), custom_call_target="tpu_custom_call" | custom-call | flops 377487360 | bytes 8388608 | tf_op jit(solution)/shard_map/pallas_call | solution.py:250
  16.0 1.1 copy-done.7
  17.1 0.2 fusion.pick_ref
  17.3 0.0 all-to-all-done.got_ref
  17.3 0.0 copy-done.4
  17.3 0.0 copy-start.6
  17.3 3.1 %copy-done.6 = bf16[3,3,640,640]{3,2,1,0:T(8,128)(2,1)S(1)} copy-done((bf16[3,3,640,640]{3,2,1,0:T(8,128)(2,1)S(1)}, bf16[3,3,640,640]{3,2,1,0:T(8,128)(2,1)}, u32[]{:S(2)}) %copy-start.6) | copy-done | bytes 7372824
  20.4 1.4 %copy-done.8 = bf16[128,5760]{1,0:T(8,128)(2,1)S(1)} copy-done((bf16[128,5760]{1,0:T(8,128)(2,1)S(1)}, bf16[128,5760]{1,0:T(8,128)(2,1)}, u32[]{:S(2)}) %copy-start.8) | copy-done | bytes 1474584
  21.8 7.9 %shard_map.70 = (bf16[256,640]{1,0:T(8,128)(2,1)S(1)}, f32[32,4,640]{2,1,0:T(4,128)S(1)}) custom-call(bf16[256,640]{1,0:T(8,128)(2,1)S(1)} %bitcast.17, bf16[256,640]{1,0:T(8,128)(2,1)S(1)} %bitcast.19, bf16[8,32,640]{2,1,0:T(8,128)(2,1)S(1)} %all-to-all-done.got_ref, bf16[3,288,384]{2,1,0:T(8,128)(2,1)S(1)} %fusion.pick_ref, bf16[256,640]{1,0:T(8,128)(2,1)S(1)} %bitcast.22, ...), custom_call_target="tpu_custom_call" | custom-call | flops 3244032000 | bytes 12582912 | tf_op jit(solution)/shard_map/pallas_call | solution.py:268
  29.8 18.4 %all_to_all.35.got_ref = f32[32,4,640]{2,1,0:T(4,128)S(1)} all-to-all(f32[32,4,640]{2,1,0:T(4,128)S(1)} %get-tuple-element.13), channel_id=1, replica_groups=mesh['dp'=4,'row'=2,'col'=4] {'dp','row','col'}, dimensions={0} | all-to-all | bytes 655360 | tf_op jit(solution)/shard_map/all_to_all | solution.py:35
  48.2 0.1 shard_map.71
  48.2 14.2 %all_to_all.36.got_ref = f32[32,4,640]{2,1,0:T(4,128)S(1)} all-to-all(f32[32,4,640]{2,1,0:T(4,128)S(1)} %shard_map.71), channel_id=1, replica_groups=mesh['dp'=4,'row'=2,'col'=4] {'dp','row','col'}, dimensions={0} | all-to-all | bytes 655360 | tf_op jit(solution)/shard_map/all_to_all | solution.py:35
  62.5 3.5 %all-to-all-start.4 = ((bf16[8,160,256]{2,1,0:T(8,128)(2,1)}), bf16[8,160,256]{2,1,0:T(8,128)(2,1)S(1)}, u32[]{:S(2)}, u32[]{:S(2)}) async-start(bf16[8,160,256]{2,1,0:T(8,128)(2,1)} %get-tuple-element.18), calls=%async_computation.4 | async-start | bytes 1310720 | tf_op jit(solution)/shard_map/all_to_all | solution.py:35
  66.0 0.4 shard_map.72
  66.4 10.2 %all-to-all-done.4.x_ref = bf16[8,160,256]{2,1,0:T(8,128)(2,1)S(1)} async-done(((bf16[8,160,256]{2,1,0:T(8,128)(2,1)}), bf16[8,160,256]{2,1,0:T(8,128)(2,1)S(1)}, u32[]{:S(2)}, u32[]{:S(2)}) %all-to-all-start.4) | async-done | bytes 655392 | tf_op jit(solution)/shard_map/all_to_all | solution.py:35
  76.6 11.8 %all_to_all.37.w_ref = bf16[8,256,128]{2,1,0:T(8,128)(2,1)S(1)} all-to-all(bf16[8,256,128]{2,1,0:T(8,128)(2,1)S(1)} %get-tuple-element.17), channel_id=1, replica_groups=mesh['dp'=4,'row'=2,'col'=4] {'row','col'}, dimensions={0} | all-to-all | bytes 1048576 | tf_op jit(solution)/shard_map/all_to_all | solution.py:35
  88.4 2.2 %shard_map.74 = bf16[4,384,128]{2,1,0:T(8,128)(2,1)} custom-call(bf16[8,256,128]{2,1,0:T(8,128)(2,1)S(1)} %all_to_all.37.w_ref, bf16[8,160,256]{2,1,0:T(8,128)(2,1)S(1)} %all-to-all-done.4.x_ref), custom_call_target="tpu_custom_call" | custom-call | flops 754974720 | bytes 2097152 | tf_op jit(solution)/shard_map/pallas_call | solution.py:317
  90.6 3.5 %all-to-all-start.5 = ((bf16[4,384,128]{2,1,0:T(8,128)(2,1)}), bf16[4,384,128]{2,1,0:T(8,128)(2,1)S(1)}, u32[]{:S(2)}, u32[]{:S(2)}) async-start(bf16[4,384,128]{2,1,0:T(8,128)(2,1)} %shard_map.74), calls=%async_computation.5 | async-start | bytes 786432 | tf_op jit(solution)/shard_map/all_to_all | solution.py:35
  94.1 6.4 %shard_map.73 = (f32[2,64,64]{2,1,0:T(8,128)S(1)}, f32[2,64,640]{2,1,0:T(8,128)S(1)}) custom-call(f32[128,640]{1,0:T(8,128)S(1)} %get-tuple-element.15.p_ref), custom_call_target="tpu_custom_call" | custom-call | flops 1073741824 | bytes 1048576 | tf_op jit(solution)/shard_map/pallas_call | solution.py:308
  100.5 5.8 %all-to-all-done.5.got_ref = bf16[4,384,128]{2,1,0:T(8,128)(2,1)S(1)} async-done(((bf16[4,384,128]{2,1,0:T(8,128)(2,1)}), bf16[4,384,128]{2,1,0:T(8,128)(2,1)S(1)}, u32[]{:S(2)}, u32[]{:S(2)}) %all-to-all-start.5) | async-done | bytes 393248 | tf_op jit(solution)/shard_map/all_to_all | solution.py:35
  106.3 1.8 %shard_map.75 = bf16[8,64,384]{2,1,0:T(8,128)(2,1)} custom-call(s32[3]{0:T(128)S(1)} %pad_add_fusion.place, bf16[4,384,128]{2,1,0:T(8,128)(2,1)S(1)} %all-to-all-done.5.got_ref, f32[2,64,64]{2,1,0:T(8,128)S(1)} %get-tuple-element.19.inverse_ref), custom_call_target="tpu_custom_call" | custom-call | flops 16777216 | bytes 1048576 | tf_op jit(solution)/shard_map/pallas_call | solution.py:327
  108.1 3.5 %all-to-all-start.6 = ((bf16[8,64,384]{2,1,0:T(8,128)(2,1)}), bf16[8,64,384]{2,1,0:T(8,128)(2,1)S(1)}, u32[]{:S(2)}, u32[]{:S(2)}) async-start(bf16[8,64,384]{2,1,0:T(8,128)(2,1)} %shard_map.75), calls=%async_computation.6 | async-start | bytes 786432 | tf_op jit(solution)/shard_map/all_to_all | solution.py:35
  111.6 0.8 dynamic-slice_bitcast_fusion
  112.3 7.0 %all-to-all-done.6.got_ref = bf16[8,64,384]{2,1,0:T(8,128)(2,1)S(1)} async-done(((bf16[8,64,384]{2,1,0:T(8,128)(2,1)}), bf16[8,64,384]{2,1,0:T(8,128)(2,1)S(1)}, u32[]{:S(2)}, u32[]{:S(2)}) %all-to-all-start.6) | async-done | bytes 393248 | tf_op jit(solution)/shard_map/all_to_all | solution.py:35
  119.3 1.3 %shard_map.76 = f32[2,64,1440]{2,1,0:T(8,128)} custom-call(bf16[8,64,384]{2,1,0:T(8,128)(2,1)S(1)} %all-to-all-done.6.got_ref), custom_call_target="tpu_custom_call" | custom-call | bytes 1048576 | tf_op jit(solution)/shard_map/pallas_call | solution.py:335
  (8 shorter events, 0.1 us)
Async XLA Ops:
  0.7 1.0 copy-start.1
  1.7 1.0 copy-start.3
  2.7 7.6 %copy-start.2 = (bf16[1,16,16,640]{3,2,1,0:T(8,128)(2,1)S(1)}, bf16[1,16,16,640]{3,2,1,0:T(8,128)(2,1)}, u32[]{:S(2)}) copy-start(bf16[1,16,16,640]{3,2,1,0:T(8,128)(2,1)} %param.5) | copy-start | bytes 983044
  2.7 7.6 %copy-start.5 = (bf16[1,16,16,640]{3,2,1,0:T(8,128)(2,1)S(1)}, bf16[1,16,16,640]{3,2,1,0:T(8,128)(2,1)}, u32[]{:S(2)}) copy-start(bf16[1,16,16,640]{3,2,1,0:T(8,128)(2,1)} %param.6) | copy-start | bytes 983044
  4.3 13.0 %all-to-all-start = ((bf16[8,32,640]{2,1,0:T(8,128)(2,1)}), bf16[8,32,640]{2,1,0:T(8,128)(2,1)S(1)}, u32[]{:S(2)}, u32[]{:S(2)}) async-start(bf16[8,32,640]{2,1,0:T(8,128)(2,1)} %shard_map.68), calls=%async_computation | async-start | bytes 655360 | tf_op jit(solution)/shard_map/all_to_all | solution.py:35
  10.3 1.8 %copy-start = (f32[5760,2,64]{0,2,1:T(8,128)S(1)}, f32[5760,2,64]{0,2,1:T(8,128)}, u32[]{:S(2)}) copy-start(f32[5760,2,64]{0,2,1:T(8,128)} %param.9) | copy-start | bytes 8847364
  12.1 5.2 %copy-start.4 = (bf16[1,16,16,640]{3,2,1,0:T(8,128)(2,1)S(1)}, bf16[1,16,16,640]{3,2,1,0:T(8,128)(2,1)}, u32[]{:S(2)}) copy-start(bf16[1,16,16,640]{3,2,1,0:T(8,128)(2,1)} %param.7) | copy-start | bytes 983044
  16.0 1.1 copy-start.7
  17.3 3.1 %copy-start.6 = (bf16[3,3,640,640]{3,2,1,0:T(8,128)(2,1)S(1)}, bf16[3,3,640,640]{3,2,1,0:T(8,128)(2,1)}, u32[]{:S(2)}) copy-start(bf16[3,3,640,640]{3,2,1,0:T(8,128)(2,1)} %w_ref.1) | copy-start | bytes 22118404
  20.4 1.4 %copy-start.8 = (bf16[128,5760]{1,0:T(8,128)(2,1)S(1)}, bf16[128,5760]{1,0:T(8,128)(2,1)}, u32[]{:S(2)}) copy-start(bf16[128,5760]{1,0:T(8,128)(2,1)} %copy-done.7) | copy-start | bytes 4423684
  62.5 14.1 %all-to-all-start.4 = ((bf16[8,160,256]{2,1,0:T(8,128)(2,1)}), bf16[8,160,256]{2,1,0:T(8,128)(2,1)S(1)}, u32[]{:S(2)}, u32[]{:S(2)}) async-start(bf16[8,160,256]{2,1,0:T(8,128)(2,1)} %get-tuple-element.18), calls=%async_computation.4 | async-start | bytes 1310720 | tf_op jit(solution)/shard_map/all_to_all | solution.py:35
  90.6 15.7 %all-to-all-start.5 = ((bf16[4,384,128]{2,1,0:T(8,128)(2,1)}), bf16[4,384,128]{2,1,0:T(8,128)(2,1)S(1)}, u32[]{:S(2)}, u32[]{:S(2)}) async-start(bf16[4,384,128]{2,1,0:T(8,128)(2,1)} %shard_map.74), calls=%async_computation.5 | async-start | bytes 786432 | tf_op jit(solution)/shard_map/all_to_all | solution.py:35
  108.1 11.2 %all-to-all-start.6 = ((bf16[8,64,384]{2,1,0:T(8,128)(2,1)}), bf16[8,64,384]{2,1,0:T(8,128)(2,1)S(1)}, u32[]{:S(2)}, u32[]{:S(2)}) async-start(bf16[8,64,384]{2,1,0:T(8,128)(2,1)} %shard_map.75), calls=%async_computation.6 | async-start | bytes 786432 | tf_op jit(solution)/shard_map/all_to_all | solution.py:35

commit v3 on v2

--- a/solution.py
+++ b/solution.py
@@ -12,7 +12,7 @@
 NN = ((1,), (0,))
 NT = ((1,), (1,))
 TN = ((0,), (0,))
-VMEM_LIMIT = 40 * 1024 * 1024
+MIB = 1024 * 1024
 
 
 def dot(left, right, dims, precision=None):
@@ -21,12 +21,12 @@
     )
 
 
-def call(body, out, flops, moved, **extra):
+def call(body, out, flops, moved, vmem=40, **extra):
     return pl.pallas_call(
         body,
         out_shape=out,
         cost_estimate=pl.CostEstimate(flops=flops, bytes_accessed=moved, transcendentals=0),
-        compiler_params=pltpu.CompilerParams(vmem_limit_bytes=VMEM_LIMIT),
+        compiler_params=pltpu.CompilerParams(vmem_limit_bytes=vmem * MIB),
         **extra,
     )
 
@@ -49,13 +49,16 @@
 
 def rim_body(place, x_ref, g_ref, out_ref):
     row, col = place[1], place[2]
-    rows, cols = 2, out_ref.shape[0] // 2
+    cols = out_ref.shape[0] // 2
+    line = lax.broadcasted_iota(jnp.int32, (48, 256), 0)
+    lane = lax.broadcasted_iota(jnp.int32, (48, 256), 1)
+    ends = jnp.where(line < 32, 16 * (line % 16) + 15 * (line // 16), 240 * (1 - row) + line - 32)
+    pick = jnp.where(lane == ends, 1.0, 0.0).astype(BF)
     for i, ref in enumerate((x_ref, g_ref)):
-        tile = ref[...].astype(F32)
-        first, last = tile[:, 0, :], tile[:, -1, :]
-        edge = jnp.where(row == 0, tile[-1], tile[0])
+        rims = dot(pick, ref[...], NN)
+        first, last, edge = rims[:16], rims[16:32], rims[32:]
         span = slice(16 * i, 16 * i + 16)
-        for r in range(rows):
+        for r in range(2):
             for c in range(cols):
                 along = jnp.where(c > col, last, first)
                 out_ref[r * cols + c, span] = jnp.where(row == r, along, edge).astype(BF)
@@ -77,19 +80,18 @@
     return (index == lax.broadcasted_iota(jnp.int32, (3, 288, width), 2)).astype(BF)
 
 
-def prepare_body(x_ref, act_ref, q_ref, slices_ref, q_one_ref, y_ref, hidden_ref):
-    share = slices_ref.shape[1]
-
-    @pl.when(pl.program_id(0) == 0)
-    def _():
-        act = act_ref[...].astype(F32)
-        hidden_ref[...] = (act / (1.0 + jnp.exp(-act))).astype(BF)
-        for layer, ref in enumerate((x_ref, hidden_ref)):
-            turned = ref[...].astype(F32).T
-            for k in range(4):
-                pieces = [turned[160 * j + 40 * k : 160 * j + 40 * k + 40] for j in range(4)]
-                slices_ref[4 * layer + k] = jnp.concatenate(pieces, axis=0).astype(BF)
-
+def turn_body(x_ref, act_ref, slices_ref, hidden_ref):
+    act = act_ref[...].astype(F32)
+    hidden = (act / (1.0 + jnp.exp(-act))).astype(BF)
+    hidden_ref[...] = hidden
+    for layer, value in enumerate((x_ref[...], hidden)):
+        turned = value.astype(F32).T
+        for k in range(4):
+            pieces = [turned[160 * j + 40 * k : 160 * j + 40 * k + 40] for j in range(4)]
+            slices_ref[4 * layer + k] = jnp.concatenate(pieces, axis=0).astype(BF)
+
+
+def prepare_body(hidden_ref, q_ref, q_one_ref, y_ref):
     q = q_ref[...]
     q_one_ref[...] = stacked_halves(q[:64])
     y = dot(stacked_halves(q[64:]), hidden_ref[...], NT)
@@ -178,7 +180,7 @@
         basis_ref[layer] = dot(inverse, p_ref[64 * layer : 64 * layer + 64, :], NN, high)
 
 
-def taps_body(w_ref, x_ref, out_ref, image, sums):
+def taps_body(place, w_ref, x_ref, inverse_ref, out_ref, image, sums):
     zero = jnp.zeros((1, 4, 16, 384), BF)
     image[0:1] = zero
     image[33:34] = zero
@@ -200,20 +202,21 @@
                 total = total + dot(x_ref[4 * r + c], window, NN)
         for b in range(3):
             t = 3 * a + b
-            sums[160 * t : 160 * t + 160, :] = paired_halves(total[:, 128 * b : 128 * b + 128])
+            value = total[:, 128 * b : 128 * b + 128]
+            sums[160 * t : 160 * t + 160, :] = value + pltpu.roll(value, 64, 1)
     sums[1440:1472, :] = jnp.zeros((32, 128), F32)
+    inverse = inverse_ref[place[1]]
     for i in range(4):
-        out_ref[i] = sums[360 * i : 360 * i + 384, :].astype(BF)
-
-
-def rotate_body(place, got_ref, inverse_ref, out_ref):
+        part = sums[360 * i : 360 * i + 384, :][:, :64]
+        out_ref[i] = dot(inverse, part, NT, lax.Precision.HIGHEST).astype(BF)
+
+
+def total_body(got_ref, out_ref):
     total = got_ref[0].astype(F32)
     for i in range(1, got_ref.shape[0]):
         total = total + got_ref[i].astype(F32)
-    total = total + pltpu.roll(total, 64, 1)
-    out = dot(inverse_ref[place[1]], total[:, :64], NT, lax.Precision.HIGHEST).astype(BF)
     for i in range(out_ref.shape[0]):
-        out_ref[i] = out
+        out_ref[i] = total.astype(BF)
 
 
 def place_body(got_ref, out_ref):
@@ -233,7 +236,6 @@
     z, row, col = (lax.axis_index(a) for a in ALL)
     place = jnp.stack([z, row, col]).astype(jnp.int32)
     plane, devices = rows * cols, images * rows * cols
-    x_tile, g_tile = x_input.reshape(16, 16, 640), out_grad.reshape(16, 16, 640)
     x, act, g = (v.reshape(256, 640) for v in (x_input, pre_act, out_grad))
     q_t = q_prev.transpose(1, 2, 0).reshape(128, 5760)
 
@@ -242,26 +244,29 @@
         shape((plane, 32, 640), BF),
         0,
         1 << 20,
+        vmem=62,
         in_specs=[small, whole, whole],
-    )(place, x_tile, g_tile)
+    )(place, x, g)
     got = exchange(rims, PLANE)
 
     full = lambda *dims: pl.BlockSpec(dims, lambda t: (0,) * len(dims))
-    slices, q_one, y_two = call(
+    slices, hidden = call(
+        turn_body, (shape((8, 160, 256), BF), shape((256, 640), BF)), 1 << 28, 2 << 20
+    )(x, act)
+    slices = exchange(slices, PLANE)
+    q_one, y_two = call(
         prepare_body,
-        (shape((8, 160, 256), BF), shape((128, 5760), BF), shape((9, 128, 256), BF)),
+        (shape((128, 5760), BF), shape((9, 128, 256), BF)),
         2 * 1152 * 640 * 256,
         8 << 20,
+        vmem=62,
         grid=(9,),
-        in_specs=[full(256, 640), full(256, 640), pl.BlockSpec((128, 640), lambda t: (0, t))],
+        in_specs=[full(256, 640), pl.BlockSpec((128, 640), lambda t: (0, t))],
         out_specs=(
-            full(8, 160, 256),
             pl.BlockSpec((128, 640), lambda t: (0, t)),
             pl.BlockSpec((1, 128, 256), lambda t: (t, 0, 0)),
         ),
-        scratch_shapes=[pltpu.VMEM((256, 640), BF)],
-    )(x, act, q_t)
-    slices = exchange(slices, PLANE)
+    )(hidden, q_t)
 
     each = 2 * 64 // devices if 128 % devices == 0 and devices >= 16 else 8
     parts = 128 // each
@@ -270,6 +275,7 @@
         (shape((256, 640), BF), shape((parts, each, 640), F32)),
         2 * 256 * 5760 * 1100,
         12 << 20,
+        vmem=58,
         grid=(9,),
         in_specs=[
             full(256, 640),
@@ -291,6 +297,7 @@
         ],
     )(x, g, got, rim_pick(row, col, cols), act, q_one, y_two, conv_weight)
 
+    p_part, slices = lax.optimization_barrier((p_part, slices))
     if parts == devices:
         p_got = exchange(p_part, ALL)
         p_got = call(sum_body, shape((parts, each, 640), F32), 0, 1 << 20)(p_got)
@@ -316,29 +323,22 @@
 
     sums = call(
         taps_body,
-        shape((4, 384, 128), BF),
+        shape((4, 64, 384), BF),
         2 * 160 * 2048 * 1152,
         2 << 20,
+        in_specs=[small, whole, whole, whole],
         scratch_shapes=[pltpu.VMEM((34, 4, 16, 384), BF), pltpu.VMEM((1472, 128), F32)],
-    )(w_all, slices)
+    )(place, w_all, slices, inverse)
 
     if images == 4:
         sums = exchange(sums, ("dp",))
-        mine = call(
-            rotate_body,
-            shape((plane, 64, 384), BF),
-            1 << 24,
-            1 << 20,
-            in_specs=[small, whole, whole],
-        )(place, sums, inverse)
+        mine = call(total_body, shape((plane, 64, 384), BF), 0, 1 << 20)(sums)
         every = exchange(mine, PLANE)
         q_out = call(place_body, shape((2, 64, 1440), F32), 0, 1 << 20)(every)
         q_out = q_out.transpose(2, 0, 1)
     else:
-        sums = sums[:, :360, :64].astype(F32) + sums[:, :360, 64:].astype(F32)
-        sums = lax.psum(sums, "dp")
-        mine = jnp.einsum("sr,cir->csi", inverse[row], sums, precision=lax.Precision.HIGHEST)
-        every = lax.all_gather(mine, PLANE).reshape(rows, cols, 4, 64, 9, 40)
+        sums = lax.psum(sums[:, :, :360].astype(F32), "dp")
+        every = lax.all_gather(sums, PLANE).reshape(rows, cols, 4, 64, 9, 40)
         every = every.transpose(2, 4, 1, 5, 0, 3).reshape(5760, 2, 64)
         count = 5760 // images
         q_out = lax.dynamic_slice_in_dim(every, z * count, count, 0)

time: 121 us -> 115 us (0.950)
  Pallas kernels: 25.6 us -> 35.9 us
  waiting for transfers between devices: 23 us -> 14.2 us
  local copies, waits for them, and re-layouts: 10.9 us -> 2.22 us
  other arithmetic: 0.3 us -> 1.7 us
    all_to_all x4, waiting for transfers between devices: 23 us -> 14.2 us  [exchange(): return lax.all_to_all(chunks, axes, 0, 0, tiled=True)]
    unnamed x18 -> x14, local copies, waits for them, and re-layouts: 9.39 us -> 0.75 us
    pallas_call x1, Pallas kernels: 7.95 us -> 12.9 us  [on_device(): call(power_body, (shape((256, 640), BF), shape((parts, each, 640), F32)),...]
    pallas_call x4 -> x5, Pallas kernels: 9.47 us -> 14 us  [the longest x1 7.13 us: on_device(): call(prepare_body, (shape((128, 5760), BF), shape((9, 128, 256), BF)), 2...]
  transfers between devices with their start and end apart: 4 -> 4, of which waited for: 3 -> 3; matrix products, arithmetic and copies ran while one was open for 1% -> 2% of each run, Pallas kernels for 9% -> 24%
where the time goes in v3:
time: 115 us; the launch traced here: 114 us
  blocking collectives  43.3 us (38%)
  Pallas kernels  35.9 us (31%)
  starting transfers between devices  15.7 us (14%)
  waiting for transfers between devices  14.2 us (12%)
  local copies, waits for them, and re-layouts  2.22 us (2%)
  other arithmetic  1.7 us (1%)
    all_to_all x3, blocking collectives, exchange(): return lax.all_to_all(chunks, axes, 0, 0, tiled=True)  43.3 us
    all_to_all x4, starting transfers between devices, exchange(): return lax.all_to_all(chunks, axes, 0, 0, tiled=True)  15.7 us
    all_to_all x4, waiting for transfers between devices, exchange(): return lax.all_to_all(chunks, axes, 0, 0, tiled=True)  14.2 us
    pallas_call x1, Pallas kernels, on_device(): call(power_body, (shape((256, 640), BF), shape((parts, each, 640), F32)),...  12.9 us
    pallas_call x1, Pallas kernels, on_device(): call(prepare_body, (shape((128, 5760), BF), shape((9, 128, 256), BF)), 2...  7.13 us
    pallas_call x1, Pallas kernels, on_device(): call(factor_body, (shape((2, 64, 64), F32), shape((2, 64, 640), F32)), 1...  6.42 us
    pallas_call x1, Pallas kernels, on_device(): call(taps_body, shape((4, 64, 384), BF), 2 * 160 * 2048 * 1152, 2 << 20,...  2.85 us
  transfers between devices with their start and end apart: 4, of which 3 were waited for; matrix products, arithmetic and copies ran while one was open for 2% of the time, Pallas kernels for 24%

profile of v3, /device:TPU:0, one launch (start us, length us, event | category | flops | bytes accessed | tf_op | source)
XLA Modules:
  0.0 113.8 jit_solution(660138603104114430)
XLA Ops:
  0.6 0.0 copy-start.1
  0.6 0.0 copy-start.5
  0.7 0.6 pad_add_fusion.place
  1.3 2.0 %shard_map.68 = bf16[8,32,640]{2,1,0:T(8,128)(2,1)} custom-call(s32[3]{0:T(128)} %pad_add_fusion.place, bf16[256,640]{1,0:T(8,128)(2,1)} %bitcast.15, bf16[256,640]{1,0:T(8,128)(2,1)} %bitcast.12), custom_call_target="tpu_custom_call" | custom-call | bytes 1048576 | tf_op jit(solution)/shard_map/pallas_call | solution.py:242
  3.3 5.2 %all-to-all-start = ((bf16[8,32,640]{2,1,0:T(8,128)(2,1)}), bf16[8,32,640]{2,1,0:T(8,128)(2,1)S(1)}, u32[]{:S(2)}, u32[]{:S(2)}) async-start(bf16[8,32,640]{2,1,0:T(8,128)(2,1)} %shard_map.68), calls=%async_computation | async-start | bytes 655360 | tf_op jit(solution)/shard_map/all_to_all | solution.py:35
  8.5 0.1 iota.100
  8.6 0.1 iota.101
  8.7 0.1 iota.103
  8.8 0.1 select_n.80
  8.9 0.1 iota.112
  8.9 0.1 iota.113
  9.0 0.1 iota.109
  9.1 0.1 iota.110
  9.2 0.1 iota.106
  9.3 0.0 copy-done.1
  9.3 0.0 copy-done.5
  9.3 1.2 %shard_map.69 = (bf16[8,160,256]{2,1,0:T(8,128)(2,1)}, bf16[256,640]{1,0:T(8,128)(2,1)S(1)}) custom-call(bf16[256,640]{1,0:T(8,128)(2,1)S(1)} %bitcast.17, bf16[256,640]{1,0:T(8,128)(2,1)S(1)} %bitcast.19), custom_call_target="tpu_custom_call" | custom-call | flops 268435456 | bytes 2097152 | tf_op jit(solution)/shard_map/pallas_call | solution.py:253
  10.5 0.0 copy-start.2
  10.5 0.7 copy-done.2
  11.2 4.5 %all-to-all-done.got_ref = bf16[8,32,640]{2,1,0:T(8,128)(2,1)S(1)} async-done(((bf16[8,32,640]{2,1,0:T(8,128)(2,1)}), bf16[8,32,640]{2,1,0:T(8,128)(2,1)S(1)}, u32[]{:S(2)}, u32[]{:S(2)}) %all-to-all-start) | async-done | bytes 327712 | tf_op jit(solution)/shard_map/all_to_all | solution.py:35
  15.7 0.0 copy-start.6
  15.7 3.5 %all-to-all-start.1 = ((bf16[8,160,256]{2,1,0:T(8,128)(2,1)}), bf16[8,160,256]{2,1,0:T(8,128)(2,1)S(1)}, u32[]{:S(2)}, u32[]{:S(2)}) async-start(bf16[8,160,256]{2,1,0:T(8,128)(2,1)} %get-tuple-element.18), calls=%async_computation.1 | async-start | bytes 1310720 | tf_op jit(solution)/shard_map/all_to_all | solution.py:35
  19.3 7.1 %shard_map.70 = (bf16[128,5760]{1,0:T(8,128)(2,1)}, bf16[9,128,256]{2,1,0:T(8,128)(2,1)}) custom-call(bf16[256,640]{1,0:T(8,128)(2,1)} %copy-done.2, f32[128,5760]{1,0:T(8,128)} %bitcast.20), custom_call_target="tpu_custom_call" | custom-call | flops 377487360 | bytes 8388608 | tf_op jit(solution)/shard_map/pallas_call | solution.py:257
  26.4 0.0 copy-done.6
  26.4 1.0 fusion.pick_ref
  27.4 12.9 %shard_map.71 = (bf16[256,640]{1,0:T(8,128)(2,1)}, f32[32,4,640]{2,1,0:T(4,128)}) custom-call(bf16[256,640]{1,0:T(8,128)(2,1)} %bitcast.16, bf16[256,640]{1,0:T(8,128)(2,1)} %bitcast.13, bf16[8,32,640]{2,1,0:T(8,128)(2,1)} %copy-done.6, bf16[3,288,384]{2,1,0:T(8,128)(2,1)} %fusion.pick_ref, bf16[256,640]{1,0:T(8,128)(2,1)} %bitcast.18, ...), custom_call_target="tpu_custom_call" | custom-call | flops 3244032000 | bytes 12582912 | tf_op jit(solution)/shard_map/pallas_call | solution.py:273
  40.3 0.0 copy-start
  40.3 0.0 copy-start.3
  40.3 0.0 all-to-all-done.1.x_ref
  40.3 18.5 %all_to_all.35.got_ref = f32[32,4,640]{2,1,0:T(4,128)S(1)} all-to-all(f32[32,4,640]{2,1,0:T(4,128)} %get-tuple-element.19), channel_id=1, replica_groups=mesh['dp'=4,'row'=2,'col'=4] {'dp','row','col'}, dimensions={0} | all-to-all | bytes 655360 | tf_op jit(solution)/shard_map/all_to_all | solution.py:35
  58.8 0.1 shard_map.72
  58.9 14.2 %all_to_all.36.got_ref = f32[32,4,640]{2,1,0:T(4,128)S(1)} all-to-all(f32[32,4,640]{2,1,0:T(4,128)S(1)} %shard_map.72), channel_id=1, replica_groups=mesh['dp'=4,'row'=2,'col'=4] {'dp','row','col'}, dimensions={0} | all-to-all | bytes 655360 | tf_op jit(solution)/shard_map/all_to_all | solution.py:35
  73.1 0.0 copy-done
  73.1 0.0 copy-done.3
  73.1 1.2 %shard_map.73 = (bf16[8,256,128]{2,1,0:T(8,128)(2,1)}, f32[128,640]{1,0:T(8,128)S(1)}) custom-call(f32[32,4,640]{2,1,0:T(4,128)S(1)} %all_to_all.36.got_ref, bf16[256,640]{1,0:T(8,128)(2,1)S(1)} %copy-done.3, bf16[256,640]{1,0:T(8,128)(2,1)S(1)} %bitcast.14), custom_call_target="tpu_custom_call" | custom-call | flops 83886080 | bytes 2097152 | tf_op jit(solution)/shard_map/pallas_call | solution.py:308
  74.3 3.5 %all-to-all-start.4 = ((bf16[8,256,128]{2,1,0:T(8,128)(2,1)}), bf16[8,256,128]{2,1,0:T(8,128)(2,1)S(1)}, u32[]{:S(2)}, u32[]{:S(2)}) async-start(bf16[8,256,128]{2,1,0:T(8,128)(2,1)} %get-tuple-element.23), calls=%async_computation.4 | async-start | bytes 1048576 | tf_op jit(solution)/shard_map/all_to_all | solution.py:35
  77.8 0.0 copy-start.4
  77.9 6.4 %shard_map.74 = (f32[2,64,64]{2,1,0:T(8,128)S(1)}, f32[2,64,640]{2,1,0:T(8,128)S(1)}) custom-call(f32[128,640]{1,0:T(8,128)S(1)} %get-tuple-element.21.p_ref), custom_call_target="tpu_custom_call" | custom-call | flops 1073741824 | bytes 1048576 | tf_op jit(solution)/shard_map/pallas_call | solution.py:315
  84.3 2.8 %all-to-all-done.4.w_ref = bf16[8,256,128]{2,1,0:T(8,128)(2,1)S(1)} async-done(((bf16[8,256,128]{2,1,0:T(8,128)(2,1)}), bf16[8,256,128]{2,1,0:T(8,128)(2,1)S(1)}, u32[]{:S(2)}, u32[]{:S(2)}) %all-to-all-start.4) | async-done | bytes 524320 | tf_op jit(solution)/shard_map/all_to_all | solution.py:35
  87.0 0.0 copy-done.4
  87.0 2.8 %shard_map.75 = bf16[4,64,384]{2,1,0:T(8,128)(2,1)S(1)} custom-call(s32[3]{0:T(128)S(1)} %copy-done.4, bf16[8,256,128]{2,1,0:T(8,128)(2,1)S(1)} %all-to-all-done.4.w_ref, bf16[8,160,256]{2,1,0:T(8,128)(2,1)S(1)} %all-to-all-done.1.x_ref, f32[2,64,64]{2,1,0:T(8,128)S(1)} %get-tuple-element.25.inverse_ref), custom_call_target="tpu_custom_call" | custom-call | flops 754974720 | bytes 2097152 | tf_op jit(solution)/shard_map/pallas_call | solution.py:324
  89.9 10.6 %all_to_all.37.got_ref = bf16[4,64,384]{2,1,0:T(8,128)(2,1)S(1)} all-to-all(bf16[4,64,384]{2,1,0:T(8,128)(2,1)S(1)} %shard_map.75), channel_id=1, replica_groups=mesh['dp'=4,'row'=2,'col'=4] {'dp'}, dimensions={0} | all-to-all | bytes 393216 | tf_op jit(solution)/shard_map/all_to_all | solution.py:35
  100.5 0.8 shard_map.76
  101.2 3.5 %all-to-all-start.6 = ((bf16[8,64,384]{2,1,0:T(8,128)(2,1)}), bf16[8,64,384]{2,1,0:T(8,128)(2,1)S(1)}, u32[]{:S(2)}, u32[]{:S(2)}) async-start(bf16[8,64,384]{2,1,0:T(8,128)(2,1)} %shard_map.76), calls=%async_computation.6 | async-start | bytes 786432 | tf_op jit(solution)/shard_map/all_to_all | solution.py:35
  104.7 0.8 dynamic-slice_bitcast_fusion
  105.5 7.0 %all-to-all-done.6.got_ref = bf16[8,64,384]{2,1,0:T(8,128)(2,1)S(1)} async-done(((bf16[8,64,384]{2,1,0:T(8,128)(2,1)}), bf16[8,64,384]{2,1,0:T(8,128)(2,1)S(1)}, u32[]{:S(2)}, u32[]{:S(2)}) %all-to-all-start.6) | async-done | bytes 393248 | tf_op jit(solution)/shard_map/all_to_all | solution.py:35
  112.5 1.3 %shard_map.77 = f32[2,64,1440]{2,1,0:T(8,128)} custom-call(bf16[8,64,384]{2,1,0:T(8,128)(2,1)S(1)} %all-to-all-done.6.got_ref), custom_call_target="tpu_custom_call" | custom-call | bytes 1048576 | tf_op jit(solution)/shard_map/pallas_call | solution.py:337
  (6 shorter events, 0.0 us)
Async XLA Ops:
  0.6 8.6 %copy-start.1 = (bf16[1,16,16,640]{3,2,1,0:T(8,128)(2,1)S(1)}, bf16[1,16,16,640]{3,2,1,0:T(8,128)(2,1)}, u32[]{:S(2)}) copy-start(bf16[1,16,16,640]{3,2,1,0:T(8,128)(2,1)} %param.5) | copy-start | bytes 983044
  0.6 8.6 %copy-start.5 = (bf16[1,16,16,640]{3,2,1,0:T(8,128)(2,1)S(1)}, bf16[1,16,16,640]{3,2,1,0:T(8,128)(2,1)}, u32[]{:S(2)}) copy-start(bf16[1,16,16,640]{3,2,1,0:T(8,128)(2,1)} %param.6) | copy-start | bytes 983044
  3.3 12.4 %all-to-all-start = ((bf16[8,32,640]{2,1,0:T(8,128)(2,1)}), bf16[8,32,640]{2,1,0:T(8,128)(2,1)S(1)}, u32[]{:S(2)}, u32[]{:S(2)}) async-start(bf16[8,32,640]{2,1,0:T(8,128)(2,1)} %shard_map.68), calls=%async_computation | async-start | bytes 655360 | tf_op jit(solution)/shard_map/all_to_all | solution.py:35
  10.5 0.7 copy-start.2
  15.7 10.7 %copy-start.6 = (bf16[8,32,640]{2,1,0:T(8,128)(2,1)}, bf16[8,32,640]{2,1,0:T(8,128)(2,1)S(1)}, u32[]{:S(2)}) copy-start(bf16[8,32,640]{2,1,0:T(8,128)(2,1)S(1)} %all-to-all-done.got_ref) | copy-start | bytes 983044
  15.7 24.6 %all-to-all-start.1 = ((bf16[8,160,256]{2,1,0:T(8,128)(2,1)}), bf16[8,160,256]{2,1,0:T(8,128)(2,1)S(1)}, u32[]{:S(2)}, u32[]{:S(2)}) async-start(bf16[8,160,256]{2,1,0:T(8,128)(2,1)} %get-tuple-element.18), calls=%async_computation.1 | async-start | bytes 1310720 | tf_op jit(solution)/shard_map/all_to_all | solution.py:35
  40.3 32.8 %copy-start = (bf16[1,16,16,640]{3,2,1,0:T(8,128)(2,1)S(1)}, bf16[1,16,16,640]{3,2,1,0:T(8,128)(2,1)}, u32[]{:S(2)}) copy-start(bf16[1,16,16,640]{3,2,1,0:T(8,128)(2,1)} %param.7) | copy-start | bytes 983044
  40.3 32.8 %copy-start.3 = (bf16[256,640]{1,0:T(8,128)(2,1)S(1)}, bf16[256,640]{1,0:T(8,128)(2,1)}, u32[]{:S(2)}) copy-start(bf16[256,640]{1,0:T(8,128)(2,1)} %get-tuple-element.20.grad_ref) | copy-start | bytes 983044
  74.3 12.7 %all-to-all-start.4 = ((bf16[8,256,128]{2,1,0:T(8,128)(2,1)}), bf16[8,256,128]{2,1,0:T(8,128)(2,1)S(1)}, u32[]{:S(2)}, u32[]{:S(2)}) async-start(bf16[8,256,128]{2,1,0:T(8,128)(2,1)} %get-tuple-element.23), calls=%async_computation.4 | async-start | bytes 1048576 | tf_op jit(solution)/shard_map/all_to_all | solution.py:35
  77.8 9.2 %copy-start.4 = (s32[3]{0:T(128)S(1)}, s32[3]{0:T(128)}, u32[]{:S(2)}) copy-start(s32[3]{0:T(128)} %pad_add_fusion.place) | copy-start | bytes 40
  101.2 11.2 %all-to-all-start.6 = ((bf16[8,64,384]{2,1,0:T(8,128)(2,1)}), bf16[8,64,384]{2,1,0:T(8,128)(2,1)S(1)}, u32[]{:S(2)}, u32[]{:S(2)}) async-start(bf16[8,64,384]{2,1,0:T(8,128)(2,1)} %shard_map.76), calls=%async_computation.6 | async-start | bytes 786432 | tf_op jit(solution)/shard_map/all_to_all | solution.py:35

commit v4 on v3

--- a/solution.py
+++ b/solution.py
@@ -47,14 +47,23 @@
     return jnp.where(lane < 64, high, total - high)
 
 
-def rim_body(place, x_ref, g_ref, out_ref):
-    row, col = place[1], place[2]
+def fetch(pairs, sems):
+    copies = [pltpu.make_async_copy(src, dst, sems.at[i]) for i, (src, dst) in enumerate(pairs)]
+    for copy in copies:
+        copy.start()
+    return copies
+
+
+def outgoing_body(x_hbm, g_hbm, act_hbm, out_ref, hidden_ref, x_ref, g_ref, act_ref, sems):
+    copies = fetch(((x_hbm, x_ref), (g_hbm, g_ref), (act_hbm, act_ref)), sems)
+    row, col = lax.axis_index("row"), lax.axis_index("col")
     cols = out_ref.shape[0] // 2
     line = lax.broadcasted_iota(jnp.int32, (48, 256), 0)
     lane = lax.broadcasted_iota(jnp.int32, (48, 256), 1)
     ends = jnp.where(line < 32, 16 * (line % 16) + 15 * (line // 16), 240 * (1 - row) + line - 32)
     pick = jnp.where(lane == ends, 1.0, 0.0).astype(BF)
     for i, ref in enumerate((x_ref, g_ref)):
+        copies[i].wait()
         rims = dot(pick, ref[...], NN)
         first, last, edge = rims[:16], rims[16:32], rims[32:]
         span = slice(16 * i, 16 * i + 16)
@@ -62,6 +71,24 @@
             for c in range(cols):
                 along = jnp.where(c > col, last, first)
                 out_ref[r * cols + c, span] = jnp.where(row == r, along, edge).astype(BF)
+    copies[2].wait()
+    act = act_ref[...].astype(F32)
+    hidden = (act / (1.0 + jnp.exp(-act))).astype(BF)
+    hidden_ref[...] = hidden
+    for layer, value in enumerate((x_ref[...], hidden)):
+        turned = value.astype(F32).T
+        for k in range(4):
+            pieces = [turned[160 * j + 40 * k : 160 * j + 40 * k + 40] for j in range(4)]
+            part = jnp.concatenate(pieces, axis=0).astype(BF)
+            part = jnp.concatenate([part[:, :128], part[:, 128:]], axis=0)
+            for j in range(5):
+                out_ref[4 * layer + k, 32:96, 128 * j : 128 * j + 128] = part[64 * j : 64 * j + 64]
+
+
+def slice_of(got_ref, d):
+    part = [got_ref[d, 32:96, 128 * j : 128 * j + 128] for j in range(5)]
+    part = jnp.concatenate(part, axis=0)
+    return jnp.concatenate([part[:160], part[160:]], axis=1)
 
 
 def rim_pick(row, col, cols):
@@ -80,61 +107,49 @@
     return (index == lax.broadcasted_iota(jnp.int32, (3, 288, width), 2)).astype(BF)
 
 
-def turn_body(x_ref, act_ref, slices_ref, hidden_ref):
+def prepare_body(hidden_ref, act_ref, q_hbm, q_one_ref, y_ref, slope_ref, q_all, sems):
+    copies = fetch([(q_hbm.at[:, 640 * t : 640 * t + 640], q_all.at[t]) for t in range(9)], sems)
     act = act_ref[...].astype(F32)
-    hidden = (act / (1.0 + jnp.exp(-act))).astype(BF)
-    hidden_ref[...] = hidden
-    for layer, value in enumerate((x_ref[...], hidden)):
-        turned = value.astype(F32).T
-        for k in range(4):
-            pieces = [turned[160 * j + 40 * k : 160 * j + 40 * k + 40] for j in range(4)]
-            slices_ref[4 * layer + k] = jnp.concatenate(pieces, axis=0).astype(BF)
-
-
-def prepare_body(hidden_ref, q_ref, q_one_ref, y_ref):
-    q = q_ref[...]
-    q_one_ref[...] = stacked_halves(q[:64])
-    y = dot(stacked_halves(q[64:]), hidden_ref[...], NT)
-    y_ref[0] = stacked_halves(y[:64] + y[64:])
+    sigma = 1.0 / (1.0 + jnp.exp(-act))
+    slope_ref[...] = sigma * (1.0 + act * (1.0 - sigma))
+    for t in range(9):
+        copies[t].wait()
+        q = q_all[t]
+        q_one_ref[t] = stacked_halves(q[:64])
+        y = dot(stacked_halves(q[64:]), hidden_ref[...], NT)
+        y_ref[t] = stacked_halves(y[:64] + y[64:])
 
 
 def power_body(
-    x_ref, g_ref, got_ref, pick_ref, act_ref, q_ref, y_ref, w_ref,
-    grad_ref, p_ref, x_win, g_win, back, z_sum, p_sum,
+    x_ref, g_ref, got_ref, pick_ref, slope_ref, q_ref, y_ref, w_hbm,
+    grad_ref, p_ref, x_win, g_win, back, z_sum, p_sum, w_all, sems,
 ):
-    t = pl.program_id(0)
-
-    @pl.when(t == 0)
-    def _():
-        for i, (ref, win) in enumerate(((x_ref, x_win), (g_ref, g_win))):
-            cells = got_ref[:, 16 * i : 16 * i + 16, :].reshape(-1, 640)
-            cells = jnp.concatenate([ref[...], cells], axis=0)
-            for s in range(3):
-                win[s] = dot(pick_ref[s], cells, NN).astype(BF)
-        back[...] = jnp.zeros_like(back)
-        z_sum[...] = jnp.zeros_like(z_sum)
-        p_sum[...] = jnp.zeros_like(p_sum)
-
-    a, b = t // 3, t % 3
-    grads = g_win[2 - b, pl.ds(pl.multiple_of(16 * (2 - a), 16), 256), :]
-    inputs = x_win[b, pl.ds(pl.multiple_of(16 * a, 16), 256), :]
-    back[...] += dot(grads, w_ref[0, 0], NT)
-    z_sum[...] += dot(inputs, q_ref[...], NT)
-    p_sum[...] += dot(y_ref[0], grads, NN)
-
-    @pl.when(t == 8)
-    def _():
-        act = act_ref[...].astype(F32)
-        sigma = 1.0 / (1.0 + jnp.exp(-act))
-        grad = (back[...] * (sigma * (1.0 + act * (1.0 - sigma)))).astype(BF)
-        grad_ref[...] = grad
-        one = dot(paired_halves(z_sum[...]).astype(BF), grad, TN)
-        two = p_sum[...]
-        each = p_ref.shape[1]
-        for layer, value in enumerate((one, two)):
-            value = value[:64] + value[64:]
-            for i in range(64 // each):
-                p_ref[layer * (64 // each) + i] = value[i * each : (i + 1) * each]
+    copies = fetch([(w_hbm.at[t // 3, t % 3], w_all.at[t]) for t in range(9)], sems)
+    for i, (ref, win) in enumerate(((g_ref, g_win), (x_ref, x_win))):
+        cells = got_ref[:, 16 - 16 * i : 32 - 16 * i, :].reshape(-1, 640)
+        cells = jnp.concatenate([ref[...], cells], axis=0)
+        for s in range(3):
+            win[s] = dot(pick_ref[s], cells, NN).astype(BF)
+    for t in range(9):
+        a, b = t // 3, t % 3
+        grads = g_win[2 - b, 16 * (2 - a) : 16 * (2 - a) + 256, :]
+        inputs = x_win[b, 16 * a : 16 * a + 256, :]
+        copies[t].wait()
+        terms = (
+            (back, dot(grads, w_all[t], NT)),
+            (z_sum, dot(inputs, q_ref[t], NT)),
+            (p_sum, dot(y_ref[t], grads, NN)),
+        )
+        for ref, term in terms:
+            ref[...] = term if t == 0 else ref[...] + term
+    grad = (back[...] * slope_ref[...]).astype(BF)
+    grad_ref[...] = grad
+    one = dot(paired_halves(z_sum[...]).astype(BF), grad, TN)
+    each = p_ref.shape[1]
+    for layer, value in enumerate((one, p_sum[...])):
+        value = value[:64] + value[64:]
+        for i in range(64 // each):
+            p_ref[layer * (64 // each) + i] = value[i * each : (i + 1) * each]
 
 
 def sum_body(got_ref, out_ref):
@@ -180,7 +195,7 @@
         basis_ref[layer] = dot(inverse, p_ref[64 * layer : 64 * layer + 64, :], NN, high)
 
 
-def taps_body(place, w_ref, x_ref, inverse_ref, out_ref, image, sums):
+def taps_body(w_ref, x_ref, inverse_ref, out_ref, image, sums):
     zero = jnp.zeros((1, 4, 16, 384), BF)
     image[0:1] = zero
     image[33:34] = zero
@@ -194,18 +209,19 @@
             image[1 + 16 * r : 17 + 16 * r, :, :, 128 * i : 128 * i + 128] = value.astype(BF).reshape(
                 16, 4, 16, 128
             )
+    slices = [slice_of(x_ref, d) for d in range(8)]
     for a in range(3):
         total = jnp.zeros((160, 384), F32)
         for r in range(2):
             for c in range(4):
                 window = image[16 * r + 2 - a : 16 * r + 18 - a, c].reshape(256, 384)
-                total = total + dot(x_ref[4 * r + c], window, NN)
+                total = total + dot(slices[4 * r + c], window, NN)
         for b in range(3):
             t = 3 * a + b
             value = total[:, 128 * b : 128 * b + 128]
             sums[160 * t : 160 * t + 160, :] = value + pltpu.roll(value, 64, 1)
     sums[1440:1472, :] = jnp.zeros((32, 128), F32)
-    inverse = inverse_ref[place[1]]
+    inverse = inverse_ref[lax.axis_index("row")]
     for i in range(4):
         part = sums[360 * i : 360 * i + 384, :][:, :64]
         out_ref[i] = dot(inverse, part, NT, lax.Precision.HIGHEST).astype(BF)
@@ -231,42 +247,31 @@
 def on_device(x_input, pre_act, out_grad, conv_weight, q_prev):
     shape = jax.ShapeDtypeStruct
     whole = pl.BlockSpec(memory_space=pltpu.VMEM)
-    small = pl.BlockSpec(memory_space=pltpu.SMEM)
+    far = pl.BlockSpec(memory_space=pltpu.HBM)
     images, rows, cols = (lax.axis_size(a) for a in ALL)
     z, row, col = (lax.axis_index(a) for a in ALL)
-    place = jnp.stack([z, row, col]).astype(jnp.int32)
     plane, devices = rows * cols, images * rows * cols
     x, act, g = (v.reshape(256, 640) for v in (x_input, pre_act, out_grad))
     q_t = q_prev.transpose(1, 2, 0).reshape(128, 5760)
 
-    rims = call(
-        rim_body,
-        shape((plane, 32, 640), BF),
-        0,
-        1 << 20,
-        vmem=62,
-        in_specs=[small, whole, whole],
-    )(place, x, g)
-    got = exchange(rims, PLANE)
-
-    full = lambda *dims: pl.BlockSpec(dims, lambda t: (0,) * len(dims))
-    slices, hidden = call(
-        turn_body, (shape((8, 160, 256), BF), shape((256, 640), BF)), 1 << 28, 2 << 20
-    )(x, act)
-    slices = exchange(slices, PLANE)
-    q_one, y_two = call(
+    sems = pltpu.SemaphoreType.DMA
+    send, hidden = call(
+        outgoing_body,
+        (shape((plane, 96, 640), BF), shape((256, 640), BF)),
+        1 << 28,
+        3 << 20,
+        in_specs=[far] * 3,
+        scratch_shapes=[pltpu.VMEM((256, 640), BF)] * 3 + [sems((3,))],
+    )(x, g, act)
+    got = exchange(send, PLANE)
+    q_one, y_two, slope = call(
         prepare_body,
-        (shape((128, 5760), BF), shape((9, 128, 256), BF)),
+        (shape((9, 128, 640), BF), shape((9, 128, 256), BF), shape((256, 640), F32)),
         2 * 1152 * 640 * 256,
         8 << 20,
-        vmem=62,
-        grid=(9,),
-        in_specs=[full(256, 640), pl.BlockSpec((128, 640), lambda t: (0, t))],
-        out_specs=(
-            pl.BlockSpec((128, 640), lambda t: (0, t)),
-            pl.BlockSpec((1, 128, 256), lambda t: (t, 0, 0)),
-        ),
-    )(hidden, q_t)
+        in_specs=[whole, whole, far],
+        scratch_shapes=[pltpu.VMEM((9, 128, 640), F32), sems((9,))],
+    )(hidden, act, q_t)
 
     each = 2 * 64 // devices if 128 % devices == 0 and devices >= 16 else 8
     parts = 128 // each
@@ -275,29 +280,18 @@
         (shape((256, 640), BF), shape((parts, each, 640), F32)),
         2 * 256 * 5760 * 1100,
         12 << 20,
-        vmem=58,
-        grid=(9,),
-        in_specs=[
-            full(256, 640),
-            full(256, 640),
-            full(plane, 32, 640),
-            full(3, 288, 256 + 32 * cols),
-            full(256, 640),
-            pl.BlockSpec((128, 640), lambda t: (0, t)),
-            pl.BlockSpec((1, 128, 256), lambda t: (t, 0, 0)),
-            pl.BlockSpec((1, 1, 640, 640), lambda t: (t // 3, t % 3, 0, 0)),
-        ],
-        out_specs=(full(256, 640), full(parts, each, 640)),
+        in_specs=[whole] * 7 + [far],
         scratch_shapes=[
             pltpu.VMEM((3, 288, 640), BF),
             pltpu.VMEM((3, 288, 640), BF),
             pltpu.VMEM((256, 640), F32),
             pltpu.VMEM((256, 128), F32),
             pltpu.VMEM((128, 640), F32),
+            pltpu.VMEM((9, 640, 640), BF),
+            sems((9,)),
         ],
-    )(x, g, got, rim_pick(row, col, cols), act, q_one, y_two, conv_weight)
-
-    p_part, slices = lax.optimization_barrier((p_part, slices))
+    )(x, g, got, rim_pick(row, col, cols), slope, q_one, y_two, conv_weight)
+
     if parts == devices:
         p_got = exchange(p_part, ALL)
         p_got = call(sum_body, shape((parts, each, 640), F32), 0, 1 << 20)(p_got)
@@ -326,9 +320,8 @@
         shape((4, 64, 384), BF),
         2 * 160 * 2048 * 1152,
         2 << 20,
-        in_specs=[small, whole, whole, whole],
         scratch_shapes=[pltpu.VMEM((34, 4, 16, 384), BF), pltpu.VMEM((1472, 128), F32)],
-    )(place, w_all, slices, inverse)
+    )(w_all, got, inverse)
 
     if images == 4:
         sums = exchange(sums, ("dp",))

time: 115 us -> 113 us (0.983)
  local copies, waits for them, and re-layouts: 2.22 us -> 16.8 us
  Pallas kernels: 35.9 us -> 26.5 us
  starting transfers between devices: 15.7 us -> 12.3 us
  blocking collectives: 43.3 us -> 41.4 us
  other arithmetic: 1.7 us -> 0.22 us
    unnamed x14 -> x28, local copies, waits for them, and re-layouts: 0.75 us -> 15.3 us
    pallas_call x3 -> x2, Pallas kernels: 10.4 us -> 5.54 us  [the longest x1 3.48 us: on_device(): call(prepare_body, (shape((9, 128, 640), BF), shape((9, 128, 256), BF), s...]
    pallas_call x1, Pallas kernels: 12.9 us -> 8.85 us  [on_device(): call(power_body, (shape((256, 640), BF), shape((parts, each, 640), F32)),...]
    all_to_all x4 -> x3, starting transfers between devices: 15.7 us -> 12.3 us  [exchange(): return lax.all_to_all(chunks, axes, 0, 0, tiled=True)]
    all_to_all x3, blocking collectives: 43.3 us -> 41.4 us  [exchange(): return lax.all_to_all(chunks, axes, 0, 0, tiled=True)]
    all_to_all x4 -> x3, waiting for transfers between devices: 14.2 us -> 13.9 us  [exchange(): return lax.all_to_all(chunks, axes, 0, 0, tiled=True)]
  transfers between devices with their start and end apart: 4 -> 3, of which waited for: 3 -> 3; matrix products, arithmetic and copies ran while one was open for 2% -> 2% of each run, Pallas kernels for 24% -> 9%
where the time goes in v4:
time: 113 us; the launch traced here: 112 us
  blocking collectives  41.4 us (37%)
  Pallas kernels  26.5 us (23%)
  local copies, waits for them, and re-layouts  16.8 us (15%)
  waiting for transfers between devices  13.9 us (12%)
  starting transfers between devices  12.3 us (11%)
    all_to_all x3, blocking collectives, exchange(): return lax.all_to_all(chunks, axes, 0, 0, tiled=True)  41.4 us
    unnamed x28, local copies, waits for them, and re-layouts  15.3 us
    all_to_all x3, waiting for transfers between devices, exchange(): return lax.all_to_all(chunks, axes, 0, 0, tiled=True)  13.9 us
    all_to_all x3, starting transfers between devices, exchange(): return lax.all_to_all(chunks, axes, 0, 0, tiled=True)  12.3 us
    pallas_call x1, Pallas kernels, on_device(): call(power_body, (shape((256, 640), BF), shape((parts, each, 640), F32)),...  8.85 us
    pallas_call x1, Pallas kernels, on_device(): call(factor_body, (shape((2, 64, 64), F32), shape((2, 64, 640), F32)), 1...  6.41 us
    pallas_call x1, Pallas kernels, on_device(): call(prepare_body, (shape((9, 128, 640), BF), shape((9, 128, 256), BF), s...  3.48 us
    pallas_call x1, Pallas kernels, on_device(): call(taps_body, shape((4, 64, 384), BF), 2 * 160 * 2048 * 1152, 2 << 20,...  2.32 us
  transfers between devices with their start and end apart: 3, of which 3 were waited for; matrix products, arithmetic and copies ran while one was open for 2% of the time, Pallas kernels for 9%

profile of v4, /device:TPU:0, one launch (start us, length us, event | category | flops | bytes accessed | tf_op | source)
XLA Modules:
  0.0 111.8 jit_solution(10281191926332066298)
XLA Ops:
  0.6 0.0 copy-start.2
  0.6 1.0 copy-done.2
  1.6 0.0 copy-start.8
  1.6 1.0 copy-done.8
  2.6 0.0 copy-start.12
  2.6 1.0 copy-done.12
  3.6 2.1 %shard_map.68 = (bf16[8,96,640]{2,1,0:T(8,128)(2,1)}, bf16[256,640]{1,0:T(8,128)(2,1)S(1)}) custom-call(bf16[256,640]{1,0:T(8,128)(2,1)S(1)} %bitcast.15, bf16[256,640]{1,0:T(8,128)(2,1)S(1)} %bitcast.10, bf16[256,640]{1,0:T(8,128)(2,1)S(1)} %bitcast.13), custom_call_target="tpu_custom_call" | custom-call | flops 268435456 | bytes 3145728 | tf_op jit(solution)/shard_map/pallas_call | solution.py:258
  5.6 0.0 copy-start.10
  5.6 0.7 copy-done.10
  6.3 5.2 %all-to-all-start = ((bf16[8,96,640]{2,1,0:T(8,128)(2,1)}), bf16[8,96,640]{2,1,0:T(8,128)(2,1)S(1)}, u32[]{:S(2)}, u32[]{:S(2)}) async-start(bf16[8,96,640]{2,1,0:T(8,128)(2,1)} %get-tuple-element.13), calls=%async_computation | async-start | bytes 1966080 | tf_op jit(solution)/shard_map/all_to_all | solution.py:35
  11.5 0.1 iota.100
  11.6 0.1 iota.101
  11.7 0.1 iota.103
  11.8 0.1 select_n.80
  11.9 0.1 iota.112
  11.9 0.1 iota.113
  12.0 0.1 iota.109
  12.1 0.1 iota.110
  12.2 0.1 iota.106
  12.3 1.8 %copy-done.1 = f32[5760,2,64]{0,2,1:T(8,128)S(1)} copy-done((f32[5760,2,64]{0,2,1:T(8,128)S(1)}, f32[5760,2,64]{0,2,1:T(8,128)}, u32[]{:S(2)}) %copy-start.1) | copy-done | bytes 2949144
  14.1 1.0 copy-done.9
  15.1 1.0 copy-done.11
  16.1 3.5 %shard_map.69 = (bf16[9,128,640]{2,1,0:T(8,128)(2,1)S(1)}, bf16[9,128,256]{2,1,0:T(8,128)(2,1)S(1)}, f32[256,640]{1,0:T(8,128)S(1)}) custom-call(bf16[256,640]{1,0:T(8,128)(2,1)S(1)} %copy-done.11, bf16[256,640]{1,0:T(8,128)(2,1)S(1)} %bitcast.14, f32[128,5760]{1,0:T(8,128)S(1)} %bitcast.9), custom_call_target="tpu_custom_call" | custom-call | flops 377487360 | bytes 8388608 | tf_op jit(solution)/shard_map/pallas_call | solution.py:267
  19.6 0.0 copy-start.4
  19.6 0.8 copy-done.4
  20.4 0.8 copy-done.6
  21.2 0.2 fusion.pick_ref
  21.4 4.3 %all-to-all-done.got_ref.x_ref = bf16[8,96,640]{2,1,0:T(8,128)(2,1)S(1)} async-done(((bf16[8,96,640]{2,1,0:T(8,128)(2,1)}), bf16[8,96,640]{2,1,0:T(8,128)(2,1)S(1)}, u32[]{:S(2)}, u32[]{:S(2)}) %all-to-all-start) | async-done | bytes 983072 | tf_op jit(solution)/shard_map/all_to_all | solution.py:35
  25.7 0.0 copy-done.3
  25.7 3.1 %copy-done = bf16[3,3,640,640]{3,2,1,0:T(8,128)(2,1)S(1)} copy-done((bf16[3,3,640,640]{3,2,1,0:T(8,128)(2,1)S(1)}, bf16[3,3,640,640]{3,2,1,0:T(8,128)(2,1)}, u32[]{:S(2)}) %copy-start) | copy-done | bytes 7372824
  28.8 1.1 copy-done.5
  29.9 1.1 copy-done.7
  30.9 1.0 copy-done.13
  31.9 8.9 %shard_map.70 = (bf16[256,640]{1,0:T(8,128)(2,1)S(1)}, f32[32,4,640]{2,1,0:T(4,128)S(1)}) custom-call(bf16[256,640]{1,0:T(8,128)(2,1)S(1)} %bitcast.16, bf16[256,640]{1,0:T(8,128)(2,1)S(1)} %bitcast.11, bf16[8,96,640]{2,1,0:T(8,128)(2,1)S(1)} %all-to-all-done.got_ref.x_ref, bf16[3,288,384]{2,1,0:T(8,128)(2,1)S(1)} %fusion.pick_ref, ...), custom_call_target="tpu_custom_call" | custom-call | flops 3244032000 | bytes 12582912 | tf_op jit(solution)/shard_map/pallas_call | solution.py:278
  40.8 16.6 %all_to_all.30.got_ref = f32[32,4,640]{2,1,0:T(4,128)S(1)} all-to-all(f32[32,4,640]{2,1,0:T(4,128)S(1)} %get-tuple-element.18), channel_id=1, replica_groups=mesh['dp'=4,'row'=2,'col'=4] {'dp','row','col'}, dimensions={0} | all-to-all | bytes 655360 | tf_op jit(solution)/shard_map/all_to_all | solution.py:35
  57.4 0.1 shard_map.71
  57.4 14.2 %all_to_all.31.got_ref = f32[32,4,640]{2,1,0:T(4,128)S(1)} all-to-all(f32[32,4,640]{2,1,0:T(4,128)S(1)} %shard_map.71), channel_id=1, replica_groups=mesh['dp'=4,'row'=2,'col'=4] {'dp','row','col'}, dimensions={0} | all-to-all | bytes 655360 | tf_op jit(solution)/shard_map/all_to_all | solution.py:35
  71.7 1.2 %shard_map.72 = (bf16[8,256,128]{2,1,0:T(8,128)(2,1)}, f32[128,640]{1,0:T(8,128)S(1)}) custom-call(f32[32,4,640]{2,1,0:T(4,128)S(1)} %all_to_all.31.got_ref, bf16[256,640]{1,0:T(8,128)(2,1)S(1)} %get-tuple-element.19.grad_ref, bf16[256,640]{1,0:T(8,128)(2,1)S(1)} %bitcast.12), custom_call_target="tpu_custom_call" | custom-call | flops 83886080 | bytes 2097152 | tf_op jit(solution)/shard_map/pallas_call | solution.py:302
  72.9 3.7 %all-to-all-start.3 = ((bf16[8,256,128]{2,1,0:T(8,128)(2,1)}), bf16[8,256,128]{2,1,0:T(8,128)(2,1)S(1)}, u32[]{:S(2)}, u32[]{:S(2)}) async-start(bf16[8,256,128]{2,1,0:T(8,128)(2,1)} %get-tuple-element.22), calls=%async_computation.3 | async-start | bytes 1048576 | tf_op jit(solution)/shard_map/all_to_all | solution.py:35
  76.6 6.4 %shard_map.73 = (f32[2,64,64]{2,1,0:T(8,128)S(1)}, f32[2,64,640]{2,1,0:T(8,128)S(1)}) custom-call(f32[128,640]{1,0:T(8,128)S(1)} %get-tuple-element.20.p_ref), custom_call_target="tpu_custom_call" | custom-call | flops 1073741824 | bytes 1048576 | tf_op jit(solution)/shard_map/pallas_call | solution.py:309
  83.0 2.6 %all-to-all-done.3.w_ref = bf16[8,256,128]{2,1,0:T(8,128)(2,1)S(1)} async-done(((bf16[8,256,128]{2,1,0:T(8,128)(2,1)}), bf16[8,256,128]{2,1,0:T(8,128)(2,1)S(1)}, u32[]{:S(2)}, u32[]{:S(2)}) %all-to-all-start.3) | async-done | bytes 524320 | tf_op jit(solution)/shard_map/all_to_all | solution.py:35
  85.6 2.3 %shard_map.74 = bf16[4,64,384]{2,1,0:T(8,128)(2,1)S(1)} custom-call(bf16[8,256,128]{2,1,0:T(8,128)(2,1)S(1)} %all-to-all-done.3.w_ref, bf16[8,96,640]{2,1,0:T(8,128)(2,1)S(1)} %all-to-all-done.got_ref.x_ref, f32[2,64,64]{2,1,0:T(8,128)S(1)} %get-tuple-element.23.inverse_ref), custom_call_target="tpu_custom_call" | custom-call | flops 754974720 | bytes 2097152 | tf_op jit(solution)/shard_map/pallas_call | solution.py:318
  87.9 10.6 %all_to_all.32.got_ref = bf16[4,64,384]{2,1,0:T(8,128)(2,1)S(1)} all-to-all(bf16[4,64,384]{2,1,0:T(8,128)(2,1)S(1)} %shard_map.74), channel_id=1, replica_groups=mesh['dp'=4,'row'=2,'col'=4] {'dp'}, dimensions={0} | all-to-all | bytes 393216 | tf_op jit(solution)/shard_map/all_to_all | solution.py:35
  98.5 0.8 shard_map.75
  99.2 3.5 %all-to-all-start.5 = ((bf16[8,64,384]{2,1,0:T(8,128)(2,1)}), bf16[8,64,384]{2,1,0:T(8,128)(2,1)S(1)}, u32[]{:S(2)}, u32[]{:S(2)}) async-start(bf16[8,64,384]{2,1,0:T(8,128)(2,1)} %shard_map.75), calls=%async_computation.5 | async-start | bytes 786432 | tf_op jit(solution)/shard_map/all_to_all | solution.py:35
  102.7 0.8 dynamic-slice_bitcast_fusion
  103.5 7.0 %all-to-all-done.5.got_ref = bf16[8,64,384]{2,1,0:T(8,128)(2,1)S(1)} async-done(((bf16[8,64,384]{2,1,0:T(8,128)(2,1)}), bf16[8,64,384]{2,1,0:T(8,128)(2,1)S(1)}, u32[]{:S(2)}, u32[]{:S(2)}) %all-to-all-start.5) | async-done | bytes 393248 | tf_op jit(solution)/shard_map/all_to_all | solution.py:35
  110.5 1.3 %shard_map.76 = f32[2,64,1440]{2,1,0:T(8,128)} custom-call(bf16[8,64,384]{2,1,0:T(8,128)(2,1)S(1)} %all-to-all-done.5.got_ref), custom_call_target="tpu_custom_call" | custom-call | bytes 1048576 | tf_op jit(solution)/shard_map/pallas_call | solution.py:330
  (15 shorter events, 0.1 us)
Async XLA Ops:
  0.6 1.0 copy-start.2
  1.6 1.0 copy-start.8
  2.6 1.0 copy-start.12
  5.6 0.7 copy-start.10
  6.3 19.4 %all-to-all-start = ((bf16[8,96,640]{2,1,0:T(8,128)(2,1)}), bf16[8,96,640]{2,1,0:T(8,128)(2,1)S(1)}, u32[]{:S(2)}, u32[]{:S(2)}) async-start(bf16[8,96,640]{2,1,0:T(8,128)(2,1)} %get-tuple-element.13), calls=%async_computation | async-start | bytes 1966080 | tf_op jit(solution)/shard_map/all_to_all | solution.py:35
  12.3 1.8 %copy-start.1 = (f32[5760,2,64]{0,2,1:T(8,128)S(1)}, f32[5760,2,64]{0,2,1:T(8,128)}, u32[]{:S(2)}) copy-start(f32[5760,2,64]{0,2,1:T(8,128)} %param.9) | copy-start | bytes 8847364
  14.1 1.0 copy-start.9
  15.1 1.0 copy-start.11
  16.1 9.6 %copy-start.3 = (bf16[1,16,16,640]{3,2,1,0:T(8,128)(2,1)S(1)}, bf16[1,16,16,640]{3,2,1,0:T(8,128)(2,1)}, u32[]{:S(2)}) copy-start(bf16[1,16,16,640]{3,2,1,0:T(8,128)(2,1)} %param.7) | copy-start | bytes 983044
  19.6 0.8 copy-start.4
  20.4 0.8 copy-start.6
  25.7 3.1 %copy-start = (bf16[3,3,640,640]{3,2,1,0:T(8,128)(2,1)S(1)}, bf16[3,3,640,640]{3,2,1,0:T(8,128)(2,1)}, u32[]{:S(2)}) copy-start(bf16[3,3,640,640]{3,2,1,0:T(8,128)(2,1)} %w_hbm.1) | copy-start | bytes 22118404
  28.8 1.1 copy-start.5
  29.9 1.1 copy-start.7
  30.9 1.0 copy-start.13
  72.9 12.7 %all-to-all-start.3 = ((bf16[8,256,128]{2,1,0:T(8,128)(2,1)}), bf16[8,256,128]{2,1,0:T(8,128)(2,1)S(1)}, u32[]{:S(2)}, u32[]{:S(2)}) async-start(bf16[8,256,128]{2,1,0:T(8,128)(2,1)} %get-tuple-element.22), calls=%async_computation.3 | async-start | bytes 1048576 | tf_op jit(solution)/shard_map/all_to_all | solution.py:35
  99.2 11.2 %all-to-all-start.5 = ((bf16[8,64,384]{2,1,0:T(8,128)(2,1)}), bf16[8,64,384]{2,1,0:T(8,128)(2,1)S(1)}, u32[]{:S(2)}, u32[]{:S(2)}) async-start(bf16[8,64,384]{2,1,0:T(8,128)(2,1)} %shard_map.75), calls=%async_computation.5 | async-start | bytes 786432 | tf_op jit(solution)/shard_map/all_to_all | solution.py:35

commit v5 on v4

--- a/solution.py
+++ b/solution.py
@@ -54,8 +54,8 @@
     return copies
 
 
-def outgoing_body(x_hbm, g_hbm, act_hbm, out_ref, hidden_ref, x_ref, g_ref, act_ref, sems):
-    copies = fetch(((x_hbm, x_ref), (g_hbm, g_ref), (act_hbm, act_ref)), sems)
+def rim_body(x_hbm, g_hbm, out_ref, x_ref, g_ref, sems):
+    copies = fetch(((x_hbm, x_ref), (g_hbm, g_ref)), sems)
     row, col = lax.axis_index("row"), lax.axis_index("col")
     cols = out_ref.shape[0] // 2
     line = lax.broadcasted_iota(jnp.int32, (48, 256), 0)
@@ -71,24 +71,6 @@
             for c in range(cols):
                 along = jnp.where(c > col, last, first)
                 out_ref[r * cols + c, span] = jnp.where(row == r, along, edge).astype(BF)
-    copies[2].wait()
-    act = act_ref[...].astype(F32)
-    hidden = (act / (1.0 + jnp.exp(-act))).astype(BF)
-    hidden_ref[...] = hidden
-    for layer, value in enumerate((x_ref[...], hidden)):
-        turned = value.astype(F32).T
-        for k in range(4):
-            pieces = [turned[160 * j + 40 * k : 160 * j + 40 * k + 40] for j in range(4)]
-            part = jnp.concatenate(pieces, axis=0).astype(BF)
-            part = jnp.concatenate([part[:, :128], part[:, 128:]], axis=0)
-            for j in range(5):
-                out_ref[4 * layer + k, 32:96, 128 * j : 128 * j + 128] = part[64 * j : 64 * j + 64]
-
-
-def slice_of(got_ref, d):
-    part = [got_ref[d, 32:96, 128 * j : 128 * j + 128] for j in range(5)]
-    part = jnp.concatenate(part, axis=0)
-    return jnp.concatenate([part[:160], part[160:]], axis=1)
 
 
 def rim_pick(row, col, cols):
@@ -107,34 +89,55 @@
     return (index == lax.broadcasted_iota(jnp.int32, (3, 288, width), 2)).astype(BF)
 
 
-def prepare_body(hidden_ref, act_ref, q_hbm, q_one_ref, y_ref, slope_ref, q_all, sems):
-    copies = fetch([(q_hbm.at[:, 640 * t : 640 * t + 640], q_all.at[t]) for t in range(9)], sems)
+def prepare_body(
+    x_hbm, act_hbm, q_hbm, slices_ref, q_one_ref, y_ref, slope_ref, x_ref, act_ref, q_all, sems
+):
+    pairs = [(x_hbm, x_ref), (act_hbm, act_ref)]
+    pairs += [(q_hbm.at[:, 640 * t : 640 * t + 640], q_all.at[t]) for t in range(9)]
+    copies = fetch(pairs, sems)
+    copies[0].wait()
+    copies[1].wait()
     act = act_ref[...].astype(F32)
     sigma = 1.0 / (1.0 + jnp.exp(-act))
+    hidden = (act * sigma).astype(BF)
     slope_ref[...] = sigma * (1.0 + act * (1.0 - sigma))
+    for layer, value in enumerate((x_ref[...], hidden)):
+        turned = value.astype(F32).T
+        for k in range(4):
+            pieces = [turned[160 * j + 40 * k : 160 * j + 40 * k + 40] for j in range(4)]
+            slices_ref[4 * layer + k] = jnp.concatenate(pieces, axis=0).astype(BF)
     for t in range(9):
-        copies[t].wait()
+        copies[2 + t].wait()
         q = q_all[t]
         q_one_ref[t] = stacked_halves(q[:64])
-        y = dot(stacked_halves(q[64:]), hidden_ref[...], NT)
+        y = dot(stacked_halves(q[64:]), hidden, NT)
         y_ref[t] = stacked_halves(y[:64] + y[64:])
 
 
 def power_body(
-    x_ref, g_ref, got_ref, pick_ref, slope_ref, q_ref, y_ref, w_hbm,
-    grad_ref, p_ref, x_win, g_win, back, z_sum, p_sum, w_all, sems,
+    x_hbm, g_hbm, got_hbm, pick_hbm, slope_hbm, q_hbm, y_hbm, w_hbm,
+    grad_ref, p_ref,
+    x_ref, g_ref, got_ref, pick_ref, slope_ref, q_ref, y_ref, w_all,
+    x_win, g_win, back, z_sum, p_sum, sems,
 ):
-    copies = fetch([(w_hbm.at[t // 3, t % 3], w_all.at[t]) for t in range(9)], sems)
+    pairs = [(got_hbm, got_ref), (g_hbm, g_ref), (pick_hbm, pick_ref), (x_hbm, x_ref)]
+    pairs += [(q_hbm, q_ref), (y_hbm, y_ref), (slope_hbm, slope_ref)]
+    pairs += [(w_hbm.at[t // 3, t % 3], w_all.at[t]) for t in range(9)]
+    copies = fetch(pairs, sems)
+    for i in range(4):
+        copies[i].wait()
     for i, (ref, win) in enumerate(((g_ref, g_win), (x_ref, x_win))):
         cells = got_ref[:, 16 - 16 * i : 32 - 16 * i, :].reshape(-1, 640)
         cells = jnp.concatenate([ref[...], cells], axis=0)
         for s in range(3):
             win[s] = dot(pick_ref[s], cells, NN).astype(BF)
+    copies[4].wait()
+    copies[5].wait()
     for t in range(9):
         a, b = t // 3, t % 3
         grads = g_win[2 - b, 16 * (2 - a) : 16 * (2 - a) + 256, :]
         inputs = x_win[b, 16 * a : 16 * a + 256, :]
-        copies[t].wait()
+        copies[7 + t].wait()
         terms = (
             (back, dot(grads, w_all[t], NT)),
             (z_sum, dot(inputs, q_ref[t], NT)),
@@ -142,6 +145,7 @@
         )
         for ref, term in terms:
             ref[...] = term if t == 0 else ref[...] + term
+    copies[6].wait()
     grad = (back[...] * slope_ref[...]).astype(BF)
     grad_ref[...] = grad
     one = dot(paired_halves(z_sum[...]).astype(BF), grad, TN)
@@ -209,13 +213,12 @@
             image[1 + 16 * r : 17 + 16 * r, :, :, 128 * i : 128 * i + 128] = value.astype(BF).reshape(
                 16, 4, 16, 128
             )
-    slices = [slice_of(x_ref, d) for d in range(8)]
     for a in range(3):
         total = jnp.zeros((160, 384), F32)
         for r in range(2):
             for c in range(4):
                 window = image[16 * r + 2 - a : 16 * r + 18 - a, c].reshape(256, 384)
-                total = total + dot(slices[4 * r + c], window, NN)
+                total = total + dot(x_ref[4 * r + c], window, NN)
         for b in range(3):
             t = 3 * a + b
             value = total[:, 128 * b : 128 * b + 128]
@@ -255,23 +258,32 @@
     q_t = q_prev.transpose(1, 2, 0).reshape(128, 5760)
 
     sems = pltpu.SemaphoreType.DMA
-    send, hidden = call(
-        outgoing_body,
-        (shape((plane, 96, 640), BF), shape((256, 640), BF)),
-        1 << 28,
-        3 << 20,
-        in_specs=[far] * 3,
-        scratch_shapes=[pltpu.VMEM((256, 640), BF)] * 3 + [sems((3,))],
-    )(x, g, act)
-    got = exchange(send, PLANE)
-    q_one, y_two, slope = call(
+    rims = call(
+        rim_body,
+        shape((plane, 32, 640), BF),
+        1 << 24,
+        1 << 20,
+        vmem=62,
+        in_specs=[far] * 2,
+        scratch_shapes=[pltpu.VMEM((256, 640), BF)] * 2 + [sems((2,))],
+    )(x, g)
+    got = exchange(rims, PLANE)
+    slices, q_one, y_two, slope = call(
         prepare_body,
-        (shape((9, 128, 640), BF), shape((9, 128, 256), BF), shape((256, 640), F32)),
+        (
+            shape((8, 160, 256), BF),
+            shape((9, 128, 640), BF),
+            shape((9, 128, 256), BF),
+            shape((256, 640), F32),
+        ),
         2 * 1152 * 640 * 256,
         8 << 20,
-        in_specs=[whole, whole, far],
-        scratch_shapes=[pltpu.VMEM((9, 128, 640), F32), sems((9,))],
-    )(hidden, act, q_t)
+        vmem=62,
+        in_specs=[far] * 3,
+        scratch_shapes=[pltpu.VMEM((256, 640), BF)] * 2
+        + [pltpu.VMEM((9, 128, 640), F32), sems((11,))],
+    )(x, act, q_t)
+    slices = exchange(slices, PLANE)
 
     each = 2 * 64 // devices if 128 % devices == 0 and devices >= 16 else 8
     parts = 128 // each
@@ -280,18 +292,27 @@
         (shape((256, 640), BF), shape((parts, each, 640), F32)),
         2 * 256 * 5760 * 1100,
         12 << 20,
-        in_specs=[whole] * 7 + [far],
+        vmem=62,
+        in_specs=[far] * 8,
         scratch_shapes=[
+            pltpu.VMEM((256, 640), BF),
+            pltpu.VMEM((256, 640), BF),
+            pltpu.VMEM((plane, 32, 640), BF),
+            pltpu.VMEM((3, 288, 256 + 32 * cols), BF),
+            pltpu.VMEM((256, 640), F32),
+            pltpu.VMEM((9, 128, 640), BF),
+            pltpu.VMEM((9, 128, 256), BF),
+            pltpu.VMEM((9, 640, 640), BF),
             pltpu.VMEM((3, 288, 640), BF),
             pltpu.VMEM((3, 288, 640), BF),
             pltpu.VMEM((256, 640), F32),
             pltpu.VMEM((256, 128), F32),
             pltpu.VMEM((128, 640), F32),
-            pltpu.VMEM((9, 640, 640), BF),
-            sems((9,)),
+            sems((16,)),
         ],
     )(x, g, got, rim_pick(row, col, cols), slope, q_one, y_two, conv_weight)
 
+    p_part, slices = lax.optimization_barrier((p_part, slices))
     if parts == devices:
         p_got = exchange(p_part, ALL)
         p_got = call(sum_body, shape((parts, each, 640), F32), 0, 1 << 20)(p_got)
@@ -321,7 +342,7 @@
         2 * 160 * 2048 * 1152,
         2 << 20,
         scratch_shapes=[pltpu.VMEM((34, 4, 16, 384), BF), pltpu.VMEM((1472, 128), F32)],
-    )(w_all, got, inverse)
+    )(w_all, slices, inverse)
 
     if images == 4:
         sums = exchange(sums, ("dp",))

time: 113 us -> 104 us (0.920)
  local copies, waits for them, and re-layouts: 16.8 us -> 1.49 us
  Pallas kernels: 26.5 us -> 30.4 us
  waiting for transfers between devices: 13.9 us -> 10.2 us
  starting transfers between devices: 12.3 us -> 16 us
  blocking collectives: 41.4 us -> 43.4 us
    unnamed x28 -> x6, local copies, waits for them, and re-layouts: 15.3 us -> 0.01 us
    all_to_all x3 -> x4, waiting for transfers between devices: 13.9 us -> 10.2 us  [exchange(): return lax.all_to_all(chunks, axes, 0, 0, tiled=True)]
    all_to_all x3 -> x4, starting transfers between devices: 12.3 us -> 16 us  [exchange(): return lax.all_to_all(chunks, axes, 0, 0, tiled=True)]
    pallas_call x2, Pallas kernels: 5.54 us -> 7.97 us  [the longest x1 5.88 us: on_device(): call(prepare_body, (shape((8, 160, 256), BF), shape((9, 128, 640), BF), s...]
    all_to_all x3, blocking collectives: 41.4 us -> 43.4 us  [exchange(): return lax.all_to_all(chunks, axes, 0, 0, tiled=True)]
    pallas_call x1, Pallas kernels: 8.85 us -> 10.3 us  [on_device(): call(power_body, (shape((256, 640), BF), shape((parts, each, 640), F32)),...]
  transfers between devices with their start and end apart: 3 -> 4, of which waited for: 3 -> 3; matrix products, arithmetic and copies ran while one was open for 2% -> 2% of each run, Pallas kernels for 9% -> 22%
where the time goes in v5:
time: 104 us; the launch traced here: 103 us
  blocking collectives  43.4 us (42%)
  Pallas kernels  30.4 us (29%)
  starting transfers between devices  16 us (15%)
  waiting for transfers between devices  10.2 us (10%)
  local copies, waits for them, and re-layouts  1.49 us (1%)
  other arithmetic  1.06 us (1%)
    all_to_all x3, blocking collectives, exchange(): return lax.all_to_all(chunks, axes, 0, 0, tiled=True)  43.4 us
    all_to_all x4, starting transfers between devices, exchange(): return lax.all_to_all(chunks, axes, 0, 0, tiled=True)  16 us
    pallas_call x1, Pallas kernels, on_device(): call(power_body, (shape((256, 640), BF), shape((parts, each, 640), F32)),...  10.3 us
    all_to_all x4, waiting for transfers between devices, exchange(): return lax.all_to_all(chunks, axes, 0, 0, tiled=True)  10.2 us
    pallas_call x1, Pallas kernels, on_device(): call(factor_body, (shape((2, 64, 64), F32), shape((2, 64, 640), F32)), 1...  6.41 us
    pallas_call x1, Pallas kernels, on_device(): call(prepare_body, (shape((8, 160, 256), BF), shape((9, 128, 640), BF), s...  5.88 us
    pallas_call x1, Pallas kernels, on_device(): call(taps_body, shape((4, 64, 384), BF), 2 * 160 * 2048 * 1152, 2 << 20,...  2.31 us
    pallas_call x1, Pallas kernels, on_device(): call(rim_body, shape((plane, 32, 640), BF), 1 << 24, 1 << 20, vmem=62, in...  2.1 us
  transfers between devices with their start and end apart: 4, of which 3 were waited for; matrix products, arithmetic and copies ran while one was open for 2% of the time, Pallas kernels for 22%

profile of v5, /device:TPU:0, one launch (start us, length us, event | category | flops | bytes accessed | tf_op | source)
XLA Modules:
  0.0 103.2 jit_solution(11208023758620795696)
XLA Ops:
  0.6 2.1 %shard_map.68 = bf16[8,32,640]{2,1,0:T(8,128)(2,1)} custom-call(bf16[256,640]{1,0:T(8,128)(2,1)} %bitcast.13, bf16[256,640]{1,0:T(8,128)(2,1)} %bitcast.9), custom_call_target="tpu_custom_call" | custom-call | flops 16777216 | bytes 1048576 | tf_op jit(solution)/shard_map/pallas_call | solution.py:261
  2.7 5.2 %all-to-all-start = ((bf16[8,32,640]{2,1,0:T(8,128)(2,1)}), bf16[8,32,640]{2,1,0:T(8,128)(2,1)S(1)}, u32[]{:S(2)}, u32[]{:S(2)}) async-start(bf16[8,32,640]{2,1,0:T(8,128)(2,1)} %shard_map.68), calls=%async_computation | async-start | bytes 655360 | tf_op jit(solution)/shard_map/all_to_all | solution.py:35
  7.9 0.1 iota.100
  8.0 0.1 iota.101
  8.1 0.1 iota.103
  8.2 0.1 select_n.80
  8.3 0.1 iota.112
  8.3 0.1 iota.113
  8.4 0.1 iota.109
  8.5 0.1 iota.110
  8.6 0.1 iota.106
  8.7 5.9 %shard_map.69 = (bf16[8,160,256]{2,1,0:T(8,128)(2,1)}, bf16[9,128,640]{2,1,0:T(8,128)(2,1)}, bf16[9,128,256]{2,1,0:T(8,128)(2,1)}, f32[256,640]{1,0:T(8,128)}) custom-call(bf16[256,640]{1,0:T(8,128)(2,1)} %bitcast.14, bf16[256,640]{1,0:T(8,128)(2,1)} %bitcast.17, f32[128,5760]{1,0:T(8,128)} %bitcast.12), custom_call_target="tpu_custom_call" | custom-call | flops 377487360 | bytes 8388608 | tf_op jit(solution)/shard_map/pallas_call | solution.py:271
  14.6 0.6 all-to-all-done.got_hbm
  15.1 0.0 copy-start.2
  15.1 3.7 %all-to-all-start.1 = ((bf16[8,160,256]{2,1,0:T(8,128)(2,1)}), bf16[8,160,256]{2,1,0:T(8,128)(2,1)S(1)}, u32[]{:S(2)}, u32[]{:S(2)}) async-start(bf16[8,160,256]{2,1,0:T(8,128)(2,1)} %get-tuple-element.18), calls=%async_computation.1 | async-start | bytes 1310720 | tf_op jit(solution)/shard_map/all_to_all | solution.py:35
  18.8 1.0 fusion.pick_hbm
  19.8 0.0 copy-done.2
  19.8 10.3 %shard_map.70 = (bf16[256,640]{1,0:T(8,128)(2,1)}, f32[32,4,640]{2,1,0:T(4,128)}) custom-call(bf16[256,640]{1,0:T(8,128)(2,1)} %bitcast.15, bf16[256,640]{1,0:T(8,128)(2,1)} %bitcast.10, bf16[8,32,640]{2,1,0:T(8,128)(2,1)} %copy-done.2, bf16[3,288,384]{2,1,0:T(8,128)(2,1)} %fusion.pick_hbm, f32[256,640]{1,0:T(8,128)} %get-tuple-element.14.slope_hbm, ...), custom_call_target="tpu_custom_call" | custom-call | flops 3244032000 | bytes 12582912 | tf_op jit(solution)/shard_map/pallas_call | solution.py:290
  30.1 0.0 copy-start
  30.2 0.0 copy-start.1
  30.2 0.0 all-to-all-done.1.x_ref
  30.2 18.6 %all_to_all.35.got_ref = f32[32,4,640]{2,1,0:T(4,128)S(1)} all-to-all(f32[32,4,640]{2,1,0:T(4,128)} %get-tuple-element.19), channel_id=1, replica_groups=mesh['dp'=4,'row'=2,'col'=4] {'dp','row','col'}, dimensions={0} | all-to-all | bytes 655360 | tf_op jit(solution)/shard_map/all_to_all | solution.py:35
  48.8 0.1 shard_map.71
  48.9 14.2 %all_to_all.36.got_ref = f32[32,4,640]{2,1,0:T(4,128)S(1)} all-to-all(f32[32,4,640]{2,1,0:T(4,128)S(1)} %shard_map.71), channel_id=1, replica_groups=mesh['dp'=4,'row'=2,'col'=4] {'dp','row','col'}, dimensions={0} | all-to-all | bytes 655360 | tf_op jit(solution)/shard_map/all_to_all | solution.py:35
  63.1 0.0 copy-done
  63.1 0.0 copy-done.1
  63.1 1.2 %shard_map.72 = (bf16[8,256,128]{2,1,0:T(8,128)(2,1)}, f32[128,640]{1,0:T(8,128)S(1)}) custom-call(f32[32,4,640]{2,1,0:T(4,128)S(1)} %all_to_all.36.got_ref, bf16[256,640]{1,0:T(8,128)(2,1)S(1)} %copy-done.1, bf16[256,640]{1,0:T(8,128)(2,1)S(1)} %bitcast.11), custom_call_target="tpu_custom_call" | custom-call | flops 83886080 | bytes 2097152 | tf_op jit(solution)/shard_map/pallas_call | solution.py:323
  64.3 3.7 %all-to-all-start.4 = ((bf16[8,256,128]{2,1,0:T(8,128)(2,1)}), bf16[8,256,128]{2,1,0:T(8,128)(2,1)S(1)}, u32[]{:S(2)}, u32[]{:S(2)}) async-start(bf16[8,256,128]{2,1,0:T(8,128)(2,1)} %get-tuple-element.23), calls=%async_computation.4 | async-start | bytes 1048576 | tf_op jit(solution)/shard_map/all_to_all | solution.py:35
  68.0 6.4 %shard_map.73 = (f32[2,64,64]{2,1,0:T(8,128)S(1)}, f32[2,64,640]{2,1,0:T(8,128)S(1)}) custom-call(f32[128,640]{1,0:T(8,128)S(1)} %get-tuple-element.21.p_ref), custom_call_target="tpu_custom_call" | custom-call | flops 1073741824 | bytes 1048576 | tf_op jit(solution)/shard_map/pallas_call | solution.py:330
  74.4 2.6 %all-to-all-done.4.w_ref = bf16[8,256,128]{2,1,0:T(8,128)(2,1)S(1)} async-done(((bf16[8,256,128]{2,1,0:T(8,128)(2,1)}), bf16[8,256,128]{2,1,0:T(8,128)(2,1)S(1)}, u32[]{:S(2)}, u32[]{:S(2)}) %all-to-all-start.4) | async-done | bytes 524320 | tf_op jit(solution)/shard_map/all_to_all | solution.py:35
  77.0 2.3 %shard_map.74 = bf16[4,64,384]{2,1,0:T(8,128)(2,1)S(1)} custom-call(bf16[8,256,128]{2,1,0:T(8,128)(2,1)S(1)} %all-to-all-done.4.w_ref, bf16[8,160,256]{2,1,0:T(8,128)(2,1)S(1)} %all-to-all-done.1.x_ref, f32[2,64,64]{2,1,0:T(8,128)S(1)} %get-tuple-element.25.inverse_ref), custom_call_target="tpu_custom_call" | custom-call | flops 754974720 | bytes 2097152 | tf_op jit(solution)/shard_map/pallas_call | solution.py:339
  79.3 10.6 %all_to_all.37.got_ref = bf16[4,64,384]{2,1,0:T(8,128)(2,1)S(1)} all-to-all(bf16[4,64,384]{2,1,0:T(8,128)(2,1)S(1)} %shard_map.74), channel_id=1, replica_groups=mesh['dp'=4,'row'=2,'col'=4] {'dp'}, dimensions={0} | all-to-all | bytes 393216 | tf_op jit(solution)/shard_map/all_to_all | solution.py:35
  89.9 0.8 shard_map.75
  90.7 3.5 %all-to-all-start.6 = ((bf16[8,64,384]{2,1,0:T(8,128)(2,1)}), bf16[8,64,384]{2,1,0:T(8,128)(2,1)S(1)}, u32[]{:S(2)}, u32[]{:S(2)}) async-start(bf16[8,64,384]{2,1,0:T(8,128)(2,1)} %shard_map.75), calls=%async_computation.6 | async-start | bytes 786432 | tf_op jit(solution)/shard_map/all_to_all | solution.py:35
  94.1 0.8 dynamic-slice_bitcast_fusion
  94.9 7.0 %all-to-all-done.6.got_ref = bf16[8,64,384]{2,1,0:T(8,128)(2,1)S(1)} async-done(((bf16[8,64,384]{2,1,0:T(8,128)(2,1)}), bf16[8,64,384]{2,1,0:T(8,128)(2,1)S(1)}, u32[]{:S(2)}, u32[]{:S(2)}) %all-to-all-start.6) | async-done | bytes 393248 | tf_op jit(solution)/shard_map/all_to_all | solution.py:35
  101.9 1.3 %shard_map.76 = f32[2,64,1440]{2,1,0:T(8,128)} custom-call(bf16[8,64,384]{2,1,0:T(8,128)(2,1)S(1)} %all-to-all-done.6.got_ref), custom_call_target="tpu_custom_call" | custom-call | bytes 1048576 | tf_op jit(solution)/shard_map/pallas_call | solution.py:351
  (6 shorter events, 0.0 us)
Async XLA Ops:
  2.7 12.4 %all-to-all-start = ((bf16[8,32,640]{2,1,0:T(8,128)(2,1)}), bf16[8,32,640]{2,1,0:T(8,128)(2,1)S(1)}, u32[]{:S(2)}, u32[]{:S(2)}) async-start(bf16[8,32,640]{2,1,0:T(8,128)(2,1)} %shard_map.68), calls=%async_computation | async-start | bytes 655360 | tf_op jit(solution)/shard_map/all_to_all | solution.py:35
  15.1 4.7 %copy-start.2 = (bf16[8,32,640]{2,1,0:T(8,128)(2,1)}, bf16[8,32,640]{2,1,0:T(8,128)(2,1)S(1)}, u32[]{:S(2)}) copy-start(bf16[8,32,640]{2,1,0:T(8,128)(2,1)S(1)} %all-to-all-done.got_hbm) | copy-start | bytes 983044
  15.1 15.1 %all-to-all-start.1 = ((bf16[8,160,256]{2,1,0:T(8,128)(2,1)}), bf16[8,160,256]{2,1,0:T(8,128)(2,1)S(1)}, u32[]{:S(2)}, u32[]{:S(2)}) async-start(bf16[8,160,256]{2,1,0:T(8,128)(2,1)} %get-tuple-element.18), calls=%async_computation.1 | async-start | bytes 1310720 | tf_op jit(solution)/shard_map/all_to_all | solution.py:35
  30.1 33.0 %copy-start = (bf16[1,16,16,640]{3,2,1,0:T(8,128)(2,1)S(1)}, bf16[1,16,16,640]{3,2,1,0:T(8,128)(2,1)}, u32[]{:S(2)}) copy-start(bf16[1,16,16,640]{3,2,1,0:T(8,128)(2,1)} %param.7) | copy-start | bytes 983044
  30.2 32.9 %copy-start.1 = (bf16[256,640]{1,0:T(8,128)(2,1)S(1)}, bf16[256,640]{1,0:T(8,128)(2,1)}, u32[]{:S(2)}) copy-start(bf16[256,640]{1,0:T(8,128)(2,1)} %get-tuple-element.20.grad_ref) | copy-start | bytes 983044
  64.3 12.7 %all-to-all-start.4 = ((bf16[8,256,128]{2,1,0:T(8,128)(2,1)}), bf16[8,256,128]{2,1,0:T(8,128)(2,1)S(1)}, u32[]{:S(2)}, u32[]{:S(2)}) async-start(bf16[8,256,128]{2,1,0:T(8,128)(2,1)} %get-tuple-element.23), calls=%async_computation.4 | async-start | bytes 1048576 | tf_op jit(solution)/shard_map/all_to_all | solution.py:35
  90.7 11.2 %all-to-all-start.6 = ((bf16[8,64,384]{2,1,0:T(8,128)(2,1)}), bf16[8,64,384]{2,1,0:T(8,128)(2,1)S(1)}, u32[]{:S(2)}, u32[]{:S(2)}) async-start(bf16[8,64,384]{2,1,0:T(8,128)(2,1)} %shard_map.75), calls=%async_computation.6 | async-start | bytes 786432 | tf_op jit(solution)/shard_map/all_to_all | solution.py:35

commit v6 on v5

--- a/solution.py
+++ b/solution.py
@@ -73,20 +73,18 @@
                 out_ref[r * cols + c, span] = jnp.where(row == r, along, edge).astype(BF)
 
 
-def rim_pick(row, col, cols):
-    shape = (3, 18, 16)
-    s, y, x = (lax.broadcasted_iota(jnp.int32, shape, i) for i in range(3))
-    y, x = y - 1, x + s - 1
+def rim_pick(row, col, cols, s, first, count, start, width):
+    cell = first + lax.broadcasted_iota(jnp.int32, (count, width), 0)
+    lane = start + lax.broadcasted_iota(jnp.int32, (count, width), 1)
+    y, x = cell // 16 - 1, cell % 16 + s - 1
     up = jnp.where(y < 0, -1, jnp.where(y > 15, 1, 0))
     side = jnp.where(x < 0, -1, jnp.where(x > 15, 1, 0))
     there_r, there_c = row + up, col + side
     inside = (there_r >= 0) & (there_r < 2) & (there_c >= 0) & (there_c < cols)
-    cell = jnp.where(up != 0, x - 16 * side, y)
-    got = 256 + (there_r * cols + there_c) * 16 + cell
+    got = 256 + (there_r * cols + there_c) * 16 + jnp.where(up != 0, x - 16 * side, y)
     index = jnp.where((up == 0) & (side == 0), 16 * y + x, got)
-    index = jnp.where(inside, index, -1).reshape(3, 288, 1)
-    width = 256 + 32 * cols
-    return (index == lax.broadcasted_iota(jnp.int32, (3, 288, width), 2)).astype(BF)
+    hit = inside & (index == lane)
+    return jnp.where(hit, 1.0, 0.0).astype(BF)
 
 
 def prepare_body(
@@ -106,54 +104,72 @@
         for k in range(4):
             pieces = [turned[160 * j + 40 * k : 160 * j + 40 * k + 40] for j in range(4)]
             slices_ref[4 * layer + k] = jnp.concatenate(pieces, axis=0).astype(BF)
-    for t in range(9):
-        copies[2 + t].wait()
-        q = q_all[t]
-        q_one_ref[t] = stacked_halves(q[:64])
-        y = dot(stacked_halves(q[64:]), hidden, NT)
-        y_ref[t] = stacked_halves(y[:64] + y[64:])
+    for b in range(3):
+        shifted = jnp.zeros((64, 384), F32)
+        for a in range(3):
+            t = 3 * a + b
+            copies[2 + t].wait()
+            q = q_all[t]
+            q_one_ref[b, 128 * a : 128 * a + 128] = stacked_halves(q[:64])
+            y = dot(stacked_halves(q[64:]), hidden, NT)
+            y = jnp.concatenate([y[:64] + y[64:], jnp.zeros((64, 128), F32)], axis=1)
+            shifted = shifted + (pltpu.roll(y, 16 * (2 - a), 1) if a < 2 else y)
+        y_ref[b] = stacked_halves(shifted)
 
 
 def power_body(
-    x_hbm, g_hbm, got_hbm, pick_hbm, slope_hbm, q_hbm, y_hbm, w_hbm,
+    x_hbm, g_hbm, got_hbm, slope_hbm, q_hbm, y_hbm, w_hbm,
     grad_ref, p_ref,
-    x_ref, g_ref, got_ref, pick_ref, slope_ref, q_ref, y_ref, w_all,
-    x_win, g_win, back, z_sum, p_sum, sems,
+    x_ref, g_ref, got_ref, slope_ref, q_ref, y_ref, w_all,
+    x_win, g_win, back, sems,
 ):
-    pairs = [(got_hbm, got_ref), (g_hbm, g_ref), (pick_hbm, pick_ref), (x_hbm, x_ref)]
-    pairs += [(q_hbm, q_ref), (y_hbm, y_ref), (slope_hbm, slope_ref)]
+    pairs = [(got_hbm, got_ref), (g_hbm, g_ref), (x_hbm, x_ref)]
+    pairs += [(y_hbm, y_ref), (q_hbm, q_ref), (slope_hbm, slope_ref)]
     pairs += [(w_hbm.at[t // 3, t % 3], w_all.at[t]) for t in range(9)]
     copies = fetch(pairs, sems)
-    for i in range(4):
-        copies[i].wait()
+    row, col = lax.axis_index("row"), lax.axis_index("col")
+    cols = got_ref.shape[0] // 2
+    width = 256 + 32 * cols
+    picks = [rim_pick(row, col, cols, s, 0, 288, 0, width) for s in (0, 2)]
+    ends = [rim_pick(row, col, cols, 1, r, 16, 256, 32 * cols) for r in (0, 272)]
+    picks = [picks[0], jnp.concatenate(ends, axis=0), picks[1]]
+    copies[0].wait()
     for i, (ref, win) in enumerate(((g_ref, g_win), (x_ref, x_win))):
-        cells = got_ref[:, 16 - 16 * i : 32 - 16 * i, :].reshape(-1, 640)
-        cells = jnp.concatenate([ref[...], cells], axis=0)
-        for s in range(3):
-            win[s] = dot(pick_ref[s], cells, NN).astype(BF)
+        copies[1 + i].wait()
+        rims = got_ref[:, 16 - 16 * i : 32 - 16 * i, :].reshape(-1, 640)
+        lines = dot(picks[1], rims, NN).astype(BF)
+        win[1, 0:16] = lines[:16]
+        win[1, 16:272] = ref[...]
+        win[1, 272:288] = lines[16:]
+        cells = jnp.concatenate([ref[...], rims], axis=0)
+        for s in (0, 2):
+            win[s] = dot(picks[s], cells, NN).astype(BF)
+    copies[3].wait()
     copies[4].wait()
-    copies[5].wait()
-    for t in range(9):
-        a, b = t // 3, t % 3
-        grads = g_win[2 - b, 16 * (2 - a) : 16 * (2 - a) + 256, :]
-        inputs = x_win[b, 16 * a : 16 * a + 256, :]
-        copies[7 + t].wait()
-        terms = (
-            (back, dot(grads, w_all[t], NT)),
-            (z_sum, dot(inputs, q_ref[t], NT)),
-            (p_sum, dot(y_ref[t], grads, NN)),
-        )
-        for ref, term in terms:
-            ref[...] = term if t == 0 else ref[...] + term
-    copies[6].wait()
-    grad = (back[...] * slope_ref[...]).astype(BF)
-    grad_ref[...] = grad
-    one = dot(paired_halves(z_sum[...]).astype(BF), grad, TN)
+    two, z_sum = 0.0, 0.0
+    for b in range(3):
+        two = two + dot(y_ref[b][:, :288], g_win[2 - b], NN)
+        wide = dot(x_win[b], q_ref[b], NT)
+        for a in range(3):
+            z_sum = z_sum + wide[16 * a : 16 * a + 256, 128 * a : 128 * a + 128]
     each = p_ref.shape[1]
-    for layer, value in enumerate((one, p_sum[...])):
+
+    def put(layer, value):
         value = value[:64] + value[64:]
         for i in range(64 // each):
             p_ref[layer * (64 // each) + i] = value[i * each : (i + 1) * each]
+
+    put(1, two)
+    z_sum = paired_halves(z_sum).astype(BF)
+    for t in range(9):
+        a, b = t // 3, t % 3
+        copies[6 + t].wait()
+        term = dot(g_win[2 - b, 16 * (2 - a) : 16 * (2 - a) + 256, :], w_all[t], NT)
+        back[...] = term if t == 0 else back[...] + term
+    copies[5].wait()
+    grad = (back[...] * slope_ref[...]).astype(BF)
+    grad_ref[...] = grad
+    put(0, dot(z_sum, grad, TN))
 
 
 def sum_body(got_ref, out_ref):
@@ -252,7 +268,7 @@
     whole = pl.BlockSpec(memory_space=pltpu.VMEM)
     far = pl.BlockSpec(memory_space=pltpu.HBM)
     images, rows, cols = (lax.axis_size(a) for a in ALL)
-    z, row, col = (lax.axis_index(a) for a in ALL)
+    z = lax.axis_index("dp")
     plane, devices = rows * cols, images * rows * cols
     x, act, g = (v.reshape(256, 640) for v in (x_input, pre_act, out_grad))
     q_t = q_prev.transpose(1, 2, 0).reshape(128, 5760)
@@ -272,8 +288,8 @@
         prepare_body,
         (
             shape((8, 160, 256), BF),
-            shape((9, 128, 640), BF),
-            shape((9, 128, 256), BF),
+            shape((3, 384, 640), BF),
+            shape((3, 128, 384), BF),
             shape((256, 640), F32),
         ),
         2 * 1152 * 640 * 256,
@@ -293,24 +309,21 @@
         2 * 256 * 5760 * 1100,
         12 << 20,
         vmem=62,
-        in_specs=[far] * 8,
+        in_specs=[far] * 7,
         scratch_shapes=[
             pltpu.VMEM((256, 640), BF),
             pltpu.VMEM((256, 640), BF),
             pltpu.VMEM((plane, 32, 640), BF),
-            pltpu.VMEM((3, 288, 256 + 32 * cols), BF),
             pltpu.VMEM((256, 640), F32),
-            pltpu.VMEM((9, 128, 640), BF),
-            pltpu.VMEM((9, 128, 256), BF),
+            pltpu.VMEM((3, 384, 640), BF),
+            pltpu.VMEM((3, 128, 384), BF),
             pltpu.VMEM((9, 640, 640), BF),
             pltpu.VMEM((3, 288, 640), BF),
             pltpu.VMEM((3, 288, 640), BF),
             pltpu.VMEM((256, 640), F32),
-            pltpu.VMEM((256, 128), F32),
-            pltpu.VMEM((128, 640), F32),
-            sems((16,)),
+            sems((15,)),
         ],
-    )(x, g, got, rim_pick(row, col, cols), slope, q_one, y_two, conv_weight)
+    )(x, g, got, slope, q_one, y_two, conv_weight)
 
     p_part, slices = lax.optimization_barrier((p_part, slices))
     if parts == devices:

time: 104 us -> 103 us (level)
  waiting for transfers between devices: 10.2 us -> 11.5 us
  other arithmetic: 1.06 us -> 0 us
    all_to_all x4, waiting for transfers between devices: 10.2 us -> 11.5 us  [exchange(): return lax.all_to_all(chunks, axes, 0, 0, tiled=True)]
  transfers between devices with their start and end apart: 4 -> 4, of which waited for: 3 -> 4; matrix products, arithmetic and copies ran while one was open for 2% -> 1% of each run, Pallas kernels for 22% -> 22%
where the time goes in v6:
time: 103 us; the launch traced here: 102 us
  blocking collectives  42.5 us (41%)
  Pallas kernels  30.1 us (29%)
  starting transfers between devices  15.9 us (15%)
  waiting for transfers between devices  11.5 us (11%)
  local copies, waits for them, and re-layouts  1.75 us (2%)
    all_to_all x3, blocking collectives, exchange(): return lax.all_to_all(chunks, axes, 0, 0, tiled=True)  42.5 us
    all_to_all x4, starting transfers between devices, exchange(): return lax.all_to_all(chunks, axes, 0, 0, tiled=True)  15.9 us
    all_to_all x4, waiting for transfers between devices, exchange(): return lax.all_to_all(chunks, axes, 0, 0, tiled=True)  11.5 us
    pallas_call x1, Pallas kernels, on_device(): call(power_body, (shape((256, 640), BF), shape((parts, each, 640), F32)),...  9.72 us
    pallas_call x1, Pallas kernels, on_device(): call(factor_body, (shape((2, 64, 64), F32), shape((2, 64, 640), F32)), 1...  6.41 us
    pallas_call x1, Pallas kernels, on_device(): call(prepare_body, (shape((8, 160, 256), BF), shape((3, 384, 640), BF), s...  6.2 us
    pallas_call x1, Pallas kernels, on_device(): call(taps_body, shape((4, 64, 384), BF), 2 * 160 * 2048 * 1152, 2 << 20,...  2.31 us
    pallas_call x1, Pallas kernels, on_device(): call(rim_body, shape((plane, 32, 640), BF), 1 << 24, 1 << 20, vmem=62, in...  2.09 us
  transfers between devices with their start and end apart: 4, of which 4 were waited for; matrix products, arithmetic and copies ran while one was open for 1% of the time, Pallas kernels for 22%

profile of v6, /device:TPU:0, one launch (start us, length us, event | category | flops | bytes accessed | tf_op | source)
XLA Modules:
  0.0 102.3 jit_solution(2319507972331435487)
XLA Ops:
  0.6 2.1 %shard_map.68 = bf16[8,32,640]{2,1,0:T(8,128)(2,1)} custom-call(bf16[256,640]{1,0:T(8,128)(2,1)} %bitcast.13, bf16[256,640]{1,0:T(8,128)(2,1)} %bitcast.9), custom_call_target="tpu_custom_call" | custom-call | flops 16777216 | bytes 1048576 | tf_op jit(solution)/shard_map/pallas_call | solution.py:277
  2.7 5.2 %all-to-all-start = ((bf16[8,32,640]{2,1,0:T(8,128)(2,1)}), bf16[8,32,640]{2,1,0:T(8,128)(2,1)S(1)}, u32[]{:S(2)}, u32[]{:S(2)}) async-start(bf16[8,32,640]{2,1,0:T(8,128)(2,1)} %shard_map.68), calls=%async_computation | async-start | bytes 655360 | tf_op jit(solution)/shard_map/all_to_all | solution.py:35
  7.9 6.2 %shard_map.69 = (bf16[8,160,256]{2,1,0:T(8,128)(2,1)}, bf16[3,384,640]{2,1,0:T(8,128)(2,1)}, bf16[3,128,384]{2,1,0:T(8,128)(2,1)}, f32[256,640]{1,0:T(8,128)}) custom-call(bf16[256,640]{1,0:T(8,128)(2,1)} %bitcast.14, bf16[256,640]{1,0:T(8,128)(2,1)} %bitcast.17, f32[128,5760]{1,0:T(8,128)} %bitcast.12), custom_call_target="tpu_custom_call" | custom-call | flops 377487360 | bytes 8388608 | tf_op jit(solution)/shard_map/pallas_call | solution.py:287
  14.1 1.0 all-to-all-done.got_hbm
  15.1 0.0 copy-start.2
  15.1 3.5 %all-to-all-start.1 = ((bf16[8,160,256]{2,1,0:T(8,128)(2,1)}), bf16[8,160,256]{2,1,0:T(8,128)(2,1)S(1)}, u32[]{:S(2)}, u32[]{:S(2)}) async-start(bf16[8,160,256]{2,1,0:T(8,128)(2,1)} %get-tuple-element.18), calls=%async_computation.1 | async-start | bytes 1310720 | tf_op jit(solution)/shard_map/all_to_all | solution.py:35
  18.7 0.0 copy-done.2
  18.7 0.0 copy-start
  18.7 9.7 %shard_map.70 = (bf16[256,640]{1,0:T(8,128)(2,1)}, f32[32,4,640]{2,1,0:T(4,128)}) custom-call(bf16[256,640]{1,0:T(8,128)(2,1)} %bitcast.15, bf16[256,640]{1,0:T(8,128)(2,1)} %bitcast.10, bf16[8,32,640]{2,1,0:T(8,128)(2,1)} %copy-done.2, f32[256,640]{1,0:T(8,128)} %get-tuple-element.14.slope_hbm, bf16[3,384,640]{2,1,0:T(8,128)(2,1)} %get-tuple-element.15.q_hbm, ...), custom_call_target="tpu_custom_call" | custom-call | flops 3244032000 | bytes 12582912 | tf_op jit(solution)/shard_map/pallas_call | solution.py:306
  28.4 0.8 all-to-all-done.1.x_ref
  29.3 17.7 %all_to_all.35.got_ref = f32[32,4,640]{2,1,0:T(4,128)S(1)} all-to-all(f32[32,4,640]{2,1,0:T(4,128)} %get-tuple-element.19), channel_id=1, replica_groups=mesh['dp'=4,'row'=2,'col'=4] {'dp','row','col'}, dimensions={0} | all-to-all | bytes 655360 | tf_op jit(solution)/shard_map/all_to_all | solution.py:35
  46.9 0.1 shard_map.71
  47.0 14.2 %all_to_all.36.got_ref = f32[32,4,640]{2,1,0:T(4,128)S(1)} all-to-all(f32[32,4,640]{2,1,0:T(4,128)S(1)} %shard_map.71), channel_id=1, replica_groups=mesh['dp'=4,'row'=2,'col'=4] {'dp','row','col'}, dimensions={0} | all-to-all | bytes 655360 | tf_op jit(solution)/shard_map/all_to_all | solution.py:35
  61.2 0.0 copy-done
  61.2 0.0 copy-start.1
  61.2 1.0 copy-done.1
  62.2 1.2 %shard_map.72 = (bf16[8,256,128]{2,1,0:T(8,128)(2,1)}, f32[128,640]{1,0:T(8,128)S(1)}) custom-call(f32[32,4,640]{2,1,0:T(4,128)S(1)} %all_to_all.36.got_ref, bf16[256,640]{1,0:T(8,128)(2,1)S(1)} %copy-done.1, bf16[256,640]{1,0:T(8,128)(2,1)S(1)} %bitcast.11), custom_call_target="tpu_custom_call" | custom-call | flops 83886080 | bytes 2097152 | tf_op jit(solution)/shard_map/pallas_call | solution.py:336
  63.4 3.7 %all-to-all-start.4 = ((bf16[8,256,128]{2,1,0:T(8,128)(2,1)}), bf16[8,256,128]{2,1,0:T(8,128)(2,1)S(1)}, u32[]{:S(2)}, u32[]{:S(2)}) async-start(bf16[8,256,128]{2,1,0:T(8,128)(2,1)} %get-tuple-element.23), calls=%async_computation.4 | async-start | bytes 1048576 | tf_op jit(solution)/shard_map/all_to_all | solution.py:35
  67.1 6.4 %shard_map.73 = (f32[2,64,64]{2,1,0:T(8,128)S(1)}, f32[2,64,640]{2,1,0:T(8,128)S(1)}) custom-call(f32[128,640]{1,0:T(8,128)S(1)} %get-tuple-element.21.p_ref), custom_call_target="tpu_custom_call" | custom-call | flops 1073741824 | bytes 1048576 | tf_op jit(solution)/shard_map/pallas_call | solution.py:343
  73.5 2.6 %all-to-all-done.4.w_ref = bf16[8,256,128]{2,1,0:T(8,128)(2,1)S(1)} async-done(((bf16[8,256,128]{2,1,0:T(8,128)(2,1)}), bf16[8,256,128]{2,1,0:T(8,128)(2,1)S(1)}, u32[]{:S(2)}, u32[]{:S(2)}) %all-to-all-start.4) | async-done | bytes 524320 | tf_op jit(solution)/shard_map/all_to_all | solution.py:35
  76.1 2.3 %shard_map.74 = bf16[4,64,384]{2,1,0:T(8,128)(2,1)S(1)} custom-call(bf16[8,256,128]{2,1,0:T(8,128)(2,1)S(1)} %all-to-all-done.4.w_ref, bf16[8,160,256]{2,1,0:T(8,128)(2,1)S(1)} %all-to-all-done.1.x_ref, f32[2,64,64]{2,1,0:T(8,128)S(1)} %get-tuple-element.25.inverse_ref), custom_call_target="tpu_custom_call" | custom-call | flops 754974720 | bytes 2097152 | tf_op jit(solution)/shard_map/pallas_call | solution.py:352
  78.4 10.6 %all_to_all.37.got_ref = bf16[4,64,384]{2,1,0:T(8,128)(2,1)S(1)} all-to-all(bf16[4,64,384]{2,1,0:T(8,128)(2,1)S(1)} %shard_map.74), channel_id=1, replica_groups=mesh['dp'=4,'row'=2,'col'=4] {'dp'}, dimensions={0} | all-to-all | bytes 393216 | tf_op jit(solution)/shard_map/all_to_all | solution.py:35
  89.0 0.8 shard_map.75
  89.8 3.5 %all-to-all-start.6 = ((bf16[8,64,384]{2,1,0:T(8,128)(2,1)}), bf16[8,64,384]{2,1,0:T(8,128)(2,1)S(1)}, u32[]{:S(2)}, u32[]{:S(2)}) async-start(bf16[8,64,384]{2,1,0:T(8,128)(2,1)} %shard_map.75), calls=%async_computation.6 | async-start | bytes 786432 | tf_op jit(solution)/shard_map/all_to_all | solution.py:35
  93.2 0.8 dynamic-slice_bitcast_fusion
  94.0 7.0 %all-to-all-done.6.got_ref = bf16[8,64,384]{2,1,0:T(8,128)(2,1)S(1)} async-done(((bf16[8,64,384]{2,1,0:T(8,128)(2,1)}), bf16[8,64,384]{2,1,0:T(8,128)(2,1)S(1)}, u32[]{:S(2)}, u32[]{:S(2)}) %all-to-all-start.6) | async-done | bytes 393248 | tf_op jit(solution)/shard_map/all_to_all | solution.py:35
  101.0 1.3 %shard_map.76 = f32[2,64,1440]{2,1,0:T(8,128)} custom-call(bf16[8,64,384]{2,1,0:T(8,128)(2,1)S(1)} %all-to-all-done.6.got_ref), custom_call_target="tpu_custom_call" | custom-call | bytes 1048576 | tf_op jit(solution)/shard_map/pallas_call | solution.py:364
Async XLA Ops:
  2.7 12.4 %all-to-all-start = ((bf16[8,32,640]{2,1,0:T(8,128)(2,1)}), bf16[8,32,640]{2,1,0:T(8,128)(2,1)S(1)}, u32[]{:S(2)}, u32[]{:S(2)}) async-start(bf16[8,32,640]{2,1,0:T(8,128)(2,1)} %shard_map.68), calls=%async_computation | async-start | bytes 655360 | tf_op jit(solution)/shard_map/all_to_all | solution.py:35
  15.1 3.6 %copy-start.2 = (bf16[8,32,640]{2,1,0:T(8,128)(2,1)}, bf16[8,32,640]{2,1,0:T(8,128)(2,1)S(1)}, u32[]{:S(2)}) copy-start(bf16[8,32,640]{2,1,0:T(8,128)(2,1)S(1)} %all-to-all-done.got_hbm) | copy-start | bytes 983044
  15.1 14.1 %all-to-all-start.1 = ((bf16[8,160,256]{2,1,0:T(8,128)(2,1)}), bf16[8,160,256]{2,1,0:T(8,128)(2,1)S(1)}, u32[]{:S(2)}, u32[]{:S(2)}) async-start(bf16[8,160,256]{2,1,0:T(8,128)(2,1)} %get-tuple-element.18), calls=%async_computation.1 | async-start | bytes 1310720 | tf_op jit(solution)/shard_map/all_to_all | solution.py:35
  18.7 42.6 %copy-start = (bf16[1,16,16,640]{3,2,1,0:T(8,128)(2,1)S(1)}, bf16[1,16,16,640]{3,2,1,0:T(8,128)(2,1)}, u32[]{:S(2)}) copy-start(bf16[1,16,16,640]{3,2,1,0:T(8,128)(2,1)} %param.7) | copy-start | bytes 983044
  61.2 1.0 copy-start.1
  63.4 12.7 %all-to-all-start.4 = ((bf16[8,256,128]{2,1,0:T(8,128)(2,1)}), bf16[8,256,128]{2,1,0:T(8,128)(2,1)S(1)}, u32[]{:S(2)}, u32[]{:S(2)}) async-start(bf16[8,256,128]{2,1,0:T(8,128)(2,1)} %get-tuple-element.23), calls=%async_computation.4 | async-start | bytes 1048576 | tf_op jit(solution)/shard_map/all_to_all | solution.py:35
  89.8 11.2 %all-to-all-start.6 = ((bf16[8,64,384]{2,1,0:T(8,128)(2,1)}), bf16[8,64,384]{2,1,0:T(8,128)(2,1)S(1)}, u32[]{:S(2)}, u32[]{:S(2)}) async-start(bf16[8,64,384]{2,1,0:T(8,128)(2,1)} %shard_map.75), calls=%async_computation.6 | async-start | bytes 786432 | tf_op jit(solution)/shard_map/all_to_all | solution.py:35

commit v7 on v6

--- a/solution.py
+++ b/solution.py
@@ -161,11 +161,13 @@
 
     put(1, two)
     z_sum = paired_halves(z_sum).astype(BF)
-    for t in range(9):
-        a, b = t // 3, t % 3
-        copies[6 + t].wait()
-        term = dot(g_win[2 - b, 16 * (2 - a) : 16 * (2 - a) + 256, :], w_all[t], NT)
-        back[...] = term if t == 0 else back[...] + term
+    for a in range(3):
+        windows = [g_win[2 - b, 16 * (2 - a) : 16 * (2 - a) + 256, :] for b in range(3)]
+        for b in range(3):
+            copies[6 + 3 * a + b].wait()
+        taps = jnp.concatenate([w_all[3 * a + b] for b in range(3)], axis=1)
+        term = dot(jnp.concatenate(windows, axis=1), taps, NT)
+        back[...] = term if a == 0 else back[...] + term
     copies[5].wait()
     grad = (back[...] * slope_ref[...]).astype(BF)
     grad_ref[...] = grad
@@ -178,13 +180,15 @@
         out_ref[i] = total
 
 
-def project_body(got_ref, grad_ref, g_ref, w_ref, p_ref):
+def project_body(got_ref, grad_hbm, g_hbm, w_ref, p_ref, grad_ref, g_ref, sems):
+    copies = fetch(((grad_hbm, grad_ref), (g_hbm, g_ref)), sems)
     each = got_ref.shape[1]
     for i in range(16):
         rows = [got_ref[i * (8 // each) + j] for j in range(8 // each)]
         p_ref[8 * i : 8 * i + 8, :] = jnp.concatenate(rows, axis=0)
     for layer, ref in enumerate((grad_ref, g_ref)):
         factor = stacked_halves(p_ref[64 * layer : 64 * layer + 64, :])
+        copies[layer].wait()
         out = paired_halves(dot(ref[...], factor, NT)).astype(BF)
         for k in range(4):
             w_ref[4 * layer + k] = out
@@ -229,12 +233,10 @@
             image[1 + 16 * r : 17 + 16 * r, :, :, 128 * i : 128 * i + 128] = value.astype(BF).reshape(
                 16, 4, 16, 128
             )
+    slices = jnp.concatenate([x_ref[4 * r + c] for c in range(4) for r in range(2)], axis=1)
     for a in range(3):
-        total = jnp.zeros((160, 384), F32)
-        for r in range(2):
-            for c in range(4):
-                window = image[16 * r + 2 - a : 16 * r + 18 - a, c].reshape(256, 384)
-                total = total + dot(x_ref[4 * r + c], window, NN)
+        windows = [image[2 - a : 34 - a, c].reshape(512, 384) for c in range(4)]
+        total = dot(slices, jnp.concatenate(windows, axis=0), NN)
         for b in range(3):
             t = 3 * a + b
             value = total[:, 128 * b : 128 * b + 128]
@@ -338,6 +340,9 @@
         (shape((8, 256, 128), BF), shape((128, 640), F32)),
         2 * 512 * 640 * 128,
         2 << 20,
+        vmem=62,
+        in_specs=[whole, far, far],
+        scratch_shapes=[pltpu.VMEM((256, 640), BF)] * 2 + [sems((2,))],
     )(p_all, pre_grad, g)
     w_all = exchange(w_own, PLANE)
     inverse, basis = call(

time: 103 us -> 104 us (level)
  Pallas kernels: 30.1 us -> 31.5 us
    pallas_call x1, Pallas kernels: 1.21 us -> 3.5 us  [on_device(): call(project_body, (shape((8, 256, 128), BF), shape((128, 640), F32)), 2...]
  transfers between devices with their start and end apart: 4 -> 4, of which waited for: 4 -> 4; matrix products, arithmetic and copies ran while one was open for 1% -> 1% of each run, Pallas kernels for 22% -> 21%
where the time goes in v7:
time: 104 us; the launch traced here: 103 us
  blocking collectives  42 us (40%)
  Pallas kernels  31.5 us (30%)
  starting transfers between devices  15.9 us (15%)
  waiting for transfers between devices  11.4 us (11%)
  local copies, waits for them, and re-layouts  1.73 us (2%)
    all_to_all x3, blocking collectives, exchange(): return lax.all_to_all(chunks, axes, 0, 0, tiled=True)  42 us
    all_to_all x4, starting transfers between devices, exchange(): return lax.all_to_all(chunks, axes, 0, 0, tiled=True)  15.9 us
    all_to_all x4, waiting for transfers between devices, exchange(): return lax.all_to_all(chunks, axes, 0, 0, tiled=True)  11.4 us
    pallas_call x1, Pallas kernels, on_device(): call(power_body, (shape((256, 640), BF), shape((parts, each, 640), F32)),...  8.79 us
    pallas_call x1, Pallas kernels, on_device(): call(factor_body, (shape((2, 64, 64), F32), shape((2, 64, 640), F32)), 1...  6.42 us
    pallas_call x1, Pallas kernels, on_device(): call(prepare_body, (shape((8, 160, 256), BF), shape((3, 384, 640), BF), s...  6.2 us
    pallas_call x1, Pallas kernels, on_device(): call(project_body, (shape((8, 256, 128), BF), shape((128, 640), F32)), 2...  3.5 us
    pallas_call x1, Pallas kernels, on_device(): call(taps_body, shape((4, 64, 384), BF), 2 * 160 * 2048 * 1152, 2 << 20,...  2.32 us
  transfers between devices with their start and end apart: 4, of which 4 were waited for; matrix products, arithmetic and copies ran while one was open for 1% of the time, Pallas kernels for 21%

profile of v7, /device:TPU:0, one launch (start us, length us, event | category | flops | bytes accessed | tf_op | source)
XLA Modules:
  0.0 103.2 jit_solution(13314659072816330760)
XLA Ops:
  0.6 2.1 %shard_map.68 = bf16[8,32,640]{2,1,0:T(8,128)(2,1)} custom-call(bf16[256,640]{1,0:T(8,128)(2,1)} %bitcast.10, bf16[256,640]{1,0:T(8,128)(2,1)} %bitcast.13), custom_call_target="tpu_custom_call" | custom-call | flops 16777216 | bytes 1048576 | tf_op jit(solution)/shard_map/pallas_call | solution.py:279
  2.7 5.2 %all-to-all-start = ((bf16[8,32,640]{2,1,0:T(8,128)(2,1)}), bf16[8,32,640]{2,1,0:T(8,128)(2,1)S(1)}, u32[]{:S(2)}, u32[]{:S(2)}) async-start(bf16[8,32,640]{2,1,0:T(8,128)(2,1)} %shard_map.68), calls=%async_computation | async-start | bytes 655360 | tf_op jit(solution)/shard_map/all_to_all | solution.py:35
  7.9 6.2 %shard_map.69 = (bf16[8,160,256]{2,1,0:T(8,128)(2,1)}, bf16[3,384,640]{2,1,0:T(8,128)(2,1)}, bf16[3,128,384]{2,1,0:T(8,128)(2,1)}, f32[256,640]{1,0:T(8,128)}) custom-call(bf16[256,640]{1,0:T(8,128)(2,1)} %bitcast.11, bf16[256,640]{1,0:T(8,128)(2,1)} %bitcast.17, f32[128,5760]{1,0:T(8,128)} %bitcast.9), custom_call_target="tpu_custom_call" | custom-call | flops 377487360 | bytes 8388608 | tf_op jit(solution)/shard_map/pallas_call | solution.py:289
  14.1 1.0 all-to-all-done.got_hbm
  15.1 0.0 copy-start.1
  15.1 3.5 %all-to-all-start.1 = ((bf16[8,160,256]{2,1,0:T(8,128)(2,1)}), bf16[8,160,256]{2,1,0:T(8,128)(2,1)S(1)}, u32[]{:S(2)}, u32[]{:S(2)}) async-start(bf16[8,160,256]{2,1,0:T(8,128)(2,1)} %get-tuple-element.18), calls=%async_computation.1 | async-start | bytes 1310720 | tf_op jit(solution)/shard_map/all_to_all | solution.py:35
  18.7 0.0 copy-done.1
  18.7 8.8 %shard_map.70 = (bf16[256,640]{1,0:T(8,128)(2,1)}, f32[32,4,640]{2,1,0:T(4,128)}) custom-call(bf16[256,640]{1,0:T(8,128)(2,1)} %bitcast.12, bf16[256,640]{1,0:T(8,128)(2,1)} %bitcast.14, bf16[8,32,640]{2,1,0:T(8,128)(2,1)} %copy-done.1, f32[256,640]{1,0:T(8,128)} %get-tuple-element.14.slope_hbm, bf16[3,384,640]{2,1,0:T(8,128)(2,1)} %get-tuple-element.15.q_hbm, ...), custom_call_target="tpu_custom_call" | custom-call | flops 3244032000 | bytes 12582912 | tf_op jit(solution)/shard_map/pallas_call | solution.py:308
  27.5 1.8 %all-to-all-done.1.x_ref = bf16[8,160,256]{2,1,0:T(8,128)(2,1)S(1)} async-done(((bf16[8,160,256]{2,1,0:T(8,128)(2,1)}), bf16[8,160,256]{2,1,0:T(8,128)(2,1)S(1)}, u32[]{:S(2)}, u32[]{:S(2)}) %all-to-all-start.1) | async-done | bytes 655392 | tf_op jit(solution)/shard_map/all_to_all | solution.py:35
  29.3 16.8 %all_to_all.35.got_ref = f32[32,4,640]{2,1,0:T(4,128)S(1)} all-to-all(f32[32,4,640]{2,1,0:T(4,128)} %get-tuple-element.19), channel_id=1, replica_groups=mesh['dp'=4,'row'=2,'col'=4] {'dp','row','col'}, dimensions={0} | all-to-all | bytes 655360 | tf_op jit(solution)/shard_map/all_to_all | solution.py:35
  46.0 0.1 shard_map.71
  46.1 14.7 %all_to_all.36.got_ref = f32[32,4,640]{2,1,0:T(4,128)} all-to-all(f32[32,4,640]{2,1,0:T(4,128)S(1)} %shard_map.71), channel_id=1, replica_groups=mesh['dp'=4,'row'=2,'col'=4] {'dp','row','col'}, dimensions={0} | all-to-all | bytes 655360 | tf_op jit(solution)/shard_map/all_to_all | solution.py:35
  60.8 3.5 %shard_map.72 = (bf16[8,256,128]{2,1,0:T(8,128)(2,1)}, f32[128,640]{1,0:T(8,128)}) custom-call(f32[32,4,640]{2,1,0:T(4,128)} %all_to_all.36.got_ref, bf16[256,640]{1,0:T(8,128)(2,1)} %get-tuple-element.20.grad_hbm, bf16[256,640]{1,0:T(8,128)(2,1)} %bitcast.15), custom_call_target="tpu_custom_call" | custom-call | flops 83886080 | bytes 2097152 | tf_op jit(solution)/shard_map/pallas_call | solution.py:338
  64.3 3.7 %all-to-all-start.4 = ((bf16[8,256,128]{2,1,0:T(8,128)(2,1)}), bf16[8,256,128]{2,1,0:T(8,128)(2,1)S(1)}, u32[]{:S(2)}, u32[]{:S(2)}) async-start(bf16[8,256,128]{2,1,0:T(8,128)(2,1)} %get-tuple-element.23), calls=%async_computation.4 | async-start | bytes 1048576 | tf_op jit(solution)/shard_map/all_to_all | solution.py:35
  68.0 0.0 copy-start
  68.0 1.0 copy-done
  69.0 6.4 %shard_map.73 = (f32[2,64,64]{2,1,0:T(8,128)S(1)}, f32[2,64,640]{2,1,0:T(8,128)S(1)}) custom-call(f32[128,640]{1,0:T(8,128)S(1)} %copy-done), custom_call_target="tpu_custom_call" | custom-call | flops 1073741824 | bytes 1048576 | tf_op jit(solution)/shard_map/pallas_call | solution.py:348
  75.4 1.6 %all-to-all-done.4.w_ref = bf16[8,256,128]{2,1,0:T(8,128)(2,1)S(1)} async-done(((bf16[8,256,128]{2,1,0:T(8,128)(2,1)}), bf16[8,256,128]{2,1,0:T(8,128)(2,1)S(1)}, u32[]{:S(2)}, u32[]{:S(2)}) %all-to-all-start.4) | async-done | bytes 524320 | tf_op jit(solution)/shard_map/all_to_all | solution.py:35
  77.0 2.3 %shard_map.74 = bf16[4,64,384]{2,1,0:T(8,128)(2,1)S(1)} custom-call(bf16[8,256,128]{2,1,0:T(8,128)(2,1)S(1)} %all-to-all-done.4.w_ref, bf16[8,160,256]{2,1,0:T(8,128)(2,1)S(1)} %all-to-all-done.1.x_ref, f32[2,64,64]{2,1,0:T(8,128)S(1)} %get-tuple-element.25.inverse_ref), custom_call_target="tpu_custom_call" | custom-call | flops 754974720 | bytes 2097152 | tf_op jit(solution)/shard_map/pallas_call | solution.py:357
  79.3 10.6 %all_to_all.37.got_ref = bf16[4,64,384]{2,1,0:T(8,128)(2,1)S(1)} all-to-all(bf16[4,64,384]{2,1,0:T(8,128)(2,1)S(1)} %shard_map.74), channel_id=1, replica_groups=mesh['dp'=4,'row'=2,'col'=4] {'dp'}, dimensions={0} | all-to-all | bytes 393216 | tf_op jit(solution)/shard_map/all_to_all | solution.py:35
  89.9 0.8 shard_map.75
  90.7 3.5 %all-to-all-start.6 = ((bf16[8,64,384]{2,1,0:T(8,128)(2,1)}), bf16[8,64,384]{2,1,0:T(8,128)(2,1)S(1)}, u32[]{:S(2)}, u32[]{:S(2)}) async-start(bf16[8,64,384]{2,1,0:T(8,128)(2,1)} %shard_map.75), calls=%async_computation.6 | async-start | bytes 786432 | tf_op jit(solution)/shard_map/all_to_all | solution.py:35
  94.2 0.8 dynamic-slice_bitcast_fusion
  94.9 7.0 %all-to-all-done.6.got_ref = bf16[8,64,384]{2,1,0:T(8,128)(2,1)S(1)} async-done(((bf16[8,64,384]{2,1,0:T(8,128)(2,1)}), bf16[8,64,384]{2,1,0:T(8,128)(2,1)S(1)}, u32[]{:S(2)}, u32[]{:S(2)}) %all-to-all-start.6) | async-done | bytes 393248 | tf_op jit(solution)/shard_map/all_to_all | solution.py:35
  101.9 1.3 %shard_map.76 = f32[2,64,1440]{2,1,0:T(8,128)} custom-call(bf16[8,64,384]{2,1,0:T(8,128)(2,1)S(1)} %all-to-all-done.6.got_ref), custom_call_target="tpu_custom_call" | custom-call | bytes 1048576 | tf_op jit(solution)/shard_map/pallas_call | solution.py:369
Async XLA Ops:
  2.7 12.4 %all-to-all-start = ((bf16[8,32,640]{2,1,0:T(8,128)(2,1)}), bf16[8,32,640]{2,1,0:T(8,128)(2,1)S(1)}, u32[]{:S(2)}, u32[]{:S(2)}) async-start(bf16[8,32,640]{2,1,0:T(8,128)(2,1)} %shard_map.68), calls=%async_computation | async-start | bytes 655360 | tf_op jit(solution)/shard_map/all_to_all | solution.py:35
  15.1 3.6 %copy-start.1 = (bf16[8,32,640]{2,1,0:T(8,128)(2,1)}, bf16[8,32,640]{2,1,0:T(8,128)(2,1)S(1)}, u32[]{:S(2)}) copy-start(bf16[8,32,640]{2,1,0:T(8,128)(2,1)S(1)} %all-to-all-done.got_hbm) | copy-start | bytes 983044
  15.1 14.1 %all-to-all-start.1 = ((bf16[8,160,256]{2,1,0:T(8,128)(2,1)}), bf16[8,160,256]{2,1,0:T(8,128)(2,1)S(1)}, u32[]{:S(2)}, u32[]{:S(2)}) async-start(bf16[8,160,256]{2,1,0:T(8,128)(2,1)} %get-tuple-element.18), calls=%async_computation.1 | async-start | bytes 1310720 | tf_op jit(solution)/shard_map/all_to_all | solution.py:35
  64.3 12.7 %all-to-all-start.4 = ((bf16[8,256,128]{2,1,0:T(8,128)(2,1)}), bf16[8,256,128]{2,1,0:T(8,128)(2,1)S(1)}, u32[]{:S(2)}, u32[]{:S(2)}) async-start(bf16[8,256,128]{2,1,0:T(8,128)(2,1)} %get-tuple-element.23), calls=%async_computation.4 | async-start | bytes 1048576 | tf_op jit(solution)/shard_map/all_to_all | solution.py:35
  68.0 1.0 copy-start
  90.7 11.2 %all-to-all-start.6 = ((bf16[8,64,384]{2,1,0:T(8,128)(2,1)}), bf16[8,64,384]{2,1,0:T(8,128)(2,1)S(1)}, u32[]{:S(2)}, u32[]{:S(2)}) async-start(bf16[8,64,384]{2,1,0:T(8,128)(2,1)} %shard_map.75), calls=%async_computation.6 | async-start | bytes 786432 | tf_op jit(solution)/shard_map/all_to_all | solution.py:35

commit v8 on v7

--- a/solution.py
+++ b/solution.py
@@ -119,7 +119,7 @@
 
 def power_body(
     x_hbm, g_hbm, got_hbm, slope_hbm, q_hbm, y_hbm, w_hbm,
-    grad_ref, p_ref,
+    keep_ref, swap_ref, p_ref,
     x_ref, g_ref, got_ref, slope_ref, q_ref, y_ref, w_all,
     x_win, g_win, back, sems,
 ):
@@ -157,7 +157,8 @@
     def put(layer, value):
         value = value[:64] + value[64:]
         for i in range(64 // each):
-            p_ref[layer * (64 // each) + i] = value[i * each : (i + 1) * each]
+            owner = i // cols * 2 * cols + layer * cols + i % cols
+            p_ref[owner] = value[i * each : (i + 1) * each]
 
     put(1, two)
     z_sum = paired_halves(z_sum).astype(BF)
@@ -170,7 +171,8 @@
         back[...] = term if a == 0 else back[...] + term
     copies[5].wait()
     grad = (back[...] * slope_ref[...]).astype(BF)
-    grad_ref[...] = grad
+    keep_ref[...] = jnp.where(row == 0, grad, g_ref[...])
+    swap_ref[...] = jnp.where(row == 0, g_ref[...], grad)
     put(0, dot(z_sum, grad, TN))
 
 
@@ -180,59 +182,59 @@
         out_ref[i] = total
 
 
-def project_body(got_ref, grad_hbm, g_hbm, w_ref, p_ref, grad_ref, g_ref, sems):
-    copies = fetch(((grad_hbm, grad_ref), (g_hbm, g_ref)), sems)
+def project_body(got_ref, keep_ref, swap_ref, w_ref, p_ref):
+    row = lax.axis_index("row")
     each = got_ref.shape[1]
-    for i in range(16):
+    for i in range(8):
         rows = [got_ref[i * (8 // each) + j] for j in range(8 // each)]
         p_ref[8 * i : 8 * i + 8, :] = jnp.concatenate(rows, axis=0)
-    for layer, ref in enumerate((grad_ref, g_ref)):
-        factor = stacked_halves(p_ref[64 * layer : 64 * layer + 64, :])
-        copies[layer].wait()
+    factor = stacked_halves(p_ref[...])
+    for start, ref in ((row, keep_ref), (1 - row, swap_ref)):
         out = paired_halves(dot(ref[...], factor, NT)).astype(BF)
         for k in range(4):
-            w_ref[4 * layer + k] = out
-
-
-def factor_body(p_ref, inverse_ref, basis_ref):
+            w_ref[k, pl.ds(pl.multiple_of(256 * start, 256), 256), :] = out
+
+
+def factor_body(p_ref, inverse_ref, basis_ref, share_ref, slot):
     high = lax.Precision.HIGHEST
     line = lax.broadcasted_iota(jnp.int32, (64, 128), 0)
     lane = lax.broadcasted_iota(jnp.int32, (64, 128), 1)
+    p = p_ref[...]
     unit = jnp.where(lane == line + 64, 1.0, 0.0)
-    tables = []
-    for layer in range(2):
-        p = p_ref[64 * layer : 64 * layer + 64, :]
-        gram = dot(p, p, NT, high)
-        tables.append(jnp.concatenate([gram, unit[:, 64:]], axis=1))
+    table = jnp.concatenate([dot(p, p, NT, high), unit[:, 64:]], axis=1)
     for k in range(64):
-        for layer in range(2):
-            table = tables[layer]
-            pivot_row = table[k : k + 1, :]
-            scaled = pivot_row / pivot_row[:, k : k + 1]
-            column = jnp.where(line[:, :1] > k, table[:, k : k + 1], 0.0)
-            tables[layer] = table - column * scaled
-    for layer in range(2):
-        table = tables[layer]
-        pivots = jnp.sum(jnp.where(line == lane, table, 0.0), axis=1, keepdims=True)
-        inverse = table[:, 64:] / jnp.sqrt(pivots)
-        inverse_ref[layer] = inverse
-        basis_ref[layer] = dot(inverse, p_ref[64 * layer : 64 * layer + 64, :], NN, high)
+        pivot_row = table[k : k + 1, :]
+        scaled = pivot_row / pivot_row[:, k : k + 1]
+        column = jnp.where(line[:, :1] > k, table[:, k : k + 1], 0.0)
+        table = table - column * scaled
+    pivots = jnp.sum(jnp.where(line == lane, table, 0.0), axis=1, keepdims=True)
+    inverse = table[:, 64:] / jnp.sqrt(pivots)
+    inverse_ref[...] = inverse
+    basis = dot(inverse, p, NN, high)
+    basis_ref[...] = basis
+    slot[...] = basis
+    z, col = lax.axis_index("dp"), lax.axis_index("col")
+    rows = slot[pl.ds(pl.multiple_of(16 * col, 16), 16), :]
+    part = jnp.zeros((16, 160), F32)
+    for i in range(4):
+        part = jnp.where(z == i, rows[:, 160 * i : 160 * i + 160], part)
+    top = part.astype(BF).astype(F32)
+    part = jnp.concatenate([top, part - top, jnp.zeros((16, 64), F32)], axis=1)
+    share_ref[...] = part.astype(BF)
 
 
 def taps_body(w_ref, x_ref, inverse_ref, out_ref, image, sums):
     zero = jnp.zeros((1, 4, 16, 384), BF)
     image[0:1] = zero
     image[33:34] = zero
-    at = lax.broadcasted_iota(jnp.int32, (1024, 128), 0) % 64
-    for r in range(2):
-        tiles = [w_ref[4 * r + c].astype(F32).reshape(16, 16, 128) for c in range(4)]
-        flat = jnp.stack(tiles, axis=1).reshape(1024, 128)
-        left = jnp.where(at == 63, 0.0, pltpu.roll(flat, 1023, 0))
-        right = jnp.where(at == 0, 0.0, pltpu.roll(flat, 1, 0))
-        for i, value in enumerate((left, flat, right)):
-            image[1 + 16 * r : 17 + 16 * r, :, :, 128 * i : 128 * i + 128] = value.astype(BF).reshape(
-                16, 4, 16, 128
-            )
+    at = lax.broadcasted_iota(jnp.int32, (2048, 128), 0) % 64
+    strips = [w_ref[c].astype(F32).reshape(32, 16, 128) for c in range(4)]
+    flat = jnp.stack(strips, axis=1).reshape(2048, 128)
+    left = jnp.where(at == 63, 0.0, pltpu.roll(flat, 2047, 0))
+    right = jnp.where(at == 0, 0.0, pltpu.roll(flat, 1, 0))
+    for i, value in enumerate((left, flat, right)):
+        value = value.astype(BF).reshape(32, 4, 16, 128)
+        image[1:33, :, :, 128 * i : 128 * i + 128] = value
     slices = jnp.concatenate([x_ref[4 * r + c] for c in range(4) for r in range(2)], axis=1)
     for a in range(3):
         windows = [image[2 - a : 34 - a, c].reshape(512, 384) for c in range(4)]
@@ -242,27 +244,30 @@
             value = total[:, 128 * b : 128 * b + 128]
             sums[160 * t : 160 * t + 160, :] = value + pltpu.roll(value, 64, 1)
     sums[1440:1472, :] = jnp.zeros((32, 128), F32)
-    inverse = inverse_ref[lax.axis_index("row")]
+    inverse = inverse_ref[...]
     for i in range(4):
         part = sums[360 * i : 360 * i + 384, :][:, :64]
         out_ref[i] = dot(inverse, part, NT, lax.Precision.HIGHEST).astype(BF)
 
 
-def total_body(got_ref, out_ref):
+def total_body(got_ref, share_ref, out_ref):
     total = got_ref[0].astype(F32)
     for i in range(1, got_ref.shape[0]):
         total = total + got_ref[i].astype(F32)
     for i in range(out_ref.shape[0]):
-        out_ref[i] = total.astype(BF)
-
-
-def place_body(got_ref, out_ref):
+        out_ref[i, 0:64] = total.astype(BF)
+        out_ref[i, 64:80] = share_ref[...]
+
+
+def place_body(got_ref, basis_ref, out_ref):
     for layer in range(2):
         for k in range(4):
             value = got_ref[4 * layer + k].astype(F32)
             for j in range(9):
                 start = 160 * j + 40 * k
-                out_ref[layer, :, start : start + 40] = value[:, 40 * j : 40 * j + 40]
+                out_ref[layer, :, start : start + 40] = value[:64, 40 * j : 40 * j + 40]
+            basis = value[64:, :160] + value[64:, 160:320]
+            basis_ref[layer, 16 * k : 16 * k + 16, :] = basis
 
 
 def on_device(x_input, pre_act, out_grad, conv_weight, q_prev):
@@ -270,7 +275,7 @@
     whole = pl.BlockSpec(memory_space=pltpu.VMEM)
     far = pl.BlockSpec(memory_space=pltpu.HBM)
     images, rows, cols = (lax.axis_size(a) for a in ALL)
-    z = lax.axis_index("dp")
+    z, row = lax.axis_index("dp"), lax.axis_index("row")
     plane, devices = rows * cols, images * rows * cols
     x, act, g = (v.reshape(256, 640) for v in (x_input, pre_act, out_grad))
     q_t = q_prev.transpose(1, 2, 0).reshape(128, 5760)
@@ -305,9 +310,9 @@
 
     each = 2 * 64 // devices if 128 % devices == 0 and devices >= 16 else 8
     parts = 128 // each
-    pre_grad, p_part = call(
+    keep, swap, p_part = call(
         power_body,
-        (shape((256, 640), BF), shape((parts, each, 640), F32)),
+        (shape((256, 640), BF), shape((256, 640), BF), shape((parts, each, 640), F32)),
         2 * 256 * 5760 * 1100,
         12 << 20,
         vmem=62,
@@ -327,32 +332,31 @@
         ],
     )(x, g, got, slope, q_one, y_two, conv_weight)
 
+    swap = lax.ppermute(swap, "row", [(0, 1), (1, 0)])
     p_part, slices = lax.optimization_barrier((p_part, slices))
     if parts == devices:
         p_got = exchange(p_part, ALL)
-        p_got = call(sum_body, shape((parts, each, 640), F32), 0, 1 << 20)(p_got)
-        p_all = exchange(p_got, ALL)
+        p_got = call(sum_body, shape((parts // 2, each, 640), F32), 0, 1 << 20)(p_got)
+        p_own = exchange(p_got, ("dp", "col"))
     else:
-        p_all = lax.psum(p_part, ALL)
+        p_part = p_part.reshape(-1, 2, cols, each, 640).transpose(1, 0, 2, 3, 4)
+        p_part = lax.psum(p_part.reshape(2, parts // 2, each, 640), ALL)
+        p_own = lax.dynamic_index_in_dim(p_part, row, 0, False)
 
     w_own, p_t = call(
         project_body,
-        (shape((8, 256, 128), BF), shape((128, 640), F32)),
+        (shape((4, 512, 128), BF), shape((64, 640), F32)),
         2 * 512 * 640 * 128,
         2 << 20,
-        vmem=62,
-        in_specs=[whole, far, far],
-        scratch_shapes=[pltpu.VMEM((256, 640), BF)] * 2 + [sems((2,))],
-    )(p_all, pre_grad, g)
-    w_all = exchange(w_own, PLANE)
-    inverse, basis = call(
+    )(p_own, keep, swap)
+    w_all = exchange(w_own, ("col",))
+    inverse, basis, share = call(
         factor_body,
-        (shape((2, 64, 64), F32), shape((2, 64, 640), F32)),
+        (shape((64, 64), F32), shape((64, 640), F32), shape((16, 384), BF)),
         1 << 30,
         1 << 20,
+        scratch_shapes=[pltpu.VMEM((64, 640), F32)],
     )(p_t)
-    count = 640 // images
-    basis_out = lax.dynamic_slice_in_dim(basis, z * count, count, 2).transpose(2, 0, 1)
 
     sums = call(
         taps_body,
@@ -364,17 +368,18 @@
 
     if images == 4:
         sums = exchange(sums, ("dp",))
-        mine = call(total_body, shape((plane, 64, 384), BF), 0, 1 << 20)(sums)
+        mine = call(total_body, shape((plane, 80, 384), BF), 0, 1 << 20)(sums, share)
         every = exchange(mine, PLANE)
-        q_out = call(place_body, shape((2, 64, 1440), F32), 0, 1 << 20)(every)
-        q_out = q_out.transpose(2, 0, 1)
-    else:
-        sums = lax.psum(sums[:, :, :360].astype(F32), "dp")
-        every = lax.all_gather(sums, PLANE).reshape(rows, cols, 4, 64, 9, 40)
-        every = every.transpose(2, 4, 1, 5, 0, 3).reshape(5760, 2, 64)
-        count = 5760 // images
-        q_out = lax.dynamic_slice_in_dim(every, z * count, count, 0)
-    return basis_out, q_out
+        basis_out, q_out = call(
+            place_body, (shape((2, 64, 160), F32), shape((2, 64, 1440), F32)), 0, 1 << 20
+        )(every)
+        return basis_out.transpose(2, 0, 1), q_out.transpose(2, 0, 1)
+    sums = lax.psum(sums[:, :, :360].astype(F32), "dp")
+    every = lax.all_gather(sums, PLANE).reshape(rows, cols, 4, 64, 9, 40)
+    every = every.transpose(2, 4, 1, 5, 0, 3).reshape(5760, 2, 64)
+    q_out = lax.dynamic_slice_in_dim(every, z * (5760 // images), 5760 // images, 0)
+    bases = lax.all_gather(basis, "row").transpose(2, 0, 1)
+    return lax.dynamic_slice_in_dim(bases, z * (640 // images), 640 // images, 0), q_out
 
 
 def solution(mesh):

time: 104 us -> 97.4 us (0.937)
  blocking collectives: 42 us -> 22.1 us
  waiting for transfers between devices: 11.4 us -> 22.6 us
  starting transfers between devices: 15.9 us -> 20.7 us
  Pallas kernels: 31.5 us -> 29.6 us
    all_to_all x3 -> x2, blocking collectives: 42 us -> 22.1 us  [exchange(): return lax.all_to_all(chunks, axes, 0, 0, tiled=True)]
    all_to_all x4 -> x5, waiting for transfers between devices: 11.4 us -> 22.6 us  [exchange(): return lax.all_to_all(chunks, axes, 0, 0, tiled=True)]
    all_to_all x4 -> x5, starting transfers between devices: 15.9 us -> 20.4 us  [exchange(): return lax.all_to_all(chunks, axes, 0, 0, tiled=True)]
    pallas_call x6, Pallas kernels: 20.9 us -> 19 us  [the longest x1 8.85 us: on_device(): call(power_body, (shape((256, 640), BF), shape((256, 640), BF), shape((pa...]
  transfers between devices with their start and end apart: 4 -> 6, of which waited for: 4 -> 4; matrix products, arithmetic and copies ran while one was open for 1% -> 0% of each run, Pallas kernels for 21% -> 23%
where the time goes in v8:
time: 97.4 us; the launch traced here: 96.7 us
  Pallas kernels  29.6 us (30%)
  waiting for transfers between devices  22.6 us (23%)
  blocking collectives  22.1 us (23%)
  starting transfers between devices  20.7 us (21%)
  local copies, waits for them, and re-layouts  0.98 us (1%)
    all_to_all x5, waiting for transfers between devices, exchange(): return lax.all_to_all(chunks, axes, 0, 0, tiled=True)  22.6 us
    all_to_all x2, blocking collectives, exchange(): return lax.all_to_all(chunks, axes, 0, 0, tiled=True)  22.1 us
    all_to_all x5, starting transfers between devices, exchange(): return lax.all_to_all(chunks, axes, 0, 0, tiled=True)  20.4 us
    pallas_call x1, Pallas kernels, on_device(): call(power_body, (shape((256, 640), BF), shape((256, 640), BF), shape((pa...  8.85 us
    pallas_call x1, Pallas kernels, on_device(): call(factor_body, (shape((64, 64), F32), shape((64, 640), F32), shape((16...  6.8 us
    pallas_call x1, Pallas kernels, on_device(): call(prepare_body, (shape((8, 160, 256), BF), shape((3, 384, 640), BF), s...  6.18 us
    pallas_call x1, Pallas kernels, on_device(): call(taps_body, shape((4, 64, 384), BF), 2 * 160 * 2048 * 1152, 2 << 20,...  2.33 us
    pallas_call x1, Pallas kernels, on_device(): call(rim_body, shape((plane, 32, 640), BF), 1 << 24, 1 << 20, vmem=62, in...  2.1 us
  transfers between devices with their start and end apart: 6, of which 4 were waited for; matrix products, arithmetic and copies ran while one was open for 0% of the time, Pallas kernels for 23%

profile of v8, /device:TPU:0, one launch (start us, length us, event | category | flops | bytes accessed | tf_op | source)
XLA Modules:
  0.0 96.7 jit_solution(5627939924702888746)
XLA Ops:
  0.6 2.1 %shard_map.68 = bf16[8,32,640]{2,1,0:T(8,128)(2,1)} custom-call(bf16[256,640]{1,0:T(8,128)(2,1)} %bitcast.9, bf16[256,640]{1,0:T(8,128)(2,1)} %bitcast.13), custom_call_target="tpu_custom_call" | custom-call | flops 16777216 | bytes 1048576 | tf_op jit(solution)/shard_map/pallas_call | solution.py:284
  2.7 5.2 %all-to-all-start = ((bf16[8,32,640]{2,1,0:T(8,128)(2,1)}), bf16[8,32,640]{2,1,0:T(8,128)(2,1)S(1)}, u32[]{:S(2)}, u32[]{:S(2)}) async-start(bf16[8,32,640]{2,1,0:T(8,128)(2,1)} %shard_map.68), calls=%async_computation | async-start | bytes 655360 | tf_op jit(solution)/shard_map/all_to_all | solution.py:35
  7.9 6.2 %shard_map.69 = (bf16[8,160,256]{2,1,0:T(8,128)(2,1)}, bf16[3,384,640]{2,1,0:T(8,128)(2,1)}, bf16[3,128,384]{2,1,0:T(8,128)(2,1)}, f32[256,640]{1,0:T(8,128)}) custom-call(bf16[256,640]{1,0:T(8,128)(2,1)} %bitcast.10, bf16[256,640]{1,0:T(8,128)(2,1)} %bitcast.12, f32[128,5760]{1,0:T(8,128)} %bitcast.8), custom_call_target="tpu_custom_call" | custom-call | flops 377487360 | bytes 8388608 | tf_op jit(solution)/shard_map/pallas_call | solution.py:294
  14.1 1.0 %all-to-all-done.got_hbm = bf16[8,32,640]{2,1,0:T(8,128)(2,1)S(1)} async-done(((bf16[8,32,640]{2,1,0:T(8,128)(2,1)}), bf16[8,32,640]{2,1,0:T(8,128)(2,1)S(1)}, u32[]{:S(2)}, u32[]{:S(2)}) %all-to-all-start) | async-done | bytes 327712 | tf_op jit(solution)/shard_map/all_to_all | solution.py:35
  15.1 0.0 copy-start.1
  15.1 3.5 %all-to-all-start.1 = ((bf16[8,160,256]{2,1,0:T(8,128)(2,1)}), bf16[8,160,256]{2,1,0:T(8,128)(2,1)S(1)}, u32[]{:S(2)}, u32[]{:S(2)}) async-start(bf16[8,160,256]{2,1,0:T(8,128)(2,1)} %get-tuple-element.21), calls=%async_computation.1 | async-start | bytes 1310720 | tf_op jit(solution)/shard_map/all_to_all | solution.py:35
  18.7 0.0 copy-done.1
  18.7 8.8 %shard_map.70 = (bf16[256,640]{1,0:T(8,128)(2,1)}, bf16[256,640]{1,0:T(8,128)(2,1)}, f32[32,4,640]{2,1,0:T(4,128)}) custom-call(bf16[256,640]{1,0:T(8,128)(2,1)} %bitcast.11, bf16[256,640]{1,0:T(8,128)(2,1)} %bitcast.14, bf16[8,32,640]{2,1,0:T(8,128)(2,1)} %copy-done.1, f32[256,640]{1,0:T(8,128)} %get-tuple-element.17.slope_hbm, ...), custom_call_target="tpu_custom_call" | custom-call | flops 3244032000 | bytes 12582912 | tf_op jit(solution)/shard_map/pallas_call | solution.py:313
  27.5 1.7 %all-to-all-done.1.x_ref = bf16[8,160,256]{2,1,0:T(8,128)(2,1)S(1)} async-done(((bf16[8,160,256]{2,1,0:T(8,128)(2,1)}), bf16[8,160,256]{2,1,0:T(8,128)(2,1)S(1)}, u32[]{:S(2)}, u32[]{:S(2)}) %all-to-all-start.1) | async-done | bytes 655392 | tf_op jit(solution)/shard_map/all_to_all | solution.py:35
  29.3 4.5 %all-to-all-start.2 = ((f32[32,4,640]{2,1,0:T(4,128)}), f32[32,4,640]{2,1,0:T(4,128)S(1)}, u32[]{:S(2)}, u32[]{:S(2)}) async-start(f32[32,4,640]{2,1,0:T(4,128)} %get-tuple-element.22), calls=%async_computation.2 | async-start | bytes 655360 | tf_op jit(solution)/shard_map/all_to_all | solution.py:35
  33.8 0.3 collective-permute-start
  34.1 12.0 %all-to-all-done.2.got_ref = f32[32,4,640]{2,1,0:T(4,128)S(1)} async-done(((f32[32,4,640]{2,1,0:T(4,128)}), f32[32,4,640]{2,1,0:T(4,128)S(1)}, u32[]{:S(2)}, u32[]{:S(2)}) %all-to-all-start.2) | async-done | bytes 327712 | tf_op jit(solution)/shard_map/all_to_all | solution.py:35
  46.1 0.7 shard_map.71
  46.8 3.5 %all-to-all-start.3 = ((f32[16,4,640]{2,1,0:T(4,128)}), f32[16,4,640]{2,1,0:T(4,128)S(1)}, u32[]{:S(2)}, u32[]{:S(2)}) async-start(f32[16,4,640]{2,1,0:T(4,128)} %shard_map.71), calls=%async_computation.3 | async-start | bytes 327680 | tf_op jit(solution)/shard_map/all_to_all | solution.py:35
  50.3 0.0 collective-permute-done.swap_ref
  50.3 7.9 %all-to-all-done.3.got_ref = f32[16,4,640]{2,1,0:T(4,128)S(1)} async-done(((f32[16,4,640]{2,1,0:T(4,128)}), f32[16,4,640]{2,1,0:T(4,128)S(1)}, u32[]{:S(2)}, u32[]{:S(2)}) %all-to-all-start.3) | async-done | bytes 163872 | tf_op jit(solution)/shard_map/all_to_all | solution.py:35
  58.2 0.0 copy-start
  58.2 1.0 %copy-done = bf16[256,640]{1,0:T(8,128)(2,1)S(1)} copy-done((bf16[256,640]{1,0:T(8,128)(2,1)S(1)}, bf16[256,640]{1,0:T(8,128)(2,1)}, u32[]{:S(2)}) %copy-start) | copy-done | bytes 327704
  59.2 1.2 %shard_map.72 = (bf16[4,512,128]{2,1,0:T(8,128)(2,1)}, f32[64,640]{1,0:T(8,128)S(1)}) custom-call(f32[16,4,640]{2,1,0:T(4,128)S(1)} %all-to-all-done.3.got_ref, bf16[256,640]{1,0:T(8,128)(2,1)S(1)} %copy-done, bf16[256,640]{1,0:T(8,128)(2,1)S(1)} %collective-permute-done.swap_ref), custom_call_target="tpu_custom_call" | custom-call | flops 83886080 | bytes 2097152 | tf_op jit(solution)/shard_map/pallas_call | solution.py:346
  60.4 3.7 %all-to-all-start.4 = ((bf16[4,512,128]{2,1,0:T(8,128)(2,1)}), bf16[4,512,128]{2,1,0:T(8,128)(2,1)S(1)}, u32[]{:S(2)}, u32[]{:S(2)}) async-start(bf16[4,512,128]{2,1,0:T(8,128)(2,1)} %get-tuple-element.25), calls=%async_computation.4 | async-start | bytes 1048576 | tf_op jit(solution)/shard_map/all_to_all | solution.py:35
  64.1 6.8 %shard_map.73 = (f32[64,64]{1,0:T(8,128)S(1)}, f32[64,640]{1,0:T(8,128)}, bf16[16,384]{1,0:T(8,128)(2,1)S(1)}) custom-call(f32[64,640]{1,0:T(8,128)S(1)} %get-tuple-element.27.p_ref), custom_call_target="tpu_custom_call" | custom-call | flops 1073741824 | bytes 1048576 | tf_op jit(solution)/shard_map/pallas_call | solution.py:353
  70.9 0.0 all-to-all-done.4.w_ref
  70.9 2.3 %shard_map.74 = bf16[4,64,384]{2,1,0:T(8,128)(2,1)S(1)} custom-call(bf16[4,512,128]{2,1,0:T(8,128)(2,1)S(1)} %all-to-all-done.4.w_ref, bf16[8,160,256]{2,1,0:T(8,128)(2,1)S(1)} %all-to-all-done.1.x_ref, f32[64,64]{1,0:T(8,128)S(1)} %get-tuple-element.28.inverse_ref), custom_call_target="tpu_custom_call" | custom-call | flops 754974720 | bytes 2097152 | tf_op jit(solution)/shard_map/pallas_call | solution.py:361
  73.2 9.2 %all_to_all.35.got_ref = bf16[4,64,384]{2,1,0:T(8,128)(2,1)S(1)} all-to-all(bf16[4,64,384]{2,1,0:T(8,128)(2,1)S(1)} %shard_map.74), channel_id=1, replica_groups=mesh['dp'=4,'row'=2,'col'=4] {'dp'}, dimensions={0} | all-to-all | bytes 393216 | tf_op jit(solution)/shard_map/all_to_all | solution.py:35
  82.5 12.9 %all_to_all.36.got_ref = bf16[8,80,384]{2,1,0:T(8,128)(2,1)S(1)} all-to-all(bf16[8,80,384]{2,1,0:T(8,128)(2,1)S(1)} %shard_map.75), channel_id=1, replica_groups=mesh['dp'=4,'row'=2,'col'=4] {'row','col'}, dimensions={0} | all-to-all | bytes 983040 | tf_op jit(solution)/shard_map/all_to_all | solution.py:35
  95.4 1.4 %shard_map.76 = (f32[2,64,160]{2,1,0:T(8,128)}, f32[2,64,1440]{2,1,0:T(8,128)}) custom-call(bf16[8,80,384]{2,1,0:T(8,128)(2,1)S(1)} %all_to_all.36.got_ref), custom_call_target="tpu_custom_call" | custom-call | bytes 1048576 | tf_op jit(solution)/shard_map/pallas_call | solution.py:373
  (1 shorter events, 0.0 us)
Async XLA Ops:
  2.7 12.4 %all-to-all-start = ((bf16[8,32,640]{2,1,0:T(8,128)(2,1)}), bf16[8,32,640]{2,1,0:T(8,128)(2,1)S(1)}, u32[]{:S(2)}, u32[]{:S(2)}) async-start(bf16[8,32,640]{2,1,0:T(8,128)(2,1)} %shard_map.68), calls=%async_computation | async-start | bytes 655360 | tf_op jit(solution)/shard_map/all_to_all | solution.py:35
  15.1 3.6 %copy-start.1 = (bf16[8,32,640]{2,1,0:T(8,128)(2,1)}, bf16[8,32,640]{2,1,0:T(8,128)(2,1)S(1)}, u32[]{:S(2)}) copy-start(bf16[8,32,640]{2,1,0:T(8,128)(2,1)S(1)} %all-to-all-done.got_hbm) | copy-start | bytes 983044
  15.1 14.1 %all-to-all-start.1 = ((bf16[8,160,256]{2,1,0:T(8,128)(2,1)}), bf16[8,160,256]{2,1,0:T(8,128)(2,1)S(1)}, u32[]{:S(2)}, u32[]{:S(2)}) async-start(bf16[8,160,256]{2,1,0:T(8,128)(2,1)} %get-tuple-element.21), calls=%async_computation.1 | async-start | bytes 1310720 | tf_op jit(solution)/shard_map/all_to_all | solution.py:35
  29.3 16.8 %all-to-all-start.2 = ((f32[32,4,640]{2,1,0:T(4,128)}), f32[32,4,640]{2,1,0:T(4,128)S(1)}, u32[]{:S(2)}, u32[]{:S(2)}) async-start(f32[32,4,640]{2,1,0:T(4,128)} %get-tuple-element.22), calls=%async_computation.2 | async-start | bytes 655360 | tf_op jit(solution)/shard_map/all_to_all | solution.py:35
  33.8 16.6 %collective-permute-start = (bf16[256,640]{1,0:T(8,128)(2,1)}, bf16[256,640]{1,0:T(8,128)(2,1)S(1)}, u32[]{:S(2)}, u32[]{:S(2)}) collective-permute-start(bf16[256,640]{1,0:T(8,128)(2,1)} %get-tuple-element.24), channel_id=1, source_target_pairs={{0,4},{4,0},{1,5},{5,1},{2,6},{6,2},{3,7},{7,3},{8,12},{12,8},{9,1... | collective-permute-start | bytes 983048 | tf_op jit(solution)/shard_map/ppermute | solution.py:335
  46.8 11.4 %all-to-all-start.3 = ((f32[16,4,640]{2,1,0:T(4,128)}), f32[16,4,640]{2,1,0:T(4,128)S(1)}, u32[]{:S(2)}, u32[]{:S(2)}) async-start(f32[16,4,640]{2,1,0:T(4,128)} %shard_map.71), calls=%async_computation.3 | async-start | bytes 327680 | tf_op jit(solution)/shard_map/all_to_all | solution.py:35
  58.2 1.0 %copy-start = (bf16[256,640]{1,0:T(8,128)(2,1)S(1)}, bf16[256,640]{1,0:T(8,128)(2,1)}, u32[]{:S(2)}) copy-start(bf16[256,640]{1,0:T(8,128)(2,1)} %get-tuple-element.23.keep_ref) | copy-start | bytes 983044
  60.4 10.5 %all-to-all-start.4 = ((bf16[4,512,128]{2,1,0:T(8,128)(2,1)}), bf16[4,512,128]{2,1,0:T(8,128)(2,1)S(1)}, u32[]{:S(2)}, u32[]{:S(2)}) async-start(bf16[4,512,128]{2,1,0:T(8,128)(2,1)} %get-tuple-element.25), calls=%async_computation.4 | async-start | bytes 1048576 | tf_op jit(solution)/shard_map/all_to_all | solution.py:35

commit v9 on v8

--- a/solution.py
+++ b/solution.py
@@ -119,7 +119,7 @@
 
 def power_body(
     x_hbm, g_hbm, got_hbm, slope_hbm, q_hbm, y_hbm, w_hbm,
-    keep_ref, swap_ref, p_ref,
+    keep_ref, swap_ref, p_keep_ref, p_swap_ref,
     x_ref, g_ref, got_ref, slope_ref, q_ref, y_ref, w_all,
     x_win, g_win, back, sems,
 ):
@@ -152,15 +152,6 @@
         wide = dot(x_win[b], q_ref[b], NT)
         for a in range(3):
             z_sum = z_sum + wide[16 * a : 16 * a + 256, 128 * a : 128 * a + 128]
-    each = p_ref.shape[1]
-
-    def put(layer, value):
-        value = value[:64] + value[64:]
-        for i in range(64 // each):
-            owner = i // cols * 2 * cols + layer * cols + i % cols
-            p_ref[owner] = value[i * each : (i + 1) * each]
-
-    put(1, two)
     z_sum = paired_halves(z_sum).astype(BF)
     for a in range(3):
         windows = [g_win[2 - b, 16 * (2 - a) : 16 * (2 - a) + 256, :] for b in range(3)]
@@ -173,10 +164,22 @@
     grad = (back[...] * slope_ref[...]).astype(BF)
     keep_ref[...] = jnp.where(row == 0, grad, g_ref[...])
     swap_ref[...] = jnp.where(row == 0, g_ref[...], grad)
-    put(0, dot(z_sum, grad, TN))
-
-
-def sum_body(got_ref, out_ref):
+    one = dot(z_sum, grad, TN)
+    one, two = one[:64] + one[64:], two[:64] + two[64:]
+    each = p_keep_ref.shape[1]
+    for ref, value in (
+        (p_keep_ref, jnp.where(row == 0, one, two)),
+        (p_swap_ref, jnp.where(row == 0, two, one)),
+    ):
+        for i in range(64 // each):
+            ref[i] = value[i * each : (i + 1) * each]
+
+
+def add_body(left_ref, right_ref, out_ref):
+    out_ref[...] = left_ref[...] + right_ref[...]
+
+
+def sum_body(got_ref, keep_ref, swap_ref, out_ref):
     total = jnp.sum(got_ref[...], axis=0)
     for i in range(out_ref.shape[0]):
         out_ref[i] = total
@@ -195,7 +198,7 @@
             w_ref[k, pl.ds(pl.multiple_of(256 * start, 256), 256), :] = out
 
 
-def factor_body(p_ref, inverse_ref, basis_ref, share_ref, slot):
+def factor_body(p_ref, inverse_ref, basis_ref, share_ref):
     high = lax.Precision.HIGHEST
     line = lax.broadcasted_iota(jnp.int32, (64, 128), 0)
     lane = lax.broadcasted_iota(jnp.int32, (64, 128), 1)
@@ -212,15 +215,11 @@
     inverse_ref[...] = inverse
     basis = dot(inverse, p, NN, high)
     basis_ref[...] = basis
-    slot[...] = basis
-    z, col = lax.axis_index("dp"), lax.axis_index("col")
-    rows = slot[pl.ds(pl.multiple_of(16 * col, 16), 16), :]
-    part = jnp.zeros((16, 160), F32)
-    for i in range(4):
-        part = jnp.where(z == i, rows[:, 160 * i : 160 * i + 160], part)
-    top = part.astype(BF).astype(F32)
-    part = jnp.concatenate([top, part - top, jnp.zeros((16, 64), F32)], axis=1)
-    share_ref[...] = part.astype(BF)
+    z = lax.axis_index("dp")
+    part = basis[:, :160]
+    for i in range(1, 4):
+        part = jnp.where(z == i, basis[:, 160 * i : 160 * i + 160], part)
+    share_ref[...] = part
 
 
 def taps_body(w_ref, x_ref, inverse_ref, out_ref, image, sums):
@@ -250,24 +249,24 @@
         out_ref[i] = dot(inverse, part, NT, lax.Precision.HIGHEST).astype(BF)
 
 
-def total_body(got_ref, share_ref, out_ref):
+def total_body(got_ref, out_ref):
     total = got_ref[0].astype(F32)
     for i in range(1, got_ref.shape[0]):
         total = total + got_ref[i].astype(F32)
     for i in range(out_ref.shape[0]):
-        out_ref[i, 0:64] = total.astype(BF)
-        out_ref[i, 64:80] = share_ref[...]
-
-
-def place_body(got_ref, basis_ref, out_ref):
-    for layer in range(2):
+        out_ref[i] = total.astype(BF)
+
+
+def place_body(got_ref, other_ref, share_ref, other_share_ref, basis_ref, out_ref):
+    row = lax.axis_index("row")
+    for layer, ref, share in ((row, got_ref, share_ref), (1 - row, other_ref, other_share_ref)):
+        basis_ref[layer] = share[...]
+        out = out_ref.at[layer]
         for k in range(4):
-            value = got_ref[4 * layer + k].astype(F32)
+            value = ref[k].astype(F32)
             for j in range(9):
                 start = 160 * j + 40 * k
-                out_ref[layer, :, start : start + 40] = value[:64, 40 * j : 40 * j + 40]
-            basis = value[64:, :160] + value[64:, 160:320]
-            basis_ref[layer, 16 * k : 16 * k + 16, :] = basis
+                out[:, start : start + 40] = value[:, 40 * j : 40 * j + 40]
 
 
 def on_device(x_input, pre_act, out_grad, conv_weight, q_prev):
@@ -276,7 +275,7 @@
     far = pl.BlockSpec(memory_space=pltpu.HBM)
     images, rows, cols = (lax.axis_size(a) for a in ALL)
     z, row = lax.axis_index("dp"), lax.axis_index("row")
-    plane, devices = rows * cols, images * rows * cols
+    plane = rows * cols
     x, act, g = (v.reshape(256, 640) for v in (x_input, pre_act, out_grad))
     q_t = q_prev.transpose(1, 2, 0).reshape(128, 5760)
 
@@ -308,11 +307,13 @@
     )(x, act, q_t)
     slices = exchange(slices, PLANE)
 
-    each = 2 * 64 // devices if 128 % devices == 0 and devices >= 16 else 8
-    parts = 128 // each
-    keep, swap, p_part = call(
+    strip = images * cols
+    each = 64 // strip if 64 % strip == 0 and strip >= 8 else 8
+    parts = 64 // each
+    p_shape = shape((parts, each, 640), F32)
+    keep, swap, p_keep, p_swap = call(
         power_body,
-        (shape((256, 640), BF), shape((256, 640), BF), shape((parts, each, 640), F32)),
+        (shape((256, 640), BF), shape((256, 640), BF), p_shape, p_shape),
         2 * 256 * 5760 * 1100,
         12 << 20,
         vmem=62,
@@ -332,16 +333,16 @@
         ],
     )(x, g, got, slope, q_one, y_two, conv_weight)
 
-    swap = lax.ppermute(swap, "row", [(0, 1), (1, 0)])
+    across = [(0, 1), (1, 0)]
+    p_part = call(add_body, p_shape, 0, 1 << 20)(p_keep, lax.ppermute(p_swap, "row", across))
+    swap = lax.ppermute(swap, "row", across)
     p_part, slices = lax.optimization_barrier((p_part, slices))
-    if parts == devices:
-        p_got = exchange(p_part, ALL)
-        p_got = call(sum_body, shape((parts // 2, each, 640), F32), 0, 1 << 20)(p_got)
+    if parts == strip:
+        p_got = exchange(p_part, ("dp", "col"))
+        p_got = call(sum_body, p_shape, 0, 1 << 20)(p_got, keep, swap)
         p_own = exchange(p_got, ("dp", "col"))
     else:
-        p_part = p_part.reshape(-1, 2, cols, each, 640).transpose(1, 0, 2, 3, 4)
-        p_part = lax.psum(p_part.reshape(2, parts // 2, each, 640), ALL)
-        p_own = lax.dynamic_index_in_dim(p_part, row, 0, False)
+        p_own = lax.psum(p_part, ("dp", "col"))
 
     w_own, p_t = call(
         project_body,
@@ -352,10 +353,9 @@
     w_all = exchange(w_own, ("col",))
     inverse, basis, share = call(
         factor_body,
-        (shape((64, 64), F32), shape((64, 640), F32), shape((16, 384), BF)),
+        (shape((64, 64), F32), shape((64, 640), F32), shape((64, 160), F32)),
         1 << 30,
         1 << 20,
-        scratch_shapes=[pltpu.VMEM((64, 640), F32)],
     )(p_t)
 
     sums = call(
@@ -367,12 +367,14 @@
     )(w_all, slices, inverse)
 
     if images == 4:
+        other_share = lax.ppermute(share, "row", across)
         sums = exchange(sums, ("dp",))
-        mine = call(total_body, shape((plane, 80, 384), BF), 0, 1 << 20)(sums, share)
-        every = exchange(mine, PLANE)
+        mine = call(total_body, shape((cols, 64, 384), BF), 0, 1 << 20)(sums)
+        every = exchange(mine, ("col",))
+        other = lax.ppermute(every, "row", across)
         basis_out, q_out = call(
             place_body, (shape((2, 64, 160), F32), shape((2, 64, 1440), F32)), 0, 1 << 20
-        )(every)
+        )(every, other, share, other_share)
         return basis_out.transpose(2, 0, 1), q_out.transpose(2, 0, 1)
     sums = lax.psum(sums[:, :, :360].astype(F32), "dp")
     every = lax.all_gather(sums, PLANE).reshape(rows, cols, 4, 64, 9, 40)

time: 97.4 us -> 94.5 us (0.970)
  waiting for transfers between devices: 22.6 us -> 11.3 us
  blocking collectives: 22.1 us -> 29.9 us
    all_to_all x5 -> x4, waiting for transfers between devices: 22.6 us -> 9.14 us  [exchange(): return lax.all_to_all(chunks, axes, 0, 0, tiled=True)]
    all_to_all x2 -> x3, blocking collectives: 22.1 us -> 29.9 us  [exchange(): return lax.all_to_all(chunks, axes, 0, 0, tiled=True)]
    ppermute x1 -> x4, waiting for transfers between devices: 0.01 us -> 2.18 us  [the longest x1 1.15 us: on_device(): lax.ppermute(p_swap, 'row', across)]
    all_to_all x5 -> x4, starting transfers between devices: 20.4 us -> 19.6 us  [exchange(): return lax.all_to_all(chunks, axes, 0, 0, tiled=True)]
    pallas_call x4 -> x5, Pallas kernels: 16.4 us -> 16.3 us  [the longest x1 8.75 us: on_device(): call(power_body, (shape((256, 640), BF), shape((256, 640), BF), p_shape,...]
  transfers between devices with their start and end apart: 6 -> 8, of which waited for: 4 -> 4; matrix products, arithmetic and copies ran while one was open for 0% -> 0% of each run, Pallas kernels for 23% -> 24%
where the time goes in v9:
time: 94.5 us; the launch traced here: 93.9 us
  blocking collectives  29.9 us (32%)
  Pallas kernels  29.4 us (31%)
  starting transfers between devices  20.6 us (22%)
  waiting for transfers between devices  11.3 us (12%)
  local copies, waits for them, and re-layouts  1.89 us (2%)
    all_to_all x3, blocking collectives, exchange(): return lax.all_to_all(chunks, axes, 0, 0, tiled=True)  29.9 us
    all_to_all x4, starting transfers between devices, exchange(): return lax.all_to_all(chunks, axes, 0, 0, tiled=True)  19.6 us
    all_to_all x4, waiting for transfers between devices, exchange(): return lax.all_to_all(chunks, axes, 0, 0, tiled=True)  9.14 us
    pallas_call x1, Pallas kernels, on_device(): call(power_body, (shape((256, 640), BF), shape((256, 640), BF), p_shape,...  8.75 us
    pallas_call x1, Pallas kernels, on_device(): call(factor_body, (shape((64, 64), F32), shape((64, 640), F32), shape((64...  6.78 us
    pallas_call x1, Pallas kernels, on_device(): call(prepare_body, (shape((8, 160, 256), BF), shape((3, 384, 640), BF), s...  6.21 us
    pallas_call x1, Pallas kernels, on_device(): call(taps_body, shape((4, 64, 384), BF), 2 * 160 * 2048 * 1152, 2 << 20,...  2.33 us
    pallas_call x1, Pallas kernels, on_device(): call(rim_body, shape((plane, 32, 640), BF), 1 << 24, 1 << 20, vmem=62, in...  2.09 us
  transfers between devices with their start and end apart: 8, of which 4 were waited for; matrix products, arithmetic and copies ran while one was open for 0% of the time, Pallas kernels for 24%

profile of v9, /device:TPU:0, one launch (start us, length us, event | category | flops | bytes accessed | tf_op | source)
XLA Modules:
  0.0 93.9 jit_solution(2339947912060010956)
XLA Ops:
  0.6 2.1 %shard_map.68 = bf16[8,32,640]{2,1,0:T(8,128)(2,1)} custom-call(bf16[256,640]{1,0:T(8,128)(2,1)} %bitcast.9, bf16[256,640]{1,0:T(8,128)(2,1)} %bitcast.13), custom_call_target="tpu_custom_call" | custom-call | flops 16777216 | bytes 1048576 | tf_op jit(solution)/shard_map/pallas_call | solution.py:283
  2.7 5.2 %all-to-all-start = ((bf16[8,32,640]{2,1,0:T(8,128)(2,1)}), bf16[8,32,640]{2,1,0:T(8,128)(2,1)S(1)}, u32[]{:S(2)}, u32[]{:S(2)}) async-start(bf16[8,32,640]{2,1,0:T(8,128)(2,1)} %shard_map.68), calls=%async_computation | async-start | bytes 655360 | tf_op jit(solution)/shard_map/all_to_all | solution.py:35
  7.9 6.2 %shard_map.69 = (bf16[8,160,256]{2,1,0:T(8,128)(2,1)}, bf16[3,384,640]{2,1,0:T(8,128)(2,1)}, bf16[3,128,384]{2,1,0:T(8,128)(2,1)}, f32[256,640]{1,0:T(8,128)}) custom-call(bf16[256,640]{1,0:T(8,128)(2,1)} %bitcast.10, bf16[256,640]{1,0:T(8,128)(2,1)} %bitcast.12, f32[128,5760]{1,0:T(8,128)} %bitcast.8), custom_call_target="tpu_custom_call" | custom-call | flops 377487360 | bytes 8388608 | tf_op jit(solution)/shard_map/pallas_call | solution.py:293
  14.1 1.0 %all-to-all-done.got_hbm = bf16[8,32,640]{2,1,0:T(8,128)(2,1)S(1)} async-done(((bf16[8,32,640]{2,1,0:T(8,128)(2,1)}), bf16[8,32,640]{2,1,0:T(8,128)(2,1)S(1)}, u32[]{:S(2)}, u32[]{:S(2)}) %all-to-all-start) | async-done | bytes 327712 | tf_op jit(solution)/shard_map/all_to_all | solution.py:35
  15.1 0.0 copy-start.2
  15.1 3.5 %all-to-all-start.1 = ((bf16[8,160,256]{2,1,0:T(8,128)(2,1)}), bf16[8,160,256]{2,1,0:T(8,128)(2,1)S(1)}, u32[]{:S(2)}, u32[]{:S(2)}) async-start(bf16[8,160,256]{2,1,0:T(8,128)(2,1)} %get-tuple-element.23), calls=%async_computation.1 | async-start | bytes 1310720 | tf_op jit(solution)/shard_map/all_to_all | solution.py:35
  18.7 0.0 copy-done.2
  18.7 8.7 %shard_map.70 = (bf16[256,640]{1,0:T(8,128)(2,1)}, bf16[256,640]{1,0:T(8,128)(2,1)}, f32[16,4,640]{2,1,0:T(4,128)}, f32[16,4,640]{2,1,0:T(4,128)}) custom-call(bf16[256,640]{1,0:T(8,128)(2,1)} %bitcast.11, bf16[256,640]{1,0:T(8,128)(2,1)} %bitcast.14, bf16[8,32,640]{2,1,0:T(8,128)(2,1)} %copy-done.2, f32[256,640]{1,0:T(8,128)} %get-tuple-element.18.slope_hbm, ...), custom_call_target="tpu_custom_call" | custom-call | flops 3244032000 | bytes 12582912 | tf_op jit(solution)/shard_map/pallas_call | solution.py:314
  27.4 0.5 collective-permute-start
  27.9 0.1 collective-permute-start.1
  28.0 1.2 %collective-permute-done.right_ref = f32[16,4,640]{2,1,0:T(4,128)S(1)} collective-permute-done((f32[16,4,640]{2,1,0:T(4,128)}, f32[16,4,640]{2,1,0:T(4,128)S(1)}, u32[]{:S(2)}, u32[]{:S(2)}) %collective-permute-start) | collective-permute-done | bytes 163872 | tf_op jit(solution)/shard_map/ppermute | solution.py:337
  29.2 0.0 copy-start.1
  29.2 0.9 copy-done.1
  30.1 0.7 shard_map.71
  30.7 0.0 all-to-all-done.1.x_ref
  30.7 7.2 %all-to-all-start.2 = ((f32[16,4,640]{2,1,0:T(4,128)}), f32[16,4,640]{2,1,0:T(4,128)S(1)}, u32[]{:S(2)}, u32[]{:S(2)}) async-start(f32[16,4,640]{2,1,0:T(4,128)} %shard_map.71), calls=%async_computation.2 | async-start | bytes 327680 | tf_op jit(solution)/shard_map/all_to_all | solution.py:35
  37.9 0.0 collective-permute-done.1.swap_ref
  37.9 8.2 %all-to-all-done.2.got_ref = f32[16,4,640]{2,1,0:T(4,128)S(1)} async-done(((f32[16,4,640]{2,1,0:T(4,128)}), f32[16,4,640]{2,1,0:T(4,128)S(1)}, u32[]{:S(2)}, u32[]{:S(2)}) %all-to-all-start.2) | async-done | bytes 163872 | tf_op jit(solution)/shard_map/all_to_all | solution.py:35
  46.1 0.0 copy-start
  46.1 1.0 %copy-done = bf16[256,640]{1,0:T(8,128)(2,1)S(1)} copy-done((bf16[256,640]{1,0:T(8,128)(2,1)S(1)}, bf16[256,640]{1,0:T(8,128)(2,1)}, u32[]{:S(2)}) %copy-start) | copy-done | bytes 327704
  47.1 11.2 %all_to_all.35.got_ref = f32[16,4,640]{2,1,0:T(4,128)S(1)} all-to-all(f32[16,4,640]{2,1,0:T(4,128)S(1)} %shard_map.72), channel_id=1, replica_groups=mesh['dp'=4,'row'=2,'col'=4] {'dp','col'}, dimensions={0} | all-to-all | bytes 327680 | tf_op jit(solution)/shard_map/all_to_all | solution.py:35
  58.3 1.2 %shard_map.73 = (bf16[4,512,128]{2,1,0:T(8,128)(2,1)}, f32[64,640]{1,0:T(8,128)S(1)}) custom-call(f32[16,4,640]{2,1,0:T(4,128)S(1)} %all_to_all.35.got_ref, bf16[256,640]{1,0:T(8,128)(2,1)S(1)} %copy-done, bf16[256,640]{1,0:T(8,128)(2,1)S(1)} %collective-permute-done.1.swap_ref), custom_call_target="tpu_custom_call" | custom-call | flops 83886080 | bytes 2097152 | tf_op jit(solution)/shard_map/pallas_call | solution.py:347
  59.5 3.7 %all-to-all-start.4 = ((bf16[4,512,128]{2,1,0:T(8,128)(2,1)}), bf16[4,512,128]{2,1,0:T(8,128)(2,1)S(1)}, u32[]{:S(2)}, u32[]{:S(2)}) async-start(bf16[4,512,128]{2,1,0:T(8,128)(2,1)} %get-tuple-element.27), calls=%async_computation.4 | async-start | bytes 1048576 | tf_op jit(solution)/shard_map/all_to_all | solution.py:35
  63.2 6.8 %shard_map.74 = (f32[64,64]{1,0:T(8,128)S(1)}, f32[64,640]{1,0:T(8,128)}, f32[64,160]{1,0:T(8,128)S(1)}) custom-call(f32[64,640]{1,0:T(8,128)S(1)} %get-tuple-element.29.p_ref), custom_call_target="tpu_custom_call" | custom-call | flops 1073741824 | bytes 1048576 | tf_op jit(solution)/shard_map/pallas_call | solution.py:354
  70.0 0.0 all-to-all-done.4.w_ref
  70.0 2.3 %shard_map.75 = bf16[4,64,384]{2,1,0:T(8,128)(2,1)S(1)} custom-call(bf16[4,512,128]{2,1,0:T(8,128)(2,1)S(1)} %all-to-all-done.4.w_ref, bf16[8,160,256]{2,1,0:T(8,128)(2,1)S(1)} %all-to-all-done.1.x_ref, f32[64,64]{1,0:T(8,128)S(1)} %get-tuple-element.30.inverse_ref), custom_call_target="tpu_custom_call" | custom-call | flops 754974720 | bytes 2097152 | tf_op jit(solution)/shard_map/pallas_call | solution.py:361
  72.3 9.4 %all_to_all.36.got_ref = bf16[4,64,384]{2,1,0:T(8,128)(2,1)S(1)} all-to-all(bf16[4,64,384]{2,1,0:T(8,128)(2,1)S(1)} %shard_map.75), channel_id=1, replica_groups=mesh['dp'=4,'row'=2,'col'=4] {'dp'}, dimensions={0} | all-to-all | bytes 393216 | tf_op jit(solution)/shard_map/all_to_all | solution.py:35
  81.7 9.3 %all_to_all.37.got_ref = bf16[4,64,384]{2,1,0:T(8,128)(2,1)S(1)} all-to-all(bf16[4,64,384]{2,1,0:T(8,128)(2,1)S(1)} %shard_map.76), channel_id=1, replica_groups=mesh['dp'=4,'row'=2,'col'=4] {'col'}, dimensions={0} | all-to-all | bytes 393216 | tf_op jit(solution)/shard_map/all_to_all | solution.py:35
  91.0 0.0 collective-permute-start.2
  91.0 0.5 collective-permute-start.3
  91.5 1.0 %collective-permute-done.3.other_share_ref = f32[64,160]{1,0:T(8,128)S(1)} collective-permute-done((f32[64,160]{1,0:T(8,128)S(1)}, f32[64,160]{1,0:T(8,128)S(1)}, u32[]{:S(2)}, u32[]{:S(2)}) %collective-permute-start.3) | collective-permute-done | bytes 40992 | tf_op jit(solution)/shard_map/ppermute | solution.py:370
  92.6 0.0 collective-permute-done.2.other_ref
  92.6 1.3 %shard_map.77 = (f32[2,64,160]{2,1,0:T(8,128)}, f32[2,64,1440]{2,1,0:T(8,128)}) custom-call(bf16[4,64,384]{2,1,0:T(8,128)(2,1)S(1)} %all_to_all.37.got_ref, bf16[4,64,384]{2,1,0:T(8,128)(2,1)S(1)} %collective-permute-done.2.other_ref, f32[64,160]{1,0:T(8,128)S(1)} %get-tuple-element.31.share_ref, f32[64,160]{1,0:T(8,128)S(1)} %collective-permute-done.3.other_share_ref), custom_call_target="tpu_custom_call" | custom-call | bytes 1048576 | tf_op jit(solution)/shard_map/pallas_call | solution.py:375
  (2 shorter events, 0.1 us)
Async XLA Ops:
  2.7 12.4 %all-to-all-start = ((bf16[8,32,640]{2,1,0:T(8,128)(2,1)}), bf16[8,32,640]{2,1,0:T(8,128)(2,1)S(1)}, u32[]{:S(2)}, u32[]{:S(2)}) async-start(bf16[8,32,640]{2,1,0:T(8,128)(2,1)} %shard_map.68), calls=%async_computation | async-start | bytes 655360 | tf_op jit(solution)/shard_map/all_to_all | solution.py:35
  15.1 3.6 %copy-start.2 = (bf16[8,32,640]{2,1,0:T(8,128)(2,1)}, bf16[8,32,640]{2,1,0:T(8,128)(2,1)S(1)}, u32[]{:S(2)}) copy-start(bf16[8,32,640]{2,1,0:T(8,128)(2,1)S(1)} %all-to-all-done.got_hbm) | copy-start | bytes 983044
  15.1 15.6 %all-to-all-start.1 = ((bf16[8,160,256]{2,1,0:T(8,128)(2,1)}), bf16[8,160,256]{2,1,0:T(8,128)(2,1)S(1)}, u32[]{:S(2)}, u32[]{:S(2)}) async-start(bf16[8,160,256]{2,1,0:T(8,128)(2,1)} %get-tuple-element.23), calls=%async_computation.1 | async-start | bytes 1310720 | tf_op jit(solution)/shard_map/all_to_all | solution.py:35
  27.4 1.7 %collective-permute-start = (f32[16,4,640]{2,1,0:T(4,128)}, f32[16,4,640]{2,1,0:T(4,128)S(1)}, u32[]{:S(2)}, u32[]{:S(2)}) collective-permute-start(f32[16,4,640]{2,1,0:T(4,128)} %get-tuple-element.22), channel_id=1, source_target_pairs={{0,4},{4,0},{1,5},{5,1},{2,6},{6,2},{3,7},{7,3},{8,12},{12,8},{9,1... | collective-permute-start | bytes 491528 | tf_op jit(solution)/shard_map/ppermute | solution.py:337
  27.9 10.0 %collective-permute-start.1 = (bf16[256,640]{1,0:T(8,128)(2,1)}, bf16[256,640]{1,0:T(8,128)(2,1)S(1)}, u32[]{:S(2)}, u32[]{:S(2)}) collective-permute-start(bf16[256,640]{1,0:T(8,128)(2,1)} %get-tuple-element.26), channel_id=1, source_target_pairs={{0,4},{4,0},{1,5},{5,1},{2,6},{6,2},{3,7},{7,3},{8,12},{12,8},{9,1... | collective-permute-start | bytes 983048 | tf_op jit(solution)/shard_map/ppermute | solution.py:338
  29.2 0.9 copy-start.1
  30.7 15.4 %all-to-all-start.2 = ((f32[16,4,640]{2,1,0:T(4,128)}), f32[16,4,640]{2,1,0:T(4,128)S(1)}, u32[]{:S(2)}, u32[]{:S(2)}) async-start(f32[16,4,640]{2,1,0:T(4,128)} %shard_map.71), calls=%async_computation.2 | async-start | bytes 327680 | tf_op jit(solution)/shard_map/all_to_all | solution.py:35
  46.1 1.0 %copy-start = (bf16[256,640]{1,0:T(8,128)(2,1)S(1)}, bf16[256,640]{1,0:T(8,128)(2,1)}, u32[]{:S(2)}) copy-start(bf16[256,640]{1,0:T(8,128)(2,1)} %get-tuple-element.25.keep_ref) | copy-start | bytes 983044
  59.5 10.4 %all-to-all-start.4 = ((bf16[4,512,128]{2,1,0:T(8,128)(2,1)}), bf16[4,512,128]{2,1,0:T(8,128)(2,1)S(1)}, u32[]{:S(2)}, u32[]{:S(2)}) async-start(bf16[4,512,128]{2,1,0:T(8,128)(2,1)} %get-tuple-element.27), calls=%async_computation.4 | async-start | bytes 1048576 | tf_op jit(solution)/shard_map/all_to_all | solution.py:35
  91.0 1.5 %collective-permute-start.2 = (bf16[4,64,384]{2,1,0:T(8,128)(2,1)S(1)}, bf16[4,64,384]{2,1,0:T(8,128)(2,1)S(1)}, u32[]{:S(2)}, u32[]{:S(2)}) collective-permute-start(bf16[4,64,384]{2,1,0:T(8,128)(2,1)S(1)} %all_to_all.37.got_ref), channel_id=1, source_target_pairs={{0,4},{4,0},{1,5},{5,1},{2,6},{6,2},{3,7},{7,3},{8,12},{12,8},{9,1... | collective-permute-start | bytes 589832 | tf_op jit(solution)/shard_map/ppermute | solution.py:374
  91.0 1.5 %collective-permute-start.3 = (f32[64,160]{1,0:T(8,128)S(1)}, f32[64,160]{1,0:T(8,128)S(1)}, u32[]{:S(2)}, u32[]{:S(2)}) collective-permute-start(f32[64,160]{1,0:T(8,128)S(1)} %get-tuple-element.31.share_ref), channel_id=1, source_target_pairs={{0,4},{4,0},{1,5},{5,1},{2,6},{6,2},{3,7},{7,3},{8,12},{12,8},{9,1... | collective-permute-start | bytes 122888 | tf_op jit(solution)/shard_map/ppermute | solution.py:370

commit v10 on v9

--- a/solution.py
+++ b/solution.py
@@ -1,3 +1,5 @@
+import functools
+
 import jax
 import jax.numpy as jnp
 from jax import lax
@@ -33,6 +35,14 @@
 
 def exchange(chunks, axes):
     return lax.all_to_all(chunks, axes, 0, 0, tiled=True)
+
+
+def shifts(values, axis):
+    size = lax.axis_size(axis)
+    moved = [values[0]]
+    for s in range(1, len(values)):
+        moved.append(lax.ppermute(values[s], axis, [(i, (i + s) % size) for i in range(size)]))
+    return moved
 
 
 def stacked_halves(value):
@@ -194,8 +204,7 @@
     factor = stacked_halves(p_ref[...])
     for start, ref in ((row, keep_ref), (1 - row, swap_ref)):
         out = paired_halves(dot(ref[...], factor, NT)).astype(BF)
-        for k in range(4):
-            w_ref[k, pl.ds(pl.multiple_of(256 * start, 256), 256), :] = out
+        w_ref[pl.ds(pl.multiple_of(256 * start, 256), 256), :] = out
 
 
 def factor_body(p_ref, inverse_ref, basis_ref, share_ref):
@@ -222,7 +231,12 @@
     share_ref[...] = part
 
 
-def taps_body(w_ref, x_ref, inverse_ref, out_ref, image, sums):
+def taps_body(own_order, *refs):
+    w_refs, (x_ref, inverse_ref) = refs[:4], refs[4:6]
+    out_refs, (w_ref, image, sums) = refs[6:10], refs[10:]
+    col = lax.axis_index("col")
+    for s in range(4):
+        w_ref[lax.rem(col + 4 - s, 4)] = w_refs[s][...]
     zero = jnp.zeros((1, 4, 16, 384), BF)
     image[0:1] = zero
     image[33:34] = zero
@@ -244,29 +258,32 @@
             sums[160 * t : 160 * t + 160, :] = value + pltpu.roll(value, 64, 1)
     sums[1440:1472, :] = jnp.zeros((32, 128), F32)
     inverse = inverse_ref[...]
-    for i in range(4):
-        part = sums[360 * i : 360 * i + 384, :][:, :64]
-        out_ref[i] = dot(inverse, part, NT, lax.Precision.HIGHEST).astype(BF)
-
-
-def total_body(got_ref, out_ref):
-    total = got_ref[0].astype(F32)
-    for i in range(1, got_ref.shape[0]):
-        total = total + got_ref[i].astype(F32)
-    for i in range(out_ref.shape[0]):
-        out_ref[i] = total.astype(BF)
-
-
-def place_body(got_ref, other_ref, share_ref, other_share_ref, basis_ref, out_ref):
-    row = lax.axis_index("row")
-    for layer, ref, share in ((row, got_ref, share_ref), (1 - row, other_ref, other_share_ref)):
+    for s in range(4):
+        i = lax.rem(lax.axis_index("dp") + s, 4) if own_order else s
+        part = sums[pl.ds(pl.multiple_of(360 * i, 8), 384), :][:, :64]
+        out_refs[s][...] = dot(inverse, part, NT, lax.Precision.HIGHEST).astype(BF)
+
+
+def total_body(a_ref, b_ref, c_ref, d_ref, out_ref):
+    total = a_ref[...].astype(F32) + b_ref[...].astype(F32)
+    total = total + (c_ref[...].astype(F32) + d_ref[...].astype(F32))
+    out_ref[...] = total.astype(BF)
+
+
+def place_body(*refs):
+    own, other, shares = refs[:4], refs[4:8], refs[8:10]
+    basis_ref, out_ref, held = refs[10:]
+    row, col = lax.axis_index("row"), lax.axis_index("col")
+    for layer, parts, share in ((row, own, shares[0]), (1 - row, other, shares[1])):
         basis_ref[layer] = share[...]
-        out = out_ref.at[layer]
+        for s in range(4):
+            held[layer, lax.rem(col + 4 - s, 4)] = parts[s][...]
+    for layer in range(2):
         for k in range(4):
-            value = ref[k].astype(F32)
+            value = held[layer, k].astype(F32)
             for j in range(9):
                 start = 160 * j + 40 * k
-                out[:, start : start + 40] = value[:, 40 * j : 40 * j + 40]
+                out_ref[layer, :, start : start + 40] = value[:, 40 * j : 40 * j + 40]
 
 
 def on_device(x_input, pre_act, out_grad, conv_weight, q_prev):
@@ -346,11 +363,11 @@
 
     w_own, p_t = call(
         project_body,
-        (shape((4, 512, 128), BF), shape((64, 640), F32)),
+        (shape((512, 128), BF), shape((64, 640), F32)),
         2 * 512 * 640 * 128,
         2 << 20,
     )(p_own, keep, swap)
-    w_all = exchange(w_own, ("col",))
+    w_all = shifts([w_own] * 4, "col")
     inverse, basis, share = call(
         factor_body,
         (shape((64, 64), F32), shape((64, 640), F32), shape((64, 160), F32)),
@@ -359,23 +376,31 @@
     )(p_t)
 
     sums = call(
-        taps_body,
-        shape((4, 64, 384), BF),
+        functools.partial(taps_body, images == 4),
+        (shape((64, 384), BF),) * 4,
         2 * 160 * 2048 * 1152,
         2 << 20,
-        scratch_shapes=[pltpu.VMEM((34, 4, 16, 384), BF), pltpu.VMEM((1472, 128), F32)],
-    )(w_all, slices, inverse)
+        scratch_shapes=[
+            pltpu.VMEM((4, 512, 128), BF),
+            pltpu.VMEM((34, 4, 16, 384), BF),
+            pltpu.VMEM((1472, 128), F32),
+        ],
+    )(*w_all, slices, inverse)
 
     if images == 4:
         other_share = lax.ppermute(share, "row", across)
-        sums = exchange(sums, ("dp",))
-        mine = call(total_body, shape((cols, 64, 384), BF), 0, 1 << 20)(sums)
-        every = exchange(mine, ("col",))
-        other = lax.ppermute(every, "row", across)
+        mine = call(total_body, shape((64, 384), BF), 0, 1 << 20)(*shifts(sums, "dp"))
+        every = shifts([mine] * 4, "col")
+        other = [lax.ppermute(part, "row", across) for part in every]
         basis_out, q_out = call(
-            place_body, (shape((2, 64, 160), F32), shape((2, 64, 1440), F32)), 0, 1 << 20
-        )(every, other, share, other_share)
+            place_body,
+            (shape((2, 64, 160), F32), shape((2, 64, 1440), F32)),
+            0,
+            1 << 20,
+            scratch_shapes=[pltpu.VMEM((2, 4, 64, 384), BF)],
+        )(*every, *other, share, other_share)
         return basis_out.transpose(2, 0, 1), q_out.transpose(2, 0, 1)
+    sums = jnp.stack(sums)
     sums = lax.psum(sums[:, :, :360].astype(F32), "dp")
     every = lax.all_gather(sums, PLANE).reshape(rows, cols, 4, 64, 9, 40)
     every = every.transpose(2, 4, 1, 5, 0, 3).reshape(5760, 2, 64)

time: 94.5 us -> 89.4 us (0.946)
  blocking collectives: 29.9 us -> 11.2 us
  waiting for transfers between devices: 11.3 us -> 18.9 us
  starting transfers between devices: 20.6 us -> 27.1 us
    all_to_all x3 -> x1, blocking collectives: 29.9 us -> 11.2 us  [exchange(): return lax.all_to_all(chunks, axes, 0, 0, tiled=True)]
    ppermute x1 -> x13, starting transfers between devices: 0.01 us -> 10.1 us  [the longest x9 10.1 us: shifts(): lax.ppermute(values[s], axis, [(i, (i + s) % size) for i in range(size)])]
    ppermute x1 -> x13, waiting for transfers between devices: 0.01 us -> 7.69 us  [the longest x9 7.68 us: shifts(): lax.ppermute(values[s], axis, [(i, (i + s) % size) for i in range(size)])]
    all_to_all x4 -> x3, starting transfers between devices: 19.6 us -> 15.9 us  [exchange(): return lax.all_to_all(chunks, axes, 0, 0, tiled=True)]
    all_to_all x4 -> x3, waiting for transfers between devices: 9.14 us -> 9.14 us  [exchange(): return lax.all_to_all(chunks, axes, 0, 0, tiled=True)]
  transfers between devices with their start and end apart: 8 -> 19, of which waited for: 4 -> 9; matrix products, arithmetic and copies ran while one was open for 0% -> 0% of each run, Pallas kernels for 24% -> 25%
where the time goes in v10:
time: 89.4 us; the launch traced here: 88.9 us
  Pallas kernels  29.1 us (33%)
  starting transfers between devices  27.1 us (30%)
  waiting for transfers between devices  18.9 us (21%)
  blocking collectives  11.2 us (13%)
  local copies, waits for them, and re-layouts  1.89 us (2%)
    all_to_all x3, starting transfers between devices, exchange(): return lax.all_to_all(chunks, axes, 0, 0, tiled=True)  15.9 us
    all_to_all x1, blocking collectives, exchange(): return lax.all_to_all(chunks, axes, 0, 0, tiled=True)  11.2 us
    ppermute x9, starting transfers between devices, shifts(): lax.ppermute(values[s], axis, [(i, (i + s) % size) for i in range(size)])  10.1 us
    all_to_all x3, waiting for transfers between devices, exchange(): return lax.all_to_all(chunks, axes, 0, 0, tiled=True)  9.14 us
    pallas_call x1, Pallas kernels, on_device(): call(power_body, (shape((256, 640), BF), shape((256, 640), BF), p_shape,...  8.76 us
    ppermute x9, waiting for transfers between devices, shifts(): lax.ppermute(values[s], axis, [(i, (i + s) % size) for i in range(size)])  7.68 us
    pallas_call x1, Pallas kernels, on_device(): call(factor_body, (shape((64, 64), F32), shape((64, 640), F32), shape((64...  6.79 us
    pallas_call x1, Pallas kernels, on_device(): call(prepare_body, (shape((8, 160, 256), BF), shape((3, 384, 640), BF), s...  6.2 us
  transfers between devices with their start and end apart: 19, of which 9 were waited for; matrix products, arithmetic and copies ran while one was open for 0% of the time, Pallas kernels for 25%

profile of v10, /device:TPU:0, one launch (start us, length us, event | category | flops | bytes accessed | tf_op | source)
XLA Modules:
  0.0 88.9 jit_solution(16196612840166806302)
XLA Ops:
  0.6 2.1 %shard_map.68 = bf16[8,32,640]{2,1,0:T(8,128)(2,1)} custom-call(bf16[256,640]{1,0:T(8,128)(2,1)} %bitcast.9, bf16[256,640]{1,0:T(8,128)(2,1)} %bitcast.13), custom_call_target="tpu_custom_call" | custom-call | flops 16777216 | bytes 1048576 | tf_op jit(solution)/shard_map/pallas_call | solution.py:300
  2.7 5.2 %all-to-all-start = ((bf16[8,32,640]{2,1,0:T(8,128)(2,1)}), bf16[8,32,640]{2,1,0:T(8,128)(2,1)S(1)}, u32[]{:S(2)}, u32[]{:S(2)}) async-start(bf16[8,32,640]{2,1,0:T(8,128)(2,1)} %shard_map.68), calls=%async_computation | async-start | bytes 655360 | tf_op jit(solution)/shard_map/all_to_all | solution.py:37
  7.9 6.2 %shard_map.69 = (bf16[8,160,256]{2,1,0:T(8,128)(2,1)}, bf16[3,384,640]{2,1,0:T(8,128)(2,1)}, bf16[3,128,384]{2,1,0:T(8,128)(2,1)}, f32[256,640]{1,0:T(8,128)}) custom-call(bf16[256,640]{1,0:T(8,128)(2,1)} %bitcast.10, bf16[256,640]{1,0:T(8,128)(2,1)} %bitcast.12, f32[128,5760]{1,0:T(8,128)} %bitcast.8), custom_call_target="tpu_custom_call" | custom-call | flops 377487360 | bytes 8388608 | tf_op jit(solution)/shard_map/pallas_call | solution.py:310
  14.1 1.0 %all-to-all-done.got_hbm = bf16[8,32,640]{2,1,0:T(8,128)(2,1)S(1)} async-done(((bf16[8,32,640]{2,1,0:T(8,128)(2,1)}), bf16[8,32,640]{2,1,0:T(8,128)(2,1)S(1)}, u32[]{:S(2)}, u32[]{:S(2)}) %all-to-all-start) | async-done | bytes 327712 | tf_op jit(solution)/shard_map/all_to_all | solution.py:37
  15.1 3.5 %all-to-all-start.1 = ((bf16[8,160,256]{2,1,0:T(8,128)(2,1)}), bf16[8,160,256]{2,1,0:T(8,128)(2,1)S(1)}, u32[]{:S(2)}, u32[]{:S(2)}) async-start(bf16[8,160,256]{2,1,0:T(8,128)(2,1)} %get-tuple-element.27), calls=%async_computation.1 | async-start | bytes 1310720 | tf_op jit(solution)/shard_map/all_to_all | solution.py:37
  18.7 8.8 %shard_map.70 = (bf16[256,640]{1,0:T(8,128)(2,1)}, bf16[256,640]{1,0:T(8,128)(2,1)}, f32[16,4,640]{2,1,0:T(4,128)}, f32[16,4,640]{2,1,0:T(4,128)}) custom-call(bf16[256,640]{1,0:T(8,128)(2,1)} %bitcast.11, bf16[256,640]{1,0:T(8,128)(2,1)} %bitcast.14, bf16[8,32,640]{2,1,0:T(8,128)(2,1)} %copy-done.2, f32[256,640]{1,0:T(8,128)} %get-tuple-element.22.slope_hbm, ...), custom_call_target="tpu_custom_call" | custom-call | flops 3244032000 | bytes 12582912 | tf_op jit(solution)/shard_map/pallas_call | solution.py:331
  27.4 0.5 collective-permute-start
  27.9 0.1 collective-permute-start.1
  28.0 1.1 %collective-permute-done.right_ref = f32[16,4,640]{2,1,0:T(4,128)S(1)} collective-permute-done((f32[16,4,640]{2,1,0:T(4,128)}, f32[16,4,640]{2,1,0:T(4,128)S(1)}, u32[]{:S(2)}, u32[]{:S(2)}) %collective-permute-start) | collective-permute-done | bytes 163872 | tf_op jit(solution)/shard_map/ppermute | solution.py:354
  29.2 0.9 %copy-done.1 = f32[16,4,640]{2,1,0:T(4,128)S(1)} copy-done((f32[16,4,640]{2,1,0:T(4,128)S(1)}, f32[16,4,640]{2,1,0:T(4,128)}, u32[]{:S(2)}) %copy-start.1) | copy-done | bytes 163864
  30.1 0.7 shard_map.71
  30.8 0.0 all-to-all-done.1.refs_4_
  30.8 7.2 %all-to-all-start.2 = ((f32[16,4,640]{2,1,0:T(4,128)}), f32[16,4,640]{2,1,0:T(4,128)S(1)}, u32[]{:S(2)}, u32[]{:S(2)}) async-start(f32[16,4,640]{2,1,0:T(4,128)} %shard_map.71), calls=%async_computation.2 | async-start | bytes 327680 | tf_op jit(solution)/shard_map/all_to_all | solution.py:37
  38.0 0.0 collective-permute-done.1.swap_ref
  38.0 8.1 %all-to-all-done.2.got_ref = f32[16,4,640]{2,1,0:T(4,128)S(1)} async-done(((f32[16,4,640]{2,1,0:T(4,128)}), f32[16,4,640]{2,1,0:T(4,128)S(1)}, u32[]{:S(2)}, u32[]{:S(2)}) %all-to-all-start.2) | async-done | bytes 163872 | tf_op jit(solution)/shard_map/all_to_all | solution.py:37
  46.1 1.0 %copy-done = bf16[256,640]{1,0:T(8,128)(2,1)S(1)} copy-done((bf16[256,640]{1,0:T(8,128)(2,1)S(1)}, bf16[256,640]{1,0:T(8,128)(2,1)}, u32[]{:S(2)}) %copy-start) | copy-done | bytes 327704
  47.1 11.2 %all_to_all.20.got_ref = f32[16,4,640]{2,1,0:T(4,128)S(1)} all-to-all(f32[16,4,640]{2,1,0:T(4,128)S(1)} %shard_map.72), channel_id=1, replica_groups=mesh['dp'=4,'row'=2,'col'=4] {'dp','col'}, dimensions={0} | all-to-all | bytes 327680 | tf_op jit(solution)/shard_map/all_to_all | solution.py:37
  58.3 0.4 shard_map.73
  58.7 0.8 collective-permute-start.4
  59.6 1.9 %collective-permute-start.3 = (bf16[512,128]{1,0:T(8,128)(2,1)S(1)}, bf16[512,128]{1,0:T(8,128)(2,1)S(1)}, u32[]{:S(2)}, u32[]{:S(2)}) collective-permute-start(bf16[512,128]{1,0:T(8,128)(2,1)S(1)} %get-tuple-element.31.refs_0_), channel_id=1, source_target_pairs={{0,2},{1,3},{2,0},{3,1},{4,6},{5,7},{6,4},{7,5},{8,10},{9,11},{10,... | collective-permute-start | bytes 393224 | tf_op jit(solution)/shard_map/ppermute | solution.py:44
  61.5 0.1 collective-permute-start.2
  61.6 6.8 %shard_map.74 = (f32[64,64]{1,0:T(8,128)S(1)}, f32[64,640]{1,0:T(8,128)}, f32[64,160]{1,0:T(8,128)S(1)}) custom-call(f32[64,640]{1,0:T(8,128)S(1)} %get-tuple-element.33.p_ref), custom_call_target="tpu_custom_call" | custom-call | flops 1073741824 | bytes 1048576 | tf_op jit(solution)/shard_map/pallas_call | solution.py:371
  68.4 0.0 collective-permute-done.4.refs_3_
  68.4 0.0 collective-permute-done.3.refs_2_
  68.4 0.0 collective-permute-done.2.refs_1_
  68.4 2.8 %shard_map.75 = (bf16[64,384]{1,0:T(8,128)(2,1)S(1)}, bf16[64,384]{1,0:T(8,128)(2,1)S(1)}, bf16[64,384]{1,0:T(8,128)(2,1)S(1)}, bf16[64,384]{1,0:T(8,128)(2,1)S(1)}) custom-call(bf16[512,128]{1,0:T(8,128)(2,1)S(1)} %get-tuple-element.31.refs_0_, bf16[512,128]{1,0:T(8,128)(2,1)S(1)} %collective-permute-done.2.refs_1_, ...), custom_call_target="tpu_custom_call" | custom-call | flops 754974720 | bytes 2097152 | tf_op jit(solution)/shard_map/pallas_call | solution.py:378
  71.2 0.9 %collective-permute-start.5 = (bf16[64,384]{1,0:T(8,128)(2,1)S(1)}, bf16[64,384]{1,0:T(8,128)(2,1)S(1)}, u32[]{:S(2)}, u32[]{:S(2)}) collective-permute-start(bf16[64,384]{1,0:T(8,128)(2,1)S(1)} %get-tuple-element.36), channel_id=1, source_target_pairs={{0,8},{8,16},{16,24},{24,0},{1,9},{9,17},{17,25},{25,1},{2,10},{10... | collective-permute-start | bytes 147464 | tf_op jit(solution)/shard_map/ppermute | solution.py:44
  72.1 1.2 %collective-permute-start.6 = (bf16[64,384]{1,0:T(8,128)(2,1)S(1)}, bf16[64,384]{1,0:T(8,128)(2,1)S(1)}, u32[]{:S(2)}, u32[]{:S(2)}) collective-permute-start(bf16[64,384]{1,0:T(8,128)(2,1)S(1)} %get-tuple-element.37), channel_id=1, source_target_pairs={{0,16},{8,24},{16,0},{24,8},{1,17},{9,25},{17,1},{25,9},{2,18},{10... | collective-permute-start | bytes 147464 | tf_op jit(solution)/shard_map/ppermute | solution.py:44
  73.3 1.9 %collective-permute-start.7 = (bf16[64,384]{1,0:T(8,128)(2,1)S(1)}, bf16[64,384]{1,0:T(8,128)(2,1)S(1)}, u32[]{:S(2)}, u32[]{:S(2)}) collective-permute-start(bf16[64,384]{1,0:T(8,128)(2,1)S(1)} %get-tuple-element.38), channel_id=1, source_target_pairs={{0,24},{8,0},{16,8},{24,16},{1,25},{9,1},{17,9},{25,17},{2,26},{10... | collective-permute-start | bytes 147464 | tf_op jit(solution)/shard_map/ppermute | solution.py:44
  75.2 2.1 %collective-permute-done.5.b_ref = bf16[64,384]{1,0:T(8,128)(2,1)S(1)} collective-permute-done((bf16[64,384]{1,0:T(8,128)(2,1)S(1)}, bf16[64,384]{1,0:T(8,128)(2,1)S(1)}, u32[]{:S(2)}, u32[]{:S(2)}) %collective-permute-start.5) | collective-permute-done | bytes 49184 | tf_op jit(solution)/shard_map/ppermute | solution.py:44
  77.2 0.9 %collective-permute-done.6.c_ref = bf16[64,384]{1,0:T(8,128)(2,1)S(1)} collective-permute-done((bf16[64,384]{1,0:T(8,128)(2,1)S(1)}, bf16[64,384]{1,0:T(8,128)(2,1)S(1)}, u32[]{:S(2)}, u32[]{:S(2)}) %collective-permute-start.6) | collective-permute-done | bytes 49184 | tf_op jit(solution)/shard_map/ppermute | solution.py:44
  78.1 0.0 collective-permute-done.7.d_ref
  78.2 2.4 %collective-permute-start.10 = (bf16[64,384]{1,0:T(8,128)(2,1)S(1)}, bf16[64,384]{1,0:T(8,128)(2,1)S(1)}, u32[]{:S(2)}, u32[]{:S(2)}) collective-permute-start(bf16[64,384]{1,0:T(8,128)(2,1)S(1)} %shard_map.76.refs_0_), channel_id=1, source_target_pairs={{0,3},{1,0},{2,1},{3,2},{4,7},{5,4},{6,5},{7,6},{8,11},{9,8},{10,9... | collective-permute-start | bytes 147464 | tf_op jit(solution)/shard_map/ppermute | solution.py:44
  80.6 0.6 collective-permute-start.9
  81.1 0.3 collective-permute-start.8
  81.4 0.9 %collective-permute-done.10.refs_3_ = bf16[64,384]{1,0:T(8,128)(2,1)S(1)} collective-permute-done((bf16[64,384]{1,0:T(8,128)(2,1)S(1)}, bf16[64,384]{1,0:T(8,128)(2,1)S(1)}, u32[]{:S(2)}, u32[]{:S(2)}) %collective-permute-start.10) | collective-permute-done | bytes 49184 | tf_op jit(solution)/shard_map/ppermute | solution.py:44
  82.3 0.0 collective-permute-start.14
  82.3 2.3 %collective-permute-done.9.refs_2_ = bf16[64,384]{1,0:T(8,128)(2,1)S(1)} collective-permute-done((bf16[64,384]{1,0:T(8,128)(2,1)S(1)}, bf16[64,384]{1,0:T(8,128)(2,1)S(1)}, u32[]{:S(2)}, u32[]{:S(2)}) %collective-permute-start.9) | collective-permute-done | bytes 49184 | tf_op jit(solution)/shard_map/ppermute | solution.py:44
  84.7 0.0 collective-permute-start.13
  84.7 1.5 %collective-permute-done.8.refs_1_ = bf16[64,384]{1,0:T(8,128)(2,1)S(1)} collective-permute-done((bf16[64,384]{1,0:T(8,128)(2,1)S(1)}, bf16[64,384]{1,0:T(8,128)(2,1)S(1)}, u32[]{:S(2)}, u32[]{:S(2)}) %collective-permute-start.8) | collective-permute-done | bytes 49184 | tf_op jit(solution)/shard_map/ppermute | solution.py:44
  86.1 0.0 collective-permute-start.12
  86.1 0.5 collective-permute-start.15
  86.6 0.9 %collective-permute-done.15.refs_9_ = f32[64,160]{1,0:T(8,128)S(1)} collective-permute-done((f32[64,160]{1,0:T(8,128)S(1)}, f32[64,160]{1,0:T(8,128)S(1)}, u32[]{:S(2)}, u32[]{:S(2)}) %collective-permute-start.15) | collective-permute-done | bytes 40992 | tf_op jit(solution)/shard_map/ppermute | solution.py:391
  87.5 0.0 collective-permute-done.11.refs_4_
  87.6 0.0 collective-permute-done.14.refs_7_
  87.6 0.0 collective-permute-done.13.refs_6_
  87.6 0.0 collective-permute-done.12.refs_5_
  87.6 1.4 %shard_map.77 = (f32[2,64,160]{2,1,0:T(8,128)}, f32[2,64,1440]{2,1,0:T(8,128)}) custom-call(bf16[64,384]{1,0:T(8,128)(2,1)S(1)} %shard_map.76.refs_0_, bf16[64,384]{1,0:T(8,128)(2,1)S(1)} %collective-permute-done.8.refs_1_, bf16[64,384]{1,0:T(8,128)(2,1)S(1)} %collective-permute-done.9.refs_2_, bf16[64,384]{1,0:T(8,128)(2,1)S(1)} %collective-permute-done.10.refs_3_, ...), custom_call_target="tpu_custom_call" | custom-call | bytes 1048576 | tf_op jit(solution)/shard_map/pallas_call | solution.py:395
  (7 shorter events, 0.1 us)
Async XLA Ops:
  2.7 12.4 %all-to-all-start = ((bf16[8,32,640]{2,1,0:T(8,128)(2,1)}), bf16[8,32,640]{2,1,0:T(8,128)(2,1)S(1)}, u32[]{:S(2)}, u32[]{:S(2)}) async-start(bf16[8,32,640]{2,1,0:T(8,128)(2,1)} %shard_map.68), calls=%async_computation | async-start | bytes 655360 | tf_op jit(solution)/shard_map/all_to_all | solution.py:37
  15.1 3.6 %copy-start.2 = (bf16[8,32,640]{2,1,0:T(8,128)(2,1)}, bf16[8,32,640]{2,1,0:T(8,128)(2,1)S(1)}, u32[]{:S(2)}) copy-start(bf16[8,32,640]{2,1,0:T(8,128)(2,1)S(1)} %all-to-all-done.got_hbm) | copy-start | bytes 983044
  15.1 15.7 %all-to-all-start.1 = ((bf16[8,160,256]{2,1,0:T(8,128)(2,1)}), bf16[8,160,256]{2,1,0:T(8,128)(2,1)S(1)}, u32[]{:S(2)}, u32[]{:S(2)}) async-start(bf16[8,160,256]{2,1,0:T(8,128)(2,1)} %get-tuple-element.27), calls=%async_computation.1 | async-start | bytes 1310720 | tf_op jit(solution)/shard_map/all_to_all | solution.py:37
  27.4 1.7 %collective-permute-start = (f32[16,4,640]{2,1,0:T(4,128)}, f32[16,4,640]{2,1,0:T(4,128)S(1)}, u32[]{:S(2)}, u32[]{:S(2)}) collective-permute-start(f32[16,4,640]{2,1,0:T(4,128)} %get-tuple-element.26), channel_id=1, source_target_pairs={{0,4},{4,0},{1,5},{5,1},{2,6},{6,2},{3,7},{7,3},{8,12},{12,8},{9,1... | collective-permute-start | bytes 491528 | tf_op jit(solution)/shard_map/ppermute | solution.py:354
  27.9 10.0 %collective-permute-start.1 = (bf16[256,640]{1,0:T(8,128)(2,1)}, bf16[256,640]{1,0:T(8,128)(2,1)S(1)}, u32[]{:S(2)}, u32[]{:S(2)}) collective-permute-start(bf16[256,640]{1,0:T(8,128)(2,1)} %get-tuple-element.30), channel_id=1, source_target_pairs={{0,4},{4,0},{1,5},{5,1},{2,6},{6,2},{3,7},{7,3},{8,12},{12,8},{9,1... | collective-permute-start | bytes 983048 | tf_op jit(solution)/shard_map/ppermute | solution.py:355
  29.2 0.9 %copy-start.1 = (f32[16,4,640]{2,1,0:T(4,128)S(1)}, f32[16,4,640]{2,1,0:T(4,128)}, u32[]{:S(2)}) copy-start(f32[16,4,640]{2,1,0:T(4,128)} %get-tuple-element.25.left_ref) | copy-start | bytes 491524
  30.8 15.3 %all-to-all-start.2 = ((f32[16,4,640]{2,1,0:T(4,128)}), f32[16,4,640]{2,1,0:T(4,128)S(1)}, u32[]{:S(2)}, u32[]{:S(2)}) async-start(f32[16,4,640]{2,1,0:T(4,128)} %shard_map.71), calls=%async_computation.2 | async-start | bytes 327680 | tf_op jit(solution)/shard_map/all_to_all | solution.py:37
  46.1 1.0 %copy-start = (bf16[256,640]{1,0:T(8,128)(2,1)S(1)}, bf16[256,640]{1,0:T(8,128)(2,1)}, u32[]{:S(2)}) copy-start(bf16[256,640]{1,0:T(8,128)(2,1)} %get-tuple-element.29.keep_ref) | copy-start | bytes 983044
  58.7 9.7 %collective-permute-start.4 = (bf16[512,128]{1,0:T(8,128)(2,1)S(1)}, bf16[512,128]{1,0:T(8,128)(2,1)S(1)}, u32[]{:S(2)}, u32[]{:S(2)}) collective-permute-start(bf16[512,128]{1,0:T(8,128)(2,1)S(1)} %get-tuple-element.31.refs_0_), channel_id=1, source_target_pairs={{0,3},{1,0},{2,1},{3,2},{4,7},{5,4},{6,5},{7,6},{8,11},{9,8},{10,9... | collective-permute-start | bytes 393224 | tf_op jit(solution)/shard_map/ppermute | solution.py:44
  59.6 8.8 %collective-permute-start.3 = (bf16[512,128]{1,0:T(8,128)(2,1)S(1)}, bf16[512,128]{1,0:T(8,128)(2,1)S(1)}, u32[]{:S(2)}, u32[]{:S(2)}) collective-permute-start(bf16[512,128]{1,0:T(8,128)(2,1)S(1)} %get-tuple-element.31.refs_0_), channel_id=1, source_target_pairs={{0,2},{1,3},{2,0},{3,1},{4,6},{5,7},{6,4},{7,5},{8,10},{9,11},{10,... | collective-permute-start | bytes 393224 | tf_op jit(solution)/shard_map/ppermute | solution.py:44
  61.5 6.9 %collective-permute-start.2 = (bf16[512,128]{1,0:T(8,128)(2,1)S(1)}, bf16[512,128]{1,0:T(8,128)(2,1)S(1)}, u32[]{:S(2)}, u32[]{:S(2)}) collective-permute-start(bf16[512,128]{1,0:T(8,128)(2,1)S(1)} %get-tuple-element.31.refs_0_), channel_id=1, source_target_pairs={{0,1},{1,2},{2,3},{3,0},{4,5},{5,6},{6,7},{7,4},{8,9},{9,10},{10,1... | collective-permute-start | bytes 393224 | tf_op jit(solution)/shard_map/ppermute | solution.py:44
  71.2 6.0 %collective-permute-start.5 = (bf16[64,384]{1,0:T(8,128)(2,1)S(1)}, bf16[64,384]{1,0:T(8,128)(2,1)S(1)}, u32[]{:S(2)}, u32[]{:S(2)}) collective-permute-start(bf16[64,384]{1,0:T(8,128)(2,1)S(1)} %get-tuple-element.36), channel_id=1, source_target_pairs={{0,8},{8,16},{16,24},{24,0},{1,9},{9,17},{17,25},{25,1},{2,10},{10... | collective-permute-start | bytes 147464 | tf_op jit(solution)/shard_map/ppermute | solution.py:44
  72.1 6.0 %collective-permute-start.6 = (bf16[64,384]{1,0:T(8,128)(2,1)S(1)}, bf16[64,384]{1,0:T(8,128)(2,1)S(1)}, u32[]{:S(2)}, u32[]{:S(2)}) collective-permute-start(bf16[64,384]{1,0:T(8,128)(2,1)S(1)} %get-tuple-element.37), channel_id=1, source_target_pairs={{0,16},{8,24},{16,0},{24,8},{1,17},{9,25},{17,1},{25,9},{2,18},{10... | collective-permute-start | bytes 147464 | tf_op jit(solution)/shard_map/ppermute | solution.py:44
  73.3 4.8 %collective-permute-start.7 = (bf16[64,384]{1,0:T(8,128)(2,1)S(1)}, bf16[64,384]{1,0:T(8,128)(2,1)S(1)}, u32[]{:S(2)}, u32[]{:S(2)}) collective-permute-start(bf16[64,384]{1,0:T(8,128)(2,1)S(1)} %get-tuple-element.38), channel_id=1, source_target_pairs={{0,24},{8,0},{16,8},{24,16},{1,25},{9,1},{17,9},{25,17},{2,26},{10... | collective-permute-start | bytes 147464 | tf_op jit(solution)/shard_map/ppermute | solution.py:44
  78.2 4.2 %collective-permute-start.10 = (bf16[64,384]{1,0:T(8,128)(2,1)S(1)}, bf16[64,384]{1,0:T(8,128)(2,1)S(1)}, u32[]{:S(2)}, u32[]{:S(2)}) collective-permute-start(bf16[64,384]{1,0:T(8,128)(2,1)S(1)} %shard_map.76.refs_0_), channel_id=1, source_target_pairs={{0,3},{1,0},{2,1},{3,2},{4,7},{5,4},{6,5},{7,6},{8,11},{9,8},{10,9... | collective-permute-start | bytes 147464 | tf_op jit(solution)/shard_map/ppermute | solution.py:44
  80.6 4.1 %collective-permute-start.9 = (bf16[64,384]{1,0:T(8,128)(2,1)S(1)}, bf16[64,384]{1,0:T(8,128)(2,1)S(1)}, u32[]{:S(2)}, u32[]{:S(2)}) collective-permute-start(bf16[64,384]{1,0:T(8,128)(2,1)S(1)} %shard_map.76.refs_0_), channel_id=1, source_target_pairs={{0,2},{1,3},{2,0},{3,1},{4,6},{5,7},{6,4},{7,5},{8,10},{9,11},{10,... | collective-permute-start | bytes 147464 | tf_op jit(solution)/shard_map/ppermute | solution.py:44
  81.1 5.0 %collective-permute-start.8 = (bf16[64,384]{1,0:T(8,128)(2,1)S(1)}, bf16[64,384]{1,0:T(8,128)(2,1)S(1)}, u32[]{:S(2)}, u32[]{:S(2)}) collective-permute-start(bf16[64,384]{1,0:T(8,128)(2,1)S(1)} %shard_map.76.refs_0_), channel_id=1, source_target_pairs={{0,1},{1,2},{2,3},{3,0},{4,5},{5,6},{6,7},{7,4},{8,9},{9,10},{10,1... | collective-permute-start | bytes 147464 | tf_op jit(solution)/shard_map/ppermute | solution.py:44
  81.4 6.1 %collective-permute-start.11 = (bf16[64,384]{1,0:T(8,128)(2,1)S(1)}, bf16[64,384]{1,0:T(8,128)(2,1)S(1)}, u32[]{:S(2)}, u32[]{:S(2)}) collective-permute-start(bf16[64,384]{1,0:T(8,128)(2,1)S(1)} %shard_map.76.refs_0_), channel_id=1, source_target_pairs={{0,4},{4,0},{1,5},{5,1},{2,6},{6,2},{3,7},{7,3},{8,12},{12,8},{9,1... | collective-permute-start | bytes 147464 | tf_op jit(solution)/shard_map/ppermute | solution.py:394
  82.3 5.2 %collective-permute-start.14 = (bf16[64,384]{1,0:T(8,128)(2,1)S(1)}, bf16[64,384]{1,0:T(8,128)(2,1)S(1)}, u32[]{:S(2)}, u32[]{:S(2)}) collective-permute-start(bf16[64,384]{1,0:T(8,128)(2,1)S(1)} %collective-permute-done.10.refs_3_), channel_id=1, source_target_pairs={{0,4},{4,0},{1,5},{5,1},{2,6},{6,2},{3,7},{7,3},{8,12},{12,8},{9,1... | collective-permute-start | bytes 147464 | tf_op jit(solution)/shard_map/ppermute | solution.py:394
  84.7 2.9 %collective-permute-start.13 = (bf16[64,384]{1,0:T(8,128)(2,1)S(1)}, bf16[64,384]{1,0:T(8,128)(2,1)S(1)}, u32[]{:S(2)}, u32[]{:S(2)}) collective-permute-start(bf16[64,384]{1,0:T(8,128)(2,1)S(1)} %collective-permute-done.9.refs_2_), channel_id=1, source_target_pairs={{0,4},{4,0},{1,5},{5,1},{2,6},{6,2},{3,7},{7,3},{8,12},{12,8},{9,1... | collective-permute-start | bytes 147464 | tf_op jit(solution)/shard_map/ppermute | solution.py:394
  86.1 1.4 %collective-permute-start.12 = (bf16[64,384]{1,0:T(8,128)(2,1)S(1)}, bf16[64,384]{1,0:T(8,128)(2,1)S(1)}, u32[]{:S(2)}, u32[]{:S(2)}) collective-permute-start(bf16[64,384]{1,0:T(8,128)(2,1)S(1)} %collective-permute-done.8.refs_1_), channel_id=1, source_target_pairs={{0,4},{4,0},{1,5},{5,1},{2,6},{6,2},{3,7},{7,3},{8,12},{12,8},{9,1... | collective-permute-start | bytes 147464 | tf_op jit(solution)/shard_map/ppermute | solution.py:394
  86.1 1.4 %collective-permute-start.15 = (f32[64,160]{1,0:T(8,128)S(1)}, f32[64,160]{1,0:T(8,128)S(1)}, u32[]{:S(2)}, u32[]{:S(2)}) collective-permute-start(f32[64,160]{1,0:T(8,128)S(1)} %get-tuple-element.39.refs_8_), channel_id=1, source_target_pairs={{0,4},{4,0},{1,5},{5,1},{2,6},{6,2},{3,7},{7,3},{8,12},{12,8},{9,1... | collective-permute-start | bytes 122888 | tf_op jit(solution)/shard_map/ppermute | solution.py:391

commit v11 on v10

--- a/solution.py
+++ b/solution.py
@@ -189,7 +189,11 @@
     out_ref[...] = left_ref[...] + right_ref[...]
 
 
-def sum_body(got_ref, keep_ref, swap_ref, out_ref):
+def stage_body(keep_ref, out_ref):
+    out_ref[...] = keep_ref[...]
+
+
+def sum_body(got_ref, out_ref):
     total = jnp.sum(got_ref[...], axis=0)
     for i in range(out_ref.shape[0]):
         out_ref[i] = total
@@ -214,11 +218,19 @@
     p = p_ref[...]
     unit = jnp.where(lane == line + 64, 1.0, 0.0)
     table = jnp.concatenate([dot(p, p, NT, high), unit[:, 64:]], axis=1)
-    for k in range(64):
-        pivot_row = table[k : k + 1, :]
-        scaled = pivot_row / pivot_row[:, k : k + 1]
-        column = jnp.where(line[:, :1] > k, table[:, k : k + 1], 0.0)
-        table = table - column * scaled
+    for k in range(0, 64, 2):
+        row_a, row_b = table[k : k + 1, :], table[k + 1 : k + 2, :]
+        col_a = jnp.broadcast_to(table[:, k : k + 1], (64, 128))
+        col_b = jnp.broadcast_to(table[:, k + 1 : k + 2], (64, 128))
+        over = 1.0 / col_a[k : k + 1, :]
+        first = col_a * over
+        cross = col_b[k : k + 1, :]
+        row_b = row_b - first[k + 1 : k + 2, :] * row_a
+        col_b = col_b - first * cross
+        second = col_b * (1.0 / col_b[k + 1 : k + 2, :])
+        first = jnp.where(line > k, first, 0.0)
+        second = jnp.where(line > k + 1, second, 0.0)
+        table = table - first * row_a - second * row_b
     pivots = jnp.sum(jnp.where(line == lane, table, 0.0), axis=1, keepdims=True)
     inverse = table[:, 64:] / jnp.sqrt(pivots)
     inverse_ref[...] = inverse
@@ -353,10 +365,11 @@
     across = [(0, 1), (1, 0)]
     p_part = call(add_body, p_shape, 0, 1 << 20)(p_keep, lax.ppermute(p_swap, "row", across))
     swap = lax.ppermute(swap, "row", across)
+    keep = call(stage_body, shape((256, 640), BF), 0, 8 << 20)(keep)
     p_part, slices = lax.optimization_barrier((p_part, slices))
     if parts == strip:
         p_got = exchange(p_part, ("dp", "col"))
-        p_got = call(sum_body, p_shape, 0, 1 << 20)(p_got, keep, swap)
+        p_got = call(sum_body, p_shape, 0, 1 << 20)(p_got)
         p_own = exchange(p_got, ("dp", "col"))
     else:
         p_own = lax.psum(p_part, ("dp", "col"))

time: 89.4 us -> 88.3 us (0.988)
  blocking collectives: 11.2 us -> 0 us
  waiting for transfers between devices: 18.9 us -> 25.8 us
  starting transfers between devices: 27.1 us -> 30.5 us
    all_to_all x1 -> x0, blocking collectives: 11.2 us -> none  [exchange(): return lax.all_to_all(chunks, axes, 0, 0, tiled=True)]
    all_to_all x3 -> x4, waiting for transfers between devices: 9.14 us -> 16 us  [exchange(): return lax.all_to_all(chunks, axes, 0, 0, tiled=True)]
    all_to_all x3 -> x4, starting transfers between devices: 15.9 us -> 19.4 us  [exchange(): return lax.all_to_all(chunks, axes, 0, 0, tiled=True)]
    pallas_call x1, Pallas kernels: 6.79 us -> 5.67 us  [on_device(): call(factor_body, (shape((64, 64), F32), shape((64, 640), F32), shape((64...]
  transfers between devices with their start and end apart: 19 -> 20, of which waited for: 9 -> 11; matrix products, arithmetic and copies ran while one was open for 0% -> 0% of each run, Pallas kernels for 25% -> 25%
where the time goes in v11:
time: 88.3 us; the launch traced here: 87.7 us
  starting transfers between devices  30.5 us (35%)
  Pallas kernels  28.7 us (33%)
  waiting for transfers between devices  25.8 us (29%)
  local copies, waits for them, and re-layouts  1.88 us (2%)
    all_to_all x4, starting transfers between devices, exchange(): return lax.all_to_all(chunks, axes, 0, 0, tiled=True)  19.4 us
    all_to_all x4, waiting for transfers between devices, exchange(): return lax.all_to_all(chunks, axes, 0, 0, tiled=True)  16 us
    ppermute x9, starting transfers between devices, shifts(): lax.ppermute(values[s], axis, [(i, (i + s) % size) for i in range(size)])  10 us
    pallas_call x1, Pallas kernels, on_device(): call(power_body, (shape((256, 640), BF), shape((256, 640), BF), p_shape,...  8.74 us
    ppermute x9, waiting for transfers between devices, shifts(): lax.ppermute(values[s], axis, [(i, (i + s) % size) for i in range(size)])  7.74 us
    pallas_call x1, Pallas kernels, on_device(): call(prepare_body, (shape((8, 160, 256), BF), shape((3, 384, 640), BF), s...  6.19 us
    pallas_call x1, Pallas kernels, on_device(): call(factor_body, (shape((64, 64), F32), shape((64, 640), F32), shape((64...  5.67 us
    pallas_call x1, Pallas kernels, on_device(): call(functools.partial(taps_body, images == 4), (shape((64, 384), BF),) *...  2.77 us
  transfers between devices with their start and end apart: 20, of which 11 were waited for; matrix products, arithmetic and copies ran while one was open for 0% of the time, Pallas kernels for 25%

profile of v11, /device:TPU:0, one launch (start us, length us, event | category | flops | bytes accessed | tf_op | source)
XLA Modules:
  0.0 87.7 jit_solution(17761201338425746170)
XLA Ops:
  0.6 2.1 %shard_map.68 = bf16[8,32,640]{2,1,0:T(8,128)(2,1)} custom-call(bf16[256,640]{1,0:T(8,128)(2,1)} %bitcast.9, bf16[256,640]{1,0:T(8,128)(2,1)} %bitcast.13), custom_call_target="tpu_custom_call" | custom-call | flops 16777216 | bytes 1048576 | tf_op jit(solution)/shard_map/pallas_call | solution.py:312
  2.7 5.2 %all-to-all-start = ((bf16[8,32,640]{2,1,0:T(8,128)(2,1)}), bf16[8,32,640]{2,1,0:T(8,128)(2,1)S(1)}, u32[]{:S(2)}, u32[]{:S(2)}) async-start(bf16[8,32,640]{2,1,0:T(8,128)(2,1)} %shard_map.68), calls=%async_computation | async-start | bytes 655360 | tf_op jit(solution)/shard_map/all_to_all | solution.py:37
  7.9 6.2 %shard_map.69 = (bf16[8,160,256]{2,1,0:T(8,128)(2,1)}, bf16[3,384,640]{2,1,0:T(8,128)(2,1)}, bf16[3,128,384]{2,1,0:T(8,128)(2,1)}, f32[256,640]{1,0:T(8,128)}) custom-call(bf16[256,640]{1,0:T(8,128)(2,1)} %bitcast.10, bf16[256,640]{1,0:T(8,128)(2,1)} %bitcast.12, f32[128,5760]{1,0:T(8,128)} %bitcast.8), custom_call_target="tpu_custom_call" | custom-call | flops 377487360 | bytes 8388608 | tf_op jit(solution)/shard_map/pallas_call | solution.py:322
  14.1 1.0 %all-to-all-done.got_hbm = bf16[8,32,640]{2,1,0:T(8,128)(2,1)S(1)} async-done(((bf16[8,32,640]{2,1,0:T(8,128)(2,1)}), bf16[8,32,640]{2,1,0:T(8,128)(2,1)S(1)}, u32[]{:S(2)}, u32[]{:S(2)}) %all-to-all-start) | async-done | bytes 327712 | tf_op jit(solution)/shard_map/all_to_all | solution.py:37
  15.1 3.5 %all-to-all-start.1 = ((bf16[8,160,256]{2,1,0:T(8,128)(2,1)}), bf16[8,160,256]{2,1,0:T(8,128)(2,1)S(1)}, u32[]{:S(2)}, u32[]{:S(2)}) async-start(bf16[8,160,256]{2,1,0:T(8,128)(2,1)} %get-tuple-element.27), calls=%async_computation.1 | async-start | bytes 1310720 | tf_op jit(solution)/shard_map/all_to_all | solution.py:37
  18.7 8.7 %shard_map.70 = (bf16[256,640]{1,0:T(8,128)(2,1)}, bf16[256,640]{1,0:T(8,128)(2,1)}, f32[16,4,640]{2,1,0:T(4,128)}, f32[16,4,640]{2,1,0:T(4,128)}) custom-call(bf16[256,640]{1,0:T(8,128)(2,1)} %bitcast.11, bf16[256,640]{1,0:T(8,128)(2,1)} %bitcast.14, bf16[8,32,640]{2,1,0:T(8,128)(2,1)} %copy-done.2, f32[256,640]{1,0:T(8,128)} %get-tuple-element.22.slope_hbm, ...), custom_call_target="tpu_custom_call" | custom-call | flops 3244032000 | bytes 12582912 | tf_op jit(solution)/shard_map/pallas_call | solution.py:343
  27.4 0.5 collective-permute-start
  27.9 1.2 %collective-permute-done.right_ref = f32[16,4,640]{2,1,0:T(4,128)S(1)} collective-permute-done((f32[16,4,640]{2,1,0:T(4,128)}, f32[16,4,640]{2,1,0:T(4,128)S(1)}, u32[]{:S(2)}, u32[]{:S(2)}) %collective-permute-start) | collective-permute-done | bytes 163872 | tf_op jit(solution)/shard_map/ppermute | solution.py:366
  29.2 0.9 %copy-done.1 = f32[16,4,640]{2,1,0:T(4,128)S(1)} copy-done((f32[16,4,640]{2,1,0:T(4,128)S(1)}, f32[16,4,640]{2,1,0:T(4,128)}, u32[]{:S(2)}) %copy-start.1) | copy-done | bytes 163864
  30.1 0.7 shard_map.71
  30.8 0.0 all-to-all-done.1.refs_4_
  30.8 7.2 %all-to-all-start.2 = ((f32[16,4,640]{2,1,0:T(4,128)}), f32[16,4,640]{2,1,0:T(4,128)S(1)}, u32[]{:S(2)}, u32[]{:S(2)}) async-start(f32[16,4,640]{2,1,0:T(4,128)} %shard_map.71), calls=%async_computation.2 | async-start | bytes 327680 | tf_op jit(solution)/shard_map/all_to_all | solution.py:37
  38.0 0.1 collective-permute-start.1
  38.0 8.1 %all-to-all-done.2.got_ref = f32[16,4,640]{2,1,0:T(4,128)S(1)} async-done(((f32[16,4,640]{2,1,0:T(4,128)}), f32[16,4,640]{2,1,0:T(4,128)S(1)}, u32[]{:S(2)}, u32[]{:S(2)}) %all-to-all-start.2) | async-done | bytes 163872 | tf_op jit(solution)/shard_map/all_to_all | solution.py:37
  46.1 0.7 shard_map.72
  46.8 3.5 %all-to-all-start.3 = ((f32[16,4,640]{2,1,0:T(4,128)}), f32[16,4,640]{2,1,0:T(4,128)S(1)}, u32[]{:S(2)}, u32[]{:S(2)}) async-start(f32[16,4,640]{2,1,0:T(4,128)} %shard_map.72), calls=%async_computation.3 | async-start | bytes 327680 | tf_op jit(solution)/shard_map/all_to_all | solution.py:37
  50.3 1.0 %copy-done = bf16[256,640]{1,0:T(8,128)(2,1)S(1)} copy-done((bf16[256,640]{1,0:T(8,128)(2,1)S(1)}, bf16[256,640]{1,0:T(8,128)(2,1)}, u32[]{:S(2)}) %copy-start) | copy-done | bytes 327704
  51.3 0.0 collective-permute-done.1.swap_ref
  51.4 6.9 %all-to-all-done.3.got_ref = f32[16,4,640]{2,1,0:T(4,128)S(1)} async-done(((f32[16,4,640]{2,1,0:T(4,128)}), f32[16,4,640]{2,1,0:T(4,128)S(1)}, u32[]{:S(2)}, u32[]{:S(2)}) %all-to-all-start.3) | async-done | bytes 163872 | tf_op jit(solution)/shard_map/all_to_all | solution.py:37
  58.2 0.4 shard_map.74
  58.7 0.8 collective-permute-start.4
  59.5 1.9 %collective-permute-start.3 = (bf16[512,128]{1,0:T(8,128)(2,1)S(1)}, bf16[512,128]{1,0:T(8,128)(2,1)S(1)}, u32[]{:S(2)}, u32[]{:S(2)}) collective-permute-start(bf16[512,128]{1,0:T(8,128)(2,1)S(1)} %get-tuple-element.31.refs_0_), channel_id=1, source_target_pairs={{0,2},{1,3},{2,0},{3,1},{4,6},{5,7},{6,4},{7,5},{8,10},{9,11},{10,... | collective-permute-start | bytes 393224 | tf_op jit(solution)/shard_map/ppermute | solution.py:44
  61.4 0.1 collective-permute-start.2
  61.5 5.7 %shard_map.75 = (f32[64,64]{1,0:T(8,128)S(1)}, f32[64,640]{1,0:T(8,128)}, f32[64,160]{1,0:T(8,128)S(1)}) custom-call(f32[64,640]{1,0:T(8,128)S(1)} %get-tuple-element.33.p_ref), custom_call_target="tpu_custom_call" | custom-call | flops 1073741824 | bytes 1048576 | tf_op jit(solution)/shard_map/pallas_call | solution.py:384
  67.2 0.0 collective-permute-done.4.refs_3_
  67.2 0.0 collective-permute-done.3.refs_2_
  67.2 0.1 collective-permute-done.2.refs_1_
  67.2 2.8 %shard_map.76 = (bf16[64,384]{1,0:T(8,128)(2,1)S(1)}, bf16[64,384]{1,0:T(8,128)(2,1)S(1)}, bf16[64,384]{1,0:T(8,128)(2,1)S(1)}, bf16[64,384]{1,0:T(8,128)(2,1)S(1)}) custom-call(bf16[512,128]{1,0:T(8,128)(2,1)S(1)} %get-tuple-element.31.refs_0_, bf16[512,128]{1,0:T(8,128)(2,1)S(1)} %collective-permute-done.2.refs_1_, ...), custom_call_target="tpu_custom_call" | custom-call | flops 754974720 | bytes 2097152 | tf_op jit(solution)/shard_map/pallas_call | solution.py:391
  70.0 0.8 collective-permute-start.5
  70.9 1.2 %collective-permute-start.6 = (bf16[64,384]{1,0:T(8,128)(2,1)S(1)}, bf16[64,384]{1,0:T(8,128)(2,1)S(1)}, u32[]{:S(2)}, u32[]{:S(2)}) collective-permute-start(bf16[64,384]{1,0:T(8,128)(2,1)S(1)} %get-tuple-element.37), channel_id=1, source_target_pairs={{0,16},{8,24},{16,0},{24,8},{1,17},{9,25},{17,1},{25,9},{2,18},{10... | collective-permute-start | bytes 147464 | tf_op jit(solution)/shard_map/ppermute | solution.py:44
  72.1 1.9 %collective-permute-start.7 = (bf16[64,384]{1,0:T(8,128)(2,1)S(1)}, bf16[64,384]{1,0:T(8,128)(2,1)S(1)}, u32[]{:S(2)}, u32[]{:S(2)}) collective-permute-start(bf16[64,384]{1,0:T(8,128)(2,1)S(1)} %get-tuple-element.38), channel_id=1, source_target_pairs={{0,24},{8,0},{16,8},{24,16},{1,25},{9,1},{17,9},{25,17},{2,26},{10... | collective-permute-start | bytes 147464 | tf_op jit(solution)/shard_map/ppermute | solution.py:44
  74.0 2.1 %collective-permute-done.5.b_ref = bf16[64,384]{1,0:T(8,128)(2,1)S(1)} collective-permute-done((bf16[64,384]{1,0:T(8,128)(2,1)S(1)}, bf16[64,384]{1,0:T(8,128)(2,1)S(1)}, u32[]{:S(2)}, u32[]{:S(2)}) %collective-permute-start.5) | collective-permute-done | bytes 49184 | tf_op jit(solution)/shard_map/ppermute | solution.py:44
  76.1 0.8 collective-permute-done.6.c_ref
  76.9 2.4 %collective-permute-start.10 = (bf16[64,384]{1,0:T(8,128)(2,1)S(1)}, bf16[64,384]{1,0:T(8,128)(2,1)S(1)}, u32[]{:S(2)}, u32[]{:S(2)}) collective-permute-start(bf16[64,384]{1,0:T(8,128)(2,1)S(1)} %shard_map.77.refs_0_), channel_id=1, source_target_pairs={{0,3},{1,0},{2,1},{3,2},{4,7},{5,4},{6,5},{7,6},{8,11},{9,8},{10,9... | collective-permute-start | bytes 147464 | tf_op jit(solution)/shard_map/ppermute | solution.py:44
  79.4 0.6 collective-permute-start.9
  79.9 0.3 collective-permute-start.8
  80.2 0.0 collective-permute-start.11
  80.2 0.9 %collective-permute-done.10.refs_3_ = bf16[64,384]{1,0:T(8,128)(2,1)S(1)} collective-permute-done((bf16[64,384]{1,0:T(8,128)(2,1)S(1)}, bf16[64,384]{1,0:T(8,128)(2,1)S(1)}, u32[]{:S(2)}, u32[]{:S(2)}) %collective-permute-start.10) | collective-permute-done | bytes 49184 | tf_op jit(solution)/shard_map/ppermute | solution.py:44
  81.1 2.3 %collective-permute-done.9.refs_2_ = bf16[64,384]{1,0:T(8,128)(2,1)S(1)} collective-permute-done((bf16[64,384]{1,0:T(8,128)(2,1)S(1)}, bf16[64,384]{1,0:T(8,128)(2,1)S(1)}, u32[]{:S(2)}, u32[]{:S(2)}) %collective-permute-start.9) | collective-permute-done | bytes 49184 | tf_op jit(solution)/shard_map/ppermute | solution.py:44
  83.5 0.0 collective-permute-start.13
  83.5 1.5 %collective-permute-done.8.refs_1_ = bf16[64,384]{1,0:T(8,128)(2,1)S(1)} collective-permute-done((bf16[64,384]{1,0:T(8,128)(2,1)S(1)}, bf16[64,384]{1,0:T(8,128)(2,1)S(1)}, u32[]{:S(2)}, u32[]{:S(2)}) %collective-permute-start.8) | collective-permute-done | bytes 49184 | tf_op jit(solution)/shard_map/ppermute | solution.py:44
  84.9 0.0 collective-permute-start.12
  84.9 0.5 collective-permute-start.15
  85.4 0.9 %collective-permute-done.15.refs_9_ = f32[64,160]{1,0:T(8,128)S(1)} collective-permute-done((f32[64,160]{1,0:T(8,128)S(1)}, f32[64,160]{1,0:T(8,128)S(1)}, u32[]{:S(2)}, u32[]{:S(2)}) %collective-permute-start.15) | collective-permute-done | bytes 40992 | tf_op jit(solution)/shard_map/ppermute | solution.py:404
  86.3 0.0 collective-permute-done.11.refs_4_
  86.3 0.0 collective-permute-done.14.refs_7_
  86.3 0.0 collective-permute-done.13.refs_6_
  86.4 1.4 %shard_map.78 = (f32[2,64,160]{2,1,0:T(8,128)}, f32[2,64,1440]{2,1,0:T(8,128)}) custom-call(bf16[64,384]{1,0:T(8,128)(2,1)S(1)} %shard_map.77.refs_0_, bf16[64,384]{1,0:T(8,128)(2,1)S(1)} %collective-permute-done.8.refs_1_, bf16[64,384]{1,0:T(8,128)(2,1)S(1)} %collective-permute-done.9.refs_2_, bf16[64,384]{1,0:T(8,128)(2,1)S(1)} %collective-permute-done.10.refs_3_, ...), custom_call_target="tpu_custom_call" | custom-call | bytes 1048576 | tf_op jit(solution)/shard_map/pallas_call | solution.py:408
  (9 shorter events, 0.1 us)
Async XLA Ops:
  2.7 12.4 %all-to-all-start = ((bf16[8,32,640]{2,1,0:T(8,128)(2,1)}), bf16[8,32,640]{2,1,0:T(8,128)(2,1)S(1)}, u32[]{:S(2)}, u32[]{:S(2)}) async-start(bf16[8,32,640]{2,1,0:T(8,128)(2,1)} %shard_map.68), calls=%async_computation | async-start | bytes 655360 | tf_op jit(solution)/shard_map/all_to_all | solution.py:37
  15.1 3.6 %copy-start.2 = (bf16[8,32,640]{2,1,0:T(8,128)(2,1)}, bf16[8,32,640]{2,1,0:T(8,128)(2,1)S(1)}, u32[]{:S(2)}) copy-start(bf16[8,32,640]{2,1,0:T(8,128)(2,1)S(1)} %all-to-all-done.got_hbm) | copy-start | bytes 983044
  15.1 15.6 %all-to-all-start.1 = ((bf16[8,160,256]{2,1,0:T(8,128)(2,1)}), bf16[8,160,256]{2,1,0:T(8,128)(2,1)S(1)}, u32[]{:S(2)}, u32[]{:S(2)}) async-start(bf16[8,160,256]{2,1,0:T(8,128)(2,1)} %get-tuple-element.27), calls=%async_computation.1 | async-start | bytes 1310720 | tf_op jit(solution)/shard_map/all_to_all | solution.py:37
  27.4 1.7 %collective-permute-start = (f32[16,4,640]{2,1,0:T(4,128)}, f32[16,4,640]{2,1,0:T(4,128)S(1)}, u32[]{:S(2)}, u32[]{:S(2)}) collective-permute-start(f32[16,4,640]{2,1,0:T(4,128)} %get-tuple-element.26), channel_id=1, source_target_pairs={{0,4},{4,0},{1,5},{5,1},{2,6},{6,2},{3,7},{7,3},{8,12},{12,8},{9,1... | collective-permute-start | bytes 491528 | tf_op jit(solution)/shard_map/ppermute | solution.py:366
  29.2 0.9 %copy-start.1 = (f32[16,4,640]{2,1,0:T(4,128)S(1)}, f32[16,4,640]{2,1,0:T(4,128)}, u32[]{:S(2)}) copy-start(f32[16,4,640]{2,1,0:T(4,128)} %get-tuple-element.25.left_ref) | copy-start | bytes 491524
  30.8 15.3 %all-to-all-start.2 = ((f32[16,4,640]{2,1,0:T(4,128)}), f32[16,4,640]{2,1,0:T(4,128)S(1)}, u32[]{:S(2)}, u32[]{:S(2)}) async-start(f32[16,4,640]{2,1,0:T(4,128)} %shard_map.71), calls=%async_computation.2 | async-start | bytes 327680 | tf_op jit(solution)/shard_map/all_to_all | solution.py:37
  38.0 13.4 %collective-permute-start.1 = (bf16[256,640]{1,0:T(8,128)(2,1)}, bf16[256,640]{1,0:T(8,128)(2,1)S(1)}, u32[]{:S(2)}, u32[]{:S(2)}) collective-permute-start(bf16[256,640]{1,0:T(8,128)(2,1)} %get-tuple-element.30), channel_id=1, source_target_pairs={{0,4},{4,0},{1,5},{5,1},{2,6},{6,2},{3,7},{7,3},{8,12},{12,8},{9,1... | collective-permute-start | bytes 983048 | tf_op jit(solution)/shard_map/ppermute | solution.py:367
  46.8 11.4 %all-to-all-start.3 = ((f32[16,4,640]{2,1,0:T(4,128)}), f32[16,4,640]{2,1,0:T(4,128)S(1)}, u32[]{:S(2)}, u32[]{:S(2)}) async-start(f32[16,4,640]{2,1,0:T(4,128)} %shard_map.72), calls=%async_computation.3 | async-start | bytes 327680 | tf_op jit(solution)/shard_map/all_to_all | solution.py:37
  50.3 1.0 %copy-start = (bf16[256,640]{1,0:T(8,128)(2,1)S(1)}, bf16[256,640]{1,0:T(8,128)(2,1)}, u32[]{:S(2)}) copy-start(bf16[256,640]{1,0:T(8,128)(2,1)} %get-tuple-element.29.keep_ref) | copy-start | bytes 983044
  58.7 8.5 %collective-permute-start.4 = (bf16[512,128]{1,0:T(8,128)(2,1)S(1)}, bf16[512,128]{1,0:T(8,128)(2,1)S(1)}, u32[]{:S(2)}, u32[]{:S(2)}) collective-permute-start(bf16[512,128]{1,0:T(8,128)(2,1)S(1)} %get-tuple-element.31.refs_0_), channel_id=1, source_target_pairs={{0,3},{1,0},{2,1},{3,2},{4,7},{5,4},{6,5},{7,6},{8,11},{9,8},{10,9... | collective-permute-start | bytes 393224 | tf_op jit(solution)/shard_map/ppermute | solution.py:44
  59.5 7.7 %collective-permute-start.3 = (bf16[512,128]{1,0:T(8,128)(2,1)S(1)}, bf16[512,128]{1,0:T(8,128)(2,1)S(1)}, u32[]{:S(2)}, u32[]{:S(2)}) collective-permute-start(bf16[512,128]{1,0:T(8,128)(2,1)S(1)} %get-tuple-element.31.refs_0_), channel_id=1, source_target_pairs={{0,2},{1,3},{2,0},{3,1},{4,6},{5,7},{6,4},{7,5},{8,10},{9,11},{10,... | collective-permute-start | bytes 393224 | tf_op jit(solution)/shard_map/ppermute | solution.py:44
  61.4 5.9 %collective-permute-start.2 = (bf16[512,128]{1,0:T(8,128)(2,1)S(1)}, bf16[512,128]{1,0:T(8,128)(2,1)S(1)}, u32[]{:S(2)}, u32[]{:S(2)}) collective-permute-start(bf16[512,128]{1,0:T(8,128)(2,1)S(1)} %get-tuple-element.31.refs_0_), channel_id=1, source_target_pairs={{0,1},{1,2},{2,3},{3,0},{4,5},{5,6},{6,7},{7,4},{8,9},{9,10},{10,1... | collective-permute-start | bytes 393224 | tf_op jit(solution)/shard_map/ppermute | solution.py:44
  70.0 6.0 %collective-permute-start.5 = (bf16[64,384]{1,0:T(8,128)(2,1)S(1)}, bf16[64,384]{1,0:T(8,128)(2,1)S(1)}, u32[]{:S(2)}, u32[]{:S(2)}) collective-permute-start(bf16[64,384]{1,0:T(8,128)(2,1)S(1)} %get-tuple-element.36), channel_id=1, source_target_pairs={{0,8},{8,16},{16,24},{24,0},{1,9},{9,17},{17,25},{25,1},{2,10},{10... | collective-permute-start | bytes 147464 | tf_op jit(solution)/shard_map/ppermute | solution.py:44
  70.9 6.0 %collective-permute-start.6 = (bf16[64,384]{1,0:T(8,128)(2,1)S(1)}, bf16[64,384]{1,0:T(8,128)(2,1)S(1)}, u32[]{:S(2)}, u32[]{:S(2)}) collective-permute-start(bf16[64,384]{1,0:T(8,128)(2,1)S(1)} %get-tuple-element.37), channel_id=1, source_target_pairs={{0,16},{8,24},{16,0},{24,8},{1,17},{9,25},{17,1},{25,9},{2,18},{10... | collective-permute-start | bytes 147464 | tf_op jit(solution)/shard_map/ppermute | solution.py:44
  72.1 4.8 %collective-permute-start.7 = (bf16[64,384]{1,0:T(8,128)(2,1)S(1)}, bf16[64,384]{1,0:T(8,128)(2,1)S(1)}, u32[]{:S(2)}, u32[]{:S(2)}) collective-permute-start(bf16[64,384]{1,0:T(8,128)(2,1)S(1)} %get-tuple-element.38), channel_id=1, source_target_pairs={{0,24},{8,0},{16,8},{24,16},{1,25},{9,1},{17,9},{25,17},{2,26},{10... | collective-permute-start | bytes 147464 | tf_op jit(solution)/shard_map/ppermute | solution.py:44
  76.9 4.2 %collective-permute-start.10 = (bf16[64,384]{1,0:T(8,128)(2,1)S(1)}, bf16[64,384]{1,0:T(8,128)(2,1)S(1)}, u32[]{:S(2)}, u32[]{:S(2)}) collective-permute-start(bf16[64,384]{1,0:T(8,128)(2,1)S(1)} %shard_map.77.refs_0_), channel_id=1, source_target_pairs={{0,3},{1,0},{2,1},{3,2},{4,7},{5,4},{6,5},{7,6},{8,11},{9,8},{10,9... | collective-permute-start | bytes 147464 | tf_op jit(solution)/shard_map/ppermute | solution.py:44
  79.4 4.1 %collective-permute-start.9 = (bf16[64,384]{1,0:T(8,128)(2,1)S(1)}, bf16[64,384]{1,0:T(8,128)(2,1)S(1)}, u32[]{:S(2)}, u32[]{:S(2)}) collective-permute-start(bf16[64,384]{1,0:T(8,128)(2,1)S(1)} %shard_map.77.refs_0_), channel_id=1, source_target_pairs={{0,2},{1,3},{2,0},{3,1},{4,6},{5,7},{6,4},{7,5},{8,10},{9,11},{10,... | collective-permute-start | bytes 147464 | tf_op jit(solution)/shard_map/ppermute | solution.py:44
  79.9 5.0 %collective-permute-start.8 = (bf16[64,384]{1,0:T(8,128)(2,1)S(1)}, bf16[64,384]{1,0:T(8,128)(2,1)S(1)}, u32[]{:S(2)}, u32[]{:S(2)}) collective-permute-start(bf16[64,384]{1,0:T(8,128)(2,1)S(1)} %shard_map.77.refs_0_), channel_id=1, source_target_pairs={{0,1},{1,2},{2,3},{3,0},{4,5},{5,6},{6,7},{7,4},{8,9},{9,10},{10,1... | collective-permute-start | bytes 147464 | tf_op jit(solution)/shard_map/ppermute | solution.py:44
  80.2 6.1 %collective-permute-start.11 = (bf16[64,384]{1,0:T(8,128)(2,1)S(1)}, bf16[64,384]{1,0:T(8,128)(2,1)S(1)}, u32[]{:S(2)}, u32[]{:S(2)}) collective-permute-start(bf16[64,384]{1,0:T(8,128)(2,1)S(1)} %shard_map.77.refs_0_), channel_id=1, source_target_pairs={{0,4},{4,0},{1,5},{5,1},{2,6},{6,2},{3,7},{7,3},{8,12},{12,8},{9,1... | collective-permute-start | bytes 147464 | tf_op jit(solution)/shard_map/ppermute | solution.py:407
  81.1 5.2 %collective-permute-start.14 = (bf16[64,384]{1,0:T(8,128)(2,1)S(1)}, bf16[64,384]{1,0:T(8,128)(2,1)S(1)}, u32[]{:S(2)}, u32[]{:S(2)}) collective-permute-start(bf16[64,384]{1,0:T(8,128)(2,1)S(1)} %collective-permute-done.10.refs_3_), channel_id=1, source_target_pairs={{0,4},{4,0},{1,5},{5,1},{2,6},{6,2},{3,7},{7,3},{8,12},{12,8},{9,1... | collective-permute-start | bytes 147464 | tf_op jit(solution)/shard_map/ppermute | solution.py:407
  83.5 2.9 %collective-permute-start.13 = (bf16[64,384]{1,0:T(8,128)(2,1)S(1)}, bf16[64,384]{1,0:T(8,128)(2,1)S(1)}, u32[]{:S(2)}, u32[]{:S(2)}) collective-permute-start(bf16[64,384]{1,0:T(8,128)(2,1)S(1)} %collective-permute-done.9.refs_2_), channel_id=1, source_target_pairs={{0,4},{4,0},{1,5},{5,1},{2,6},{6,2},{3,7},{7,3},{8,12},{12,8},{9,1... | collective-permute-start | bytes 147464 | tf_op jit(solution)/shard_map/ppermute | solution.py:407
  84.9 1.4 %collective-permute-start.12 = (bf16[64,384]{1,0:T(8,128)(2,1)S(1)}, bf16[64,384]{1,0:T(8,128)(2,1)S(1)}, u32[]{:S(2)}, u32[]{:S(2)}) collective-permute-start(bf16[64,384]{1,0:T(8,128)(2,1)S(1)} %collective-permute-done.8.refs_1_), channel_id=1, source_target_pairs={{0,4},{4,0},{1,5},{5,1},{2,6},{6,2},{3,7},{7,3},{8,12},{12,8},{9,1... | collective-permute-start | bytes 147464 | tf_op jit(solution)/shard_map/ppermute | solution.py:407
  84.9 1.4 %collective-permute-start.15 = (f32[64,160]{1,0:T(8,128)S(1)}, f32[64,160]{1,0:T(8,128)S(1)}, u32[]{:S(2)}, u32[]{:S(2)}) collective-permute-start(f32[64,160]{1,0:T(8,128)S(1)} %get-tuple-element.39.refs_8_), channel_id=1, source_target_pairs={{0,4},{4,0},{1,5},{5,1},{2,6},{6,2},{3,7},{7,3},{8,12},{12,8},{9,1... | collective-permute-start | bytes 122888 | tf_op jit(solution)/shard_map/ppermute | solution.py:404

commit v12 on v11

--- a/solution.py
+++ b/solution.py
@@ -185,10 +185,6 @@
             ref[i] = value[i * each : (i + 1) * each]
 
 
-def add_body(left_ref, right_ref, out_ref):
-    out_ref[...] = left_ref[...] + right_ref[...]
-
-
 def stage_body(keep_ref, out_ref):
     out_ref[...] = keep_ref[...]
 
@@ -363,7 +359,7 @@
     )(x, g, got, slope, q_one, y_two, conv_weight)
 
     across = [(0, 1), (1, 0)]
-    p_part = call(add_body, p_shape, 0, 1 << 20)(p_keep, lax.ppermute(p_swap, "row", across))
+    p_part = p_keep + lax.ppermute(p_swap, "row", across)
     swap = lax.ppermute(swap, "row", across)
     keep = call(stage_body, shape((256, 640), BF), 0, 8 << 20)(keep)
     p_part, slices = lax.optimization_barrier((p_part, slices))

time: 88.3 us -> 88.3 us (level)
  other arithmetic: 0 us -> 1.62 us
  local copies, waits for them, and re-layouts: 1.88 us -> 0.97 us
    add x0 -> x1, other arithmetic: none -> 1.62 us  [on_device(): p_part = p_keep + lax.ppermute(p_swap, 'row', across)]
    unnamed x6 -> x4, local copies, waits for them, and re-layouts: 1.88 us -> 0.97 us
  transfers between devices with their start and end apart: 20 -> 20, of which waited for: 11 -> 11; matrix products, arithmetic and copies ran while one was open for 0% -> 2% of each run, Pallas kernels for 25% -> 24%
where the time goes in v12:
time: 88.3 us; the launch traced here: 87.8 us
  starting transfers between devices  30.5 us (35%)
  Pallas kernels  28 us (32%)
  waiting for transfers between devices  25.9 us (29%)
  other arithmetic  1.62 us (2%)
  local copies, waits for them, and re-layouts  0.97 us (1%)
    all_to_all x4, starting transfers between devices, exchange(): return lax.all_to_all(chunks, axes, 0, 0, tiled=True)  19.4 us
    all_to_all x4, waiting for transfers between devices, exchange(): return lax.all_to_all(chunks, axes, 0, 0, tiled=True)  16 us
    ppermute x9, starting transfers between devices, shifts(): lax.ppermute(values[s], axis, [(i, (i + s) % size) for i in range(size)])  10 us
    pallas_call x1, Pallas kernels, on_device(): call(power_body, (shape((256, 640), BF), shape((256, 640), BF), p_shape,...  8.76 us
    ppermute x9, waiting for transfers between devices, shifts(): lax.ppermute(values[s], axis, [(i, (i + s) % size) for i in range(size)])  7.74 us
    pallas_call x1, Pallas kernels, on_device(): call(prepare_body, (shape((8, 160, 256), BF), shape((3, 384, 640), BF), s...  6.2 us
    pallas_call x1, Pallas kernels, on_device(): call(factor_body, (shape((64, 64), F32), shape((64, 640), F32), shape((64...  5.67 us
    pallas_call x1, Pallas kernels, on_device(): call(functools.partial(taps_body, images == 4), (shape((64, 384), BF),) *...  2.77 us
  transfers between devices with their start and end apart: 20, of which 11 were waited for; matrix products, arithmetic and copies ran while one was open for 2% of the time, Pallas kernels for 24%

profile of v12, /device:TPU:0, one launch (start us, length us, event | category | flops | bytes accessed | tf_op | source)
XLA Modules:
  0.0 87.8 jit_solution(5117520397392957080)
XLA Ops:
  0.6 2.1 %shard_map.68 = bf16[8,32,640]{2,1,0:T(8,128)(2,1)} custom-call(bf16[256,640]{1,0:T(8,128)(2,1)} %bitcast.9, bf16[256,640]{1,0:T(8,128)(2,1)} %bitcast.13), custom_call_target="tpu_custom_call" | custom-call | flops 16777216 | bytes 1048576 | tf_op jit(solution)/shard_map/pallas_call | solution.py:308
  2.7 5.2 %all-to-all-start = ((bf16[8,32,640]{2,1,0:T(8,128)(2,1)}), bf16[8,32,640]{2,1,0:T(8,128)(2,1)S(1)}, u32[]{:S(2)}, u32[]{:S(2)}) async-start(bf16[8,32,640]{2,1,0:T(8,128)(2,1)} %shard_map.68), calls=%async_computation | async-start | bytes 655360 | tf_op jit(solution)/shard_map/all_to_all | solution.py:37
  7.9 6.2 %shard_map.69 = (bf16[8,160,256]{2,1,0:T(8,128)(2,1)}, bf16[3,384,640]{2,1,0:T(8,128)(2,1)}, bf16[3,128,384]{2,1,0:T(8,128)(2,1)}, f32[256,640]{1,0:T(8,128)}) custom-call(bf16[256,640]{1,0:T(8,128)(2,1)} %bitcast.10, bf16[256,640]{1,0:T(8,128)(2,1)} %bitcast.12, f32[128,5760]{1,0:T(8,128)} %bitcast.8), custom_call_target="tpu_custom_call" | custom-call | flops 377487360 | bytes 8388608 | tf_op jit(solution)/shard_map/pallas_call | solution.py:318
  14.1 1.0 %all-to-all-done.got_hbm = bf16[8,32,640]{2,1,0:T(8,128)(2,1)S(1)} async-done(((bf16[8,32,640]{2,1,0:T(8,128)(2,1)}), bf16[8,32,640]{2,1,0:T(8,128)(2,1)S(1)}, u32[]{:S(2)}, u32[]{:S(2)}) %all-to-all-start) | async-done | bytes 327712 | tf_op jit(solution)/shard_map/all_to_all | solution.py:37
  15.1 3.5 %all-to-all-start.1 = ((bf16[8,160,256]{2,1,0:T(8,128)(2,1)}), bf16[8,160,256]{2,1,0:T(8,128)(2,1)S(1)}, u32[]{:S(2)}, u32[]{:S(2)}) async-start(bf16[8,160,256]{2,1,0:T(8,128)(2,1)} %get-tuple-element.27), calls=%async_computation.1 | async-start | bytes 1310720 | tf_op jit(solution)/shard_map/all_to_all | solution.py:37
  18.7 8.8 %shard_map.70 = (bf16[256,640]{1,0:T(8,128)(2,1)}, bf16[256,640]{1,0:T(8,128)(2,1)}, f32[16,4,640]{2,1,0:T(4,128)}, f32[16,4,640]{2,1,0:T(4,128)}) custom-call(bf16[256,640]{1,0:T(8,128)(2,1)} %bitcast.11, bf16[256,640]{1,0:T(8,128)(2,1)} %bitcast.14, bf16[8,32,640]{2,1,0:T(8,128)(2,1)} %copy-done.1, f32[256,640]{1,0:T(8,128)} %get-tuple-element.22.slope_hbm, ...), custom_call_target="tpu_custom_call" | custom-call | flops 3244032000 | bytes 12582912 | tf_op jit(solution)/shard_map/pallas_call | solution.py:339
  27.4 0.5 collective-permute-start
  27.9 1.2 %collective-permute-done = f32[16,4,640]{2,1,0:T(4,128)S(1)} collective-permute-done((f32[16,4,640]{2,1,0:T(4,128)}, f32[16,4,640]{2,1,0:T(4,128)S(1)}, u32[]{:S(2)}, u32[]{:S(2)}) %collective-permute-start) | collective-permute-done | bytes 163872 | tf_op jit(solution)/shard_map/ppermute | solution.py:362
  29.2 1.6 %add.3 = f32[16,4,640]{2,1,0:T(4,128)} add(f32[16,4,640]{2,1,0:T(4,128)} %get-tuple-element.25, f32[16,4,640]{2,1,0:T(4,128)S(1)} %collective-permute-done) | non-fusion elementwise | flops 40960 | bytes 491520 | tf_op jit(solution)/shard_map/add | solution.py:362
  30.8 0.0 all-to-all-done.1.refs_4_
  30.8 7.2 %all-to-all-start.2 = ((f32[16,4,640]{2,1,0:T(4,128)}), f32[16,4,640]{2,1,0:T(4,128)S(1)}, u32[]{:S(2)}, u32[]{:S(2)}) async-start(f32[16,4,640]{2,1,0:T(4,128)} %add.3), calls=%async_computation.2 | async-start | bytes 327680 | tf_op jit(solution)/shard_map/all_to_all | solution.py:37
  38.0 0.1 collective-permute-start.1
  38.1 8.1 %all-to-all-done.2.got_ref = f32[16,4,640]{2,1,0:T(4,128)S(1)} async-done(((f32[16,4,640]{2,1,0:T(4,128)}), f32[16,4,640]{2,1,0:T(4,128)S(1)}, u32[]{:S(2)}, u32[]{:S(2)}) %all-to-all-start.2) | async-done | bytes 163872 | tf_op jit(solution)/shard_map/all_to_all | solution.py:37
  46.1 0.7 shard_map.71
  46.8 3.5 %all-to-all-start.3 = ((f32[16,4,640]{2,1,0:T(4,128)}), f32[16,4,640]{2,1,0:T(4,128)S(1)}, u32[]{:S(2)}, u32[]{:S(2)}) async-start(f32[16,4,640]{2,1,0:T(4,128)} %shard_map.71), calls=%async_computation.3 | async-start | bytes 327680 | tf_op jit(solution)/shard_map/all_to_all | solution.py:37
  50.4 1.0 %copy-done = bf16[256,640]{1,0:T(8,128)(2,1)S(1)} copy-done((bf16[256,640]{1,0:T(8,128)(2,1)S(1)}, bf16[256,640]{1,0:T(8,128)(2,1)}, u32[]{:S(2)}) %copy-start) | copy-done | bytes 327704
  51.4 0.0 collective-permute-done.1.swap_ref
  51.4 6.9 %all-to-all-done.3.got_ref = f32[16,4,640]{2,1,0:T(4,128)S(1)} async-done(((f32[16,4,640]{2,1,0:T(4,128)}), f32[16,4,640]{2,1,0:T(4,128)S(1)}, u32[]{:S(2)}, u32[]{:S(2)}) %all-to-all-start.3) | async-done | bytes 163872 | tf_op jit(solution)/shard_map/all_to_all | solution.py:37
  58.3 0.4 shard_map.73
  58.7 0.8 collective-permute-start.4
  59.5 1.9 %collective-permute-start.3 = (bf16[512,128]{1,0:T(8,128)(2,1)S(1)}, bf16[512,128]{1,0:T(8,128)(2,1)S(1)}, u32[]{:S(2)}, u32[]{:S(2)}) collective-permute-start(bf16[512,128]{1,0:T(8,128)(2,1)S(1)} %get-tuple-element.31.refs_0_), channel_id=1, source_target_pairs={{0,2},{1,3},{2,0},{3,1},{4,6},{5,7},{6,4},{7,5},{8,10},{9,11},{10,... | collective-permute-start | bytes 393224 | tf_op jit(solution)/shard_map/ppermute | solution.py:44
  61.4 0.1 collective-permute-start.2
  61.5 5.7 %shard_map.74 = (f32[64,64]{1,0:T(8,128)S(1)}, f32[64,640]{1,0:T(8,128)}, f32[64,160]{1,0:T(8,128)S(1)}) custom-call(f32[64,640]{1,0:T(8,128)S(1)} %get-tuple-element.33.p_ref), custom_call_target="tpu_custom_call" | custom-call | flops 1073741824 | bytes 1048576 | tf_op jit(solution)/shard_map/pallas_call | solution.py:380
  67.2 0.0 collective-permute-done.4.refs_3_
  67.2 0.0 collective-permute-done.3.refs_2_
  67.2 0.1 collective-permute-done.2.refs_1_
  67.3 2.8 %shard_map.75 = (bf16[64,384]{1,0:T(8,128)(2,1)S(1)}, bf16[64,384]{1,0:T(8,128)(2,1)S(1)}, bf16[64,384]{1,0:T(8,128)(2,1)S(1)}, bf16[64,384]{1,0:T(8,128)(2,1)S(1)}) custom-call(bf16[512,128]{1,0:T(8,128)(2,1)S(1)} %get-tuple-element.31.refs_0_, bf16[512,128]{1,0:T(8,128)(2,1)S(1)} %collective-permute-done.2.refs_1_, ...), custom_call_target="tpu_custom_call" | custom-call | flops 754974720 | bytes 2097152 | tf_op jit(solution)/shard_map/pallas_call | solution.py:387
  70.1 0.8 collective-permute-start.5
  70.9 1.2 %collective-permute-start.6 = (bf16[64,384]{1,0:T(8,128)(2,1)S(1)}, bf16[64,384]{1,0:T(8,128)(2,1)S(1)}, u32[]{:S(2)}, u32[]{:S(2)}) collective-permute-start(bf16[64,384]{1,0:T(8,128)(2,1)S(1)} %get-tuple-element.37), channel_id=1, source_target_pairs={{0,16},{8,24},{16,0},{24,8},{1,17},{9,25},{17,1},{25,9},{2,18},{10... | collective-permute-start | bytes 147464 | tf_op jit(solution)/shard_map/ppermute | solution.py:44
  72.1 1.8 %collective-permute-start.7 = (bf16[64,384]{1,0:T(8,128)(2,1)S(1)}, bf16[64,384]{1,0:T(8,128)(2,1)S(1)}, u32[]{:S(2)}, u32[]{:S(2)}) collective-permute-start(bf16[64,384]{1,0:T(8,128)(2,1)S(1)} %get-tuple-element.38), channel_id=1, source_target_pairs={{0,24},{8,0},{16,8},{24,16},{1,25},{9,1},{17,9},{25,17},{2,26},{10... | collective-permute-start | bytes 147464 | tf_op jit(solution)/shard_map/ppermute | solution.py:44
  74.0 2.1 %collective-permute-done.5.b_ref = bf16[64,384]{1,0:T(8,128)(2,1)S(1)} collective-permute-done((bf16[64,384]{1,0:T(8,128)(2,1)S(1)}, bf16[64,384]{1,0:T(8,128)(2,1)S(1)}, u32[]{:S(2)}, u32[]{:S(2)}) %collective-permute-start.5) | collective-permute-done | bytes 49184 | tf_op jit(solution)/shard_map/ppermute | solution.py:44
  76.1 0.8 collective-permute-done.6.c_ref
  76.9 0.0 collective-permute-done.7.d_ref
  77.0 2.4 %collective-permute-start.10 = (bf16[64,384]{1,0:T(8,128)(2,1)S(1)}, bf16[64,384]{1,0:T(8,128)(2,1)S(1)}, u32[]{:S(2)}, u32[]{:S(2)}) collective-permute-start(bf16[64,384]{1,0:T(8,128)(2,1)S(1)} %shard_map.76.refs_0_), channel_id=1, source_target_pairs={{0,3},{1,0},{2,1},{3,2},{4,7},{5,4},{6,5},{7,6},{8,11},{9,8},{10,9... | collective-permute-start | bytes 147464 | tf_op jit(solution)/shard_map/ppermute | solution.py:44
  79.4 0.6 collective-permute-start.9
  80.0 0.3 collective-permute-start.8
  80.2 0.0 collective-permute-start.11
  80.3 0.9 %collective-permute-done.10.refs_3_ = bf16[64,384]{1,0:T(8,128)(2,1)S(1)} collective-permute-done((bf16[64,384]{1,0:T(8,128)(2,1)S(1)}, bf16[64,384]{1,0:T(8,128)(2,1)S(1)}, u32[]{:S(2)}, u32[]{:S(2)}) %collective-permute-start.10) | collective-permute-done | bytes 49184 | tf_op jit(solution)/shard_map/ppermute | solution.py:44
  81.2 0.0 collective-permute-start.14
  81.2 2.3 %collective-permute-done.9.refs_2_ = bf16[64,384]{1,0:T(8,128)(2,1)S(1)} collective-permute-done((bf16[64,384]{1,0:T(8,128)(2,1)S(1)}, bf16[64,384]{1,0:T(8,128)(2,1)S(1)}, u32[]{:S(2)}, u32[]{:S(2)}) %collective-permute-start.9) | collective-permute-done | bytes 49184 | tf_op jit(solution)/shard_map/ppermute | solution.py:44
  83.5 0.0 collective-permute-start.13
  83.5 1.4 %collective-permute-done.8.refs_1_ = bf16[64,384]{1,0:T(8,128)(2,1)S(1)} collective-permute-done((bf16[64,384]{1,0:T(8,128)(2,1)S(1)}, bf16[64,384]{1,0:T(8,128)(2,1)S(1)}, u32[]{:S(2)}, u32[]{:S(2)}) %collective-permute-start.8) | collective-permute-done | bytes 49184 | tf_op jit(solution)/shard_map/ppermute | solution.py:44
  84.9 0.0 collective-permute-start.12
  84.9 0.5 collective-permute-start.15
  85.5 0.9 %collective-permute-done.15.refs_9_ = f32[64,160]{1,0:T(8,128)S(1)} collective-permute-done((f32[64,160]{1,0:T(8,128)S(1)}, f32[64,160]{1,0:T(8,128)S(1)}, u32[]{:S(2)}, u32[]{:S(2)}) %collective-permute-start.15) | collective-permute-done | bytes 40992 | tf_op jit(solution)/shard_map/ppermute | solution.py:400
  86.4 0.0 collective-permute-done.14.refs_7_
  86.4 0.0 collective-permute-done.13.refs_6_
  86.4 1.4 %shard_map.77 = (f32[2,64,160]{2,1,0:T(8,128)}, f32[2,64,1440]{2,1,0:T(8,128)}) custom-call(bf16[64,384]{1,0:T(8,128)(2,1)S(1)} %shard_map.76.refs_0_, bf16[64,384]{1,0:T(8,128)(2,1)S(1)} %collective-permute-done.8.refs_1_, bf16[64,384]{1,0:T(8,128)(2,1)S(1)} %collective-permute-done.9.refs_2_, bf16[64,384]{1,0:T(8,128)(2,1)S(1)} %collective-permute-done.10.refs_3_, ...), custom_call_target="tpu_custom_call" | custom-call | bytes 1048576 | tf_op jit(solution)/shard_map/pallas_call | solution.py:404
  (7 shorter events, 0.1 us)
Async XLA Ops:
  2.7 12.4 %all-to-all-start = ((bf16[8,32,640]{2,1,0:T(8,128)(2,1)}), bf16[8,32,640]{2,1,0:T(8,128)(2,1)S(1)}, u32[]{:S(2)}, u32[]{:S(2)}) async-start(bf16[8,32,640]{2,1,0:T(8,128)(2,1)} %shard_map.68), calls=%async_computation | async-start | bytes 655360 | tf_op jit(solution)/shard_map/all_to_all | solution.py:37
  15.1 3.6 %copy-start.1 = (bf16[8,32,640]{2,1,0:T(8,128)(2,1)}, bf16[8,32,640]{2,1,0:T(8,128)(2,1)S(1)}, u32[]{:S(2)}) copy-start(bf16[8,32,640]{2,1,0:T(8,128)(2,1)S(1)} %all-to-all-done.got_hbm) | copy-start | bytes 983044
  15.1 15.7 %all-to-all-start.1 = ((bf16[8,160,256]{2,1,0:T(8,128)(2,1)}), bf16[8,160,256]{2,1,0:T(8,128)(2,1)S(1)}, u32[]{:S(2)}, u32[]{:S(2)}) async-start(bf16[8,160,256]{2,1,0:T(8,128)(2,1)} %get-tuple-element.27), calls=%async_computation.1 | async-start | bytes 1310720 | tf_op jit(solution)/shard_map/all_to_all | solution.py:37
  27.4 1.7 %collective-permute-start = (f32[16,4,640]{2,1,0:T(4,128)}, f32[16,4,640]{2,1,0:T(4,128)S(1)}, u32[]{:S(2)}, u32[]{:S(2)}) collective-permute-start(f32[16,4,640]{2,1,0:T(4,128)} %get-tuple-element.26), channel_id=1, source_target_pairs={{0,4},{4,0},{1,5},{5,1},{2,6},{6,2},{3,7},{7,3},{8,12},{12,8},{9,1... | collective-permute-start | bytes 491528 | tf_op jit(solution)/shard_map/ppermute | solution.py:362
  30.8 15.3 %all-to-all-start.2 = ((f32[16,4,640]{2,1,0:T(4,128)}), f32[16,4,640]{2,1,0:T(4,128)S(1)}, u32[]{:S(2)}, u32[]{:S(2)}) async-start(f32[16,4,640]{2,1,0:T(4,128)} %add.3), calls=%async_computation.2 | async-start | bytes 327680 | tf_op jit(solution)/shard_map/all_to_all | solution.py:37
  38.0 13.4 %collective-permute-start.1 = (bf16[256,640]{1,0:T(8,128)(2,1)}, bf16[256,640]{1,0:T(8,128)(2,1)S(1)}, u32[]{:S(2)}, u32[]{:S(2)}) collective-permute-start(bf16[256,640]{1,0:T(8,128)(2,1)} %get-tuple-element.30), channel_id=1, source_target_pairs={{0,4},{4,0},{1,5},{5,1},{2,6},{6,2},{3,7},{7,3},{8,12},{12,8},{9,1... | collective-permute-start | bytes 983048 | tf_op jit(solution)/shard_map/ppermute | solution.py:363
  46.8 11.4 %all-to-all-start.3 = ((f32[16,4,640]{2,1,0:T(4,128)}), f32[16,4,640]{2,1,0:T(4,128)S(1)}, u32[]{:S(2)}, u32[]{:S(2)}) async-start(f32[16,4,640]{2,1,0:T(4,128)} %shard_map.71), calls=%async_computation.3 | async-start | bytes 327680 | tf_op jit(solution)/shard_map/all_to_all | solution.py:37
  50.4 1.0 %copy-start = (bf16[256,640]{1,0:T(8,128)(2,1)S(1)}, bf16[256,640]{1,0:T(8,128)(2,1)}, u32[]{:S(2)}) copy-start(bf16[256,640]{1,0:T(8,128)(2,1)} %get-tuple-element.29.keep_ref) | copy-start | bytes 983044
  58.7 8.5 %collective-permute-start.4 = (bf16[512,128]{1,0:T(8,128)(2,1)S(1)}, bf16[512,128]{1,0:T(8,128)(2,1)S(1)}, u32[]{:S(2)}, u32[]{:S(2)}) collective-permute-start(bf16[512,128]{1,0:T(8,128)(2,1)S(1)} %get-tuple-element.31.refs_0_), channel_id=1, source_target_pairs={{0,3},{1,0},{2,1},{3,2},{4,7},{5,4},{6,5},{7,6},{8,11},{9,8},{10,9... | collective-permute-start | bytes 393224 | tf_op jit(solution)/shard_map/ppermute | solution.py:44
  59.5 7.7 %collective-permute-start.3 = (bf16[512,128]{1,0:T(8,128)(2,1)S(1)}, bf16[512,128]{1,0:T(8,128)(2,1)S(1)}, u32[]{:S(2)}, u32[]{:S(2)}) collective-permute-start(bf16[512,128]{1,0:T(8,128)(2,1)S(1)} %get-tuple-element.31.refs_0_), channel_id=1, source_target_pairs={{0,2},{1,3},{2,0},{3,1},{4,6},{5,7},{6,4},{7,5},{8,10},{9,11},{10,... | collective-permute-start | bytes 393224 | tf_op jit(solution)/shard_map/ppermute | solution.py:44
  61.4 5.9 %collective-permute-start.2 = (bf16[512,128]{1,0:T(8,128)(2,1)S(1)}, bf16[512,128]{1,0:T(8,128)(2,1)S(1)}, u32[]{:S(2)}, u32[]{:S(2)}) collective-permute-start(bf16[512,128]{1,0:T(8,128)(2,1)S(1)} %get-tuple-element.31.refs_0_), channel_id=1, source_target_pairs={{0,1},{1,2},{2,3},{3,0},{4,5},{5,6},{6,7},{7,4},{8,9},{9,10},{10,1... | collective-permute-start | bytes 393224 | tf_op jit(solution)/shard_map/ppermute | solution.py:44
  70.1 6.0 %collective-permute-start.5 = (bf16[64,384]{1,0:T(8,128)(2,1)S(1)}, bf16[64,384]{1,0:T(8,128)(2,1)S(1)}, u32[]{:S(2)}, u32[]{:S(2)}) collective-permute-start(bf16[64,384]{1,0:T(8,128)(2,1)S(1)} %get-tuple-element.36), channel_id=1, source_target_pairs={{0,8},{8,16},{16,24},{24,0},{1,9},{9,17},{17,25},{25,1},{2,10},{10... | collective-permute-start | bytes 147464 | tf_op jit(solution)/shard_map/ppermute | solution.py:44
  70.9 6.0 %collective-permute-start.6 = (bf16[64,384]{1,0:T(8,128)(2,1)S(1)}, bf16[64,384]{1,0:T(8,128)(2,1)S(1)}, u32[]{:S(2)}, u32[]{:S(2)}) collective-permute-start(bf16[64,384]{1,0:T(8,128)(2,1)S(1)} %get-tuple-element.37), channel_id=1, source_target_pairs={{0,16},{8,24},{16,0},{24,8},{1,17},{9,25},{17,1},{25,9},{2,18},{10... | collective-permute-start | bytes 147464 | tf_op jit(solution)/shard_map/ppermute | solution.py:44
  72.1 4.8 %collective-permute-start.7 = (bf16[64,384]{1,0:T(8,128)(2,1)S(1)}, bf16[64,384]{1,0:T(8,128)(2,1)S(1)}, u32[]{:S(2)}, u32[]{:S(2)}) collective-permute-start(bf16[64,384]{1,0:T(8,128)(2,1)S(1)} %get-tuple-element.38), channel_id=1, source_target_pairs={{0,24},{8,0},{16,8},{24,16},{1,25},{9,1},{17,9},{25,17},{2,26},{10... | collective-permute-start | bytes 147464 | tf_op jit(solution)/shard_map/ppermute | solution.py:44
  77.0 4.2 %collective-permute-start.10 = (bf16[64,384]{1,0:T(8,128)(2,1)S(1)}, bf16[64,384]{1,0:T(8,128)(2,1)S(1)}, u32[]{:S(2)}, u32[]{:S(2)}) collective-permute-start(bf16[64,384]{1,0:T(8,128)(2,1)S(1)} %shard_map.76.refs_0_), channel_id=1, source_target_pairs={{0,3},{1,0},{2,1},{3,2},{4,7},{5,4},{6,5},{7,6},{8,11},{9,8},{10,9... | collective-permute-start | bytes 147464 | tf_op jit(solution)/shard_map/ppermute | solution.py:44
  79.4 4.1 %collective-permute-start.9 = (bf16[64,384]{1,0:T(8,128)(2,1)S(1)}, bf16[64,384]{1,0:T(8,128)(2,1)S(1)}, u32[]{:S(2)}, u32[]{:S(2)}) collective-permute-start(bf16[64,384]{1,0:T(8,128)(2,1)S(1)} %shard_map.76.refs_0_), channel_id=1, source_target_pairs={{0,2},{1,3},{2,0},{3,1},{4,6},{5,7},{6,4},{7,5},{8,10},{9,11},{10,... | collective-permute-start | bytes 147464 | tf_op jit(solution)/shard_map/ppermute | solution.py:44
  80.0 5.0 %collective-permute-start.8 = (bf16[64,384]{1,0:T(8,128)(2,1)S(1)}, bf16[64,384]{1,0:T(8,128)(2,1)S(1)}, u32[]{:S(2)}, u32[]{:S(2)}) collective-permute-start(bf16[64,384]{1,0:T(8,128)(2,1)S(1)} %shard_map.76.refs_0_), channel_id=1, source_target_pairs={{0,1},{1,2},{2,3},{3,0},{4,5},{5,6},{6,7},{7,4},{8,9},{9,10},{10,1... | collective-permute-start | bytes 147464 | tf_op jit(solution)/shard_map/ppermute | solution.py:44
  80.2 6.1 %collective-permute-start.11 = (bf16[64,384]{1,0:T(8,128)(2,1)S(1)}, bf16[64,384]{1,0:T(8,128)(2,1)S(1)}, u32[]{:S(2)}, u32[]{:S(2)}) collective-permute-start(bf16[64,384]{1,0:T(8,128)(2,1)S(1)} %shard_map.76.refs_0_), channel_id=1, source_target_pairs={{0,4},{4,0},{1,5},{5,1},{2,6},{6,2},{3,7},{7,3},{8,12},{12,8},{9,1... | collective-permute-start | bytes 147464 | tf_op jit(solution)/shard_map/ppermute | solution.py:403
  81.2 5.2 %collective-permute-start.14 = (bf16[64,384]{1,0:T(8,128)(2,1)S(1)}, bf16[64,384]{1,0:T(8,128)(2,1)S(1)}, u32[]{:S(2)}, u32[]{:S(2)}) collective-permute-start(bf16[64,384]{1,0:T(8,128)(2,1)S(1)} %collective-permute-done.10.refs_3_), channel_id=1, source_target_pairs={{0,4},{4,0},{1,5},{5,1},{2,6},{6,2},{3,7},{7,3},{8,12},{12,8},{9,1... | collective-permute-start | bytes 147464 | tf_op jit(solution)/shard_map/ppermute | solution.py:403
  83.5 2.9 %collective-permute-start.13 = (bf16[64,384]{1,0:T(8,128)(2,1)S(1)}, bf16[64,384]{1,0:T(8,128)(2,1)S(1)}, u32[]{:S(2)}, u32[]{:S(2)}) collective-permute-start(bf16[64,384]{1,0:T(8,128)(2,1)S(1)} %collective-permute-done.9.refs_2_), channel_id=1, source_target_pairs={{0,4},{4,0},{1,5},{5,1},{2,6},{6,2},{3,7},{7,3},{8,12},{12,8},{9,1... | collective-permute-start | bytes 147464 | tf_op jit(solution)/shard_map/ppermute | solution.py:403
  84.9 1.4 %collective-permute-start.12 = (bf16[64,384]{1,0:T(8,128)(2,1)S(1)}, bf16[64,384]{1,0:T(8,128)(2,1)S(1)}, u32[]{:S(2)}, u32[]{:S(2)}) collective-permute-start(bf16[64,384]{1,0:T(8,128)(2,1)S(1)} %collective-permute-done.8.refs_1_), channel_id=1, source_target_pairs={{0,4},{4,0},{1,5},{5,1},{2,6},{6,2},{3,7},{7,3},{8,12},{12,8},{9,1... | collective-permute-start | bytes 147464 | tf_op jit(solution)/shard_map/ppermute | solution.py:403
  84.9 1.4 %collective-permute-start.15 = (f32[64,160]{1,0:T(8,128)S(1)}, f32[64,160]{1,0:T(8,128)S(1)}, u32[]{:S(2)}, u32[]{:S(2)}) collective-permute-start(f32[64,160]{1,0:T(8,128)S(1)} %get-tuple-element.39.refs_8_), channel_id=1, source_target_pairs={{0,4},{4,0},{1,5},{5,1},{2,6},{6,2},{3,7},{7,3},{8,12},{12,8},{9,1... | collective-permute-start | bytes 122888 | tf_op jit(solution)/shard_map/ppermute | solution.py:400

commit v13 on v11

--- a/solution.py
+++ b/solution.py
@@ -363,7 +363,9 @@
     )(x, g, got, slope, q_one, y_two, conv_weight)
 
     across = [(0, 1), (1, 0)]
-    p_part = call(add_body, p_shape, 0, 1 << 20)(p_keep, lax.ppermute(p_swap, "row", across))
+    p_swap = lax.ppermute(p_swap, "row", across)
+    p_keep = call(stage_body, p_shape, 0, 8 << 20)(p_keep)
+    p_part = call(add_body, p_shape, 0, 1 << 20)(p_keep, p_swap)
     swap = lax.ppermute(swap, "row", across)
     keep = call(stage_body, shape((256, 640), BF), 0, 8 << 20)(keep)
     p_part, slices = lax.optimization_barrier((p_part, slices))

time: 88.3 us -> 87.3 us (0.989)
  waiting for transfers between devices: 25.8 us -> 24.9 us
    ppermute x1, waiting for transfers between devices: 1.24 us -> 0.31 us  [on_device(): p_swap = lax.ppermute(p_swap, 'row', across)]
where the time goes in v13:
time: 87.3 us; the launch traced here: 86.8 us
  starting transfers between devices  30.5 us (35%)
  Pallas kernels  28.7 us (33%)
  waiting for transfers between devices  24.9 us (29%)
  local copies, waits for them, and re-layouts  1.88 us (2%)
    all_to_all x4, starting transfers between devices, exchange(): return lax.all_to_all(chunks, axes, 0, 0, tiled=True)  19.4 us
    all_to_all x4, waiting for transfers between devices, exchange(): return lax.all_to_all(chunks, axes, 0, 0, tiled=True)  16 us
    ppermute x9, starting transfers between devices, shifts(): lax.ppermute(values[s], axis, [(i, (i + s) % size) for i in range(size)])  10 us
    pallas_call x1, Pallas kernels, on_device(): call(power_body, (shape((256, 640), BF), shape((256, 640), BF), p_shape,...  8.74 us
    ppermute x9, waiting for transfers between devices, shifts(): lax.ppermute(values[s], axis, [(i, (i + s) % size) for i in range(size)])  7.74 us
    pallas_call x1, Pallas kernels, on_device(): call(prepare_body, (shape((8, 160, 256), BF), shape((3, 384, 640), BF), s...  6.19 us
    pallas_call x1, Pallas kernels, on_device(): call(factor_body, (shape((64, 64), F32), shape((64, 640), F32), shape((64...  5.67 us
    pallas_call x1, Pallas kernels, on_device(): call(functools.partial(taps_body, images == 4), (shape((64, 384), BF),) *...  2.77 us
  transfers between devices with their start and end apart: 20, of which 11 were waited for; matrix products, arithmetic and copies ran while one was open for 0% of the time, Pallas kernels for 25%

profile of v13, /device:TPU:0, one launch (start us, length us, event | category | flops | bytes accessed | tf_op | source)
XLA Modules:
  0.0 86.8 jit_solution(15585180567111356717)
XLA Ops:
  0.6 2.1 %shard_map.68 = bf16[8,32,640]{2,1,0:T(8,128)(2,1)} custom-call(bf16[256,640]{1,0:T(8,128)(2,1)} %bitcast.9, bf16[256,640]{1,0:T(8,128)(2,1)} %bitcast.13), custom_call_target="tpu_custom_call" | custom-call | flops 16777216 | bytes 1048576 | tf_op jit(solution)/shard_map/pallas_call | solution.py:312
  2.7 5.2 %all-to-all-start = ((bf16[8,32,640]{2,1,0:T(8,128)(2,1)}), bf16[8,32,640]{2,1,0:T(8,128)(2,1)S(1)}, u32[]{:S(2)}, u32[]{:S(2)}) async-start(bf16[8,32,640]{2,1,0:T(8,128)(2,1)} %shard_map.68), calls=%async_computation | async-start | bytes 655360 | tf_op jit(solution)/shard_map/all_to_all | solution.py:37
  7.9 6.2 %shard_map.69 = (bf16[8,160,256]{2,1,0:T(8,128)(2,1)}, bf16[3,384,640]{2,1,0:T(8,128)(2,1)}, bf16[3,128,384]{2,1,0:T(8,128)(2,1)}, f32[256,640]{1,0:T(8,128)}) custom-call(bf16[256,640]{1,0:T(8,128)(2,1)} %bitcast.10, bf16[256,640]{1,0:T(8,128)(2,1)} %bitcast.12, f32[128,5760]{1,0:T(8,128)} %bitcast.8), custom_call_target="tpu_custom_call" | custom-call | flops 377487360 | bytes 8388608 | tf_op jit(solution)/shard_map/pallas_call | solution.py:322
  14.1 1.0 %all-to-all-done.got_hbm = bf16[8,32,640]{2,1,0:T(8,128)(2,1)S(1)} async-done(((bf16[8,32,640]{2,1,0:T(8,128)(2,1)}), bf16[8,32,640]{2,1,0:T(8,128)(2,1)S(1)}, u32[]{:S(2)}, u32[]{:S(2)}) %all-to-all-start) | async-done | bytes 327712 | tf_op jit(solution)/shard_map/all_to_all | solution.py:37
  15.1 3.5 %all-to-all-start.1 = ((bf16[8,160,256]{2,1,0:T(8,128)(2,1)}), bf16[8,160,256]{2,1,0:T(8,128)(2,1)S(1)}, u32[]{:S(2)}, u32[]{:S(2)}) async-start(bf16[8,160,256]{2,1,0:T(8,128)(2,1)} %get-tuple-element.27), calls=%async_computation.1 | async-start | bytes 1310720 | tf_op jit(solution)/shard_map/all_to_all | solution.py:37
  18.7 8.7 %shard_map.70 = (bf16[256,640]{1,0:T(8,128)(2,1)}, bf16[256,640]{1,0:T(8,128)(2,1)}, f32[16,4,640]{2,1,0:T(4,128)}, f32[16,4,640]{2,1,0:T(4,128)}) custom-call(bf16[256,640]{1,0:T(8,128)(2,1)} %bitcast.11, bf16[256,640]{1,0:T(8,128)(2,1)} %bitcast.14, bf16[8,32,640]{2,1,0:T(8,128)(2,1)} %copy-done.2, f32[256,640]{1,0:T(8,128)} %get-tuple-element.22.slope_hbm, ...), custom_call_target="tpu_custom_call" | custom-call | flops 3244032000 | bytes 12582912 | tf_op jit(solution)/shard_map/pallas_call | solution.py:343
  27.4 0.5 collective-permute-start
  27.9 0.9 %copy-done.1 = f32[16,4,640]{2,1,0:T(4,128)S(1)} copy-done((f32[16,4,640]{2,1,0:T(4,128)S(1)}, f32[16,4,640]{2,1,0:T(4,128)}, u32[]{:S(2)}) %copy-start.1) | copy-done | bytes 163864
  28.9 0.3 collective-permute-done.right_ref
  29.2 0.7 shard_map.72
  29.8 0.0 all-to-all-done.1.refs_4_
  29.8 7.2 %all-to-all-start.2 = ((f32[16,4,640]{2,1,0:T(4,128)}), f32[16,4,640]{2,1,0:T(4,128)S(1)}, u32[]{:S(2)}, u32[]{:S(2)}) async-start(f32[16,4,640]{2,1,0:T(4,128)} %shard_map.72), calls=%async_computation.2 | async-start | bytes 327680 | tf_op jit(solution)/shard_map/all_to_all | solution.py:37
  37.0 0.1 collective-permute-start.1
  37.1 8.1 %all-to-all-done.2.got_ref = f32[16,4,640]{2,1,0:T(4,128)S(1)} async-done(((f32[16,4,640]{2,1,0:T(4,128)}), f32[16,4,640]{2,1,0:T(4,128)S(1)}, u32[]{:S(2)}, u32[]{:S(2)}) %all-to-all-start.2) | async-done | bytes 163872 | tf_op jit(solution)/shard_map/all_to_all | solution.py:37
  45.2 0.7 shard_map.73
  45.9 3.5 %all-to-all-start.3 = ((f32[16,4,640]{2,1,0:T(4,128)}), f32[16,4,640]{2,1,0:T(4,128)S(1)}, u32[]{:S(2)}, u32[]{:S(2)}) async-start(f32[16,4,640]{2,1,0:T(4,128)} %shard_map.73), calls=%async_computation.3 | async-start | bytes 327680 | tf_op jit(solution)/shard_map/all_to_all | solution.py:37
  49.4 1.0 %copy-done = bf16[256,640]{1,0:T(8,128)(2,1)S(1)} copy-done((bf16[256,640]{1,0:T(8,128)(2,1)S(1)}, bf16[256,640]{1,0:T(8,128)(2,1)}, u32[]{:S(2)}) %copy-start) | copy-done | bytes 327704
  50.4 0.0 collective-permute-done.1.swap_ref
  50.4 6.9 %all-to-all-done.3.got_ref = f32[16,4,640]{2,1,0:T(4,128)S(1)} async-done(((f32[16,4,640]{2,1,0:T(4,128)}), f32[16,4,640]{2,1,0:T(4,128)S(1)}, u32[]{:S(2)}, u32[]{:S(2)}) %all-to-all-start.3) | async-done | bytes 163872 | tf_op jit(solution)/shard_map/all_to_all | solution.py:37
  57.3 0.4 shard_map.75
  57.7 0.8 collective-permute-start.4
  58.6 1.9 %collective-permute-start.3 = (bf16[512,128]{1,0:T(8,128)(2,1)S(1)}, bf16[512,128]{1,0:T(8,128)(2,1)S(1)}, u32[]{:S(2)}, u32[]{:S(2)}) collective-permute-start(bf16[512,128]{1,0:T(8,128)(2,1)S(1)} %get-tuple-element.31.refs_0_), channel_id=1, source_target_pairs={{0,2},{1,3},{2,0},{3,1},{4,6},{5,7},{6,4},{7,5},{8,10},{9,11},{10,... | collective-permute-start | bytes 393224 | tf_op jit(solution)/shard_map/ppermute | solution.py:44
  60.5 0.1 collective-permute-start.2
  60.6 5.7 %shard_map.76 = (f32[64,64]{1,0:T(8,128)S(1)}, f32[64,640]{1,0:T(8,128)}, f32[64,160]{1,0:T(8,128)S(1)}) custom-call(f32[64,640]{1,0:T(8,128)S(1)} %get-tuple-element.33.p_ref), custom_call_target="tpu_custom_call" | custom-call | flops 1073741824 | bytes 1048576 | tf_op jit(solution)/shard_map/pallas_call | solution.py:386
  66.2 0.0 collective-permute-done.4.refs_3_
  66.3 0.0 collective-permute-done.3.refs_2_
  66.3 0.1 collective-permute-done.2.refs_1_
  66.3 2.8 %shard_map.77 = (bf16[64,384]{1,0:T(8,128)(2,1)S(1)}, bf16[64,384]{1,0:T(8,128)(2,1)S(1)}, bf16[64,384]{1,0:T(8,128)(2,1)S(1)}, bf16[64,384]{1,0:T(8,128)(2,1)S(1)}) custom-call(bf16[512,128]{1,0:T(8,128)(2,1)S(1)} %get-tuple-element.31.refs_0_, bf16[512,128]{1,0:T(8,128)(2,1)S(1)} %collective-permute-done.2.refs_1_, ...), custom_call_target="tpu_custom_call" | custom-call | flops 754974720 | bytes 2097152 | tf_op jit(solution)/shard_map/pallas_call | solution.py:393
  69.1 0.8 collective-permute-start.5
  70.0 1.2 %collective-permute-start.6 = (bf16[64,384]{1,0:T(8,128)(2,1)S(1)}, bf16[64,384]{1,0:T(8,128)(2,1)S(1)}, u32[]{:S(2)}, u32[]{:S(2)}) collective-permute-start(bf16[64,384]{1,0:T(8,128)(2,1)S(1)} %get-tuple-element.37), channel_id=1, source_target_pairs={{0,16},{8,24},{16,0},{24,8},{1,17},{9,25},{17,1},{25,9},{2,18},{10... | collective-permute-start | bytes 147464 | tf_op jit(solution)/shard_map/ppermute | solution.py:44
  71.2 1.9 %collective-permute-start.7 = (bf16[64,384]{1,0:T(8,128)(2,1)S(1)}, bf16[64,384]{1,0:T(8,128)(2,1)S(1)}, u32[]{:S(2)}, u32[]{:S(2)}) collective-permute-start(bf16[64,384]{1,0:T(8,128)(2,1)S(1)} %get-tuple-element.38), channel_id=1, source_target_pairs={{0,24},{8,0},{16,8},{24,16},{1,25},{9,1},{17,9},{25,17},{2,26},{10... | collective-permute-start | bytes 147464 | tf_op jit(solution)/shard_map/ppermute | solution.py:44
  73.0 2.1 %collective-permute-done.5.b_ref = bf16[64,384]{1,0:T(8,128)(2,1)S(1)} collective-permute-done((bf16[64,384]{1,0:T(8,128)(2,1)S(1)}, bf16[64,384]{1,0:T(8,128)(2,1)S(1)}, u32[]{:S(2)}, u32[]{:S(2)}) %collective-permute-start.5) | collective-permute-done | bytes 49184 | tf_op jit(solution)/shard_map/ppermute | solution.py:44
  75.2 0.8 collective-permute-done.6.c_ref
  76.0 0.0 collective-permute-done.7.d_ref
  76.0 2.4 %collective-permute-start.10 = (bf16[64,384]{1,0:T(8,128)(2,1)S(1)}, bf16[64,384]{1,0:T(8,128)(2,1)S(1)}, u32[]{:S(2)}, u32[]{:S(2)}) collective-permute-start(bf16[64,384]{1,0:T(8,128)(2,1)S(1)} %shard_map.78.refs_0_), channel_id=1, source_target_pairs={{0,3},{1,0},{2,1},{3,2},{4,7},{5,4},{6,5},{7,6},{8,11},{9,8},{10,9... | collective-permute-start | bytes 147464 | tf_op jit(solution)/shard_map/ppermute | solution.py:44
  78.5 0.6 collective-permute-start.9
  79.0 0.3 collective-permute-start.8
  79.3 0.0 collective-permute-start.11
  79.3 0.9 %collective-permute-done.10.refs_3_ = bf16[64,384]{1,0:T(8,128)(2,1)S(1)} collective-permute-done((bf16[64,384]{1,0:T(8,128)(2,1)S(1)}, bf16[64,384]{1,0:T(8,128)(2,1)S(1)}, u32[]{:S(2)}, u32[]{:S(2)}) %collective-permute-start.10) | collective-permute-done | bytes 49184 | tf_op jit(solution)/shard_map/ppermute | solution.py:44
  80.2 0.0 collective-permute-start.14
  80.2 2.3 %collective-permute-done.9.refs_2_ = bf16[64,384]{1,0:T(8,128)(2,1)S(1)} collective-permute-done((bf16[64,384]{1,0:T(8,128)(2,1)S(1)}, bf16[64,384]{1,0:T(8,128)(2,1)S(1)}, u32[]{:S(2)}, u32[]{:S(2)}) %collective-permute-start.9) | collective-permute-done | bytes 49184 | tf_op jit(solution)/shard_map/ppermute | solution.py:44
  82.5 0.0 collective-permute-start.13
  82.5 1.5 %collective-permute-done.8.refs_1_ = bf16[64,384]{1,0:T(8,128)(2,1)S(1)} collective-permute-done((bf16[64,384]{1,0:T(8,128)(2,1)S(1)}, bf16[64,384]{1,0:T(8,128)(2,1)S(1)}, u32[]{:S(2)}, u32[]{:S(2)}) %collective-permute-start.8) | collective-permute-done | bytes 49184 | tf_op jit(solution)/shard_map/ppermute | solution.py:44
  84.0 0.5 collective-permute-start.15
  84.5 0.9 %collective-permute-done.15.refs_9_ = f32[64,160]{1,0:T(8,128)S(1)} collective-permute-done((f32[64,160]{1,0:T(8,128)S(1)}, f32[64,160]{1,0:T(8,128)S(1)}, u32[]{:S(2)}, u32[]{:S(2)}) %collective-permute-start.15) | collective-permute-done | bytes 40992 | tf_op jit(solution)/shard_map/ppermute | solution.py:406
  85.4 0.0 collective-permute-done.11.refs_4_
  85.4 0.0 collective-permute-done.12.refs_5_
  85.4 1.4 %shard_map.79 = (f32[2,64,160]{2,1,0:T(8,128)}, f32[2,64,1440]{2,1,0:T(8,128)}) custom-call(bf16[64,384]{1,0:T(8,128)(2,1)S(1)} %shard_map.78.refs_0_, bf16[64,384]{1,0:T(8,128)(2,1)S(1)} %collective-permute-done.8.refs_1_, bf16[64,384]{1,0:T(8,128)(2,1)S(1)} %collective-permute-done.9.refs_2_, bf16[64,384]{1,0:T(8,128)(2,1)S(1)} %collective-permute-done.10.refs_3_, ...), custom_call_target="tpu_custom_call" | custom-call | bytes 1048576 | tf_op jit(solution)/shard_map/pallas_call | solution.py:410
  (10 shorter events, 0.1 us)
Async XLA Ops:
  2.7 12.4 %all-to-all-start = ((bf16[8,32,640]{2,1,0:T(8,128)(2,1)}), bf16[8,32,640]{2,1,0:T(8,128)(2,1)S(1)}, u32[]{:S(2)}, u32[]{:S(2)}) async-start(bf16[8,32,640]{2,1,0:T(8,128)(2,1)} %shard_map.68), calls=%async_computation | async-start | bytes 655360 | tf_op jit(solution)/shard_map/all_to_all | solution.py:37
  15.1 3.6 %copy-start.2 = (bf16[8,32,640]{2,1,0:T(8,128)(2,1)}, bf16[8,32,640]{2,1,0:T(8,128)(2,1)S(1)}, u32[]{:S(2)}) copy-start(bf16[8,32,640]{2,1,0:T(8,128)(2,1)S(1)} %all-to-all-done.got_hbm) | copy-start | bytes 983044
  15.1 14.7 %all-to-all-start.1 = ((bf16[8,160,256]{2,1,0:T(8,128)(2,1)}), bf16[8,160,256]{2,1,0:T(8,128)(2,1)S(1)}, u32[]{:S(2)}, u32[]{:S(2)}) async-start(bf16[8,160,256]{2,1,0:T(8,128)(2,1)} %get-tuple-element.27), calls=%async_computation.1 | async-start | bytes 1310720 | tf_op jit(solution)/shard_map/all_to_all | solution.py:37
  27.4 1.7 %collective-permute-start = (f32[16,4,640]{2,1,0:T(4,128)}, f32[16,4,640]{2,1,0:T(4,128)S(1)}, u32[]{:S(2)}, u32[]{:S(2)}) collective-permute-start(f32[16,4,640]{2,1,0:T(4,128)} %get-tuple-element.26), channel_id=1, source_target_pairs={{0,4},{4,0},{1,5},{5,1},{2,6},{6,2},{3,7},{7,3},{8,12},{12,8},{9,1... | collective-permute-start | bytes 491528 | tf_op jit(solution)/shard_map/ppermute | solution.py:366
  27.9 0.9 %copy-start.1 = (f32[16,4,640]{2,1,0:T(4,128)S(1)}, f32[16,4,640]{2,1,0:T(4,128)}, u32[]{:S(2)}) copy-start(f32[16,4,640]{2,1,0:T(4,128)} %get-tuple-element.25.keep_ref) | copy-start | bytes 491524
  29.8 15.3 %all-to-all-start.2 = ((f32[16,4,640]{2,1,0:T(4,128)}), f32[16,4,640]{2,1,0:T(4,128)S(1)}, u32[]{:S(2)}, u32[]{:S(2)}) async-start(f32[16,4,640]{2,1,0:T(4,128)} %shard_map.72), calls=%async_computation.2 | async-start | bytes 327680 | tf_op jit(solution)/shard_map/all_to_all | solution.py:37
  37.0 13.4 %collective-permute-start.1 = (bf16[256,640]{1,0:T(8,128)(2,1)}, bf16[256,640]{1,0:T(8,128)(2,1)S(1)}, u32[]{:S(2)}, u32[]{:S(2)}) collective-permute-start(bf16[256,640]{1,0:T(8,128)(2,1)} %get-tuple-element.30), channel_id=1, source_target_pairs={{0,4},{4,0},{1,5},{5,1},{2,6},{6,2},{3,7},{7,3},{8,12},{12,8},{9,1... | collective-permute-start | bytes 983048 | tf_op jit(solution)/shard_map/ppermute | solution.py:369
  45.9 11.4 %all-to-all-start.3 = ((f32[16,4,640]{2,1,0:T(4,128)}), f32[16,4,640]{2,1,0:T(4,128)S(1)}, u32[]{:S(2)}, u32[]{:S(2)}) async-start(f32[16,4,640]{2,1,0:T(4,128)} %shard_map.73), calls=%async_computation.3 | async-start | bytes 327680 | tf_op jit(solution)/shard_map/all_to_all | solution.py:37
  49.4 1.0 %copy-start = (bf16[256,640]{1,0:T(8,128)(2,1)S(1)}, bf16[256,640]{1,0:T(8,128)(2,1)}, u32[]{:S(2)}) copy-start(bf16[256,640]{1,0:T(8,128)(2,1)} %get-tuple-element.29.keep_ref) | copy-start | bytes 983044
  57.7 8.5 %collective-permute-start.4 = (bf16[512,128]{1,0:T(8,128)(2,1)S(1)}, bf16[512,128]{1,0:T(8,128)(2,1)S(1)}, u32[]{:S(2)}, u32[]{:S(2)}) collective-permute-start(bf16[512,128]{1,0:T(8,128)(2,1)S(1)} %get-tuple-element.31.refs_0_), channel_id=1, source_target_pairs={{0,3},{1,0},{2,1},{3,2},{4,7},{5,4},{6,5},{7,6},{8,11},{9,8},{10,9... | collective-permute-start | bytes 393224 | tf_op jit(solution)/shard_map/ppermute | solution.py:44
  58.6 7.7 %collective-permute-start.3 = (bf16[512,128]{1,0:T(8,128)(2,1)S(1)}, bf16[512,128]{1,0:T(8,128)(2,1)S(1)}, u32[]{:S(2)}, u32[]{:S(2)}) collective-permute-start(bf16[512,128]{1,0:T(8,128)(2,1)S(1)} %get-tuple-element.31.refs_0_), channel_id=1, source_target_pairs={{0,2},{1,3},{2,0},{3,1},{4,6},{5,7},{6,4},{7,5},{8,10},{9,11},{10,... | collective-permute-start | bytes 393224 | tf_op jit(solution)/shard_map/ppermute | solution.py:44
  60.5 5.9 %collective-permute-start.2 = (bf16[512,128]{1,0:T(8,128)(2,1)S(1)}, bf16[512,128]{1,0:T(8,128)(2,1)S(1)}, u32[]{:S(2)}, u32[]{:S(2)}) collective-permute-start(bf16[512,128]{1,0:T(8,128)(2,1)S(1)} %get-tuple-element.31.refs_0_), channel_id=1, source_target_pairs={{0,1},{1,2},{2,3},{3,0},{4,5},{5,6},{6,7},{7,4},{8,9},{9,10},{10,1... | collective-permute-start | bytes 393224 | tf_op jit(solution)/shard_map/ppermute | solution.py:44
  69.1 6.0 %collective-permute-start.5 = (bf16[64,384]{1,0:T(8,128)(2,1)S(1)}, bf16[64,384]{1,0:T(8,128)(2,1)S(1)}, u32[]{:S(2)}, u32[]{:S(2)}) collective-permute-start(bf16[64,384]{1,0:T(8,128)(2,1)S(1)} %get-tuple-element.36), channel_id=1, source_target_pairs={{0,8},{8,16},{16,24},{24,0},{1,9},{9,17},{17,25},{25,1},{2,10},{10... | collective-permute-start | bytes 147464 | tf_op jit(solution)/shard_map/ppermute | solution.py:44
  70.0 6.0 %collective-permute-start.6 = (bf16[64,384]{1,0:T(8,128)(2,1)S(1)}, bf16[64,384]{1,0:T(8,128)(2,1)S(1)}, u32[]{:S(2)}, u32[]{:S(2)}) collective-permute-start(bf16[64,384]{1,0:T(8,128)(2,1)S(1)} %get-tuple-element.37), channel_id=1, source_target_pairs={{0,16},{8,24},{16,0},{24,8},{1,17},{9,25},{17,1},{25,9},{2,18},{10... | collective-permute-start | bytes 147464 | tf_op jit(solution)/shard_map/ppermute | solution.py:44
  71.2 4.8 %collective-permute-start.7 = (bf16[64,384]{1,0:T(8,128)(2,1)S(1)}, bf16[64,384]{1,0:T(8,128)(2,1)S(1)}, u32[]{:S(2)}, u32[]{:S(2)}) collective-permute-start(bf16[64,384]{1,0:T(8,128)(2,1)S(1)} %get-tuple-element.38), channel_id=1, source_target_pairs={{0,24},{8,0},{16,8},{24,16},{1,25},{9,1},{17,9},{25,17},{2,26},{10... | collective-permute-start | bytes 147464 | tf_op jit(solution)/shard_map/ppermute | solution.py:44
  76.0 4.2 %collective-permute-start.10 = (bf16[64,384]{1,0:T(8,128)(2,1)S(1)}, bf16[64,384]{1,0:T(8,128)(2,1)S(1)}, u32[]{:S(2)}, u32[]{:S(2)}) collective-permute-start(bf16[64,384]{1,0:T(8,128)(2,1)S(1)} %shard_map.78.refs_0_), channel_id=1, source_target_pairs={{0,3},{1,0},{2,1},{3,2},{4,7},{5,4},{6,5},{7,6},{8,11},{9,8},{10,9... | collective-permute-start | bytes 147464 | tf_op jit(solution)/shard_map/ppermute | solution.py:44
  78.5 4.1 %collective-permute-start.9 = (bf16[64,384]{1,0:T(8,128)(2,1)S(1)}, bf16[64,384]{1,0:T(8,128)(2,1)S(1)}, u32[]{:S(2)}, u32[]{:S(2)}) collective-permute-start(bf16[64,384]{1,0:T(8,128)(2,1)S(1)} %shard_map.78.refs_0_), channel_id=1, source_target_pairs={{0,2},{1,3},{2,0},{3,1},{4,6},{5,7},{6,4},{7,5},{8,10},{9,11},{10,... | collective-permute-start | bytes 147464 | tf_op jit(solution)/shard_map/ppermute | solution.py:44
  79.0 5.0 %collective-permute-start.8 = (bf16[64,384]{1,0:T(8,128)(2,1)S(1)}, bf16[64,384]{1,0:T(8,128)(2,1)S(1)}, u32[]{:S(2)}, u32[]{:S(2)}) collective-permute-start(bf16[64,384]{1,0:T(8,128)(2,1)S(1)} %shard_map.78.refs_0_), channel_id=1, source_target_pairs={{0,1},{1,2},{2,3},{3,0},{4,5},{5,6},{6,7},{7,4},{8,9},{9,10},{10,1... | collective-permute-start | bytes 147464 | tf_op jit(solution)/shard_map/ppermute | solution.py:44
  79.3 6.1 %collective-permute-start.11 = (bf16[64,384]{1,0:T(8,128)(2,1)S(1)}, bf16[64,384]{1,0:T(8,128)(2,1)S(1)}, u32[]{:S(2)}, u32[]{:S(2)}) collective-permute-start(bf16[64,384]{1,0:T(8,128)(2,1)S(1)} %shard_map.78.refs_0_), channel_id=1, source_target_pairs={{0,4},{4,0},{1,5},{5,1},{2,6},{6,2},{3,7},{7,3},{8,12},{12,8},{9,1... | collective-permute-start | bytes 147464 | tf_op jit(solution)/shard_map/ppermute | solution.py:409
  80.2 5.2 %collective-permute-start.14 = (bf16[64,384]{1,0:T(8,128)(2,1)S(1)}, bf16[64,384]{1,0:T(8,128)(2,1)S(1)}, u32[]{:S(2)}, u32[]{:S(2)}) collective-permute-start(bf16[64,384]{1,0:T(8,128)(2,1)S(1)} %collective-permute-done.10.refs_3_), channel_id=1, source_target_pairs={{0,4},{4,0},{1,5},{5,1},{2,6},{6,2},{3,7},{7,3},{8,12},{12,8},{9,1... | collective-permute-start | bytes 147464 | tf_op jit(solution)/shard_map/ppermute | solution.py:409
  82.5 2.9 %collective-permute-start.13 = (bf16[64,384]{1,0:T(8,128)(2,1)S(1)}, bf16[64,384]{1,0:T(8,128)(2,1)S(1)}, u32[]{:S(2)}, u32[]{:S(2)}) collective-permute-start(bf16[64,384]{1,0:T(8,128)(2,1)S(1)} %collective-permute-done.9.refs_2_), channel_id=1, source_target_pairs={{0,4},{4,0},{1,5},{5,1},{2,6},{6,2},{3,7},{7,3},{8,12},{12,8},{9,1... | collective-permute-start | bytes 147464 | tf_op jit(solution)/shard_map/ppermute | solution.py:409
  84.0 1.4 %collective-permute-start.12 = (bf16[64,384]{1,0:T(8,128)(2,1)S(1)}, bf16[64,384]{1,0:T(8,128)(2,1)S(1)}, u32[]{:S(2)}, u32[]{:S(2)}) collective-permute-start(bf16[64,384]{1,0:T(8,128)(2,1)S(1)} %collective-permute-done.8.refs_1_), channel_id=1, source_target_pairs={{0,4},{4,0},{1,5},{5,1},{2,6},{6,2},{3,7},{7,3},{8,12},{12,8},{9,1... | collective-permute-start | bytes 147464 | tf_op jit(solution)/shard_map/ppermute | solution.py:409
  84.0 1.4 %collective-permute-start.15 = (f32[64,160]{1,0:T(8,128)S(1)}, f32[64,160]{1,0:T(8,128)S(1)}, u32[]{:S(2)}, u32[]{:S(2)}) collective-permute-start(f32[64,160]{1,0:T(8,128)S(1)} %get-tuple-element.39.refs_8_), channel_id=1, source_target_pairs={{0,4},{4,0},{1,5},{5,1},{2,6},{6,2},{3,7},{7,3},{8,12},{12,8},{9,1... | collective-permute-start | bytes 122888 | tf_op jit(solution)/shard_map/ppermute | solution.py:406
